TPU v7x, 256 devices: a whole 4x4x8 slice. The times are simulated.
256 devices in a mesh: rows: 32 (over z_lo, y, core), rep: 8 (over x, z_hi).
Axes of the slice: x: 4, y: 4, z: 8 (z_hi: 2, z_lo: 4; z = z_hi * 4 + z_lo), core: 2. Of those that a mesh axis runs over, the one named last changes fastest.
Arguments:
- features: bfloat16 [16384, 256], P('rows'), may hold values from -6 to 6
- weight: bfloat16 [256, 256], replicated, may hold values from -0.375 to 0.375
- cotangent: bfloat16 [16384, 256], P(('rows', 'rep')), may hold values from -6 to 6
- tile_values: bfloat16 [32, 32, 2, 128, 128], P('rows', 'rep'), may hold values from -1 to 1
- tile_slots: int32 [32, 32, 2], P('rows', 'rep'), may hold values from 0 to 15, as said below
- tile_count: int32 [32, 32], P('rows', 'rep'), may hold values from 1 to 2, as said below
Outputs:
- output: bfloat16 [16384, 256], P(('rows', 'rep'))
- grad_weight: float32 [256, 256], replicated
- grad_features: bfloat16 [16384, 256], P('rows')
Inputs may be any that keep to these rules, and one draw needn't show every extreme that they name: `tile_slots`: for each block pair, 2 distinct positions (tile row times 4 plus tile column); only the first tile_count of them are live. `tile_count`: 2 in at least one block pair.
All inputs are finite; a program needn't handle non-finite values.
Results may differ from a plain program's by a relative error of at most 0.0059.
Values may be sent and summed in bfloat16 or wider, within the bound.
No kernel may reach another device: no remote copies, remote signals or barrier semaphores. Data moves between devices by JAX's collectives and lax.ppermute only.
A program may use at most 64 MiB of HBM per device.

v0:
```python
import jax
import jax.numpy as jnp
from jax import lax
from jax.sharding import PartitionSpec as P


def from_root(value, axis, source):
    kept = jnp.where(lax.axis_index(axis) == source, value, 0).astype(value.dtype)
    return lax.psum(kept, axis)


def spread_forward(feature_panel, values, slot_ids, live_tiles):
    tile_size = values.shape[-1]
    feature_width = feature_panel.shape[1]
    tile_total = feature_panel.shape[0] // tile_size
    tile_rows = slot_ids // tile_total
    tile_cols = slot_ids % tile_total
    blocks = feature_panel.reshape(tile_total, tile_size, feature_width)[tile_cols]
    products = jnp.einsum("kab,kbf->kaf", values, blocks, preferred_element_type=jnp.float32)
    keep_mask = (jnp.arange(slot_ids.shape[0]) < live_tiles).astype(jnp.float32)
    products = products * keep_mask[:, None, None]
    summed = (
        jnp.zeros((tile_total, tile_size, feature_width), jnp.float32).at[tile_rows].add(products)
    )
    return summed.reshape(tile_total * tile_size, feature_width)


def spread_backward(grad_panel, values, slot_ids, live_tiles):
    tile_size = values.shape[-1]
    feature_width = grad_panel.shape[1]
    tile_total = grad_panel.shape[0] // tile_size
    tile_rows = slot_ids // tile_total
    tile_cols = slot_ids % tile_total
    blocks = grad_panel.reshape(tile_total, tile_size, feature_width)[tile_rows]
    products = jnp.einsum("kab,kaf->kbf", values, blocks, preferred_element_type=jnp.float32)
    keep_mask = (jnp.arange(slot_ids.shape[0]) < live_tiles).astype(jnp.float32)
    products = products * keep_mask[:, None, None]
    summed = (
        jnp.zeros((tile_total, tile_size, feature_width), jnp.float32).at[tile_cols].add(products)
    )
    return summed.reshape(tile_total * tile_size, feature_width)


def on_device(features, weight, cotangent, tile_values, tile_slots, tile_count):
    row_index = lax.axis_index("rows")
    rep_index = lax.axis_index("rep")
    section_count = lax.axis_size("rows") // lax.axis_size("rep")
    local_values = tile_values[0]
    local_slots = tile_slots[0]
    local_counts = tile_count[0]

    def forward_section(section_index, accum_sum):
        feature_panel = from_root(features, "rows", rep_index * section_count + section_index)
        values = lax.dynamic_index_in_dim(local_values, section_index, 0, keepdims=False)
        slot_ids = lax.dynamic_index_in_dim(local_slots, section_index, 0, keepdims=False)
        live_tiles = lax.dynamic_index_in_dim(local_counts, section_index, 0, keepdims=False)
        return accum_sum + spread_forward(feature_panel, values, slot_ids, live_tiles)

    accum_sum = lax.fori_loop(
        0, section_count, forward_section, jnp.zeros(features.shape, jnp.float32)
    )
    shares = lax.psum_scatter(accum_sum, "rep", scatter_dimension=0, tiled=True)
    aggregate = shares.astype(jnp.bfloat16)
    preact = jnp.dot(aggregate, weight, preferred_element_type=jnp.float32)
    gates = jax.nn.sigmoid(preact)
    output = (preact * gates).astype(jnp.bfloat16)
    grad_pre = (cotangent.astype(jnp.float32) * gates * (1.0 + preact * (1.0 - gates))).astype(
        jnp.bfloat16
    )
    weight_terms = jnp.einsum("na,nb->ab", aggregate, grad_pre, preferred_element_type=jnp.float32)
    grad_weight = lax.psum(weight_terms, ("rows", "rep"))
    grad_share = jnp.einsum(
        "nb,ab->na", grad_pre, weight, preferred_element_type=jnp.float32
    ).astype(jnp.bfloat16)
    grad_agg = lax.all_gather(grad_share, "rep", axis=0, tiled=True)

    def backward_section(section_index):
        values = lax.dynamic_index_in_dim(local_values, section_index, 0, keepdims=False)
        slot_ids = lax.dynamic_index_in_dim(local_slots, section_index, 0, keepdims=False)
        live_tiles = lax.dynamic_index_in_dim(local_counts, section_index, 0, keepdims=False)
        return spread_backward(grad_agg, values, slot_ids, live_tiles)

    contribs = lax.map(backward_section, jnp.arange(section_count))
    totals = lax.psum(contribs, "rows")
    own_part = lax.dynamic_index_in_dim(
        totals, row_index % section_count, 0, keepdims=False
    ).astype(jnp.bfloat16)
    grad_features = from_root(own_part, "rep", row_index // section_count)
    return (output, grad_weight, grad_features)


def solution(mesh):
    placed = (
        P("rows", None),
        P(),
        P(("rows", "rep"), None),
        P("rows", "rep", None, None, None),
        P("rows", "rep", None),
        P("rows", "rep"),
    )
    return jax.shard_map(
        on_device,
        mesh=mesh,
        in_specs=placed,
        out_specs=(P(("rows", "rep"), None), P(), P("rows", None)),
        check_vma=False,
    )
```

profile of v0, /device:TPU:32, one launch (start us, length us, event | category | flops | bytes accessed | tf_op | source)
XLA Modules:
  0.0 1658.9 jit_solution(14470283140375087136)
XLA Ops:
  8.8 1109.8 %while.29 = (s32[]{:T(128)}, f32[512,256]{1,0:T(8,128)S(1)}, s32[4,2]{1,0:T(4,128)S(1)}, bf16[4,2,128,128]{3,2,1,0:T(8,128)(2,1)}, s32[]{:T(128)}, /*index=5*/bf...) while((s32[]{:T(128)}, f32[512,256]{1,0:T(8,128)S(1)}, ...), condition=%wide.region_3.4_spmd.clone, body=%wide.region_0.3_spmd.clone.sunk | while | flops 17433668 | bytes 5706077 | solution.py:59
  9.6 1.2 dynamic_slice.109
  11.6 264.6 %all-reduce.9.cloned.1.call-done = bf16[4,128,256]{2,1,0:T(8,128)(2,1)} async-done(((bf16[4,128,256]{2,1,0:T(8,128)(2,1)}), bf16[4,128,256]{2,1,0:T(8,128)(2,1)}) %all-reduce.9.cloned.1.call-update) | async-done | bytes 262160 | tf_op jit(solution)/shard_map/while/body/eval_jaxpr/psum | solution.py:9
  276.2 1.5 gather_fusion.1
  280.4 1.2 dynamic_slice.109
  282.4 273.5 %all-reduce.9.cloned.1.call-done = bf16[4,128,256]{2,1,0:T(8,128)(2,1)} async-done(((bf16[4,128,256]{2,1,0:T(8,128)(2,1)}), bf16[4,128,256]{2,1,0:T(8,128)(2,1)}) %all-reduce.9.cloned.1.call-update) | async-done | bytes 262160 | tf_op jit(solution)/shard_map/while/body/eval_jaxpr/psum | solution.py:9
  555.9 1.5 gather_fusion.1
  560.2 1.2 dynamic_slice.109
  562.1 273.7 %all-reduce.9.cloned.1.call-done = bf16[4,128,256]{2,1,0:T(8,128)(2,1)} async-done(((bf16[4,128,256]{2,1,0:T(8,128)(2,1)}), bf16[4,128,256]{2,1,0:T(8,128)(2,1)}) %all-reduce.9.cloned.1.call-update) | async-done | bytes 262160 | tf_op jit(solution)/shard_map/while/body/eval_jaxpr/psum | solution.py:9
  835.8 1.5 gather_fusion.1
  840.0 1.2 dynamic_slice.109
  842.0 273.2 %all-reduce.9.cloned.1.call-done = bf16[4,128,256]{2,1,0:T(8,128)(2,1)} async-done(((bf16[4,128,256]{2,1,0:T(8,128)(2,1)}), bf16[4,128,256]{2,1,0:T(8,128)(2,1)}) %all-reduce.9.cloned.1.call-update) | async-done | bytes 262160 | tf_op jit(solution)/shard_map/while/body/eval_jaxpr/psum | solution.py:9
  1115.2 1.5 gather_fusion.1
  1119.5 98.5 %reduce-scatter.2.cloned.1.call-done = f32[64,256]{1,0:T(8,128)} async-done(((f32[512,256]{1,0:T(8,128)}), f32[64,256]{1,0:T(8,128)}) %reduce-scatter.2.cloned.1.call-update) | async-done | bytes 65552 | tf_op jit(solution)/shard_map/reduce_scatter | solution.py:62
  1218.0 1.6 multiply_convert_fusion.1
  1219.8 44.7 %all_gather.3 = bf16[512,256]{1,0:T(8,128)(2,1)S(1)} all-gather(bf16[64,256]{1,0:T(8,128)(2,1)S(1)} %convolution_convert_fusion), channel_id=1, replica_groups=mesh['rows'=32,'rep'=8] {'rep'}, dimensions={0}, use_global_device_ids=true | all-gather | bytes 294912 | tf_op jit(solution)/shard_map/all_gather | solution.py:75
  1264.6 27.7 %while.28 = (s32[]{:T(128)}, f32[4,512,256]{2,1,0:T(8,128)S(1)}, s32[4]{0:T(128)S(1)}, s32[4,2]{1,0:T(4,128)S(1)}, bf16[4,2,128,128]{3,2,1,0:T(8,128)(2,1)}, /*i...) while((s32[]{:T(128)}, f32[4,512,256]{2,1,0:T(8,128)S(1)}, ...), condition=%wide.region_8.9_spmd, body=%wide.region_6.8_spmd.sunk | while | flops 16909372 | bytes 3084555 | solution.py:83
  1267.7 1.2 dynamic_slice.106
  1274.6 1.2 dynamic_slice.106
  1293.3 134.6 %all-reduce.10 = bf16[4,512,256]{2,1,0:T(8,128)(2,1)S(1)} all-reduce(f32[4,512,256]{2,1,0:T(8,128)S(1)} %get-tuple-element.278), channel_id=1, replica_groups=mesh['rows'=32,'rep'=8] {'rows'}, use_global_device_ids=true, to_apply=%region_9.10 | all-reduce | flops 524288 | bytes 3145728 | tf_op jit(solution)/shard_map/psum | solution.py:84
  1428.6 109.4 %all-reduce.5.cloned.1.call-done = f32[256,256]{1,0:T(8,128)} async-done(((f32[256,256]{1,0:T(8,128)}), f32[256,256]{1,0:T(8,128)}) %all-reduce.5.cloned.1.call-update) | async-done | bytes 262160 | tf_op jit(solution)/shard_map/psum | solution.py:71
  1538.0 110.2 %all-reduce.7.cloned.1.call-done = bf16[512,256]{1,0:T(8,128)(2,1)} async-done(((bf16[512,256]{1,0:T(8,128)(2,1)}), bf16[512,256]{1,0:T(8,128)(2,1)}) %all-reduce.7.cloned.1.call-update) | async-done | bytes 262160 | tf_op jit(solution)/shard_map/psum | solution.py:9
  1648.2 1.7 copy.33
  1649.9 1.7 copy.34
  (107 shorter events, 34.0 us)
Async XLA Ops:
  8.0 1210.0 %copy-start = (bf16[256,256]{1,0:T(8,128)(2,1)S(1)}, bf16[256,256]{1,0:T(8,128)(2,1)}, u32[]{:S(2)}) copy-start(bf16[256,256]{1,0:T(8,128)(2,1)} %param.11) | copy-start | bytes 393220
  8.8 1210.8 %copy-start.3 = (bf16[64,256]{1,0:T(8,128)(2,1)S(1)}, bf16[64,256]{1,0:T(8,128)(2,1)}, u32[]{:S(2)}) copy-start(bf16[64,256]{1,0:T(8,128)(2,1)} %param.12) | copy-start | bytes 98308
  8.8 267.3 %all-reduce.9.cloned.1.call-start = ((), (), s32[]{:S(2)}) async-start(), calls=%async_computation.4 | async-start | bytes 524288 | tf_op jit(solution)/shard_map/while/body/eval_jaxpr/psum | solution.py:9
  279.6 276.3 %all-reduce.9.cloned.1.call-start = ((), (), s32[]{:S(2)}) async-start(), calls=%async_computation.4 | async-start | bytes 524288 | tf_op jit(solution)/shard_map/while/body/eval_jaxpr/psum | solution.py:9
  559.3 276.4 %all-reduce.9.cloned.1.call-start = ((), (), s32[]{:S(2)}) async-start(), calls=%async_computation.4 | async-start | bytes 524288 | tf_op jit(solution)/shard_map/while/body/eval_jaxpr/psum | solution.py:9
  839.2 276.0 %all-reduce.9.cloned.1.call-start = ((), (), s32[]{:S(2)}) async-start(), calls=%async_computation.4 | async-start | bytes 524288 | tf_op jit(solution)/shard_map/while/body/eval_jaxpr/psum | solution.py:9
  1118.6 0.8 copy-start.1
  1118.6 99.4 %reduce-scatter.2.cloned.1.call-start = ((), (), s32[]{:S(2)}) async-start(), calls=%async_computation.1 | async-start | bytes 589824 | tf_op jit(solution)/shard_map/reduce_scatter | solution.py:62
  1119.4 418.6 %all-reduce.5.cloned.1.call-start = ((), (), s32[]{:S(2)}) async-start(), calls=%async_computation.2 | async-start | bytes 524288 | tf_op jit(solution)/shard_map/psum | solution.py:71
  1264.6 27.7 %copy-start.2 = (f32[64,256]{1,0:T(8,128)S(1)}, f32[64,256]{1,0:T(8,128)}, u32[]{:S(2)}) copy-start(f32[64,256]{1,0:T(8,128)} %reduce-scatter.2.cloned.1.call-done) | copy-start | bytes 196612
  1293.2 355.0 %all-reduce.7.cloned.1.call-start = ((), (), s32[]{:S(2)}) async-start(), calls=%async_computation.3 | async-start | bytes 524288 | tf_op jit(solution)/shard_map/psum | solution.py:9
Sparse Core Ops, SparseCore 0:
  12.8 263.2 all-reduce.8
  283.6 272.2 all-reduce.8
  563.4 272.3 all-reduce.8
  842.9 272.2 all-reduce.8
Sparse Core Ops, SparseCore 1:
  1123.0 95.0 reduce-scatter.1
  1293.3 244.7 all-reduce.4
  1541.3 106.9 all-reduce.6
where the time goes:
time: 1660 us
  waiting for transfers between devices  1400 us (84%)
  blocking collectives  179 us (11%)
  local copies, waits for them, and re-layouts  25.9 us (2%)
    psum x5, waiting for transfers between devices, from_root(): return lax.psum(kept, axis)  1200 us
    psum x1, blocking collectives, on_device(): totals = lax.psum(contribs, 'rows')  135 us
    psum x1, waiting for transfers between devices, on_device(): grad_weight = lax.psum(weight_terms, ('rows', 'rep'))  109 us
    reduce_scatter x1, waiting for transfers between devices, on_device(): shares = lax.psum_scatter(accum_sum, 'rep', scatter_dimension=0, tiled=True)  98.5 us
    all_gather x1, blocking collectives, on_device(): grad_agg = lax.all_gather(grad_share, 'rep', axis=0, tiled=True)  44.7 us
  transfers between devices with their start and end apart: 7, of which 7 were waited for; matrix products, arithmetic and copies ran while one was open for 1% of the time, Pallas kernels for 0%

commit v1 on v0

v1 whole, which is shorter than its diff:
```python
import itertools

import jax
import jax.numpy as jnp
from jax import lax
from jax.experimental import pallas as pl
from jax.experimental.pallas import tpu as pltpu
from jax.sharding import PartitionSpec as P

BF = jnp.bfloat16
F32 = jnp.float32
TILE = 128
WIDTH = 256
BLOCK = 512
PART = 128
SLICE = 64
AXES = ("rows", "rep")


def u_of(y):
    return (y ^ (y >> 1)) & 1


def v_of(y):
    return y >> 1


Y_OF = {(u_of(y), v_of(y)): y for y in range(4)}
PLACES = list(itertools.product(range(4), range(4), range(2), range(4), range(2)))


def index_of(z, y, c, x, h):
    return (z * 8 + y * 2 + c) * 8 + x * 2 + h


def pairs(target):
    return [(index_of(*place), index_of(*target(*place))) for place in PLACES]


FLIP_C = pairs(lambda z, y, c, x, h: (z, y, 1 - c, x, h))
FLIP_U = pairs(lambda z, y, c, x, h: (z, Y_OF[1 - u_of(y), v_of(y)], c, x, h))
FLIP_V = pairs(lambda z, y, c, x, h: (z, Y_OF[u_of(y), 1 - v_of(y)], c, x, h))
FLIP_H = pairs(lambda z, y, c, x, h: (z, y, c, x, 1 - h))
FLIP_X = [pairs(lambda z, y, c, x, h, k=k: (z, y, c, x ^ k, h)) for k in (1, 2, 3)]
FLIP_Z = [pairs(lambda z, y, c, x, h, k=k: (z ^ k, y, c, x, h)) for k in (1, 2, 3)]
TO_COLUMN = pairs(lambda z, y, c, x, h: (x, Y_OF[y & 1, h], c, z, y >> 1))
TO_ROW = [(there, here) for here, there in TO_COLUMN]


def send(value, route):
    return lax.ppermute(value, AXES, route)


def place():
    r = lax.axis_index("rows")
    p = lax.axis_index("rep")
    y = (r >> 1) & 3
    v = y >> 1
    return dict(z=r >> 3, c=r & 1, u=(y ^ v) & 1, v=v, x=p >> 1, h=p & 1)


def at(index, size):
    return pl.ds(pl.multiple_of(index * size, size), size)


def dot(a, b, dims=((1,), (0,))):
    return lax.dot_general(a, b, (dims, ((), ())), preferred_element_type=F32)


def call(body, outs, *args, scalars=0, scratch=()):
    spaces = [pltpu.SMEM] * scalars + [pltpu.VMEM] * (len(args) - scalars)
    return pl.pallas_call(
        body,
        out_shape=[jax.ShapeDtypeStruct(shape, dtype) for shape, dtype in outs],
        in_specs=[pl.BlockSpec(memory_space=space) for space in spaces],
        out_specs=[pl.BlockSpec(memory_space=pltpu.VMEM)] * len(outs),
        scratch_shapes=list(scratch),
        compiler_params=pltpu.CompilerParams(vmem_limit_bytes=16 * 2**20),
    )(*args)


def split(value):
    high = value.astype(BF)
    return high, (value - high.astype(F32)).astype(BF)


def put_split(ref, start, value):
    high, low = split(value)
    ref[start : start + SLICE, :] = high
    ref[start + SLICE : start + 2 * SLICE, :] = low


def get_split(ref, start):
    return ref[start : start + SLICE, :].astype(F32) + ref[start + SLICE : start + 2 * SLICE, :].astype(F32)


def live_tile(slots, count, tiles, b, s):
    slot = slots[b * 2 + s]
    tile = jnp.where(s < count[b], tiles[b * 2 + s], jnp.zeros((), BF))
    return tile, slot >> 2, slot & 3


def forward_body(slots, count, tiles, f0, f1, f2, f3, to1, to2, to3, own, total):
    me = place()
    total[...] = jnp.zeros_like(total)
    for k, block in enumerate((f0, f1, f2, f3)):
        b = (me["u"] * 2 + me["c"]) ^ k
        for s in range(2):
            tile, tile_row, tile_col = live_tile(slots, count, tiles, b, s)
            total[at(tile_row, TILE), :] += dot(tile, block[at(tile_col, TILE), :])
    own[...] = total[at(me["x"], PART), :]
    for k, to in ((1, to1), (2, to2), (3, to3)):
        to[...] = total[at(me["x"] ^ k, PART), :].astype(BF)


def sum_body(own, r1, r2, r3, out):
    out[...] = own[...] + r1[...].astype(F32) + (r2[...].astype(F32) + r3[...].astype(F32))


def layer_body(mine, other, weight, cot, cot_other, output, message):
    me = place()
    aggregate = (mine[...] + other[...]).astype(BF)
    preact = dot(aggregate, weight[...])
    gates = jax.nn.sigmoid(preact)
    activation = (preact * gates).astype(BF)
    first = me["h"] == 0
    output[...] = jnp.where(first, activation[:SLICE], activation[SLICE:])
    a, b = cot[...], cot_other[...]
    cotangent = jnp.concatenate([jnp.where(first, a, b), jnp.where(first, b, a)], axis=0).astype(F32)
    message[0:PART, :] = aggregate
    message[PART:, :] = (cotangent * gates * (1.0 + preact * (1.0 - gates))).astype(BF)


def backward_body(slots, count, tiles, weight, m0, m1, m2, m3, to_c, keep, keep_w, aggregate, grad_pre, grad_agg, grad_w):
    me = place()
    for k, m in enumerate((m0, m1, m2, m3)):
        rows = at(me["x"] ^ k, PART)
        aggregate[rows, :] = m[0:PART, :]
        grad_pre[rows, :] = m[PART:, :]
    grad_agg[...] = dot(grad_pre[...], weight[...], ((1,), (1,))).astype(BF)
    grad_w[...] = dot(aggregate[...], grad_pre[...], ((0,), (0,)))
    share = grad_w[at(me["x"], SLICE), :]
    keep_w[...] = share
    to_c[2 * BLOCK :, :] = share
    for k, (ref, start) in enumerate(((keep, 0), (to_c, 0), (keep, BLOCK), (to_c, BLOCK))):
        b = (me["u"] * 2 + me["c"]) ^ k
        ref[start : start + BLOCK, :] = jnp.zeros((BLOCK, WIDTH), F32)
        for s in range(2):
            tile, tile_row, tile_col = live_tile(slots, count, tiles, b, s)
            rows = pl.ds(pl.multiple_of(start + tile_col * TILE, TILE), TILE)
            ref[rows, :] += dot(tile, grad_agg[at(tile_row, TILE), :], ((0,), (0,)))


def after_c_body(keep, keep_w, got, to_u, own, own_w):
    own[...] = keep[0:BLOCK, :] + got[0:BLOCK, :]
    to_u[0:BLOCK, :] = (keep[BLOCK:, :] + got[BLOCK : 2 * BLOCK, :]).astype(BF)
    share = keep_w[...] + got[2 * BLOCK :, :]
    put_split(to_u, BLOCK, share)
    own_w[...] = share


def after_u_body(own, own_w, got, to1, to2, to3, kept, kept_w, total):
    me = place()
    total[...] = own[...] + got[0:BLOCK, :].astype(F32)
    high, low = split(own_w[...])
    share = (high.astype(F32) + low.astype(F32)) + get_split(got, BLOCK)
    kept[...] = total[at(me["z"], PART), :]
    kept_w[...] = share
    for k, to in ((1, to1), (2, to2), (3, to3)):
        to[0:PART, :] = total[at(me["z"] ^ k, PART), :].astype(BF)
        put_split(to, PART, share)


def after_z_body(kept, kept_w, r1, r2, r3, to_v):
    total = kept[...] + r1[0:PART, :].astype(F32)
    to_v[0:PART, :] = total + (r2[0:PART, :].astype(F32) + r3[0:PART, :].astype(F32))
    high, low = split(kept_w[...])
    share = (high.astype(F32) + low.astype(F32)) + get_split(r1, PART)
    to_v[PART:, :] = share + (get_split(r2, PART) + get_split(r3, PART))


def after_v_body(mine, got, piece, share):
    piece[...] = (mine[0:PART, :] + got[0:PART, :]).astype(BF)
    put_split(share, 0, mine[PART:, :] + got[PART:, :])


def finish_body(p0, p1, p2, p3, w0, w1, w2, w3, grad_features, grad_weight):
    me = place()
    for k, (piece, share) in enumerate(((p0, w0), (p1, w1), (p2, w2), (p3, w3))):
        grad_features[at(me["x"] ^ k, PART), :] = piece[...]
        grad_weight[at(me["x"] ^ k, SLICE), :] = get_split(share, 0)


def on_device(features, weight, cotangent, tile_values, tile_slots, tile_count):
    tiles = tile_values.reshape(8, TILE, TILE)
    slots = tile_slots.reshape(8)
    count = tile_count.reshape(4)

    f0 = send(features, TO_COLUMN)
    cot_other = send(cotangent, FLIP_H)
    f2 = send(f0, FLIP_U)
    f1 = send(f0, FLIP_C)
    f3 = send(f2, FLIP_C)
    part = ((PART, WIDTH), BF)
    part32 = ((PART, WIDTH), F32)
    share32 = ((SLICE, WIDTH), F32)
    *to, own = call(
        forward_body, [part, part, part, part32], slots, count, tiles, f0, f1, f2, f3,
        scalars=2, scratch=[pltpu.VMEM((BLOCK, WIDTH), F32)],
    )
    got = [send(value, route) for value, route in zip(to, FLIP_X)]
    (mine,) = call(sum_body, [part32], own, *got)
    other = send(mine, FLIP_H)
    output, message = call(
        layer_body, [((SLICE, WIDTH), BF), ((2 * PART, WIDTH), BF)], mine, other, weight, cotangent, cot_other
    )
    got = [send(message, route) for route in FLIP_X]
    to_c, keep, keep_w = call(
        backward_body,
        [((2 * BLOCK + SLICE, WIDTH), F32), ((2 * BLOCK, WIDTH), F32), share32],
        slots, count, tiles, weight, message, *got,
        scalars=2,
        scratch=[
            pltpu.VMEM((BLOCK, WIDTH), BF),
            pltpu.VMEM((BLOCK, WIDTH), BF),
            pltpu.VMEM((BLOCK, WIDTH), BF),
            pltpu.VMEM((WIDTH, WIDTH), F32),
        ],
    )
    got = send(to_c, FLIP_C)
    to_u, own, own_w = call(
        after_c_body, [((BLOCK + 2 * SLICE, WIDTH), BF), ((BLOCK, WIDTH), F32), share32], keep, keep_w, got
    )
    got = send(to_u, FLIP_U)
    to_z = ((PART + 2 * SLICE, WIDTH), BF)
    *to, kept, kept_w = call(
        after_u_body, [to_z, to_z, to_z, part32, share32], own, own_w, got,
        scratch=[pltpu.VMEM((BLOCK, WIDTH), F32)],
    )
    got = [send(value, route) for value, route in zip(to, FLIP_Z)]
    (to_v,) = call(after_z_body, [((PART + SLICE, WIDTH), F32)], kept, kept_w, *got)
    got = send(to_v, FLIP_V)
    piece, share = call(after_v_body, [part, ((2 * SLICE, WIDTH), BF)], to_v, got)
    piece = send(piece, TO_ROW)
    shares = [share] + [send(share, route) for route in FLIP_X]
    pieces = [piece] + [send(piece, route) for route in FLIP_X]
    grad_features, grad_weight = call(
        finish_body, [((BLOCK, WIDTH), BF), ((WIDTH, WIDTH), F32)], *pieces, *shares
    )
    return output, grad_weight, grad_features


def solution(mesh):
    placed = (
        P("rows", None),
        P(),
        P(("rows", "rep"), None),
        P("rows", "rep", None, None, None),
        P("rows", "rep", None),
        P("rows", "rep"),
    )
    return jax.shard_map(
        on_device,
        mesh=mesh,
        in_specs=placed,
        out_specs=(P(("rows", "rep"), None), P(), P("rows", None)),
        check_vma=False,
    )
```

time: 1660 us -> 137 us (0.08)
  waiting for transfers between devices: 1400 us -> 85.2 us
  blocking collectives: 179 us -> 0 us
  starting transfers between devices: 0.26 us -> 41.9 us
  local copies, waits for them, and re-layouts: 25.9 us -> 2.47 us
    psum x6 -> x0, waiting for transfers between devices: 1300 us -> none  [the longest x5 1200 us: from_root(): return lax.psum(kept, axis)]
    psum x1 -> x0, blocking collectives: 135 us -> none  [on_device(): totals = lax.psum(contribs, 'rows')]
    reduce_scatter x1 -> x0, waiting for transfers between devices: 98.5 us -> none  [on_device(): shares = lax.psum_scatter(accum_sum, 'rep', scatter_dimension=0, tiled=True)]
    ppermute x0 -> x25, waiting for transfers between devices: none -> 85.2 us  [send(): return lax.ppermute(value, AXES, route)]
    all_gather x1 -> x0, blocking collectives: 44.7 us -> none  [on_device(): grad_agg = lax.all_gather(grad_share, 'rep', axis=0, tiled=True)]
    ppermute x0 -> x25, starting transfers between devices: none -> 41.9 us  [send(): return lax.ppermute(value, AXES, route)]
  transfers between devices with their start and end apart: 7 -> 25, of which waited for: 7 -> 18; matrix products, arithmetic and copies ran while one was open for 1% -> 1% of each run, Pallas kernels for 0% -> 0%
where the time goes in v1:
time: 137 us; the launch traced here: 135 us
  waiting for transfers between devices  85.2 us (62%)
  starting transfers between devices  41.9 us (31%)
  Pallas kernels  4.28 us (3%)
  local copies, waits for them, and re-layouts  2.47 us (2%)
    ppermute x25, waiting for transfers between devices, send(): return lax.ppermute(value, AXES, route)  85.2 us
    ppermute x25, starting transfers between devices, send(): return lax.ppermute(value, AXES, route)  41.9 us
    pallas_call x9, Pallas kernels, call(): pl.pallas_call(body, out_shape=[jax.ShapeDtypeStruct(shape, dtype) for sh...  4.28 us
  transfers between devices with their start and end apart: 25, of which 18 were waited for; matrix products, arithmetic and copies ran while one was open for 1% of the time, Pallas kernels for 0%

profile of v1, /device:TPU:32, one launch (start us, length us, event | category | flops | bytes accessed | tf_op | source)
XLA Modules:
  0.0 134.6 jit_solution(16523144093254518285)
XLA Ops:
  0.6 2.9 %collective-permute-start = (bf16[512,256]{1,0:T(8,128)(2,1)}, bf16[512,256]{1,0:T(8,128)(2,1)S(1)}, u32[]{:S(2)}, u32[]{:S(2)}) collective-permute-start(bf16[512,256]{1,0:T(8,128)(2,1)} %param.6), channel_id=1, source_target_pairs={{0,0},{1,48},{2,64},{3,112},{4,128},{5,176},{6,192},{7,240},{8,8},... | collective-permute-start | bytes 786440 | tf_op jit(solution)/shard_map/ppermute | solution.py:51
  3.6 26.7 %collective-permute-done.f0 = bf16[512,256]{1,0:T(8,128)(2,1)S(1)} collective-permute-done((bf16[512,256]{1,0:T(8,128)(2,1)}, bf16[512,256]{1,0:T(8,128)(2,1)S(1)}, u32[]{:S(2)}, u32[]{:S(2)}) %collective-permute-start) | collective-permute-done | bytes 262176 | tf_op jit(solution)/shard_map/ppermute | solution.py:51
  30.3 1.6 %collective-permute-start.2 = (bf16[512,256]{1,0:T(8,128)(2,1)S(1)}, bf16[512,256]{1,0:T(8,128)(2,1)S(1)}, u32[]{:S(2)}, u32[]{:S(2)}) collective-permute-start(bf16[512,256]{1,0:T(8,128)(2,1)S(1)} %collective-permute-done.f0), channel_id=1, source_target_pairs={{0,16},{1,17},{2,18},{3,19},{4,20},{5,21},{6,22},{7,23},{8,24},{9,... | collective-permute-start | bytes 786440 | tf_op jit(solution)/shard_map/ppermute | solution.py:51
  31.8 4.8 %collective-permute-done.2.f2 = bf16[512,256]{1,0:T(8,128)(2,1)S(1)} collective-permute-done((bf16[512,256]{1,0:T(8,128)(2,1)S(1)}, bf16[512,256]{1,0:T(8,128)(2,1)S(1)}, u32[]{:S(2)}, u32[]{:S(2)}) %collective-permute-start.2) | collective-permute-done | bytes 262176 | tf_op jit(solution)/shard_map/ppermute | solution.py:51
  40.8 5.9 %collective-permute-start.5 = (bf16[128,256]{1,0:T(8,128)(2,1)S(1)}, bf16[128,256]{1,0:T(8,128)(2,1)S(1)}, u32[]{:S(2)}, u32[]{:S(2)}) collective-permute-start(bf16[128,256]{1,0:T(8,128)(2,1)S(1)} %get-tuple-element.26), channel_id=1, source_target_pairs={{0,4},{1,5},{2,6},{3,7},{4,0},{5,1},{6,2},{7,3},{8,12},{9,13},{10,... | collective-permute-start | bytes 196616 | tf_op jit(solution)/shard_map/ppermute | solution.py:51
  46.7 3.5 %collective-permute-done.5.r2 = bf16[128,256]{1,0:T(8,128)(2,1)S(1)} collective-permute-done((bf16[128,256]{1,0:T(8,128)(2,1)S(1)}, bf16[128,256]{1,0:T(8,128)(2,1)S(1)}, u32[]{:S(2)}, u32[]{:S(2)}) %collective-permute-start.5) | collective-permute-done | bytes 65568 | tf_op jit(solution)/shard_map/ppermute | solution.py:51
  50.2 2.0 %collective-permute-done.6.r3 = bf16[128,256]{1,0:T(8,128)(2,1)S(1)} collective-permute-done((bf16[128,256]{1,0:T(8,128)(2,1)S(1)}, bf16[128,256]{1,0:T(8,128)(2,1)S(1)}, u32[]{:S(2)}, u32[]{:S(2)}) %collective-permute-start.6) | collective-permute-done | bytes 65568 | tf_op jit(solution)/shard_map/ppermute | solution.py:51
  52.2 6.1 %collective-permute-start.7 = (f32[128,256]{1,0:T(8,128)S(1)}, f32[128,256]{1,0:T(8,128)S(1)}, u32[]{:S(2)}, u32[]{:S(2)}) collective-permute-start(f32[128,256]{1,0:T(8,128)S(1)} %shard_map.86.mine), channel_id=1, source_target_pairs={{0,1},{1,0},{2,3},{3,2},{4,5},{5,4},{6,7},{7,6},{8,9},{9,8},{10,11... | collective-permute-start | bytes 393224 | tf_op jit(solution)/shard_map/ppermute | solution.py:51
  58.4 7.8 %collective-permute-done.8.cot_other = bf16[64,256]{1,0:T(8,128)(2,1)S(1)} collective-permute-done((bf16[64,256]{1,0:T(8,128)(2,1)S(1)}, bf16[64,256]{1,0:T(8,128)(2,1)S(1)}, u32[]{:S(2)}, u32[]{:S(2)}) %collective-permute-start.8) | collective-permute-done | bytes 32800 | tf_op jit(solution)/shard_map/ppermute | solution.py:51
  68.0 3.1 %collective-permute-start.9 = (bf16[256,256]{1,0:T(8,128)(2,1)S(1)}, bf16[256,256]{1,0:T(8,128)(2,1)S(1)}, u32[]{:S(2)}, u32[]{:S(2)}) collective-permute-start(bf16[256,256]{1,0:T(8,128)(2,1)S(1)} %get-tuple-element.29.m0), channel_id=1, source_target_pairs={{0,2},{1,3},{2,0},{3,1},{4,6},{5,7},{6,4},{7,5},{8,10},{9,11},{10,... | collective-permute-start | bytes 393224 | tf_op jit(solution)/shard_map/ppermute | solution.py:51
  71.1 3.5 %collective-permute-done.11.m3 = bf16[256,256]{1,0:T(8,128)(2,1)S(1)} collective-permute-done((bf16[256,256]{1,0:T(8,128)(2,1)S(1)}, bf16[256,256]{1,0:T(8,128)(2,1)S(1)}, u32[]{:S(2)}, u32[]{:S(2)}) %collective-permute-start.11) | collective-permute-done | bytes 131104 | tf_op jit(solution)/shard_map/ppermute | solution.py:51
  77.0 2.7 %collective-permute-done.12.got = f32[1088,256]{1,0:T(8,128)S(1)} collective-permute-done((f32[1088,256]{1,0:T(8,128)S(1)}, f32[1088,256]{1,0:T(8,128)S(1)}, u32[]{:S(2)}, u32[]{:S(2)}) %collective-permute-start.12) | collective-permute-done | bytes 1114144 | tf_op jit(solution)/shard_map/ppermute | solution.py:51
  80.5 9.1 %collective-permute-done.13.got = bf16[640,256]{1,0:T(8,128)(2,1)S(1)} collective-permute-done((bf16[640,256]{1,0:T(8,128)(2,1)S(1)}, bf16[640,256]{1,0:T(8,128)(2,1)S(1)}, u32[]{:S(2)}, u32[]{:S(2)}) %collective-permute-start.13) | collective-permute-done | bytes 327712 | tf_op jit(solution)/shard_map/ppermute | solution.py:51
  89.8 6.2 %collective-permute-start.14 = (bf16[256,256]{1,0:T(8,128)(2,1)S(1)}, bf16[256,256]{1,0:T(8,128)(2,1)S(1)}, u32[]{:S(2)}, u32[]{:S(2)}) collective-permute-start(bf16[256,256]{1,0:T(8,128)(2,1)S(1)} %get-tuple-element.38), channel_id=1, source_target_pairs={{0,64},{1,65},{2,66},{3,67},{4,68},{5,69},{6,70},{7,71},{8,72},{9,... | collective-permute-start | bytes 393224 | tf_op jit(solution)/shard_map/ppermute | solution.py:51
  97.6 2.8 %collective-permute-done.14.r1 = bf16[256,256]{1,0:T(8,128)(2,1)S(1)} collective-permute-done((bf16[256,256]{1,0:T(8,128)(2,1)S(1)}, bf16[256,256]{1,0:T(8,128)(2,1)S(1)}, u32[]{:S(2)}, u32[]{:S(2)}) %collective-permute-start.14) | collective-permute-done | bytes 131104 | tf_op jit(solution)/shard_map/ppermute | solution.py:51
  100.4 4.9 %collective-permute-done.15.r2 = bf16[256,256]{1,0:T(8,128)(2,1)S(1)} collective-permute-done((bf16[256,256]{1,0:T(8,128)(2,1)S(1)}, bf16[256,256]{1,0:T(8,128)(2,1)S(1)}, u32[]{:S(2)}, u32[]{:S(2)}) %collective-permute-start.15) | collective-permute-done | bytes 131104 | tf_op jit(solution)/shard_map/ppermute | solution.py:51
  105.3 3.4 %collective-permute-done.16.r3 = bf16[256,256]{1,0:T(8,128)(2,1)S(1)} collective-permute-done((bf16[256,256]{1,0:T(8,128)(2,1)S(1)}, bf16[256,256]{1,0:T(8,128)(2,1)S(1)}, u32[]{:S(2)}, u32[]{:S(2)}) %collective-permute-start.16) | collective-permute-done | bytes 131104 | tf_op jit(solution)/shard_map/ppermute | solution.py:51
  108.8 2.3 %collective-permute-start.17 = (f32[192,256]{1,0:T(8,128)S(1)}, f32[192,256]{1,0:T(8,128)S(1)}, u32[]{:S(2)}, u32[]{:S(2)}) collective-permute-start(f32[192,256]{1,0:T(8,128)S(1)} %shard_map.91.mine), channel_id=1, source_target_pairs={{0,48},{1,49},{2,50},{3,51},{4,52},{5,53},{6,54},{7,55},{8,56},{9,... | collective-permute-start | bytes 589832 | tf_op jit(solution)/shard_map/ppermute | solution.py:51
  111.1 4.7 %collective-permute-done.17.got = f32[192,256]{1,0:T(8,128)S(1)} collective-permute-done((f32[192,256]{1,0:T(8,128)S(1)}, f32[192,256]{1,0:T(8,128)S(1)}, u32[]{:S(2)}, u32[]{:S(2)}) %collective-permute-start.17) | collective-permute-done | bytes 196640 | tf_op jit(solution)/shard_map/ppermute | solution.py:51
  115.8 1.9 %collective-permute-start.18 = (bf16[128,256]{1,0:T(8,128)(2,1)S(1)}, bf16[128,256]{1,0:T(8,128)(2,1)S(1)}, u32[]{:S(2)}, u32[]{:S(2)}) collective-permute-start(bf16[128,256]{1,0:T(8,128)(2,1)S(1)} %get-tuple-element.41), channel_id=1, source_target_pairs={{0,0},{48,1},{64,2},{112,3},{128,4},{176,5},{192,6},{240,7},{8,8},... | collective-permute-start | bytes 196616 | tf_op jit(solution)/shard_map/ppermute | solution.py:51
  117.8 2.7 %collective-permute-start.24 = (bf16[128,256]{1,0:T(8,128)(2,1)S(1)}, bf16[128,256]{1,0:T(8,128)(2,1)S(1)}, u32[]{:S(2)}, u32[]{:S(2)}) collective-permute-start(bf16[128,256]{1,0:T(8,128)(2,1)S(1)} %get-tuple-element.42.w0), channel_id=1, source_target_pairs={{0,6},{1,7},{2,4},{3,5},{4,2},{5,3},{6,0},{7,1},{8,14},{9,15},{10,... | collective-permute-start | bytes 196616 | tf_op jit(solution)/shard_map/ppermute | solution.py:51
  122.0 2.7 %collective-permute-done.18.p0 = bf16[128,256]{1,0:T(8,128)(2,1)S(1)} collective-permute-done((bf16[128,256]{1,0:T(8,128)(2,1)S(1)}, bf16[128,256]{1,0:T(8,128)(2,1)S(1)}, u32[]{:S(2)}, u32[]{:S(2)}) %collective-permute-start.18) | collective-permute-done | bytes 65568 | tf_op jit(solution)/shard_map/ppermute | solution.py:51
  124.7 3.3 %collective-permute-start.21 = (bf16[128,256]{1,0:T(8,128)(2,1)S(1)}, bf16[128,256]{1,0:T(8,128)(2,1)S(1)}, u32[]{:S(2)}, u32[]{:S(2)}) collective-permute-start(bf16[128,256]{1,0:T(8,128)(2,1)S(1)} %collective-permute-done.18.p0), channel_id=1, source_target_pairs={{0,6},{1,7},{2,4},{3,5},{4,2},{5,3},{6,0},{7,1},{8,14},{9,15},{10,... | collective-permute-start | bytes 196616 | tf_op jit(solution)/shard_map/ppermute | solution.py:51
  130.6 3.3 %collective-permute-done.20.p2 = bf16[128,256]{1,0:T(8,128)(2,1)S(1)} collective-permute-done((bf16[128,256]{1,0:T(8,128)(2,1)S(1)}, bf16[128,256]{1,0:T(8,128)(2,1)S(1)}, u32[]{:S(2)}, u32[]{:S(2)}) %collective-permute-start.20) | collective-permute-done | bytes 65568 | tf_op jit(solution)/shard_map/ppermute | solution.py:51
  (49 shorter events, 15.9 us)
Async XLA Ops:
  0.6 29.6 %collective-permute-start = (bf16[512,256]{1,0:T(8,128)(2,1)}, bf16[512,256]{1,0:T(8,128)(2,1)S(1)}, u32[]{:S(2)}, u32[]{:S(2)}) collective-permute-start(bf16[512,256]{1,0:T(8,128)(2,1)} %param.6), channel_id=1, source_target_pairs={{0,0},{1,48},{2,64},{3,112},{4,128},{5,176},{6,192},{7,240},{8,8},... | collective-permute-start | bytes 786440 | tf_op jit(solution)/shard_map/ppermute | solution.py:51
  30.3 6.4 %collective-permute-start.2 = (bf16[512,256]{1,0:T(8,128)(2,1)S(1)}, bf16[512,256]{1,0:T(8,128)(2,1)S(1)}, u32[]{:S(2)}, u32[]{:S(2)}) collective-permute-start(bf16[512,256]{1,0:T(8,128)(2,1)S(1)} %collective-permute-done.f0), channel_id=1, source_target_pairs={{0,16},{1,17},{2,18},{3,19},{4,20},{5,21},{6,22},{7,23},{8,24},{9,... | collective-permute-start | bytes 786440 | tf_op jit(solution)/shard_map/ppermute | solution.py:51
  31.8 5.7 %collective-permute-start.1 = (bf16[512,256]{1,0:T(8,128)(2,1)S(1)}, bf16[512,256]{1,0:T(8,128)(2,1)S(1)}, u32[]{:S(2)}, u32[]{:S(2)}) collective-permute-start(bf16[512,256]{1,0:T(8,128)(2,1)S(1)} %collective-permute-done.f0), channel_id=1, source_target_pairs={{0,8},{1,9},{2,10},{3,11},{4,12},{5,13},{6,14},{7,15},{8,0},{9,1},... | collective-permute-start | bytes 786440 | tf_op jit(solution)/shard_map/ppermute | solution.py:51
  40.7 6.0 %collective-permute-start.4 = (bf16[128,256]{1,0:T(8,128)(2,1)S(1)}, bf16[128,256]{1,0:T(8,128)(2,1)S(1)}, u32[]{:S(2)}, u32[]{:S(2)}) collective-permute-start(bf16[128,256]{1,0:T(8,128)(2,1)S(1)} %get-tuple-element.25), channel_id=1, source_target_pairs={{0,2},{1,3},{2,0},{3,1},{4,6},{5,7},{6,4},{7,5},{8,10},{9,11},{10,... | collective-permute-start | bytes 196616 | tf_op jit(solution)/shard_map/ppermute | solution.py:51
  40.8 9.4 %collective-permute-start.5 = (bf16[128,256]{1,0:T(8,128)(2,1)S(1)}, bf16[128,256]{1,0:T(8,128)(2,1)S(1)}, u32[]{:S(2)}, u32[]{:S(2)}) collective-permute-start(bf16[128,256]{1,0:T(8,128)(2,1)S(1)} %get-tuple-element.26), channel_id=1, source_target_pairs={{0,4},{1,5},{2,6},{3,7},{4,0},{5,1},{6,2},{7,3},{8,12},{9,13},{10,... | collective-permute-start | bytes 196616 | tf_op jit(solution)/shard_map/ppermute | solution.py:51
  46.7 5.5 %collective-permute-start.6 = (bf16[128,256]{1,0:T(8,128)(2,1)S(1)}, bf16[128,256]{1,0:T(8,128)(2,1)S(1)}, u32[]{:S(2)}, u32[]{:S(2)}) collective-permute-start(bf16[128,256]{1,0:T(8,128)(2,1)S(1)} %get-tuple-element.27), channel_id=1, source_target_pairs={{0,6},{1,7},{2,4},{3,5},{4,2},{5,3},{6,0},{7,1},{8,14},{9,15},{10,... | collective-permute-start | bytes 196616 | tf_op jit(solution)/shard_map/ppermute | solution.py:51
  52.2 14.0 %collective-permute-start.7 = (f32[128,256]{1,0:T(8,128)S(1)}, f32[128,256]{1,0:T(8,128)S(1)}, u32[]{:S(2)}, u32[]{:S(2)}) collective-permute-start(f32[128,256]{1,0:T(8,128)S(1)} %shard_map.86.mine), channel_id=1, source_target_pairs={{0,1},{1,0},{2,3},{3,2},{4,5},{5,4},{6,7},{7,6},{8,9},{9,8},{10,11... | collective-permute-start | bytes 393224 | tf_op jit(solution)/shard_map/ppermute | solution.py:51
  58.3 7.9 %collective-permute-start.8 = (bf16[64,256]{1,0:T(8,128)(2,1)S(1)}, bf16[64,256]{1,0:T(8,128)(2,1)S(1)}, u32[]{:S(2)}, u32[]{:S(2)}) collective-permute-start(bf16[64,256]{1,0:T(8,128)(2,1)S(1)} %copy-done.3), channel_id=1, source_target_pairs={{0,1},{1,0},{2,3},{3,2},{4,5},{5,4},{6,7},{7,6},{8,9},{9,8},{10,11... | collective-permute-start | bytes 98312 | tf_op jit(solution)/shard_map/ppermute | solution.py:51
  67.0 7.6 %collective-permute-start.11 = (bf16[256,256]{1,0:T(8,128)(2,1)S(1)}, bf16[256,256]{1,0:T(8,128)(2,1)S(1)}, u32[]{:S(2)}, u32[]{:S(2)}) collective-permute-start(bf16[256,256]{1,0:T(8,128)(2,1)S(1)} %get-tuple-element.29.m0), channel_id=1, source_target_pairs={{0,6},{1,7},{2,4},{3,5},{4,2},{5,3},{6,0},{7,1},{8,14},{9,15},{10,... | collective-permute-start | bytes 393224 | tf_op jit(solution)/shard_map/ppermute | solution.py:51
  67.3 7.3 %collective-permute-start.10 = (bf16[256,256]{1,0:T(8,128)(2,1)S(1)}, bf16[256,256]{1,0:T(8,128)(2,1)S(1)}, u32[]{:S(2)}, u32[]{:S(2)}) collective-permute-start(bf16[256,256]{1,0:T(8,128)(2,1)S(1)} %get-tuple-element.29.m0), channel_id=1, source_target_pairs={{0,4},{1,5},{2,6},{3,7},{4,0},{5,1},{6,2},{7,3},{8,12},{9,13},{10,... | collective-permute-start | bytes 393224 | tf_op jit(solution)/shard_map/ppermute | solution.py:51
  68.0 7.4 %collective-permute-start.9 = (bf16[256,256]{1,0:T(8,128)(2,1)S(1)}, bf16[256,256]{1,0:T(8,128)(2,1)S(1)}, u32[]{:S(2)}, u32[]{:S(2)}) collective-permute-start(bf16[256,256]{1,0:T(8,128)(2,1)S(1)} %get-tuple-element.29.m0), channel_id=1, source_target_pairs={{0,2},{1,3},{2,0},{3,1},{4,6},{5,7},{6,4},{7,5},{8,10},{9,11},{10,... | collective-permute-start | bytes 393224 | tf_op jit(solution)/shard_map/ppermute | solution.py:51
  76.9 2.8 %collective-permute-start.12 = (f32[1088,256]{1,0:T(8,128)S(1)}, f32[1088,256]{1,0:T(8,128)S(1)}, u32[]{:S(2)}, u32[]{:S(2)}) collective-permute-start(f32[1088,256]{1,0:T(8,128)S(1)} %get-tuple-element.32), channel_id=1, source_target_pairs={{0,8},{1,9},{2,10},{3,11},{4,12},{5,13},{6,14},{7,15},{8,0},{9,1},... | collective-permute-start | bytes 3342344 | tf_op jit(solution)/shard_map/ppermute | solution.py:51
  79.8 9.8 %collective-permute-start.13 = (bf16[640,256]{1,0:T(8,128)(2,1)S(1)}, bf16[640,256]{1,0:T(8,128)(2,1)S(1)}, u32[]{:S(2)}, u32[]{:S(2)}) collective-permute-start(bf16[640,256]{1,0:T(8,128)(2,1)S(1)} %get-tuple-element.35), channel_id=1, source_target_pairs={{0,16},{1,17},{2,18},{3,19},{4,20},{5,21},{6,22},{7,23},{8,24},{9,... | collective-permute-start | bytes 983048 | tf_op jit(solution)/shard_map/ppermute | solution.py:51
  89.8 10.6 %collective-permute-start.14 = (bf16[256,256]{1,0:T(8,128)(2,1)S(1)}, bf16[256,256]{1,0:T(8,128)(2,1)S(1)}, u32[]{:S(2)}, u32[]{:S(2)}) collective-permute-start(bf16[256,256]{1,0:T(8,128)(2,1)S(1)} %get-tuple-element.38), channel_id=1, source_target_pairs={{0,64},{1,65},{2,66},{3,67},{4,68},{5,69},{6,70},{7,71},{8,72},{9,... | collective-permute-start | bytes 393224 | tf_op jit(solution)/shard_map/ppermute | solution.py:51
  96.0 9.3 %collective-permute-start.15 = (bf16[256,256]{1,0:T(8,128)(2,1)S(1)}, bf16[256,256]{1,0:T(8,128)(2,1)S(1)}, u32[]{:S(2)}, u32[]{:S(2)}) collective-permute-start(bf16[256,256]{1,0:T(8,128)(2,1)S(1)} %get-tuple-element.39), channel_id=1, source_target_pairs={{0,128},{1,129},{2,130},{3,131},{4,132},{5,133},{6,134},{7,135},{8... | collective-permute-start | bytes 393224 | tf_op jit(solution)/shard_map/ppermute | solution.py:51
  96.0 12.7 %collective-permute-start.16 = (bf16[256,256]{1,0:T(8,128)(2,1)S(1)}, bf16[256,256]{1,0:T(8,128)(2,1)S(1)}, u32[]{:S(2)}, u32[]{:S(2)}) collective-permute-start(bf16[256,256]{1,0:T(8,128)(2,1)S(1)} %get-tuple-element.40), channel_id=1, source_target_pairs={{0,192},{1,193},{2,194},{3,195},{4,196},{5,197},{6,198},{7,199},{8... | collective-permute-start | bytes 393224 | tf_op jit(solution)/shard_map/ppermute | solution.py:51
  108.8 7.0 %collective-permute-start.17 = (f32[192,256]{1,0:T(8,128)S(1)}, f32[192,256]{1,0:T(8,128)S(1)}, u32[]{:S(2)}, u32[]{:S(2)}) collective-permute-start(f32[192,256]{1,0:T(8,128)S(1)} %shard_map.91.mine), channel_id=1, source_target_pairs={{0,48},{1,49},{2,50},{3,51},{4,52},{5,53},{6,54},{7,55},{8,56},{9,... | collective-permute-start | bytes 589832 | tf_op jit(solution)/shard_map/ppermute | solution.py:51
  115.8 8.9 %collective-permute-start.18 = (bf16[128,256]{1,0:T(8,128)(2,1)S(1)}, bf16[128,256]{1,0:T(8,128)(2,1)S(1)}, u32[]{:S(2)}, u32[]{:S(2)}) collective-permute-start(bf16[128,256]{1,0:T(8,128)(2,1)S(1)} %get-tuple-element.41), channel_id=1, source_target_pairs={{0,0},{48,1},{64,2},{112,3},{128,4},{176,5},{192,6},{240,7},{8,8},... | collective-permute-start | bytes 196616 | tf_op jit(solution)/shard_map/ppermute | solution.py:51
  117.8 10.3 %collective-permute-start.24 = (bf16[128,256]{1,0:T(8,128)(2,1)S(1)}, bf16[128,256]{1,0:T(8,128)(2,1)S(1)}, u32[]{:S(2)}, u32[]{:S(2)}) collective-permute-start(bf16[128,256]{1,0:T(8,128)(2,1)S(1)} %get-tuple-element.42.w0), channel_id=1, source_target_pairs={{0,6},{1,7},{2,4},{3,5},{4,2},{5,3},{6,0},{7,1},{8,14},{9,15},{10,... | collective-permute-start | bytes 196616 | tf_op jit(solution)/shard_map/ppermute | solution.py:51
  120.5 8.4 %collective-permute-start.23 = (bf16[128,256]{1,0:T(8,128)(2,1)S(1)}, bf16[128,256]{1,0:T(8,128)(2,1)S(1)}, u32[]{:S(2)}, u32[]{:S(2)}) collective-permute-start(bf16[128,256]{1,0:T(8,128)(2,1)S(1)} %get-tuple-element.42.w0), channel_id=1, source_target_pairs={{0,4},{1,5},{2,6},{3,7},{4,0},{5,1},{6,2},{7,3},{8,12},{9,13},{10,... | collective-permute-start | bytes 196616 | tf_op jit(solution)/shard_map/ppermute | solution.py:51
  120.5 8.8 %collective-permute-start.22 = (bf16[128,256]{1,0:T(8,128)(2,1)S(1)}, bf16[128,256]{1,0:T(8,128)(2,1)S(1)}, u32[]{:S(2)}, u32[]{:S(2)}) collective-permute-start(bf16[128,256]{1,0:T(8,128)(2,1)S(1)} %get-tuple-element.42.w0), channel_id=1, source_target_pairs={{0,2},{1,3},{2,0},{3,1},{4,6},{5,7},{6,4},{7,5},{8,10},{9,11},{10,... | collective-permute-start | bytes 196616 | tf_op jit(solution)/shard_map/ppermute | solution.py:51
  124.7 5.8 %collective-permute-start.21 = (bf16[128,256]{1,0:T(8,128)(2,1)S(1)}, bf16[128,256]{1,0:T(8,128)(2,1)S(1)}, u32[]{:S(2)}, u32[]{:S(2)}) collective-permute-start(bf16[128,256]{1,0:T(8,128)(2,1)S(1)} %collective-permute-done.18.p0), channel_id=1, source_target_pairs={{0,6},{1,7},{2,4},{3,5},{4,2},{5,3},{6,0},{7,1},{8,14},{9,15},{10,... | collective-permute-start | bytes 196616 | tf_op jit(solution)/shard_map/ppermute | solution.py:51
  128.0 5.8 %collective-permute-start.20 = (bf16[128,256]{1,0:T(8,128)(2,1)S(1)}, bf16[128,256]{1,0:T(8,128)(2,1)S(1)}, u32[]{:S(2)}, u32[]{:S(2)}) collective-permute-start(bf16[128,256]{1,0:T(8,128)(2,1)S(1)} %collective-permute-done.18.p0), channel_id=1, source_target_pairs={{0,4},{1,5},{2,6},{3,7},{4,0},{5,1},{6,2},{7,3},{8,12},{9,13},{10,... | collective-permute-start | bytes 196616 | tf_op jit(solution)/shard_map/ppermute | solution.py:51
  128.0 5.8 %collective-permute-start.19 = (bf16[128,256]{1,0:T(8,128)(2,1)S(1)}, bf16[128,256]{1,0:T(8,128)(2,1)S(1)}, u32[]{:S(2)}, u32[]{:S(2)}) collective-permute-start(bf16[128,256]{1,0:T(8,128)(2,1)S(1)} %collective-permute-done.18.p0), channel_id=1, source_target_pairs={{0,2},{1,3},{2,0},{3,1},{4,6},{5,7},{6,4},{7,5},{8,10},{9,11},{10,... | collective-permute-start | bytes 196616 | tf_op jit(solution)/shard_map/ppermute | solution.py:51
  (7 other events, 119.4 us)

commit v2 on v1

v2 whole, which is shorter than its diff:
```python
import itertools

import jax
import jax.numpy as jnp
from jax import lax
from jax.experimental import pallas as pl
from jax.experimental.pallas import tpu as pltpu
from jax.sharding import PartitionSpec as P

BF = jnp.bfloat16
F32 = jnp.float32
TILE = 128
WIDTH = 256
BLOCK = 512
PART = 128
SLICE = 64
AXES = ("rows", "rep")


def u_of(y):
    return (y ^ (y >> 1)) & 1


def v_of(y):
    return y >> 1


Y_OF = {(u_of(y), v_of(y)): y for y in range(4)}
PLACES = list(itertools.product(range(4), range(4), range(2), range(4), range(2)))


def index_of(z, y, c, x, h):
    return (z * 8 + y * 2 + c) * 8 + x * 2 + h


def pairs(target):
    return [(index_of(*place), index_of(*target(*place))) for place in PLACES]


FLIP_C = pairs(lambda z, y, c, x, h: (z, y, 1 - c, x, h))
FLIP_U = pairs(lambda z, y, c, x, h: (z, Y_OF[1 - u_of(y), v_of(y)], c, x, h))
FLIP_V = pairs(lambda z, y, c, x, h: (z, Y_OF[u_of(y), 1 - v_of(y)], c, x, h))
FLIP_H = pairs(lambda z, y, c, x, h: (z, y, c, x, 1 - h))
FLIP_X = [pairs(lambda z, y, c, x, h, k=k: (z, y, c, x ^ k, h)) for k in (1, 2, 3)]
FLIP_Z = [pairs(lambda z, y, c, x, h, k=k: (z ^ k, y, c, x, h)) for k in (1, 2, 3)]
ROUTE = (((2, 1, 3, 0), (0, 3, 2, 1), (2, 1, 0, 3), (3, 0, 2, 1)), ((0, 1, 3, 2), (0, 1, 2, 3), (0, 1, 2, 3), (1, 0, 2, 3)))
TO_ROW = pairs(lambda z, y, c, x, h: (x, Y_OF[u_of(y), h], c, ROUTE[v_of(y) == h][x][z], 1 - v_of(y)))
TO_COLUMN = [(there, here) for here, there in TO_ROW]


def chunk_table(same):
    word = sum((z << (8 * x + 2 * ROUTE[same][x][z])) for x in range(4) for z in range(4))
    return word - (1 << 32) if word >> 31 else word


CHUNKS = (chunk_table(0), chunk_table(1))


def send(value, route):
    return lax.ppermute(value, AXES, route)


def place():
    r = lax.axis_index("rows")
    p = lax.axis_index("rep")
    y = (r >> 1) & 3
    v = y >> 1
    return dict(z=r >> 3, c=r & 1, u=(y ^ v) & 1, v=v, x=p >> 1, h=p & 1)


def chunk_of(me, x):
    word = jnp.where((1 - me["h"]) == me["v"], jnp.int32(CHUNKS[1]), jnp.int32(CHUNKS[0]))
    return (word >> (8 * me["z"] + 2 * x)) & 3


def at(index, size):
    return pl.ds(pl.multiple_of(index * size, size), size)


def dot(a, b, dims=((1,), (0,))):
    return lax.dot_general(a, b, (dims, ((), ())), preferred_element_type=F32)


SMEM = pl.BlockSpec(memory_space=pltpu.SMEM)
VMEM = pl.BlockSpec(memory_space=pltpu.VMEM)
HBM = pl.BlockSpec(memory_space=pl.ANY)


def call(body, outs, *args, specs=None, scratch=()):
    return pl.pallas_call(
        body,
        out_shape=[jax.ShapeDtypeStruct(shape, dtype) for shape, dtype in outs],
        in_specs=specs or [VMEM] * len(args),
        out_specs=[VMEM] * len(outs),
        scratch_shapes=list(scratch),
        compiler_params=pltpu.CompilerParams(vmem_limit_bytes=24 * 2**20),
    )(*args)


def split(value):
    high = value.astype(BF)
    return high, (value - high.astype(F32)).astype(BF)


def put_split(ref, start, value):
    high, low = split(value)
    ref[start : start + SLICE, :] = high
    ref[start + SLICE : start + 2 * SLICE, :] = low


def get_split(ref, start):
    return ref[start : start + SLICE, :].astype(F32) + ref[start + SLICE : start + 2 * SLICE, :].astype(F32)


def chunk_body(features, out, sem):
    me = place()
    copy = pltpu.make_async_copy(features.at[at(chunk_of(me, me["x"]), PART), :], out, sem)
    copy.start()
    copy.wait()


def dense_body(slots, count, tiles, dense, dense_t):
    me = place()
    dense[...] = jnp.zeros_like(dense)
    dense_t[...] = jnp.zeros_like(dense_t)
    for k in range(4):
        b = ((me["u"] ^ me["h"]) * 2 + me["c"]) ^ k
        for s in range(2):
            slot = slots[0, b, s]
            tile = jnp.where(s < count[0, b], tiles[0, b, s], jnp.zeros((), BF))

            @pl.when(s < count[0, b])
            def _():
                dense[k, at(slot >> 2, TILE), at(slot & 3, TILE)] = tile
                dense_t[k, at(slot & 3, TILE), at(slot >> 2, TILE)] = tile.T


def block_body(p0, p1, p2, p3, block):
    me = place()
    for k, piece in enumerate((p0, p1, p2, p3)):
        block[at(me["z"] ^ k, PART), :] = piece[...]


def forward_body(dense, f0, f1, f2, f3, to1, to2, to3, own, total):
    me = place()
    total[...] = dot(dense[0], f0[...]) + dot(dense[1], f1[...]) + dot(dense[2], f2[...]) + dot(dense[3], f3[...])
    for k, to in enumerate((own, to1, to2, to3)):
        to[...] = total[at(me["x"] ^ k, PART), :]


def sum_body(own, r1, r2, r3, out):
    out[...] = own[...] + r1[...] + (r2[...] + r3[...])


def layer_body(mine, other, weight, cot, cot_other, output, message):
    me = place()
    aggregate = (mine[...] + other[...]).astype(BF)
    preact = dot(aggregate, weight[...])
    gates = jax.nn.sigmoid(preact)
    activation = (preact * gates).astype(BF)
    first = me["h"] == 0
    output[...] = jnp.where(first, activation[:SLICE], activation[SLICE:])
    a, b = cot[...], cot_other[...]
    cotangent = jnp.concatenate([jnp.where(first, a, b), jnp.where(first, b, a)], axis=0).astype(F32)
    message[0:PART, :] = aggregate
    message[PART:, :] = (cotangent * gates * (1.0 + preact * (1.0 - gates))).astype(BF)


def backward_body(dense_t, weight, m0, m1, m2, m3, to_c, aggregate, grad_pre, grad_agg):
    me = place()
    for k, m in enumerate((m0, m1, m2, m3)):
        rows = at(me["x"] ^ k, PART)
        aggregate[rows, :] = m[0:PART, :]
        grad_pre[rows, :] = m[PART:, :]
    grad = dot(grad_pre[...], weight[...], ((1,), (1,))).astype(BF)
    grad_agg[...] = grad
    to_c[0:BLOCK, :] = dot(dense_t[1], grad)
    to_c[BLOCK:, :] = dot(dense_t[3], grad)


def kept_body(dense_t, aggregate, grad_pre, grad_agg, keep, share, grad_w):
    me = place()
    grad_w[...] = dot(aggregate[...], grad_pre[...], ((0,), (0,)))
    share[...] = grad_w[at(me["x"], SLICE), :]
    grad = grad_agg[...]
    keep[0:BLOCK, :] = dot(dense_t[0], grad)
    keep[BLOCK:, :] = dot(dense_t[2], grad)


def after_c_body(keep, got, keep_w, got_w, to_u, own, own_w):
    own[...] = keep[0:BLOCK, :] + got[0:BLOCK, :]
    to_u[0:BLOCK, :] = (keep[BLOCK:, :] + got[BLOCK:, :]).astype(BF)
    share = keep_w[...] + got_w[...]
    put_split(to_u, BLOCK, share)
    own_w[...] = share


def after_u_body(own, own_w, got, to1, to2, to3, kept, kept_w, total):
    me = place()
    total[...] = own[...] + got[0:BLOCK, :].astype(F32)
    high, low = split(own_w[...])
    share = ((high.astype(F32) + low.astype(F32)) + get_split(got, BLOCK)).astype(BF)
    kept[...] = total[at(me["z"], PART), :]
    kept_w[...] = share
    for k, to in ((1, to1), (2, to2), (3, to3)):
        to[0:PART, :] = total[at(me["z"] ^ k, PART), :].astype(BF)
        to[PART:, :] = share


def after_z_body(kept, kept_w, r1, r2, r3, to_v):
    total = kept[...] + r1[0:PART, :].astype(F32)
    to_v[0:PART, :] = total + (r2[0:PART, :].astype(F32) + r3[0:PART, :].astype(F32))
    share = kept_w[...].astype(F32) + r1[PART:, :].astype(F32)
    to_v[PART:, :] = share + (r2[PART:, :].astype(F32) + r3[PART:, :].astype(F32))


def after_v_body(mine, got, piece, share):
    piece[...] = (mine[0:PART, :] + got[0:PART, :]).astype(BF)
    put_split(share, 0, mine[PART:, :] + got[PART:, :])


def finish_body(p0, p1, p2, p3, w0, w1, w2, w3, grad_features, grad_weight):
    me = place()
    for k, (piece, share) in enumerate(((p0, w0), (p1, w1), (p2, w2), (p3, w3))):
        grad_features[at(chunk_of(me, me["x"] ^ k), PART), :] = piece[...]
        grad_weight[at(me["x"] ^ k, SLICE), :] = get_split(share, 0)


def on_device(features, weight, cotangent, tile_values, tile_slots, tile_count):
    part = ((PART, WIDTH), BF)
    part32 = ((PART, WIDTH), F32)
    block = ((BLOCK, WIDTH), BF)
    share32 = ((SLICE, WIDTH), F32)
    dense_shape = ((4, BLOCK, BLOCK), BF)

    (chunk,) = call(chunk_body, [part], features, specs=[HBM], scratch=[pltpu.SemaphoreType.DMA])
    chunk = send(chunk, TO_COLUMN)
    cot_other = send(cotangent, FLIP_H)
    dense, dense_t = call(
        dense_body, [dense_shape, dense_shape], tile_slots, tile_count, tile_values, specs=[SMEM, SMEM, VMEM]
    )
    chunk, cot_other, dense, dense_t = lax.optimization_barrier((chunk, cot_other, dense, dense_t))
    (f0,) = call(block_body, [block], chunk, *[send(chunk, route) for route in FLIP_Z])
    f2 = send(f0, FLIP_U)
    f1 = send(f0, FLIP_C)
    f3 = send(f2, FLIP_C)
    *to, own = call(
        forward_body, [part32] * 4, dense, f0, f1, f2, f3, scratch=[pltpu.VMEM((BLOCK, WIDTH), F32)]
    )
    got = [send(value, route) for value, route in zip(to, FLIP_X)]
    (mine,) = call(sum_body, [part32], own, *got)
    other = send(mine, FLIP_H)
    output, message = call(
        layer_body, [((SLICE, WIDTH), BF), ((2 * PART, WIDTH), BF)], mine, other, weight, cotangent, cot_other
    )
    got = [send(message, route) for route in FLIP_X]
    to_c, aggregate, grad_pre, grad_agg = call(
        backward_body, [((2 * BLOCK, WIDTH), F32), block, block, block], dense_t, weight, message, *got
    )
    got = send(to_c, FLIP_C)
    keep, keep_w = call(
        kept_body, [((2 * BLOCK, WIDTH), F32), share32], dense_t, aggregate, grad_pre, grad_agg,
        scratch=[pltpu.VMEM((WIDTH, WIDTH), F32)],
    )
    got_w = send(keep_w, FLIP_C)
    to_u, own, own_w = call(
        after_c_body, [((BLOCK + 2 * SLICE, WIDTH), BF), ((BLOCK, WIDTH), F32), share32], keep, got, keep_w, got_w
    )
    got = send(to_u, FLIP_U)
    to_z = ((PART + SLICE, WIDTH), BF)
    *to, kept, kept_w = call(
        after_u_body, [to_z, to_z, to_z, part32, ((SLICE, WIDTH), BF)], own, own_w, got,
        scratch=[pltpu.VMEM((BLOCK, WIDTH), F32)],
    )
    got = [send(value, route) for value, route in zip(to, FLIP_Z)]
    (to_v,) = call(after_z_body, [((PART + SLICE, WIDTH), F32)], kept, kept_w, *got)
    got = send(to_v, FLIP_V)
    piece, share = call(after_v_body, [part, ((2 * SLICE, WIDTH), BF)], to_v, got)
    piece = send(piece, TO_ROW)
    shares = [share] + [send(share, route) for route in FLIP_X]
    pieces = [piece] + [send(piece, route) for route in FLIP_X]
    grad_features, grad_weight = call(
        finish_body, [((BLOCK, WIDTH), BF), ((WIDTH, WIDTH), F32)], *pieces, *shares
    )
    return output, grad_weight, grad_features


def solution(mesh):
    placed = (
        P("rows", None),
        P(),
        P(("rows", "rep"), None),
        P("rows", "rep", None, None, None),
        P("rows", "rep", None),
        P("rows", "rep"),
    )
    return jax.shard_map(
        on_device,
        mesh=mesh,
        in_specs=placed,
        out_specs=(P(("rows", "rep"), None), P(), P("rows", None)),
        check_vma=False,
    )
```

time: 137 us -> 119 us (0.87); the launches traced: 135 us -> 119 us
  waiting for transfers between devices: 85.2 us -> 60.3 us
  starting transfers between devices: 41.9 us -> 49.1 us
    ppermute x25 -> x29, waiting for transfers between devices: 85.2 us -> 60.3 us  [send(): return lax.ppermute(value, AXES, route)]
    ppermute x25 -> x29, starting transfers between devices: 41.9 us -> 49.1 us  [send(): return lax.ppermute(value, AXES, route)]
    pallas_call x9 -> x13, Pallas kernels: 4.28 us -> 5.39 us  [call(): pl.pallas_call(body, out_shape=[jax.ShapeDtypeStruct(shape, dtype) for sh...]
    unnamed x13 -> x11, local copies, waits for them, and re-layouts: 2.38 us -> 3.32 us
  transfers between devices with their start and end apart: 25 -> 29, of which waited for: 18 -> 22; matrix products, arithmetic and copies ran while one was open for 1% -> 1% of each run, Pallas kernels for 0% -> 2%
where the time goes in v2:
time: 119 us
  waiting for transfers between devices  60.3 us (51%)
  starting transfers between devices  49.1 us (41%)
  Pallas kernels  5.39 us (5%)
  local copies, waits for them, and re-layouts  3.32 us (3%)
    ppermute x29, waiting for transfers between devices, send(): return lax.ppermute(value, AXES, route)  60.3 us
    ppermute x29, starting transfers between devices, send(): return lax.ppermute(value, AXES, route)  49.1 us
    pallas_call x13, Pallas kernels, call(): pl.pallas_call(body, out_shape=[jax.ShapeDtypeStruct(shape, dtype) for sh...  5.39 us
    unnamed x11, local copies, waits for them, and re-layouts  3.32 us
  transfers between devices with their start and end apart: 29, of which 22 were waited for; matrix products, arithmetic and copies ran while one was open for 1% of the time, Pallas kernels for 2%

profile of v2, /device:TPU:32, one launch (start us, length us, event | category | flops | bytes accessed | tf_op | source)
XLA Modules:
  0.0 118.8 jit_solution(9533796062154830149)
XLA Ops:
  1.6 3.6 %collective-permute-start = (bf16[128,256]{1,0:T(8,128)(2,1)S(1)}, bf16[128,256]{1,0:T(8,128)(2,1)S(1)}, u32[]{:S(2)}, u32[]{:S(2)}) collective-permute-start(bf16[128,256]{1,0:T(8,128)(2,1)S(1)} %shard_map.85), channel_id=1, source_target_pairs={{1,0},{53,1},{65,2},{113,3},{129,4},{181,5},{195,6},{247,7},{9,8},... | collective-permute-start | bytes 196616 | tf_op jit(solution)/shard_map/ppermute | solution.py:60
  5.2 2.9 %collective-permute-start.1 = (bf16[64,256]{1,0:T(8,128)(2,1)}, bf16[64,256]{1,0:T(8,128)(2,1)S(1)}, u32[]{:S(2)}, u32[]{:S(2)}) collective-permute-start(bf16[64,256]{1,0:T(8,128)(2,1)} %cot.1), channel_id=1, source_target_pairs={{0,1},{1,0},{2,3},{3,2},{4,5},{5,4},{6,7},{7,6},{8,9},{9,8},{10,11... | collective-permute-start | bytes 98312 | tf_op jit(solution)/shard_map/ppermute | solution.py:60
  13.3 4.0 %collective-permute-start.4 = (bf16[128,256]{1,0:T(8,128)(2,1)S(1)}, bf16[128,256]{1,0:T(8,128)(2,1)S(1)}, u32[]{:S(2)}, u32[]{:S(2)}) collective-permute-start(bf16[128,256]{1,0:T(8,128)(2,1)S(1)} %collective-permute-done.p0), channel_id=1, source_target_pairs={{0,192},{1,193},{2,194},{3,195},{4,196},{5,197},{6,198},{7,199},{8... | collective-permute-start | bytes 196616 | tf_op jit(solution)/shard_map/ppermute | solution.py:60
  17.2 2.2 %collective-permute-start.3 = (bf16[128,256]{1,0:T(8,128)(2,1)S(1)}, bf16[128,256]{1,0:T(8,128)(2,1)S(1)}, u32[]{:S(2)}, u32[]{:S(2)}) collective-permute-start(bf16[128,256]{1,0:T(8,128)(2,1)S(1)} %collective-permute-done.p0), channel_id=1, source_target_pairs={{0,128},{1,129},{2,130},{3,131},{4,132},{5,133},{6,134},{7,135},{8... | collective-permute-start | bytes 196616 | tf_op jit(solution)/shard_map/ppermute | solution.py:60
  19.4 2.0 %collective-permute-done.4.p3 = bf16[128,256]{1,0:T(8,128)(2,1)S(1)} collective-permute-done((bf16[128,256]{1,0:T(8,128)(2,1)S(1)}, bf16[128,256]{1,0:T(8,128)(2,1)S(1)}, u32[]{:S(2)}, u32[]{:S(2)}) %collective-permute-start.4) | collective-permute-done | bytes 65568 | tf_op jit(solution)/shard_map/ppermute | solution.py:60
  23.9 6.3 %collective-permute-done.6.f2 = bf16[512,256]{1,0:T(8,128)(2,1)S(1)} collective-permute-done((bf16[512,256]{1,0:T(8,128)(2,1)S(1)}, bf16[512,256]{1,0:T(8,128)(2,1)S(1)}, u32[]{:S(2)}, u32[]{:S(2)}) %collective-permute-start.6) | collective-permute-done | bytes 262176 | tf_op jit(solution)/shard_map/ppermute | solution.py:60
  33.4 2.2 %collective-permute-start.9 = (f32[128,256]{1,0:T(8,128)S(1)}, f32[128,256]{1,0:T(8,128)S(1)}, u32[]{:S(2)}, u32[]{:S(2)}) collective-permute-start(f32[128,256]{1,0:T(8,128)S(1)} %get-tuple-element.39), channel_id=1, source_target_pairs={{0,4},{1,5},{2,6},{3,7},{4,0},{5,1},{6,2},{7,3},{8,12},{9,13},{10,... | collective-permute-start | bytes 393224 | tf_op jit(solution)/shard_map/ppermute | solution.py:60
  38.9 3.2 %collective-permute-done.9.r2 = f32[128,256]{1,0:T(8,128)S(1)} collective-permute-done((f32[128,256]{1,0:T(8,128)S(1)}, f32[128,256]{1,0:T(8,128)S(1)}, u32[]{:S(2)}, u32[]{:S(2)}) %collective-permute-start.9) | collective-permute-done | bytes 131104 | tf_op jit(solution)/shard_map/ppermute | solution.py:60
  42.1 2.2 %collective-permute-done.10.r3 = f32[128,256]{1,0:T(8,128)S(1)} collective-permute-done((f32[128,256]{1,0:T(8,128)S(1)}, f32[128,256]{1,0:T(8,128)S(1)}, u32[]{:S(2)}, u32[]{:S(2)}) %collective-permute-start.10) | collective-permute-done | bytes 131104 | tf_op jit(solution)/shard_map/ppermute | solution.py:60
  44.3 2.1 %collective-permute-start.11 = (f32[128,256]{1,0:T(8,128)S(1)}, f32[128,256]{1,0:T(8,128)S(1)}, u32[]{:S(2)}, u32[]{:S(2)}) collective-permute-start(f32[128,256]{1,0:T(8,128)S(1)} %shard_map.89.mine), channel_id=1, source_target_pairs={{0,1},{1,0},{2,3},{3,2},{4,5},{5,4},{6,7},{7,6},{8,9},{9,8},{10,11... | collective-permute-start | bytes 393224 | tf_op jit(solution)/shard_map/ppermute | solution.py:60
  46.4 7.1 %collective-permute-done.11.other = f32[128,256]{1,0:T(8,128)S(1)} collective-permute-done((f32[128,256]{1,0:T(8,128)S(1)}, f32[128,256]{1,0:T(8,128)S(1)}, u32[]{:S(2)}, u32[]{:S(2)}) %collective-permute-start.11) | collective-permute-done | bytes 131104 | tf_op jit(solution)/shard_map/ppermute | solution.py:60
  56.5 2.0 %collective-permute-start.12 = (bf16[256,256]{1,0:T(8,128)(2,1)S(1)}, bf16[256,256]{1,0:T(8,128)(2,1)S(1)}, u32[]{:S(2)}, u32[]{:S(2)}) collective-permute-start(bf16[256,256]{1,0:T(8,128)(2,1)S(1)} %get-tuple-element.44.m0), channel_id=1, source_target_pairs={{0,2},{1,3},{2,0},{3,1},{4,6},{5,7},{6,4},{7,5},{8,10},{9,11},{10,... | collective-permute-start | bytes 393224 | tf_op jit(solution)/shard_map/ppermute | solution.py:60
  58.5 2.4 %collective-permute-done.14.m3 = bf16[256,256]{1,0:T(8,128)(2,1)S(1)} collective-permute-done((bf16[256,256]{1,0:T(8,128)(2,1)S(1)}, bf16[256,256]{1,0:T(8,128)(2,1)S(1)}, u32[]{:S(2)}, u32[]{:S(2)}) %collective-permute-start.14) | collective-permute-done | bytes 131104 | tf_op jit(solution)/shard_map/ppermute | solution.py:60
  66.5 4.0 %collective-permute-start.17 = (bf16[640,256]{1,0:T(8,128)(2,1)S(1)}, bf16[640,256]{1,0:T(8,128)(2,1)S(1)}, u32[]{:S(2)}, u32[]{:S(2)}) collective-permute-start(bf16[640,256]{1,0:T(8,128)(2,1)S(1)} %get-tuple-element.53), channel_id=1, source_target_pairs={{0,16},{1,17},{2,18},{3,19},{4,20},{5,21},{6,22},{7,23},{8,24},{9,... | collective-permute-start | bytes 983048 | tf_op jit(solution)/shard_map/ppermute | solution.py:60
  70.4 8.0 %collective-permute-done.17.got = bf16[640,256]{1,0:T(8,128)(2,1)S(1)} collective-permute-done((bf16[640,256]{1,0:T(8,128)(2,1)S(1)}, bf16[640,256]{1,0:T(8,128)(2,1)S(1)}, u32[]{:S(2)}, u32[]{:S(2)}) %collective-permute-start.17) | collective-permute-done | bytes 327712 | tf_op jit(solution)/shard_map/ppermute | solution.py:60
  78.6 4.5 %collective-permute-start.18 = (bf16[192,256]{1,0:T(8,128)(2,1)S(1)}, bf16[192,256]{1,0:T(8,128)(2,1)S(1)}, u32[]{:S(2)}, u32[]{:S(2)}) collective-permute-start(bf16[192,256]{1,0:T(8,128)(2,1)S(1)} %get-tuple-element.56), channel_id=1, source_target_pairs={{0,64},{1,65},{2,66},{3,67},{4,68},{5,69},{6,70},{7,71},{8,72},{9,... | collective-permute-start | bytes 294920 | tf_op jit(solution)/shard_map/ppermute | solution.py:60
  86.4 3.5 %collective-permute-done.19.r2 = bf16[192,256]{1,0:T(8,128)(2,1)S(1)} collective-permute-done((bf16[192,256]{1,0:T(8,128)(2,1)S(1)}, bf16[192,256]{1,0:T(8,128)(2,1)S(1)}, u32[]{:S(2)}, u32[]{:S(2)}) %collective-permute-start.19) | collective-permute-done | bytes 98336 | tf_op jit(solution)/shard_map/ppermute | solution.py:60
  89.9 3.0 %collective-permute-done.20.r3 = bf16[192,256]{1,0:T(8,128)(2,1)S(1)} collective-permute-done((bf16[192,256]{1,0:T(8,128)(2,1)S(1)}, bf16[192,256]{1,0:T(8,128)(2,1)S(1)}, u32[]{:S(2)}, u32[]{:S(2)}) %collective-permute-start.20) | collective-permute-done | bytes 98336 | tf_op jit(solution)/shard_map/ppermute | solution.py:60
  93.0 3.2 %collective-permute-start.21 = (f32[192,256]{1,0:T(8,128)S(1)}, f32[192,256]{1,0:T(8,128)S(1)}, u32[]{:S(2)}, u32[]{:S(2)}) collective-permute-start(f32[192,256]{1,0:T(8,128)S(1)} %shard_map.95.mine), channel_id=1, source_target_pairs={{0,48},{1,49},{2,50},{3,51},{4,52},{5,53},{6,54},{7,55},{8,56},{9,... | collective-permute-start | bytes 589832 | tf_op jit(solution)/shard_map/ppermute | solution.py:60
  96.2 3.8 %collective-permute-done.21.got = f32[192,256]{1,0:T(8,128)S(1)} collective-permute-done((f32[192,256]{1,0:T(8,128)S(1)}, f32[192,256]{1,0:T(8,128)S(1)}, u32[]{:S(2)}, u32[]{:S(2)}) %collective-permute-start.21) | collective-permute-done | bytes 196640 | tf_op jit(solution)/shard_map/ppermute | solution.py:60
  100.0 2.9 %collective-permute-start.22 = (bf16[128,256]{1,0:T(8,128)(2,1)S(1)}, bf16[128,256]{1,0:T(8,128)(2,1)S(1)}, u32[]{:S(2)}, u32[]{:S(2)}) collective-permute-start(bf16[128,256]{1,0:T(8,128)(2,1)S(1)} %get-tuple-element.59), channel_id=1, source_target_pairs={{0,1},{1,53},{2,65},{3,113},{4,129},{5,181},{6,195},{7,247},{8,9},... | collective-permute-start | bytes 196616 | tf_op jit(solution)/shard_map/ppermute | solution.py:60
  102.9 2.2 %collective-permute-start.28 = (bf16[128,256]{1,0:T(8,128)(2,1)S(1)}, bf16[128,256]{1,0:T(8,128)(2,1)S(1)}, u32[]{:S(2)}, u32[]{:S(2)}) collective-permute-start(bf16[128,256]{1,0:T(8,128)(2,1)S(1)} %get-tuple-element.60.w0), channel_id=1, source_target_pairs={{0,6},{1,7},{2,4},{3,5},{4,2},{5,3},{6,0},{7,1},{8,14},{9,15},{10,... | collective-permute-start | bytes 196616 | tf_op jit(solution)/shard_map/ppermute | solution.py:60
  108.7 3.5 %collective-permute-start.25 = (bf16[128,256]{1,0:T(8,128)(2,1)S(1)}, bf16[128,256]{1,0:T(8,128)(2,1)S(1)}, u32[]{:S(2)}, u32[]{:S(2)}) collective-permute-start(bf16[128,256]{1,0:T(8,128)(2,1)S(1)} %collective-permute-done.22.p0), channel_id=1, source_target_pairs={{0,6},{1,7},{2,4},{3,5},{4,2},{5,3},{6,0},{7,1},{8,14},{9,15},{10,... | collective-permute-start | bytes 196616 | tf_op jit(solution)/shard_map/ppermute | solution.py:60
  114.7 3.3 %collective-permute-done.24.p2 = bf16[128,256]{1,0:T(8,128)(2,1)S(1)} collective-permute-done((bf16[128,256]{1,0:T(8,128)(2,1)S(1)}, bf16[128,256]{1,0:T(8,128)(2,1)S(1)}, u32[]{:S(2)}, u32[]{:S(2)}) %collective-permute-start.24) | collective-permute-done | bytes 65568 | tf_op jit(solution)/shard_map/ppermute | solution.py:60
  (58 shorter events, 34.1 us)
Async XLA Ops:
  1.6 11.6 %collective-permute-start = (bf16[128,256]{1,0:T(8,128)(2,1)S(1)}, bf16[128,256]{1,0:T(8,128)(2,1)S(1)}, u32[]{:S(2)}, u32[]{:S(2)}) collective-permute-start(bf16[128,256]{1,0:T(8,128)(2,1)S(1)} %shard_map.85), channel_id=1, source_target_pairs={{1,0},{53,1},{65,2},{113,3},{129,4},{181,5},{195,6},{247,7},{9,8},... | collective-permute-start | bytes 196616 | tf_op jit(solution)/shard_map/ppermute | solution.py:60
  5.2 8.0 %collective-permute-start.1 = (bf16[64,256]{1,0:T(8,128)(2,1)}, bf16[64,256]{1,0:T(8,128)(2,1)S(1)}, u32[]{:S(2)}, u32[]{:S(2)}) collective-permute-start(bf16[64,256]{1,0:T(8,128)(2,1)} %cot.1), channel_id=1, source_target_pairs={{0,1},{1,0},{2,3},{3,2},{4,5},{5,4},{6,7},{7,6},{8,9},{9,8},{10,11... | collective-permute-start | bytes 98312 | tf_op jit(solution)/shard_map/ppermute | solution.py:60
  13.3 8.2 %collective-permute-start.4 = (bf16[128,256]{1,0:T(8,128)(2,1)S(1)}, bf16[128,256]{1,0:T(8,128)(2,1)S(1)}, u32[]{:S(2)}, u32[]{:S(2)}) collective-permute-start(bf16[128,256]{1,0:T(8,128)(2,1)S(1)} %collective-permute-done.p0), channel_id=1, source_target_pairs={{0,192},{1,193},{2,194},{3,195},{4,196},{5,197},{6,198},{7,199},{8... | collective-permute-start | bytes 196616 | tf_op jit(solution)/shard_map/ppermute | solution.py:60
  23.7 6.5 %collective-permute-start.6 = (bf16[512,256]{1,0:T(8,128)(2,1)S(1)}, bf16[512,256]{1,0:T(8,128)(2,1)S(1)}, u32[]{:S(2)}, u32[]{:S(2)}) collective-permute-start(bf16[512,256]{1,0:T(8,128)(2,1)S(1)} %shard_map.87.f0), channel_id=1, source_target_pairs={{0,16},{1,17},{2,18},{3,19},{4,20},{5,21},{6,22},{7,23},{8,24},{9,... | collective-permute-start | bytes 786440 | tf_op jit(solution)/shard_map/ppermute | solution.py:60
  23.9 6.3 %collective-permute-start.5 = (bf16[512,256]{1,0:T(8,128)(2,1)S(1)}, bf16[512,256]{1,0:T(8,128)(2,1)S(1)}, u32[]{:S(2)}, u32[]{:S(2)}) collective-permute-start(bf16[512,256]{1,0:T(8,128)(2,1)S(1)} %shard_map.87.f0), channel_id=1, source_target_pairs={{0,8},{1,9},{2,10},{3,11},{4,12},{5,13},{6,14},{7,15},{8,0},{9,1},... | collective-permute-start | bytes 786440 | tf_op jit(solution)/shard_map/ppermute | solution.py:60
  32.5 6.4 %collective-permute-start.8 = (f32[128,256]{1,0:T(8,128)S(1)}, f32[128,256]{1,0:T(8,128)S(1)}, u32[]{:S(2)}, u32[]{:S(2)}) collective-permute-start(f32[128,256]{1,0:T(8,128)S(1)} %get-tuple-element.38), channel_id=1, source_target_pairs={{0,2},{1,3},{2,0},{3,1},{4,6},{5,7},{6,4},{7,5},{8,10},{9,11},{10,... | collective-permute-start | bytes 393224 | tf_op jit(solution)/shard_map/ppermute | solution.py:60
  33.4 8.7 %collective-permute-start.9 = (f32[128,256]{1,0:T(8,128)S(1)}, f32[128,256]{1,0:T(8,128)S(1)}, u32[]{:S(2)}, u32[]{:S(2)}) collective-permute-start(f32[128,256]{1,0:T(8,128)S(1)} %get-tuple-element.39), channel_id=1, source_target_pairs={{0,4},{1,5},{2,6},{3,7},{4,0},{5,1},{6,2},{7,3},{8,12},{9,13},{10,... | collective-permute-start | bytes 393224 | tf_op jit(solution)/shard_map/ppermute | solution.py:60
  35.6 8.7 %collective-permute-start.10 = (f32[128,256]{1,0:T(8,128)S(1)}, f32[128,256]{1,0:T(8,128)S(1)}, u32[]{:S(2)}, u32[]{:S(2)}) collective-permute-start(f32[128,256]{1,0:T(8,128)S(1)} %get-tuple-element.40), channel_id=1, source_target_pairs={{0,6},{1,7},{2,4},{3,5},{4,2},{5,3},{6,0},{7,1},{8,14},{9,15},{10,... | collective-permute-start | bytes 393224 | tf_op jit(solution)/shard_map/ppermute | solution.py:60
  44.3 9.2 %collective-permute-start.11 = (f32[128,256]{1,0:T(8,128)S(1)}, f32[128,256]{1,0:T(8,128)S(1)}, u32[]{:S(2)}, u32[]{:S(2)}) collective-permute-start(f32[128,256]{1,0:T(8,128)S(1)} %shard_map.89.mine), channel_id=1, source_target_pairs={{0,1},{1,0},{2,3},{3,2},{4,5},{5,4},{6,7},{7,6},{8,9},{9,8},{10,11... | collective-permute-start | bytes 393224 | tf_op jit(solution)/shard_map/ppermute | solution.py:60
  54.4 6.5 %collective-permute-start.14 = (bf16[256,256]{1,0:T(8,128)(2,1)S(1)}, bf16[256,256]{1,0:T(8,128)(2,1)S(1)}, u32[]{:S(2)}, u32[]{:S(2)}) collective-permute-start(bf16[256,256]{1,0:T(8,128)(2,1)S(1)} %get-tuple-element.44.m0), channel_id=1, source_target_pairs={{0,6},{1,7},{2,4},{3,5},{4,2},{5,3},{6,0},{7,1},{8,14},{9,15},{10,... | collective-permute-start | bytes 393224 | tf_op jit(solution)/shard_map/ppermute | solution.py:60
  55.9 6.5 %collective-permute-start.13 = (bf16[256,256]{1,0:T(8,128)(2,1)S(1)}, bf16[256,256]{1,0:T(8,128)(2,1)S(1)}, u32[]{:S(2)}, u32[]{:S(2)}) collective-permute-start(bf16[256,256]{1,0:T(8,128)(2,1)S(1)} %get-tuple-element.44.m0), channel_id=1, source_target_pairs={{0,4},{1,5},{2,6},{3,7},{4,0},{5,1},{6,2},{7,3},{8,12},{9,13},{10,... | collective-permute-start | bytes 393224 | tf_op jit(solution)/shard_map/ppermute | solution.py:60
  56.5 6.3 %collective-permute-start.12 = (bf16[256,256]{1,0:T(8,128)(2,1)S(1)}, bf16[256,256]{1,0:T(8,128)(2,1)S(1)}, u32[]{:S(2)}, u32[]{:S(2)}) collective-permute-start(bf16[256,256]{1,0:T(8,128)(2,1)S(1)} %get-tuple-element.44.m0), channel_id=1, source_target_pairs={{0,2},{1,3},{2,0},{3,1},{4,6},{5,7},{6,4},{7,5},{8,10},{9,11},{10,... | collective-permute-start | bytes 393224 | tf_op jit(solution)/shard_map/ppermute | solution.py:60
  66.5 12.0 %collective-permute-start.17 = (bf16[640,256]{1,0:T(8,128)(2,1)S(1)}, bf16[640,256]{1,0:T(8,128)(2,1)S(1)}, u32[]{:S(2)}, u32[]{:S(2)}) collective-permute-start(bf16[640,256]{1,0:T(8,128)(2,1)S(1)} %get-tuple-element.53), channel_id=1, source_target_pairs={{0,16},{1,17},{2,18},{3,19},{4,20},{5,21},{6,22},{7,23},{8,24},{9,... | collective-permute-start | bytes 983048 | tf_op jit(solution)/shard_map/ppermute | solution.py:60
  78.6 7.8 %collective-permute-start.18 = (bf16[192,256]{1,0:T(8,128)(2,1)S(1)}, bf16[192,256]{1,0:T(8,128)(2,1)S(1)}, u32[]{:S(2)}, u32[]{:S(2)}) collective-permute-start(bf16[192,256]{1,0:T(8,128)(2,1)S(1)} %get-tuple-element.56), channel_id=1, source_target_pairs={{0,64},{1,65},{2,66},{3,67},{4,68},{5,69},{6,70},{7,71},{8,72},{9,... | collective-permute-start | bytes 294920 | tf_op jit(solution)/shard_map/ppermute | solution.py:60
  83.1 6.8 %collective-permute-start.19 = (bf16[192,256]{1,0:T(8,128)(2,1)S(1)}, bf16[192,256]{1,0:T(8,128)(2,1)S(1)}, u32[]{:S(2)}, u32[]{:S(2)}) collective-permute-start(bf16[192,256]{1,0:T(8,128)(2,1)S(1)} %get-tuple-element.57), channel_id=1, source_target_pairs={{0,128},{1,129},{2,130},{3,131},{4,132},{5,133},{6,134},{7,135},{8... | collective-permute-start | bytes 294920 | tf_op jit(solution)/shard_map/ppermute | solution.py:60
  83.1 9.9 %collective-permute-start.20 = (bf16[192,256]{1,0:T(8,128)(2,1)S(1)}, bf16[192,256]{1,0:T(8,128)(2,1)S(1)}, u32[]{:S(2)}, u32[]{:S(2)}) collective-permute-start(bf16[192,256]{1,0:T(8,128)(2,1)S(1)} %get-tuple-element.58), channel_id=1, source_target_pairs={{0,192},{1,193},{2,194},{3,195},{4,196},{5,197},{6,198},{7,199},{8... | collective-permute-start | bytes 294920 | tf_op jit(solution)/shard_map/ppermute | solution.py:60
  93.0 7.0 %collective-permute-start.21 = (f32[192,256]{1,0:T(8,128)S(1)}, f32[192,256]{1,0:T(8,128)S(1)}, u32[]{:S(2)}, u32[]{:S(2)}) collective-permute-start(f32[192,256]{1,0:T(8,128)S(1)} %shard_map.95.mine), channel_id=1, source_target_pairs={{0,48},{1,49},{2,50},{3,51},{4,52},{5,53},{6,54},{7,55},{8,56},{9,... | collective-permute-start | bytes 589832 | tf_op jit(solution)/shard_map/ppermute | solution.py:60
  100.0 8.7 %collective-permute-start.22 = (bf16[128,256]{1,0:T(8,128)(2,1)S(1)}, bf16[128,256]{1,0:T(8,128)(2,1)S(1)}, u32[]{:S(2)}, u32[]{:S(2)}) collective-permute-start(bf16[128,256]{1,0:T(8,128)(2,1)S(1)} %get-tuple-element.59), channel_id=1, source_target_pairs={{0,1},{1,53},{2,65},{3,113},{4,129},{5,181},{6,195},{7,247},{8,9},... | collective-permute-start | bytes 196616 | tf_op jit(solution)/shard_map/ppermute | solution.py:60
  102.9 9.3 %collective-permute-start.28 = (bf16[128,256]{1,0:T(8,128)(2,1)S(1)}, bf16[128,256]{1,0:T(8,128)(2,1)S(1)}, u32[]{:S(2)}, u32[]{:S(2)}) collective-permute-start(bf16[128,256]{1,0:T(8,128)(2,1)S(1)} %get-tuple-element.60.w0), channel_id=1, source_target_pairs={{0,6},{1,7},{2,4},{3,5},{4,2},{5,3},{6,0},{7,1},{8,14},{9,15},{10,... | collective-permute-start | bytes 196616 | tf_op jit(solution)/shard_map/ppermute | solution.py:60
  105.1 8.0 %collective-permute-start.27 = (bf16[128,256]{1,0:T(8,128)(2,1)S(1)}, bf16[128,256]{1,0:T(8,128)(2,1)S(1)}, u32[]{:S(2)}, u32[]{:S(2)}) collective-permute-start(bf16[128,256]{1,0:T(8,128)(2,1)S(1)} %get-tuple-element.60.w0), channel_id=1, source_target_pairs={{0,4},{1,5},{2,6},{3,7},{4,0},{5,1},{6,2},{7,3},{8,12},{9,13},{10,... | collective-permute-start | bytes 196616 | tf_op jit(solution)/shard_map/ppermute | solution.py:60
  106.6 6.5 %collective-permute-start.26 = (bf16[128,256]{1,0:T(8,128)(2,1)S(1)}, bf16[128,256]{1,0:T(8,128)(2,1)S(1)}, u32[]{:S(2)}, u32[]{:S(2)}) collective-permute-start(bf16[128,256]{1,0:T(8,128)(2,1)S(1)} %get-tuple-element.60.w0), channel_id=1, source_target_pairs={{0,2},{1,3},{2,0},{3,1},{4,6},{5,7},{6,4},{7,5},{8,10},{9,11},{10,... | collective-permute-start | bytes 196616 | tf_op jit(solution)/shard_map/ppermute | solution.py:60
  108.7 6.0 %collective-permute-start.25 = (bf16[128,256]{1,0:T(8,128)(2,1)S(1)}, bf16[128,256]{1,0:T(8,128)(2,1)S(1)}, u32[]{:S(2)}, u32[]{:S(2)}) collective-permute-start(bf16[128,256]{1,0:T(8,128)(2,1)S(1)} %collective-permute-done.22.p0), channel_id=1, source_target_pairs={{0,6},{1,7},{2,4},{3,5},{4,2},{5,3},{6,0},{7,1},{8,14},{9,15},{10,... | collective-permute-start | bytes 196616 | tf_op jit(solution)/shard_map/ppermute | solution.py:60
  112.2 5.8 %collective-permute-start.24 = (bf16[128,256]{1,0:T(8,128)(2,1)S(1)}, bf16[128,256]{1,0:T(8,128)(2,1)S(1)}, u32[]{:S(2)}, u32[]{:S(2)}) collective-permute-start(bf16[128,256]{1,0:T(8,128)(2,1)S(1)} %collective-permute-done.22.p0), channel_id=1, source_target_pairs={{0,4},{1,5},{2,6},{3,7},{4,0},{5,1},{6,2},{7,3},{8,12},{9,13},{10,... | collective-permute-start | bytes 196616 | tf_op jit(solution)/shard_map/ppermute | solution.py:60
  112.2 5.8 %collective-permute-start.23 = (bf16[128,256]{1,0:T(8,128)(2,1)S(1)}, bf16[128,256]{1,0:T(8,128)(2,1)S(1)}, u32[]{:S(2)}, u32[]{:S(2)}) collective-permute-start(bf16[128,256]{1,0:T(8,128)(2,1)S(1)} %collective-permute-done.22.p0), channel_id=1, source_target_pairs={{0,2},{1,3},{2,0},{3,1},{4,6},{5,7},{6,4},{7,5},{8,10},{9,11},{10,... | collective-permute-start | bytes 196616 | tf_op jit(solution)/shard_map/ppermute | solution.py:60
  (10 other events, 99.4 us)

commit v3 on v2

--- a/solution.py
+++ b/solution.py
@@ -141,26 +141,31 @@
         block[at(me["z"] ^ k, PART), :] = piece[...]
 
 
-def forward_body(dense, f0, f1, f2, f3, to1, to2, to3, own, total):
+def forward_body(dense, f0, f1, f2, f3, to3, to2, to1, own, total):
     me = place()
     total[...] = dot(dense[0], f0[...]) + dot(dense[1], f1[...]) + dot(dense[2], f2[...]) + dot(dense[3], f3[...])
     for k, to in enumerate((own, to1, to2, to3)):
         to[...] = total[at(me["x"] ^ k, PART), :]
 
 
-def sum_body(own, r1, r2, r3, out):
-    out[...] = own[...] + r1[...] + (r2[...] + r3[...])
-
-
-def layer_body(mine, other, weight, cot, cot_other, output, message):
-    me = place()
-    aggregate = (mine[...] + other[...]).astype(BF)
+def sum_body(own, r3, r2, r1, cot, to_h):
+    total = own[...] + r1[...] + (r2[...] + r3[...])
+    high, low = split(total)
+    to_h[0:PART, :] = high
+    to_h[PART : 2 * PART, :] = low
+    to_h[2 * PART :, :] = cot[...]
+
+
+def layer_body(mine, got, weight, output, message):
+    me = place()
+    parts = [ref[0:PART, :].astype(F32) + ref[PART : 2 * PART, :].astype(F32) for ref in (mine, got)]
+    aggregate = (parts[0] + parts[1]).astype(BF)
     preact = dot(aggregate, weight[...])
     gates = jax.nn.sigmoid(preact)
     activation = (preact * gates).astype(BF)
     first = me["h"] == 0
     output[...] = jnp.where(first, activation[:SLICE], activation[SLICE:])
-    a, b = cot[...], cot_other[...]
+    a, b = mine[2 * PART :, :], got[2 * PART :, :]
     cotangent = jnp.concatenate([jnp.where(first, a, b), jnp.where(first, b, a)], axis=0).astype(F32)
     message[0:PART, :] = aggregate
     message[PART:, :] = (cotangent * gates * (1.0 + preact * (1.0 - gates))).astype(BF)
@@ -174,114 +179,124 @@
         grad_pre[rows, :] = m[PART:, :]
     grad = dot(grad_pre[...], weight[...], ((1,), (1,))).astype(BF)
     grad_agg[...] = grad
-    to_c[0:BLOCK, :] = dot(dense_t[1], grad)
-    to_c[BLOCK:, :] = dot(dense_t[3], grad)
-
-
-def kept_body(dense_t, aggregate, grad_pre, grad_agg, keep, share, grad_w):
-    me = place()
+    to_c[...] = dot(dense_t[3], grad)
+
+
+def kept_body(dense_t, aggregate, grad_pre, grad_agg, to_c, keep_other, keep, share, grad_w):
+    me = place()
+    grad = grad_agg[...]
+    to_c[...] = dot(dense_t[1], grad)
+    keep_other[...] = dot(dense_t[2], grad)
+    keep[...] = dot(dense_t[0], grad)
     grad_w[...] = dot(aggregate[...], grad_pre[...], ((0,), (0,)))
     share[...] = grad_w[at(me["x"], SLICE), :]
-    grad = grad_agg[...]
-    keep[0:BLOCK, :] = dot(dense_t[0], grad)
-    keep[BLOCK:, :] = dot(dense_t[2], grad)
-
-
-def after_c_body(keep, got, keep_w, got_w, to_u, own, own_w):
-    own[...] = keep[0:BLOCK, :] + got[0:BLOCK, :]
-    to_u[0:BLOCK, :] = (keep[BLOCK:, :] + got[BLOCK:, :]).astype(BF)
-    share = keep_w[...] + got_w[...]
-    put_split(to_u, BLOCK, share)
-    own_w[...] = share
-
-
-def after_u_body(own, own_w, got, to1, to2, to3, kept, kept_w, total):
-    me = place()
-    total[...] = own[...] + got[0:BLOCK, :].astype(F32)
-    high, low = split(own_w[...])
-    share = ((high.astype(F32) + low.astype(F32)) + get_split(got, BLOCK)).astype(BF)
-    kept[...] = total[at(me["z"], PART), :]
-    kept_w[...] = share
-    for k, to in ((1, to1), (2, to2), (3, to3)):
-        to[0:PART, :] = total[at(me["z"] ^ k, PART), :].astype(BF)
-        to[PART:, :] = share
-
-
-def after_z_body(kept, kept_w, r1, r2, r3, to_v):
-    total = kept[...] + r1[0:PART, :].astype(F32)
-    to_v[0:PART, :] = total + (r2[0:PART, :].astype(F32) + r3[0:PART, :].astype(F32))
-    share = kept_w[...].astype(F32) + r1[PART:, :].astype(F32)
-    to_v[PART:, :] = share + (r2[PART:, :].astype(F32) + r3[PART:, :].astype(F32))
-
-
-def after_v_body(mine, got, piece, share):
-    piece[...] = (mine[0:PART, :] + got[0:PART, :]).astype(BF)
-    put_split(share, 0, mine[PART:, :] + got[PART:, :])
-
-
-def finish_body(p0, p1, p2, p3, w0, w1, w2, w3, grad_features, grad_weight):
-    me = place()
-    for k, (piece, share) in enumerate(((p0, w0), (p1, w1), (p2, w2), (p3, w3))):
-        grad_features[at(chunk_of(me, me["x"] ^ k), PART), :] = piece[...]
-        grad_weight[at(me["x"] ^ k, SLICE), :] = get_split(share, 0)
+
+
+def to_u_body(keep, got, to3, to2, to1, to0):
+    me = place()
+    for k, to in ((3, to3), (2, to2), (1, to1), (0, to0)):
+        rows = at(me["z"] ^ k, PART)
+        to[...] = (keep[rows, :] + got[rows, :]).astype(BF)
+
+
+def after_c_body(keep, got, keep_w, got_w, s3, s2, s1, s0, share):
+    me = place()
+    for k, part in ((3, s3), (2, s2), (1, s1), (0, s0)):
+        rows = at(me["z"] ^ k, PART)
+        part[...] = keep[rows, :] + got[rows, :]
+    share[...] = (keep_w[...] + got_w[...]).astype(BF)
+
+
+def to_z_body(own, got, share, to):
+    to[0:PART, :] = (own[...] + got[...].astype(F32)).astype(BF)
+    to[PART:, :] = share[...]
+
+
+def after_z_body(own, got, share, r3, r2, r1, to_v, share_z):
+    total = own[...] + got[...].astype(F32) + r1[0:PART, :].astype(F32)
+    to_v[...] = total + (r2[0:PART, :].astype(F32) + r3[0:PART, :].astype(F32))
+    pair = share[...].astype(F32) + r1[PART:, :].astype(F32)
+    share_z[...] = pair + (r2[PART:, :].astype(F32) + r3[PART:, :].astype(F32))
+
+
+def after_v_body(mine, got, piece):
+    piece[...] = (mine[...] + got[...]).astype(BF)
+
+
+def add_body(mine, got, total):
+    total[...] = mine[...] + got[...]
+
+
+def last_body(piece, mine, got, message):
+    message[0:PART, :] = piece[...]
+    put_split(message, PART, mine[...] + got[...])
+
+
+def finish_body(m0, m1, m2, m3, grad_features, grad_weight):
+    me = place()
+    for k, message in enumerate((m0, m1, m2, m3)):
+        grad_features[at(chunk_of(me, me["x"] ^ k), PART), :] = message[0:PART, :]
+        grad_weight[at(me["x"] ^ k, SLICE), :] = get_split(message, PART)
 
 
 def on_device(features, weight, cotangent, tile_values, tile_slots, tile_count):
     part = ((PART, WIDTH), BF)
     part32 = ((PART, WIDTH), F32)
     block = ((BLOCK, WIDTH), BF)
+    block32 = ((BLOCK, WIDTH), F32)
     share32 = ((SLICE, WIDTH), F32)
     dense_shape = ((4, BLOCK, BLOCK), BF)
 
     (chunk,) = call(chunk_body, [part], features, specs=[HBM], scratch=[pltpu.SemaphoreType.DMA])
     chunk = send(chunk, TO_COLUMN)
-    cot_other = send(cotangent, FLIP_H)
     dense, dense_t = call(
         dense_body, [dense_shape, dense_shape], tile_slots, tile_count, tile_values, specs=[SMEM, SMEM, VMEM]
     )
-    chunk, cot_other, dense, dense_t = lax.optimization_barrier((chunk, cot_other, dense, dense_t))
-    (f0,) = call(block_body, [block], chunk, *[send(chunk, route) for route in FLIP_Z])
-    f2 = send(f0, FLIP_U)
+    chunk, dense, dense_t = lax.optimization_barrier((chunk, dense, dense_t))
+    chunks = [chunk] + [send(chunk, route) for route in FLIP_Z]
+    others = [send(value, FLIP_U) for value in chunks]
+    (f0,) = call(block_body, [block], *chunks)
     f1 = send(f0, FLIP_C)
+    (f2,) = call(block_body, [block], *others)
     f3 = send(f2, FLIP_C)
-    *to, own = call(
+    to3, to2, to1, own = call(
         forward_body, [part32] * 4, dense, f0, f1, f2, f3, scratch=[pltpu.VMEM((BLOCK, WIDTH), F32)]
     )
-    got = [send(value, route) for value, route in zip(to, FLIP_X)]
-    (mine,) = call(sum_body, [part32], own, *got)
-    other = send(mine, FLIP_H)
+    got = [send(value, route) for value, route in zip((to3, to2, to1), FLIP_X[::-1])]
+    (mine,) = call(sum_body, [((2 * PART + SLICE, WIDTH), BF)], own, *got, cotangent)
+    got = send(mine, FLIP_H)
     output, message = call(
-        layer_body, [((SLICE, WIDTH), BF), ((2 * PART, WIDTH), BF)], mine, other, weight, cotangent, cot_other
+        layer_body, [((SLICE, WIDTH), BF), ((2 * PART, WIDTH), BF)], mine, got, weight
     )
     got = [send(message, route) for route in FLIP_X]
+
     to_c, aggregate, grad_pre, grad_agg = call(
-        backward_body, [((2 * BLOCK, WIDTH), F32), block, block, block], dense_t, weight, message, *got
+        backward_body, [block32, block, block, block], dense_t, weight, message, *got
+    )
+    got_other = send(to_c, FLIP_C)
+    to_c, keep_other, keep, share = call(
+        kept_body, [block32, block32, block32, share32], dense_t, aggregate, grad_pre, grad_agg,
+        scratch=[pltpu.VMEM((WIDTH, WIDTH), F32)],
     )
     got = send(to_c, FLIP_C)
-    keep, keep_w = call(
-        kept_body, [((2 * BLOCK, WIDTH), F32), share32], dense_t, aggregate, grad_pre, grad_agg,
-        scratch=[pltpu.VMEM((WIDTH, WIDTH), F32)],
-    )
-    got_w = send(keep_w, FLIP_C)
-    to_u, own, own_w = call(
-        after_c_body, [((BLOCK + 2 * SLICE, WIDTH), BF), ((BLOCK, WIDTH), F32), share32], keep, got, keep_w, got_w
-    )
-    got = send(to_u, FLIP_U)
-    to_z = ((PART + SLICE, WIDTH), BF)
-    *to, kept, kept_w = call(
-        after_u_body, [to_z, to_z, to_z, part32, ((SLICE, WIDTH), BF)], own, own_w, got,
-        scratch=[pltpu.VMEM((BLOCK, WIDTH), F32)],
-    )
-    got = [send(value, route) for value, route in zip(to, FLIP_Z)]
-    (to_v,) = call(after_z_body, [((PART + SLICE, WIDTH), F32)], kept, kept_w, *got)
+    got_w = send(share, FLIP_C)
+    to_u = call(to_u_body, [part] * 4, keep_other, got_other)
+    from_u = [send(value, FLIP_U) for value in to_u]
+    *owns, share = call(after_c_body, [part32] * 4 + [((SLICE, WIDTH), BF)], keep, got, share, got_w)
+    from_z = []
+    for own, got, route in zip(owns, from_u, FLIP_Z[::-1]):
+        (to_z,) = call(to_z_body, [((PART + SLICE, WIDTH), BF)], own, got, share)
+        from_z.append(send(to_z, route))
+    to_v, share = call(after_z_body, [part32, share32], owns[3], from_u[3], share, *from_z)
     got = send(to_v, FLIP_V)
-    piece, share = call(after_v_body, [part, ((2 * SLICE, WIDTH), BF)], to_v, got)
+    got_w = send(share, FLIP_U)
+    (piece,) = call(after_v_body, [part], to_v, got)
+    (share,) = call(add_body, [share32], share, got_w)
     piece = send(piece, TO_ROW)
-    shares = [share] + [send(share, route) for route in FLIP_X]
-    pieces = [piece] + [send(piece, route) for route in FLIP_X]
-    grad_features, grad_weight = call(
-        finish_body, [((BLOCK, WIDTH), BF), ((WIDTH, WIDTH), F32)], *pieces, *shares
-    )
+    got_w = send(share, FLIP_V)
+    (message,) = call(last_body, [((PART + 2 * SLICE, WIDTH), BF)], piece, share, got_w)
+    messages = [message] + [send(message, route) for route in FLIP_X]
+    grad_features, grad_weight = call(finish_body, [block, ((WIDTH, WIDTH), F32)], *messages)
     return output, grad_weight, grad_features
 
 

time: 119 us -> 110 us (0.924)
  waiting for transfers between devices: 60.3 us -> 52.8 us
  starting transfers between devices: 49.1 us -> 47.1 us
    ppermute x29 -> x34, waiting for transfers between devices: 60.3 us -> 52.8 us  [send(): return lax.ppermute(value, AXES, route)]
    ppermute x29 -> x34, starting transfers between devices: 49.1 us -> 47.1 us  [send(): return lax.ppermute(value, AXES, route)]
    pallas_call x13 -> x19, Pallas kernels: 5.39 us -> 5.18 us  [call(): pl.pallas_call(body, out_shape=[jax.ShapeDtypeStruct(shape, dtype) for sh...]
  transfers between devices with their start and end apart: 29 -> 34, of which waited for: 22 -> 20; matrix products, arithmetic and copies ran while one was open for 1% -> 1% of each run, Pallas kernels for 2% -> 2%
where the time goes in v3:
time: 110 us; the launch traced here: 109 us
  waiting for transfers between devices  52.8 us (48%)
  starting transfers between devices  47.1 us (43%)
  Pallas kernels  5.18 us (5%)
  local copies, waits for them, and re-layouts  3.32 us (3%)
    ppermute x34, waiting for transfers between devices, send(): return lax.ppermute(value, AXES, route)  52.8 us
    ppermute x34, starting transfers between devices, send(): return lax.ppermute(value, AXES, route)  47.1 us
    pallas_call x19, Pallas kernels, call(): pl.pallas_call(body, out_shape=[jax.ShapeDtypeStruct(shape, dtype) for sh...  5.18 us
    unnamed x11, local copies, waits for them, and re-layouts  3.32 us
  transfers between devices with their start and end apart: 34, of which 20 were waited for; matrix products, arithmetic and copies ran while one was open for 1% of the time, Pallas kernels for 2%

profile of v3, /device:TPU:32, one launch (start us, length us, event | category | flops | bytes accessed | tf_op | source)
XLA Modules:
  0.0 109.2 jit_solution(14385724139793410642)
XLA Ops:
  1.6 3.6 %collective-permute-start = (bf16[128,256]{1,0:T(8,128)(2,1)S(1)}, bf16[128,256]{1,0:T(8,128)(2,1)S(1)}, u32[]{:S(2)}, u32[]{:S(2)}) collective-permute-start(bf16[128,256]{1,0:T(8,128)(2,1)S(1)} %shard_map.85), channel_id=1, source_target_pairs={{1,0},{53,1},{65,2},{113,3},{129,4},{181,5},{195,6},{247,7},{9,8},... | collective-permute-start | bytes 196616 | tf_op jit(solution)/shard_map/ppermute | solution.py:60
  8.7 3.4 %collective-permute-done.p0 = bf16[128,256]{1,0:T(8,128)(2,1)S(1)} collective-permute-done((bf16[128,256]{1,0:T(8,128)(2,1)S(1)}, bf16[128,256]{1,0:T(8,128)(2,1)S(1)}, u32[]{:S(2)}, u32[]{:S(2)}) %collective-permute-start) | collective-permute-done | bytes 65568 | tf_op jit(solution)/shard_map/ppermute | solution.py:60
  13.2 1.9 %collective-permute-start.2 = (bf16[128,256]{1,0:T(8,128)(2,1)S(1)}, bf16[128,256]{1,0:T(8,128)(2,1)S(1)}, u32[]{:S(2)}, u32[]{:S(2)}) collective-permute-start(bf16[128,256]{1,0:T(8,128)(2,1)S(1)} %collective-permute-done.p0), channel_id=1, source_target_pairs={{0,128},{1,129},{2,130},{3,131},{4,132},{5,133},{6,134},{7,135},{8... | collective-permute-start | bytes 196616 | tf_op jit(solution)/shard_map/ppermute | solution.py:60
  17.1 1.9 %collective-permute-done.3.p3 = bf16[128,256]{1,0:T(8,128)(2,1)S(1)} collective-permute-done((bf16[128,256]{1,0:T(8,128)(2,1)S(1)}, bf16[128,256]{1,0:T(8,128)(2,1)S(1)}, u32[]{:S(2)}, u32[]{:S(2)}) %collective-permute-start.3) | collective-permute-done | bytes 65568 | tf_op jit(solution)/shard_map/ppermute | solution.py:60
  27.8 4.1 %collective-permute-start.10 = (f32[128,256]{1,0:T(8,128)S(1)}, f32[128,256]{1,0:T(8,128)S(1)}, u32[]{:S(2)}, u32[]{:S(2)}) collective-permute-start(f32[128,256]{1,0:T(8,128)S(1)} %get-tuple-element.40), channel_id=1, source_target_pairs={{0,6},{1,7},{2,4},{3,5},{4,2},{5,3},{6,0},{7,1},{8,14},{9,15},{10,... | collective-permute-start | bytes 393224 | tf_op jit(solution)/shard_map/ppermute | solution.py:60
  32.9 4.9 %collective-permute-done.10.r3 = f32[128,256]{1,0:T(8,128)S(1)} collective-permute-done((f32[128,256]{1,0:T(8,128)S(1)}, f32[128,256]{1,0:T(8,128)S(1)}, u32[]{:S(2)}, u32[]{:S(2)}) %collective-permute-start.10) | collective-permute-done | bytes 131104 | tf_op jit(solution)/shard_map/ppermute | solution.py:60
  37.8 2.0 %collective-permute-done.11.r2 = f32[128,256]{1,0:T(8,128)S(1)} collective-permute-done((f32[128,256]{1,0:T(8,128)S(1)}, f32[128,256]{1,0:T(8,128)S(1)}, u32[]{:S(2)}, u32[]{:S(2)}) %collective-permute-start.11) | collective-permute-done | bytes 131104 | tf_op jit(solution)/shard_map/ppermute | solution.py:60
  39.9 3.3 %collective-permute-start.13 = (bf16[320,256]{1,0:T(8,128)(2,1)S(1)}, bf16[320,256]{1,0:T(8,128)(2,1)S(1)}, u32[]{:S(2)}, u32[]{:S(2)}) collective-permute-start(bf16[320,256]{1,0:T(8,128)(2,1)S(1)} %shard_map.90.mine), channel_id=1, source_target_pairs={{0,1},{1,0},{2,3},{3,2},{4,5},{5,4},{6,7},{7,6},{8,9},{9,8},{10,11... | collective-permute-start | bytes 491528 | tf_op jit(solution)/shard_map/ppermute | solution.py:60
  43.2 9.1 %collective-permute-done.13.got = bf16[320,256]{1,0:T(8,128)(2,1)S(1)} collective-permute-done((bf16[320,256]{1,0:T(8,128)(2,1)S(1)}, bf16[320,256]{1,0:T(8,128)(2,1)S(1)}, u32[]{:S(2)}, u32[]{:S(2)}) %collective-permute-start.13) | collective-permute-done | bytes 163872 | tf_op jit(solution)/shard_map/ppermute | solution.py:60
  53.1 2.6 %collective-permute-start.16 = (bf16[256,256]{1,0:T(8,128)(2,1)S(1)}, bf16[256,256]{1,0:T(8,128)(2,1)S(1)}, u32[]{:S(2)}, u32[]{:S(2)}) collective-permute-start(bf16[256,256]{1,0:T(8,128)(2,1)S(1)} %get-tuple-element.45.m0), channel_id=1, source_target_pairs={{0,6},{1,7},{2,4},{3,5},{4,2},{5,3},{6,0},{7,1},{8,14},{9,15},{10,... | collective-permute-start | bytes 393224 | tf_op jit(solution)/shard_map/ppermute | solution.py:60
  57.2 3.5 %collective-permute-done.16.m3 = bf16[256,256]{1,0:T(8,128)(2,1)S(1)} collective-permute-done((bf16[256,256]{1,0:T(8,128)(2,1)S(1)}, bf16[256,256]{1,0:T(8,128)(2,1)S(1)}, u32[]{:S(2)}, u32[]{:S(2)}) %collective-permute-start.16) | collective-permute-done | bytes 131104 | tf_op jit(solution)/shard_map/ppermute | solution.py:60
  65.2 2.2 %collective-permute-start.25 = (bf16[128,256]{1,0:T(8,128)(2,1)S(1)}, bf16[128,256]{1,0:T(8,128)(2,1)S(1)}, u32[]{:S(2)}, u32[]{:S(2)}) collective-permute-start(bf16[128,256]{1,0:T(8,128)(2,1)S(1)} %get-tuple-element.62), channel_id=1, source_target_pairs={{0,16},{1,17},{2,18},{3,19},{4,20},{5,21},{6,22},{7,23},{8,24},{9,... | collective-permute-start | bytes 196616 | tf_op jit(solution)/shard_map/ppermute | solution.py:60
  67.5 1.9 %collective-permute-start.21 = (bf16[128,256]{1,0:T(8,128)(2,1)S(1)}, bf16[128,256]{1,0:T(8,128)(2,1)S(1)}, u32[]{:S(2)}, u32[]{:S(2)}) collective-permute-start(bf16[128,256]{1,0:T(8,128)(2,1)S(1)} %get-tuple-element.58), channel_id=1, source_target_pairs={{0,16},{1,17},{2,18},{3,19},{4,20},{5,21},{6,22},{7,23},{8,24},{9,... | collective-permute-start | bytes 196616 | tf_op jit(solution)/shard_map/ppermute | solution.py:60
  69.9 3.2 %collective-permute-start.26 = (bf16[192,256]{1,0:T(8,128)(2,1)S(1)}, bf16[192,256]{1,0:T(8,128)(2,1)S(1)}, u32[]{:S(2)}, u32[]{:S(2)}) collective-permute-start(bf16[192,256]{1,0:T(8,128)(2,1)S(1)} %shard_map.98), channel_id=1, source_target_pairs={{0,64},{1,65},{2,66},{3,67},{4,68},{5,69},{6,70},{7,71},{8,72},{9,... | collective-permute-start | bytes 294920 | tf_op jit(solution)/shard_map/ppermute | solution.py:60
  73.5 2.5 %collective-permute-start.22 = (bf16[192,256]{1,0:T(8,128)(2,1)S(1)}, bf16[192,256]{1,0:T(8,128)(2,1)S(1)}, u32[]{:S(2)}, u32[]{:S(2)}) collective-permute-start(bf16[192,256]{1,0:T(8,128)(2,1)S(1)} %shard_map.96), channel_id=1, source_target_pairs={{0,192},{1,193},{2,194},{3,195},{4,196},{5,197},{6,198},{7,199},{8... | collective-permute-start | bytes 294920 | tf_op jit(solution)/shard_map/ppermute | solution.py:60
  76.3 3.9 %collective-permute-done.20.got = bf16[128,256]{1,0:T(8,128)(2,1)S(1)} collective-permute-done((bf16[128,256]{1,0:T(8,128)(2,1)S(1)}, bf16[128,256]{1,0:T(8,128)(2,1)S(1)}, u32[]{:S(2)}, u32[]{:S(2)}) %collective-permute-start.20) | collective-permute-done | bytes 65568 | tf_op jit(solution)/shard_map/ppermute | solution.py:60
  80.3 3.0 %collective-permute-done.22.r3 = bf16[192,256]{1,0:T(8,128)(2,1)S(1)} collective-permute-done((bf16[192,256]{1,0:T(8,128)(2,1)S(1)}, bf16[192,256]{1,0:T(8,128)(2,1)S(1)}, u32[]{:S(2)}, u32[]{:S(2)}) %collective-permute-start.22) | collective-permute-done | bytes 98336 | tf_op jit(solution)/shard_map/ppermute | solution.py:60
  83.3 2.4 %collective-permute-start.27 = (f32[128,256]{1,0:T(8,128)S(1)}, f32[128,256]{1,0:T(8,128)S(1)}, u32[]{:S(2)}, u32[]{:S(2)}) collective-permute-start(f32[128,256]{1,0:T(8,128)S(1)} %get-tuple-element.63.mine), channel_id=1, source_target_pairs={{0,48},{1,49},{2,50},{3,51},{4,52},{5,53},{6,54},{7,55},{8,56},{9,... | collective-permute-start | bytes 393224 | tf_op jit(solution)/shard_map/ppermute | solution.py:60
  86.2 3.8 %collective-permute-done.29.got = f32[64,256]{1,0:T(8,128)S(1)} collective-permute-done((f32[64,256]{1,0:T(8,128)S(1)}, f32[64,256]{1,0:T(8,128)S(1)}, u32[]{:S(2)}, u32[]{:S(2)}) %collective-permute-start.29) | collective-permute-done | bytes 65568 | tf_op jit(solution)/shard_map/ppermute | solution.py:60
  91.1 2.6 %collective-permute-start.28 = (bf16[128,256]{1,0:T(8,128)(2,1)S(1)}, bf16[128,256]{1,0:T(8,128)(2,1)S(1)}, u32[]{:S(2)}, u32[]{:S(2)}) collective-permute-start(bf16[128,256]{1,0:T(8,128)(2,1)S(1)} %shard_map.100), channel_id=1, source_target_pairs={{0,1},{1,53},{2,65},{3,113},{4,129},{5,181},{6,195},{7,247},{8,9},... | collective-permute-start | bytes 196616 | tf_op jit(solution)/shard_map/ppermute | solution.py:60
  95.6 2.9 %collective-permute-done.28.piece = bf16[128,256]{1,0:T(8,128)(2,1)S(1)} collective-permute-done((bf16[128,256]{1,0:T(8,128)(2,1)S(1)}, bf16[128,256]{1,0:T(8,128)(2,1)S(1)}, u32[]{:S(2)}, u32[]{:S(2)}) %collective-permute-start.28) | collective-permute-done | bytes 65568 | tf_op jit(solution)/shard_map/ppermute | solution.py:60
  98.5 3.4 %collective-permute-start.33 = (bf16[256,256]{1,0:T(8,128)(2,1)S(1)}, bf16[256,256]{1,0:T(8,128)(2,1)S(1)}, u32[]{:S(2)}, u32[]{:S(2)}) collective-permute-start(bf16[256,256]{1,0:T(8,128)(2,1)S(1)} %shard_map.102.m0), channel_id=1, source_target_pairs={{0,6},{1,7},{2,4},{3,5},{4,2},{5,3},{6,0},{7,1},{8,14},{9,15},{10,... | collective-permute-start | bytes 393224 | tf_op jit(solution)/shard_map/ppermute | solution.py:60
  102.8 3.0 %collective-permute-done.33.m3 = bf16[256,256]{1,0:T(8,128)(2,1)S(1)} collective-permute-done((bf16[256,256]{1,0:T(8,128)(2,1)S(1)}, bf16[256,256]{1,0:T(8,128)(2,1)S(1)}, u32[]{:S(2)}, u32[]{:S(2)}) %collective-permute-start.33) | collective-permute-done | bytes 131104 | tf_op jit(solution)/shard_map/ppermute | solution.py:60
  105.8 2.5 %collective-permute-done.32.m2 = bf16[256,256]{1,0:T(8,128)(2,1)S(1)} collective-permute-done((bf16[256,256]{1,0:T(8,128)(2,1)S(1)}, bf16[256,256]{1,0:T(8,128)(2,1)S(1)}, u32[]{:S(2)}, u32[]{:S(2)}) %collective-permute-start.32) | collective-permute-done | bytes 131104 | tf_op jit(solution)/shard_map/ppermute | solution.py:60
  (74 shorter events, 30.7 us)
Async XLA Ops:
  1.6 10.4 %collective-permute-start = (bf16[128,256]{1,0:T(8,128)(2,1)S(1)}, bf16[128,256]{1,0:T(8,128)(2,1)S(1)}, u32[]{:S(2)}, u32[]{:S(2)}) collective-permute-start(bf16[128,256]{1,0:T(8,128)(2,1)S(1)} %shard_map.85), channel_id=1, source_target_pairs={{1,0},{53,1},{65,2},{113,3},{129,4},{181,5},{195,6},{247,7},{9,8},... | collective-permute-start | bytes 196616 | tf_op jit(solution)/shard_map/ppermute | solution.py:60
  12.1 6.9 %collective-permute-start.3 = (bf16[128,256]{1,0:T(8,128)(2,1)S(1)}, bf16[128,256]{1,0:T(8,128)(2,1)S(1)}, u32[]{:S(2)}, u32[]{:S(2)}) collective-permute-start(bf16[128,256]{1,0:T(8,128)(2,1)S(1)} %collective-permute-done.p0), channel_id=1, source_target_pairs={{0,192},{1,193},{2,194},{3,195},{4,196},{5,197},{6,198},{7,199},{8... | collective-permute-start | bytes 196616 | tf_op jit(solution)/shard_map/ppermute | solution.py:60
  13.2 7.2 %collective-permute-start.2 = (bf16[128,256]{1,0:T(8,128)(2,1)S(1)}, bf16[128,256]{1,0:T(8,128)(2,1)S(1)}, u32[]{:S(2)}, u32[]{:S(2)}) collective-permute-start(bf16[128,256]{1,0:T(8,128)(2,1)S(1)} %collective-permute-done.p0), channel_id=1, source_target_pairs={{0,128},{1,129},{2,130},{3,131},{4,132},{5,133},{6,134},{7,135},{8... | collective-permute-start | bytes 196616 | tf_op jit(solution)/shard_map/ppermute | solution.py:60
  15.1 5.9 %collective-permute-start.1 = (bf16[128,256]{1,0:T(8,128)(2,1)S(1)}, bf16[128,256]{1,0:T(8,128)(2,1)S(1)}, u32[]{:S(2)}, u32[]{:S(2)}) collective-permute-start(bf16[128,256]{1,0:T(8,128)(2,1)S(1)} %collective-permute-done.p0), channel_id=1, source_target_pairs={{0,64},{1,65},{2,66},{3,67},{4,68},{5,69},{6,70},{7,71},{8,72},{9,... | collective-permute-start | bytes 196616 | tf_op jit(solution)/shard_map/ppermute | solution.py:60
  15.6 7.1 %collective-permute-start.5 = (bf16[128,256]{1,0:T(8,128)(2,1)S(1)}, bf16[128,256]{1,0:T(8,128)(2,1)S(1)}, u32[]{:S(2)}, u32[]{:S(2)}) collective-permute-start(bf16[128,256]{1,0:T(8,128)(2,1)S(1)} %collective-permute-done.p0), channel_id=1, source_target_pairs={{0,16},{1,17},{2,18},{3,19},{4,20},{5,21},{6,22},{7,23},{8,24},{9,... | collective-permute-start | bytes 196616 | tf_op jit(solution)/shard_map/ppermute | solution.py:60
  27.8 10.0 %collective-permute-start.10 = (f32[128,256]{1,0:T(8,128)S(1)}, f32[128,256]{1,0:T(8,128)S(1)}, u32[]{:S(2)}, u32[]{:S(2)}) collective-permute-start(f32[128,256]{1,0:T(8,128)S(1)} %get-tuple-element.40), channel_id=1, source_target_pairs={{0,6},{1,7},{2,4},{3,5},{4,2},{5,3},{6,0},{7,1},{8,14},{9,15},{10,... | collective-permute-start | bytes 393224 | tf_op jit(solution)/shard_map/ppermute | solution.py:60
  32.0 7.9 %collective-permute-start.11 = (f32[128,256]{1,0:T(8,128)S(1)}, f32[128,256]{1,0:T(8,128)S(1)}, u32[]{:S(2)}, u32[]{:S(2)}) collective-permute-start(f32[128,256]{1,0:T(8,128)S(1)} %get-tuple-element.41), channel_id=1, source_target_pairs={{0,4},{1,5},{2,6},{3,7},{4,0},{5,1},{6,2},{7,3},{8,12},{9,13},{10,... | collective-permute-start | bytes 393224 | tf_op jit(solution)/shard_map/ppermute | solution.py:60
  32.4 7.5 %collective-permute-start.12 = (f32[128,256]{1,0:T(8,128)S(1)}, f32[128,256]{1,0:T(8,128)S(1)}, u32[]{:S(2)}, u32[]{:S(2)}) collective-permute-start(f32[128,256]{1,0:T(8,128)S(1)} %get-tuple-element.42), channel_id=1, source_target_pairs={{0,2},{1,3},{2,0},{3,1},{4,6},{5,7},{6,4},{7,5},{8,10},{9,11},{10,... | collective-permute-start | bytes 393224 | tf_op jit(solution)/shard_map/ppermute | solution.py:60
  39.9 12.3 %collective-permute-start.13 = (bf16[320,256]{1,0:T(8,128)(2,1)S(1)}, bf16[320,256]{1,0:T(8,128)(2,1)S(1)}, u32[]{:S(2)}, u32[]{:S(2)}) collective-permute-start(bf16[320,256]{1,0:T(8,128)(2,1)S(1)} %shard_map.90.mine), channel_id=1, source_target_pairs={{0,1},{1,0},{2,3},{3,2},{4,5},{5,4},{6,7},{7,6},{8,9},{9,8},{10,11... | collective-permute-start | bytes 491528 | tf_op jit(solution)/shard_map/ppermute | solution.py:60
  53.1 7.6 %collective-permute-start.16 = (bf16[256,256]{1,0:T(8,128)(2,1)S(1)}, bf16[256,256]{1,0:T(8,128)(2,1)S(1)}, u32[]{:S(2)}, u32[]{:S(2)}) collective-permute-start(bf16[256,256]{1,0:T(8,128)(2,1)S(1)} %get-tuple-element.45.m0), channel_id=1, source_target_pairs={{0,6},{1,7},{2,4},{3,5},{4,2},{5,3},{6,0},{7,1},{8,14},{9,15},{10,... | collective-permute-start | bytes 393224 | tf_op jit(solution)/shard_map/ppermute | solution.py:60
  55.7 6.7 %collective-permute-start.15 = (bf16[256,256]{1,0:T(8,128)(2,1)S(1)}, bf16[256,256]{1,0:T(8,128)(2,1)S(1)}, u32[]{:S(2)}, u32[]{:S(2)}) collective-permute-start(bf16[256,256]{1,0:T(8,128)(2,1)S(1)} %get-tuple-element.45.m0), channel_id=1, source_target_pairs={{0,4},{1,5},{2,6},{3,7},{4,0},{5,1},{6,2},{7,3},{8,12},{9,13},{10,... | collective-permute-start | bytes 393224 | tf_op jit(solution)/shard_map/ppermute | solution.py:60
  55.7 6.7 %collective-permute-start.14 = (bf16[256,256]{1,0:T(8,128)(2,1)S(1)}, bf16[256,256]{1,0:T(8,128)(2,1)S(1)}, u32[]{:S(2)}, u32[]{:S(2)}) collective-permute-start(bf16[256,256]{1,0:T(8,128)(2,1)S(1)} %get-tuple-element.45.m0), channel_id=1, source_target_pairs={{0,2},{1,3},{2,0},{3,1},{4,6},{5,7},{6,4},{7,5},{8,10},{9,11},{10,... | collective-permute-start | bytes 393224 | tf_op jit(solution)/shard_map/ppermute | solution.py:60
  63.9 5.5 %collective-permute-start.17 = (f32[512,256]{1,0:T(8,128)S(1)}, f32[512,256]{1,0:T(8,128)S(1)}, u32[]{:S(2)}, u32[]{:S(2)}) collective-permute-start(f32[512,256]{1,0:T(8,128)S(1)} %get-tuple-element.50), channel_id=1, source_target_pairs={{0,8},{1,9},{2,10},{3,11},{4,12},{5,13},{6,14},{7,15},{8,0},{9,1},... | collective-permute-start | bytes 1572872 | tf_op jit(solution)/shard_map/ppermute | solution.py:60
  67.4 5.7 %collective-permute-start.23 = (bf16[128,256]{1,0:T(8,128)(2,1)S(1)}, bf16[128,256]{1,0:T(8,128)(2,1)S(1)}, u32[]{:S(2)}, u32[]{:S(2)}) collective-permute-start(bf16[128,256]{1,0:T(8,128)(2,1)S(1)} %get-tuple-element.60), channel_id=1, source_target_pairs={{0,16},{1,17},{2,18},{3,19},{4,20},{5,21},{6,22},{7,23},{8,24},{9,... | collective-permute-start | bytes 196616 | tf_op jit(solution)/shard_map/ppermute | solution.py:60
  67.5 6.0 %collective-permute-start.21 = (bf16[128,256]{1,0:T(8,128)(2,1)S(1)}, bf16[128,256]{1,0:T(8,128)(2,1)S(1)}, u32[]{:S(2)}, u32[]{:S(2)}) collective-permute-start(bf16[128,256]{1,0:T(8,128)(2,1)S(1)} %get-tuple-element.58), channel_id=1, source_target_pairs={{0,16},{1,17},{2,18},{3,19},{4,20},{5,21},{6,22},{7,23},{8,24},{9,... | collective-permute-start | bytes 196616 | tf_op jit(solution)/shard_map/ppermute | solution.py:60
  69.9 10.4 %collective-permute-start.26 = (bf16[192,256]{1,0:T(8,128)(2,1)S(1)}, bf16[192,256]{1,0:T(8,128)(2,1)S(1)}, u32[]{:S(2)}, u32[]{:S(2)}) collective-permute-start(bf16[192,256]{1,0:T(8,128)(2,1)S(1)} %shard_map.98), channel_id=1, source_target_pairs={{0,64},{1,65},{2,66},{3,67},{4,68},{5,69},{6,70},{7,71},{8,72},{9,... | collective-permute-start | bytes 294920 | tf_op jit(solution)/shard_map/ppermute | solution.py:60
  73.2 7.1 %collective-permute-start.24 = (bf16[192,256]{1,0:T(8,128)(2,1)S(1)}, bf16[192,256]{1,0:T(8,128)(2,1)S(1)}, u32[]{:S(2)}, u32[]{:S(2)}) collective-permute-start(bf16[192,256]{1,0:T(8,128)(2,1)S(1)} %shard_map.97), channel_id=1, source_target_pairs={{0,128},{1,129},{2,130},{3,131},{4,132},{5,133},{6,134},{7,135},{8... | collective-permute-start | bytes 294920 | tf_op jit(solution)/shard_map/ppermute | solution.py:60
  73.5 9.8 %collective-permute-start.22 = (bf16[192,256]{1,0:T(8,128)(2,1)S(1)}, bf16[192,256]{1,0:T(8,128)(2,1)S(1)}, u32[]{:S(2)}, u32[]{:S(2)}) collective-permute-start(bf16[192,256]{1,0:T(8,128)(2,1)S(1)} %shard_map.96), channel_id=1, source_target_pairs={{0,192},{1,193},{2,194},{3,195},{4,196},{5,197},{6,198},{7,199},{8... | collective-permute-start | bytes 294920 | tf_op jit(solution)/shard_map/ppermute | solution.py:60
  83.3 7.7 %collective-permute-start.27 = (f32[128,256]{1,0:T(8,128)S(1)}, f32[128,256]{1,0:T(8,128)S(1)}, u32[]{:S(2)}, u32[]{:S(2)}) collective-permute-start(f32[128,256]{1,0:T(8,128)S(1)} %get-tuple-element.63.mine), channel_id=1, source_target_pairs={{0,48},{1,49},{2,50},{3,51},{4,52},{5,53},{6,54},{7,55},{8,56},{9,... | collective-permute-start | bytes 393224 | tf_op jit(solution)/shard_map/ppermute | solution.py:60
  90.0 5.6 %collective-permute-start.30 = (f32[64,256]{1,0:T(8,128)S(1)}, f32[64,256]{1,0:T(8,128)S(1)}, u32[]{:S(2)}, u32[]{:S(2)}) collective-permute-start(f32[64,256]{1,0:T(8,128)S(1)} %shard_map.101.mine), channel_id=1, source_target_pairs={{0,48},{1,49},{2,50},{3,51},{4,52},{5,53},{6,54},{7,55},{8,56},{9,... | collective-permute-start | bytes 196616 | tf_op jit(solution)/shard_map/ppermute | solution.py:60
  91.1 7.4 %collective-permute-start.28 = (bf16[128,256]{1,0:T(8,128)(2,1)S(1)}, bf16[128,256]{1,0:T(8,128)(2,1)S(1)}, u32[]{:S(2)}, u32[]{:S(2)}) collective-permute-start(bf16[128,256]{1,0:T(8,128)(2,1)S(1)} %shard_map.100), channel_id=1, source_target_pairs={{0,1},{1,53},{2,65},{3,113},{4,129},{5,181},{6,195},{7,247},{8,9},... | collective-permute-start | bytes 196616 | tf_op jit(solution)/shard_map/ppermute | solution.py:60
  98.5 7.3 %collective-permute-start.33 = (bf16[256,256]{1,0:T(8,128)(2,1)S(1)}, bf16[256,256]{1,0:T(8,128)(2,1)S(1)}, u32[]{:S(2)}, u32[]{:S(2)}) collective-permute-start(bf16[256,256]{1,0:T(8,128)(2,1)S(1)} %shard_map.102.m0), channel_id=1, source_target_pairs={{0,6},{1,7},{2,4},{3,5},{4,2},{5,3},{6,0},{7,1},{8,14},{9,15},{10,... | collective-permute-start | bytes 393224 | tf_op jit(solution)/shard_map/ppermute | solution.py:60
  101.9 6.5 %collective-permute-start.32 = (bf16[256,256]{1,0:T(8,128)(2,1)S(1)}, bf16[256,256]{1,0:T(8,128)(2,1)S(1)}, u32[]{:S(2)}, u32[]{:S(2)}) collective-permute-start(bf16[256,256]{1,0:T(8,128)(2,1)S(1)} %shard_map.102.m0), channel_id=1, source_target_pairs={{0,4},{1,5},{2,6},{3,7},{4,0},{5,1},{6,2},{7,3},{8,12},{9,13},{10,... | collective-permute-start | bytes 393224 | tf_op jit(solution)/shard_map/ppermute | solution.py:60
  101.9 6.5 %collective-permute-start.31 = (bf16[256,256]{1,0:T(8,128)(2,1)S(1)}, bf16[256,256]{1,0:T(8,128)(2,1)S(1)}, u32[]{:S(2)}, u32[]{:S(2)}) collective-permute-start(bf16[256,256]{1,0:T(8,128)(2,1)S(1)} %shard_map.102.m0), channel_id=1, source_target_pairs={{0,2},{1,3},{2,0},{3,1},{4,6},{5,7},{6,4},{7,5},{8,10},{9,11},{10,... | collective-permute-start | bytes 393224 | tf_op jit(solution)/shard_map/ppermute | solution.py:60
  (15 other events, 98.0 us)

commit v4 on v3

--- a/solution.py
+++ b/solution.py
@@ -135,15 +135,17 @@
                 dense_t[k, at(slot & 3, TILE), at(slot >> 2, TILE)] = tile.T
 
 
-def block_body(p0, p1, p2, p3, block):
-    me = place()
-    for k, piece in enumerate((p0, p1, p2, p3)):
-        block[at(me["z"] ^ k, PART), :] = piece[...]
-
-
-def forward_body(dense, f0, f1, f2, f3, to3, to2, to1, own, total):
-    me = place()
-    total[...] = dot(dense[0], f0[...]) + dot(dense[1], f1[...]) + dot(dense[2], f2[...]) + dot(dense[3], f3[...])
+def pair_body(low, high, out):
+    out[0:PART, :] = low[...]
+    out[PART:, :] = high[...]
+
+
+def forward_body(dense, a0, b0, a1, b1, a2, b2, a3, b3, to3, to2, to1, own, blocks, total):
+    me = place()
+    for i, (first, second) in enumerate(((a0, b0), (a1, b1), (a2, b2), (a3, b3))):
+        for k, part in ((3, first[0:PART, :]), (0, first[PART:, :]), (2, second[0:PART, :]), (1, second[PART:, :])):
+            blocks[i, at(me["z"] ^ k, PART), :] = part
+    total[...] = dot(dense[0], blocks[0]) + dot(dense[1], blocks[1]) + (dot(dense[2], blocks[2]) + dot(dense[3], blocks[3]))
     for k, to in enumerate((own, to1, to2, to3)):
         to[...] = total[at(me["x"] ^ k, PART), :]
 
@@ -182,61 +184,68 @@
     to_c[...] = dot(dense_t[3], grad)
 
 
-def kept_body(dense_t, aggregate, grad_pre, grad_agg, to_c, keep_other, keep, share, grad_w):
-    me = place()
-    grad = grad_agg[...]
-    to_c[...] = dot(dense_t[1], grad)
-    keep_other[...] = dot(dense_t[2], grad)
-    keep[...] = dot(dense_t[0], grad)
+def share_body(dense_t, aggregate, grad_pre, grad_agg, keep, share, grad_w):
+    me = place()
+    keep[...] = dot(dense_t[2], grad_agg[...])
     grad_w[...] = dot(aggregate[...], grad_pre[...], ((0,), (0,)))
-    share[...] = grad_w[at(me["x"], SLICE), :]
-
-
-def to_u_body(keep, got, to3, to2, to1, to0):
-    me = place()
-    for k, to in ((3, to3), (2, to2), (1, to1), (0, to0)):
+    share[...] = grad_w[at(me["x"], SLICE), :].astype(BF)
+
+
+def to_u_body(keep, got, share, first, second):
+    me = place()
+    for k, out, start in ((3, first, 0), (2, first, PART), (1, second, 0), (0, second, PART)):
         rows = at(me["z"] ^ k, PART)
-        to[...] = (keep[rows, :] + got[rows, :]).astype(BF)
-
-
-def after_c_body(keep, got, keep_w, got_w, s3, s2, s1, s0, share):
-    me = place()
-    for k, part in ((3, s3), (2, s2), (1, s1), (0, s0)):
-        rows = at(me["z"] ^ k, PART)
-        part[...] = keep[rows, :] + got[rows, :]
-    share[...] = (keep_w[...] + got_w[...]).astype(BF)
-
-
-def to_z_body(own, got, share, to):
-    to[0:PART, :] = (own[...] + got[...].astype(F32)).astype(BF)
-    to[PART:, :] = share[...]
-
-
-def after_z_body(own, got, share, r3, r2, r1, to_v, share_z):
-    total = own[...] + got[...].astype(F32) + r1[0:PART, :].astype(F32)
-    to_v[...] = total + (r2[0:PART, :].astype(F32) + r3[0:PART, :].astype(F32))
+        out[start : start + PART, :] = (keep[rows, :] + got[rows, :]).astype(BF)
+    first[2 * PART :, :] = share[...]
+
+
+def kept_body(dense_t, grad_agg, to_c, keep):
+    to_c[...] = dot(dense_t[1], grad_agg[...])
+    keep[...] = dot(dense_t[0], grad_agg[...])
+
+
+def after_c_body(keep, got, own, total):
+    me = place()
+    total[...] = keep[...] + got[...]
+    for k in range(4):
+        own[k * PART : (k + 1) * PART, :] = total[at(me["z"] ^ k, PART), :]
+
+
+def to_z_body(own, got, share, to3, to2):
+    pair = (share[...].astype(F32) + got[2 * PART :, :].astype(F32)).astype(BF)
+    for to, start, k in ((to3, 0, 3), (to2, PART, 2)):
+        to[0:PART, :] = (own[k * PART : (k + 1) * PART, :] + got[start : start + PART, :].astype(F32)).astype(BF)
+        to[PART:, :] = pair
+
+
+def to_z1_body(own, got, share, got_first, to, kept_share):
+    to[0:PART, :] = (own[PART : 2 * PART, :] + got[0:PART, :].astype(F32)).astype(BF)
+    pair = (share[...].astype(F32) + got_first[2 * PART :, :].astype(F32)).astype(BF)
+    to[PART:, :] = pair
+    kept_share[...] = pair
+
+
+def after_z_body(own, got, share, r3, r2, r1, to_v):
+    total = own[0:PART, :] + got[PART:, :].astype(F32) + r1[0:PART, :].astype(F32)
+    to_v[0:PART, :] = total + (r2[0:PART, :].astype(F32) + r3[0:PART, :].astype(F32))
     pair = share[...].astype(F32) + r1[PART:, :].astype(F32)
-    share_z[...] = pair + (r2[PART:, :].astype(F32) + r3[PART:, :].astype(F32))
-
-
-def after_v_body(mine, got, piece):
-    piece[...] = (mine[...] + got[...]).astype(BF)
-
-
-def add_body(mine, got, total):
-    total[...] = mine[...] + got[...]
-
-
-def last_body(piece, mine, got, message):
-    message[0:PART, :] = piece[...]
-    put_split(message, PART, mine[...] + got[...])
-
-
-def finish_body(m0, m1, m2, m3, grad_features, grad_weight):
-    me = place()
-    for k, message in enumerate((m0, m1, m2, m3)):
-        grad_features[at(chunk_of(me, me["x"] ^ k), PART), :] = message[0:PART, :]
-        grad_weight[at(me["x"] ^ k, SLICE), :] = get_split(message, PART)
+    to_v[PART:, :] = pair + (r2[PART:, :].astype(F32) + r3[PART:, :].astype(F32))
+
+
+def after_v_body(mine, got, piece, share):
+    piece[...] = (mine[0:PART, :] + got[0:PART, :]).astype(BF)
+    share[...] = mine[PART:, :] + got[PART:, :]
+
+
+def last_share_body(mine, got, message):
+    put_split(message, 0, mine[...] + got[...])
+
+
+def finish_body(p0, p1, p2, p3, w0, w1, w2, w3, grad_features, grad_weight):
+    me = place()
+    for k, (piece, share) in enumerate(((p0, w0), (p1, w1), (p2, w2), (p3, w3))):
+        grad_features[at(chunk_of(me, me["x"] ^ k), PART), :] = piece[...]
+        grad_weight[at(me["x"] ^ k, SLICE), :] = get_split(share, 0)
 
 
 def on_device(features, weight, cotangent, tile_values, tile_slots, tile_count):
@@ -245,6 +254,8 @@
     block = ((BLOCK, WIDTH), BF)
     block32 = ((BLOCK, WIDTH), F32)
     share32 = ((SLICE, WIDTH), F32)
+    share16 = ((SLICE, WIDTH), BF)
+    two = ((2 * PART, WIDTH), BF)
     dense_shape = ((4, BLOCK, BLOCK), BF)
 
     (chunk,) = call(chunk_body, [part], features, specs=[HBM], scratch=[pltpu.SemaphoreType.DMA])
@@ -254,13 +265,14 @@
     )
     chunk, dense, dense_t = lax.optimization_barrier((chunk, dense, dense_t))
     chunks = [chunk] + [send(chunk, route) for route in FLIP_Z]
-    others = [send(value, FLIP_U) for value in chunks]
-    (f0,) = call(block_body, [block], *chunks)
-    f1 = send(f0, FLIP_C)
-    (f2,) = call(block_body, [block], *others)
-    f3 = send(f2, FLIP_C)
+    c0, c1, c2, c3 = chunks
+    mine = [call(pair_body, [two], c3, c0)[0], call(pair_body, [two], c2, c1)[0]]
+    by_u = [send(value, FLIP_U) for value in mine]
+    by_c = [send(value, FLIP_C) for value in mine]
+    by_uc = [send(value, FLIP_C) for value in by_u]
     to3, to2, to1, own = call(
-        forward_body, [part32] * 4, dense, f0, f1, f2, f3, scratch=[pltpu.VMEM((BLOCK, WIDTH), F32)]
+        forward_body, [part32] * 4, dense, *mine, *by_c, *by_u, *by_uc,
+        scratch=[pltpu.VMEM((4, BLOCK, WIDTH), BF), pltpu.VMEM((BLOCK, WIDTH), F32)],
     )
     got = [send(value, route) for value, route in zip((to3, to2, to1), FLIP_X[::-1])]
     (mine,) = call(sum_body, [((2 * PART + SLICE, WIDTH), BF)], own, *got, cotangent)
@@ -273,30 +285,27 @@
     to_c, aggregate, grad_pre, grad_agg = call(
         backward_body, [block32, block, block, block], dense_t, weight, message, *got
     )
-    got_other = send(to_c, FLIP_C)
-    to_c, keep_other, keep, share = call(
-        kept_body, [block32, block32, block32, share32], dense_t, aggregate, grad_pre, grad_agg,
+    got = send(to_c, FLIP_C)
+    keep, share = call(
+        share_body, [block32, share16], dense_t, aggregate, grad_pre, grad_agg,
         scratch=[pltpu.VMEM((WIDTH, WIDTH), F32)],
     )
-    got = send(to_c, FLIP_C)
-    got_w = send(share, FLIP_C)
-    to_u = call(to_u_body, [part] * 4, keep_other, got_other)
-    from_u = [send(value, FLIP_U) for value in to_u]
-    *owns, share = call(after_c_body, [part32] * 4 + [((SLICE, WIDTH), BF)], keep, got, share, got_w)
-    from_z = []
-    for own, got, route in zip(owns, from_u, FLIP_Z[::-1]):
-        (to_z,) = call(to_z_body, [((PART + SLICE, WIDTH), BF)], own, got, share)
-        from_z.append(send(to_z, route))
-    to_v, share = call(after_z_body, [part32, share32], owns[3], from_u[3], share, *from_z)
-    got = send(to_v, FLIP_V)
-    got_w = send(share, FLIP_U)
-    (piece,) = call(after_v_body, [part], to_v, got)
-    (share,) = call(add_body, [share32], share, got_w)
+    first, second = call(to_u_body, [((2 * PART + SLICE, WIDTH), BF), two], keep, got, share)
+    got_first, got_second = send(first, FLIP_U), send(second, FLIP_U)
+    to_c, keep = call(kept_body, [block32, block32], dense_t, grad_agg)
+    (own,) = call(after_c_body, [block32], keep, send(to_c, FLIP_C), scratch=[pltpu.VMEM((BLOCK, WIDTH), F32)])
+    to_z = ((PART + SLICE, WIDTH), BF)
+    to3, to2 = call(to_z_body, [to_z, to_z], own, got_first, share)
+    to1, share = call(to_z1_body, [to_z, share16], own, got_second, share, got_first)
+    from_z = [send(value, route) for value, route in zip((to3, to2, to1), FLIP_Z[::-1])]
+    (to_v,) = call(after_z_body, [((PART + SLICE, WIDTH), F32)], own, got_second, share, *from_z)
+    piece, share = call(after_v_body, [part, share32], to_v, send(to_v, FLIP_V))
     piece = send(piece, TO_ROW)
-    got_w = send(share, FLIP_V)
-    (message,) = call(last_body, [((PART + 2 * SLICE, WIDTH), BF)], piece, share, got_w)
-    messages = [message] + [send(message, route) for route in FLIP_X]
-    grad_features, grad_weight = call(finish_body, [block, ((WIDTH, WIDTH), F32)], *messages)
+    (share,) = call(last_share_body, [((2 * SLICE, WIDTH), BF)], share, send(share, FLIP_C))
+    shares = [share] + [send(share, route) for route in FLIP_X]
+    piece, *shares = lax.optimization_barrier((piece, *shares))
+    pieces = [piece] + [send(piece, route) for route in FLIP_X]
+    grad_features, grad_weight = call(finish_body, [block, ((WIDTH, WIDTH), F32)], *pieces, *shares)
     return output, grad_weight, grad_features
 
 

time: 110 us -> 112 us (1.018)
  starting transfers between devices: 47.1 us -> 50.7 us
  waiting for transfers between devices: 52.8 us -> 51 us
    ppermute x34 -> x33, starting transfers between devices: 47.1 us -> 50.7 us  [send(): return lax.ppermute(value, AXES, route)]
    ppermute x34 -> x33, waiting for transfers between devices: 52.8 us -> 51 us  [send(): return lax.ppermute(value, AXES, route)]
    pallas_call x19 -> x18, Pallas kernels: 5.18 us -> 5.57 us  [call(): pl.pallas_call(body, out_shape=[jax.ShapeDtypeStruct(shape, dtype) for sh...]
  transfers between devices with their start and end apart: 34 -> 33, of which waited for: 20 -> 23; matrix products, arithmetic and copies ran while one was open for 1% -> 1% of each run, Pallas kernels for 2% -> 2%
where the time goes in v4:
time: 112 us; the launch traced here: 111 us
  waiting for transfers between devices  51 us (46%)
  starting transfers between devices  50.7 us (45%)
  Pallas kernels  5.57 us (5%)
  local copies, waits for them, and re-layouts  3.32 us (3%)
    ppermute x33, waiting for transfers between devices, send(): return lax.ppermute(value, AXES, route)  51 us
    ppermute x33, starting transfers between devices, send(): return lax.ppermute(value, AXES, route)  50.7 us
    pallas_call x18, Pallas kernels, call(): pl.pallas_call(body, out_shape=[jax.ShapeDtypeStruct(shape, dtype) for sh...  5.57 us
    unnamed x11, local copies, waits for them, and re-layouts  3.32 us
  transfers between devices with their start and end apart: 33, of which 23 were waited for; matrix products, arithmetic and copies ran while one was open for 1% of the time, Pallas kernels for 2%

profile of v4, /device:TPU:32, one launch (start us, length us, event | category | flops | bytes accessed | tf_op | source)
XLA Modules:
  0.0 111.4 jit_solution(10670921747739734597)
XLA Ops:
  1.7 3.6 %collective-permute-start = (bf16[128,256]{1,0:T(8,128)(2,1)S(1)}, bf16[128,256]{1,0:T(8,128)(2,1)S(1)}, u32[]{:S(2)}, u32[]{:S(2)}) collective-permute-start(bf16[128,256]{1,0:T(8,128)(2,1)S(1)} %shard_map.85), channel_id=1, source_target_pairs={{1,0},{53,1},{65,2},{113,3},{129,4},{181,5},{195,6},{247,7},{9,8},... | collective-permute-start | bytes 196616 | tf_op jit(solution)/shard_map/ppermute | solution.py:60
  8.8 3.2 %collective-permute-done.high = bf16[128,256]{1,0:T(8,128)(2,1)S(1)} collective-permute-done((bf16[128,256]{1,0:T(8,128)(2,1)S(1)}, bf16[128,256]{1,0:T(8,128)(2,1)S(1)}, u32[]{:S(2)}, u32[]{:S(2)}) %collective-permute-start) | collective-permute-done | bytes 65568 | tf_op jit(solution)/shard_map/ppermute | solution.py:60
  13.2 2.3 %collective-permute-start.3 = (bf16[128,256]{1,0:T(8,128)(2,1)S(1)}, bf16[128,256]{1,0:T(8,128)(2,1)S(1)}, u32[]{:S(2)}, u32[]{:S(2)}) collective-permute-start(bf16[128,256]{1,0:T(8,128)(2,1)S(1)} %collective-permute-done.high), channel_id=1, source_target_pairs={{0,64},{1,65},{2,66},{3,67},{4,68},{5,69},{6,70},{7,71},{8,72},{9,... | collective-permute-start | bytes 196616 | tf_op jit(solution)/shard_map/ppermute | solution.py:60
  16.6 2.2 %collective-permute-start.6 = (bf16[256,256]{1,0:T(8,128)(2,1)S(1)}, bf16[256,256]{1,0:T(8,128)(2,1)S(1)}, u32[]{:S(2)}, u32[]{:S(2)}) collective-permute-start(bf16[256,256]{1,0:T(8,128)(2,1)S(1)} %shard_map.87.a0), channel_id=1, source_target_pairs={{0,16},{1,17},{2,18},{3,19},{4,20},{5,21},{6,22},{7,23},{8,24},{9,... | collective-permute-start | bytes 393224 | tf_op jit(solution)/shard_map/ppermute | solution.py:60
  22.9 2.9 %collective-permute-done.7.b2 = bf16[256,256]{1,0:T(8,128)(2,1)S(1)} collective-permute-done((bf16[256,256]{1,0:T(8,128)(2,1)S(1)}, bf16[256,256]{1,0:T(8,128)(2,1)S(1)}, u32[]{:S(2)}, u32[]{:S(2)}) %collective-permute-start.7) | collective-permute-done | bytes 131104 | tf_op jit(solution)/shard_map/ppermute | solution.py:60
  28.0 3.1 %collective-permute-start.10 = (f32[128,256]{1,0:T(8,128)S(1)}, f32[128,256]{1,0:T(8,128)S(1)}, u32[]{:S(2)}, u32[]{:S(2)}) collective-permute-start(f32[128,256]{1,0:T(8,128)S(1)} %get-tuple-element.42), channel_id=1, source_target_pairs={{0,6},{1,7},{2,4},{3,5},{4,2},{5,3},{6,0},{7,1},{8,14},{9,15},{10,... | collective-permute-start | bytes 393224 | tf_op jit(solution)/shard_map/ppermute | solution.py:60
  31.1 2.6 %collective-permute-start.11 = (f32[128,256]{1,0:T(8,128)S(1)}, f32[128,256]{1,0:T(8,128)S(1)}, u32[]{:S(2)}, u32[]{:S(2)}) collective-permute-start(f32[128,256]{1,0:T(8,128)S(1)} %get-tuple-element.43), channel_id=1, source_target_pairs={{0,4},{1,5},{2,6},{3,7},{4,0},{5,1},{6,2},{7,3},{8,12},{9,13},{10,... | collective-permute-start | bytes 393224 | tf_op jit(solution)/shard_map/ppermute | solution.py:60
  33.7 3.2 %collective-permute-done.10.r3 = f32[128,256]{1,0:T(8,128)S(1)} collective-permute-done((f32[128,256]{1,0:T(8,128)S(1)}, f32[128,256]{1,0:T(8,128)S(1)}, u32[]{:S(2)}, u32[]{:S(2)}) %collective-permute-start.10) | collective-permute-done | bytes 131104 | tf_op jit(solution)/shard_map/ppermute | solution.py:60
  36.9 2.0 %collective-permute-done.11.r2 = f32[128,256]{1,0:T(8,128)S(1)} collective-permute-done((f32[128,256]{1,0:T(8,128)S(1)}, f32[128,256]{1,0:T(8,128)S(1)}, u32[]{:S(2)}, u32[]{:S(2)}) %collective-permute-start.11) | collective-permute-done | bytes 131104 | tf_op jit(solution)/shard_map/ppermute | solution.py:60
  39.3 3.1 %collective-permute-start.13 = (bf16[320,256]{1,0:T(8,128)(2,1)S(1)}, bf16[320,256]{1,0:T(8,128)(2,1)S(1)}, u32[]{:S(2)}, u32[]{:S(2)}) collective-permute-start(bf16[320,256]{1,0:T(8,128)(2,1)S(1)} %shard_map.90.mine), channel_id=1, source_target_pairs={{0,1},{1,0},{2,3},{3,2},{4,5},{5,4},{6,7},{7,6},{8,9},{9,8},{10,11... | collective-permute-start | bytes 491528 | tf_op jit(solution)/shard_map/ppermute | solution.py:60
  42.5 7.9 %collective-permute-done.13.got = bf16[320,256]{1,0:T(8,128)(2,1)S(1)} collective-permute-done((bf16[320,256]{1,0:T(8,128)(2,1)S(1)}, bf16[320,256]{1,0:T(8,128)(2,1)S(1)}, u32[]{:S(2)}, u32[]{:S(2)}) %collective-permute-start.13) | collective-permute-done | bytes 163872 | tf_op jit(solution)/shard_map/ppermute | solution.py:60
  53.0 3.6 %collective-permute-start.15 = (bf16[256,256]{1,0:T(8,128)(2,1)S(1)}, bf16[256,256]{1,0:T(8,128)(2,1)S(1)}, u32[]{:S(2)}, u32[]{:S(2)}) collective-permute-start(bf16[256,256]{1,0:T(8,128)(2,1)S(1)} %get-tuple-element.47.m0), channel_id=1, source_target_pairs={{0,4},{1,5},{2,6},{3,7},{4,0},{5,1},{6,2},{7,3},{8,12},{9,13},{10,... | collective-permute-start | bytes 393224 | tf_op jit(solution)/shard_map/ppermute | solution.py:60
  57.7 1.8 %collective-permute-done.15.m2 = bf16[256,256]{1,0:T(8,128)(2,1)S(1)} collective-permute-done((bf16[256,256]{1,0:T(8,128)(2,1)S(1)}, bf16[256,256]{1,0:T(8,128)(2,1)S(1)}, u32[]{:S(2)}, u32[]{:S(2)}) %collective-permute-start.15) | collective-permute-done | bytes 131104 | tf_op jit(solution)/shard_map/ppermute | solution.py:60
  59.5 2.0 %collective-permute-done.14.m1 = bf16[256,256]{1,0:T(8,128)(2,1)S(1)} collective-permute-done((bf16[256,256]{1,0:T(8,128)(2,1)S(1)}, bf16[256,256]{1,0:T(8,128)(2,1)S(1)}, u32[]{:S(2)}, u32[]{:S(2)}) %collective-permute-start.14) | collective-permute-done | bytes 131104 | tf_op jit(solution)/shard_map/ppermute | solution.py:60
  64.3 2.5 %collective-permute-start.20 = (bf16[320,256]{1,0:T(8,128)(2,1)S(1)}, bf16[320,256]{1,0:T(8,128)(2,1)S(1)}, u32[]{:S(2)}, u32[]{:S(2)}) collective-permute-start(bf16[320,256]{1,0:T(8,128)(2,1)S(1)} %get-tuple-element.57), channel_id=1, source_target_pairs={{0,16},{1,17},{2,18},{3,19},{4,20},{5,21},{6,22},{7,23},{8,24},{9,... | collective-permute-start | bytes 491528 | tf_op jit(solution)/shard_map/ppermute | solution.py:60
  67.0 4.8 %collective-permute-done.20.got_first.got = bf16[320,256]{1,0:T(8,128)(2,1)S(1)} collective-permute-done((bf16[320,256]{1,0:T(8,128)(2,1)S(1)}, bf16[320,256]{1,0:T(8,128)(2,1)S(1)}, u32[]{:S(2)}, u32[]{:S(2)}) %collective-permute-start.20) | collective-permute-done | bytes 163872 | tf_op jit(solution)/shard_map/ppermute | solution.py:60
  75.9 4.7 %collective-permute-done.21.r3 = bf16[192,256]{1,0:T(8,128)(2,1)S(1)} collective-permute-done((bf16[192,256]{1,0:T(8,128)(2,1)S(1)}, bf16[192,256]{1,0:T(8,128)(2,1)S(1)}, u32[]{:S(2)}, u32[]{:S(2)}) %collective-permute-start.21) | collective-permute-done | bytes 98336 | tf_op jit(solution)/shard_map/ppermute | solution.py:60
  81.5 2.6 %collective-permute-start.24 = (f32[192,256]{1,0:T(8,128)S(1)}, f32[192,256]{1,0:T(8,128)S(1)}, u32[]{:S(2)}, u32[]{:S(2)}) collective-permute-start(f32[192,256]{1,0:T(8,128)S(1)} %shard_map.99.mine), channel_id=1, source_target_pairs={{0,48},{1,49},{2,50},{3,51},{4,52},{5,53},{6,54},{7,55},{8,56},{9,... | collective-permute-start | bytes 589832 | tf_op jit(solution)/shard_map/ppermute | solution.py:60
  84.1 4.3 %collective-permute-done.24.got = f32[192,256]{1,0:T(8,128)S(1)} collective-permute-done((f32[192,256]{1,0:T(8,128)S(1)}, f32[192,256]{1,0:T(8,128)S(1)}, u32[]{:S(2)}, u32[]{:S(2)}) %collective-permute-start.24) | collective-permute-done | bytes 196640 | tf_op jit(solution)/shard_map/ppermute | solution.py:60
  88.6 6.8 %collective-permute-start.25 = (bf16[128,256]{1,0:T(8,128)(2,1)S(1)}, bf16[128,256]{1,0:T(8,128)(2,1)S(1)}, u32[]{:S(2)}, u32[]{:S(2)}) collective-permute-start(bf16[128,256]{1,0:T(8,128)(2,1)S(1)} %get-tuple-element.62), channel_id=1, source_target_pairs={{0,1},{1,53},{2,65},{3,113},{4,129},{5,181},{6,195},{7,247},{8,9},... | collective-permute-start | bytes 196616 | tf_op jit(solution)/shard_map/ppermute | solution.py:60
  96.4 3.1 %collective-permute-start.27 = (bf16[128,256]{1,0:T(8,128)(2,1)S(1)}, bf16[128,256]{1,0:T(8,128)(2,1)S(1)}, u32[]{:S(2)}, u32[]{:S(2)}) collective-permute-start(bf16[128,256]{1,0:T(8,128)(2,1)S(1)} %shard_map.101.w0), channel_id=1, source_target_pairs={{0,2},{1,3},{2,0},{3,1},{4,6},{5,7},{6,4},{7,5},{8,10},{9,11},{10,... | collective-permute-start | bytes 196616 | tf_op jit(solution)/shard_map/ppermute | solution.py:60
  99.5 2.2 %collective-permute-done.29.w3 = bf16[128,256]{1,0:T(8,128)(2,1)S(1)} collective-permute-done((bf16[128,256]{1,0:T(8,128)(2,1)S(1)}, bf16[128,256]{1,0:T(8,128)(2,1)S(1)}, u32[]{:S(2)}, u32[]{:S(2)}) %collective-permute-start.29) | collective-permute-done | bytes 65568 | tf_op jit(solution)/shard_map/ppermute | solution.py:60
  102.8 2.0 %collective-permute-start.32 = (bf16[128,256]{1,0:T(8,128)(2,1)S(1)}, bf16[128,256]{1,0:T(8,128)(2,1)S(1)}, u32[]{:S(2)}, u32[]{:S(2)}) collective-permute-start(bf16[128,256]{1,0:T(8,128)(2,1)S(1)} %collective-permute-done.25.p0), channel_id=1, source_target_pairs={{0,6},{1,7},{2,4},{3,5},{4,2},{5,3},{6,0},{7,1},{8,14},{9,15},{10,... | collective-permute-start | bytes 196616 | tf_op jit(solution)/shard_map/ppermute | solution.py:60
  108.4 2.1 %collective-permute-done.31.p2 = bf16[128,256]{1,0:T(8,128)(2,1)S(1)} collective-permute-done((bf16[128,256]{1,0:T(8,128)(2,1)S(1)}, bf16[128,256]{1,0:T(8,128)(2,1)S(1)}, u32[]{:S(2)}, u32[]{:S(2)}) %collective-permute-start.31) | collective-permute-done | bytes 65568 | tf_op jit(solution)/shard_map/ppermute | solution.py:60
  (71 shorter events, 31.8 us)
Async XLA Ops:
  1.7 10.4 %collective-permute-start = (bf16[128,256]{1,0:T(8,128)(2,1)S(1)}, bf16[128,256]{1,0:T(8,128)(2,1)S(1)}, u32[]{:S(2)}, u32[]{:S(2)}) collective-permute-start(bf16[128,256]{1,0:T(8,128)(2,1)S(1)} %shard_map.85), channel_id=1, source_target_pairs={{1,0},{53,1},{65,2},{113,3},{129,4},{181,5},{195,6},{247,7},{9,8},... | collective-permute-start | bytes 196616 | tf_op jit(solution)/shard_map/ppermute | solution.py:60
  13.2 6.0 %collective-permute-start.3 = (bf16[128,256]{1,0:T(8,128)(2,1)S(1)}, bf16[128,256]{1,0:T(8,128)(2,1)S(1)}, u32[]{:S(2)}, u32[]{:S(2)}) collective-permute-start(bf16[128,256]{1,0:T(8,128)(2,1)S(1)} %collective-permute-done.high), channel_id=1, source_target_pairs={{0,64},{1,65},{2,66},{3,67},{4,68},{5,69},{6,70},{7,71},{8,72},{9,... | collective-permute-start | bytes 196616 | tf_op jit(solution)/shard_map/ppermute | solution.py:60
  15.6 5.2 %collective-permute-start.2 = (bf16[128,256]{1,0:T(8,128)(2,1)S(1)}, bf16[128,256]{1,0:T(8,128)(2,1)S(1)}, u32[]{:S(2)}, u32[]{:S(2)}) collective-permute-start(bf16[128,256]{1,0:T(8,128)(2,1)S(1)} %collective-permute-done.high), channel_id=1, source_target_pairs={{0,128},{1,129},{2,130},{3,131},{4,132},{5,133},{6,134},{7,135},{8... | collective-permute-start | bytes 196616 | tf_op jit(solution)/shard_map/ppermute | solution.py:60
  16.6 6.4 %collective-permute-start.6 = (bf16[256,256]{1,0:T(8,128)(2,1)S(1)}, bf16[256,256]{1,0:T(8,128)(2,1)S(1)}, u32[]{:S(2)}, u32[]{:S(2)}) collective-permute-start(bf16[256,256]{1,0:T(8,128)(2,1)S(1)} %shard_map.87.a0), channel_id=1, source_target_pairs={{0,16},{1,17},{2,18},{3,19},{4,20},{5,21},{6,22},{7,23},{8,24},{9,... | collective-permute-start | bytes 393224 | tf_op jit(solution)/shard_map/ppermute | solution.py:60
  20.7 5.1 %collective-permute-start.7 = (bf16[256,256]{1,0:T(8,128)(2,1)S(1)}, bf16[256,256]{1,0:T(8,128)(2,1)S(1)}, u32[]{:S(2)}, u32[]{:S(2)}) collective-permute-start(bf16[256,256]{1,0:T(8,128)(2,1)S(1)} %shard_map.88.b0), channel_id=1, source_target_pairs={{0,16},{1,17},{2,18},{3,19},{4,20},{5,21},{6,22},{7,23},{8,24},{9,... | collective-permute-start | bytes 393224 | tf_op jit(solution)/shard_map/ppermute | solution.py:60
  28.0 9.0 %collective-permute-start.10 = (f32[128,256]{1,0:T(8,128)S(1)}, f32[128,256]{1,0:T(8,128)S(1)}, u32[]{:S(2)}, u32[]{:S(2)}) collective-permute-start(f32[128,256]{1,0:T(8,128)S(1)} %get-tuple-element.42), channel_id=1, source_target_pairs={{0,6},{1,7},{2,4},{3,5},{4,2},{5,3},{6,0},{7,1},{8,14},{9,15},{10,... | collective-permute-start | bytes 393224 | tf_op jit(solution)/shard_map/ppermute | solution.py:60
  31.1 7.9 %collective-permute-start.11 = (f32[128,256]{1,0:T(8,128)S(1)}, f32[128,256]{1,0:T(8,128)S(1)}, u32[]{:S(2)}, u32[]{:S(2)}) collective-permute-start(f32[128,256]{1,0:T(8,128)S(1)} %get-tuple-element.43), channel_id=1, source_target_pairs={{0,4},{1,5},{2,6},{3,7},{4,0},{5,1},{6,2},{7,3},{8,12},{9,13},{10,... | collective-permute-start | bytes 393224 | tf_op jit(solution)/shard_map/ppermute | solution.py:60
  33.7 5.6 %collective-permute-start.12 = (f32[128,256]{1,0:T(8,128)S(1)}, f32[128,256]{1,0:T(8,128)S(1)}, u32[]{:S(2)}, u32[]{:S(2)}) collective-permute-start(f32[128,256]{1,0:T(8,128)S(1)} %get-tuple-element.44), channel_id=1, source_target_pairs={{0,2},{1,3},{2,0},{3,1},{4,6},{5,7},{6,4},{7,5},{8,10},{9,11},{10,... | collective-permute-start | bytes 393224 | tf_op jit(solution)/shard_map/ppermute | solution.py:60
  39.3 11.1 %collective-permute-start.13 = (bf16[320,256]{1,0:T(8,128)(2,1)S(1)}, bf16[320,256]{1,0:T(8,128)(2,1)S(1)}, u32[]{:S(2)}, u32[]{:S(2)}) collective-permute-start(bf16[320,256]{1,0:T(8,128)(2,1)S(1)} %shard_map.90.mine), channel_id=1, source_target_pairs={{0,1},{1,0},{2,3},{3,2},{4,5},{5,4},{6,7},{7,6},{8,9},{9,8},{10,11... | collective-permute-start | bytes 491528 | tf_op jit(solution)/shard_map/ppermute | solution.py:60
  51.2 6.4 %collective-permute-start.16 = (bf16[256,256]{1,0:T(8,128)(2,1)S(1)}, bf16[256,256]{1,0:T(8,128)(2,1)S(1)}, u32[]{:S(2)}, u32[]{:S(2)}) collective-permute-start(bf16[256,256]{1,0:T(8,128)(2,1)S(1)} %get-tuple-element.47.m0), channel_id=1, source_target_pairs={{0,6},{1,7},{2,4},{3,5},{4,2},{5,3},{6,0},{7,1},{8,14},{9,15},{10,... | collective-permute-start | bytes 393224 | tf_op jit(solution)/shard_map/ppermute | solution.py:60
  53.0 6.5 %collective-permute-start.15 = (bf16[256,256]{1,0:T(8,128)(2,1)S(1)}, bf16[256,256]{1,0:T(8,128)(2,1)S(1)}, u32[]{:S(2)}, u32[]{:S(2)}) collective-permute-start(bf16[256,256]{1,0:T(8,128)(2,1)S(1)} %get-tuple-element.47.m0), channel_id=1, source_target_pairs={{0,4},{1,5},{2,6},{3,7},{4,0},{5,1},{6,2},{7,3},{8,12},{9,13},{10,... | collective-permute-start | bytes 393224 | tf_op jit(solution)/shard_map/ppermute | solution.py:60
  64.3 7.4 %collective-permute-start.20 = (bf16[320,256]{1,0:T(8,128)(2,1)S(1)}, bf16[320,256]{1,0:T(8,128)(2,1)S(1)}, u32[]{:S(2)}, u32[]{:S(2)}) collective-permute-start(bf16[320,256]{1,0:T(8,128)(2,1)S(1)} %get-tuple-element.57), channel_id=1, source_target_pairs={{0,16},{1,17},{2,18},{3,19},{4,20},{5,21},{6,22},{7,23},{8,24},{9,... | collective-permute-start | bytes 491528 | tf_op jit(solution)/shard_map/ppermute | solution.py:60
  66.8 7.6 %collective-permute-start.19 = (bf16[256,256]{1,0:T(8,128)(2,1)S(1)}, bf16[256,256]{1,0:T(8,128)(2,1)S(1)}, u32[]{:S(2)}, u32[]{:S(2)}) collective-permute-start(bf16[256,256]{1,0:T(8,128)(2,1)S(1)} %get-tuple-element.56), channel_id=1, source_target_pairs={{0,16},{1,17},{2,18},{3,19},{4,20},{5,21},{6,22},{7,23},{8,24},{9,... | collective-permute-start | bytes 393224 | tf_op jit(solution)/shard_map/ppermute | solution.py:60
  71.8 8.8 %collective-permute-start.21 = (bf16[192,256]{1,0:T(8,128)(2,1)S(1)}, bf16[192,256]{1,0:T(8,128)(2,1)S(1)}, u32[]{:S(2)}, u32[]{:S(2)}) collective-permute-start(bf16[192,256]{1,0:T(8,128)(2,1)S(1)} %get-tuple-element.59), channel_id=1, source_target_pairs={{0,192},{1,193},{2,194},{3,195},{4,196},{5,197},{6,198},{7,199},{8... | collective-permute-start | bytes 294920 | tf_op jit(solution)/shard_map/ppermute | solution.py:60
  73.2 7.4 %collective-permute-start.22 = (bf16[192,256]{1,0:T(8,128)(2,1)S(1)}, bf16[192,256]{1,0:T(8,128)(2,1)S(1)}, u32[]{:S(2)}, u32[]{:S(2)}) collective-permute-start(bf16[192,256]{1,0:T(8,128)(2,1)S(1)} %get-tuple-element.60), channel_id=1, source_target_pairs={{0,128},{1,129},{2,130},{3,131},{4,132},{5,133},{6,134},{7,135},{8... | collective-permute-start | bytes 294920 | tf_op jit(solution)/shard_map/ppermute | solution.py:60
  74.4 7.0 %collective-permute-start.23 = (bf16[192,256]{1,0:T(8,128)(2,1)S(1)}, bf16[192,256]{1,0:T(8,128)(2,1)S(1)}, u32[]{:S(2)}, u32[]{:S(2)}) collective-permute-start(bf16[192,256]{1,0:T(8,128)(2,1)S(1)} %get-tuple-element.61), channel_id=1, source_target_pairs={{0,64},{1,65},{2,66},{3,67},{4,68},{5,69},{6,70},{7,71},{8,72},{9,... | collective-permute-start | bytes 294920 | tf_op jit(solution)/shard_map/ppermute | solution.py:60
  81.5 7.0 %collective-permute-start.24 = (f32[192,256]{1,0:T(8,128)S(1)}, f32[192,256]{1,0:T(8,128)S(1)}, u32[]{:S(2)}, u32[]{:S(2)}) collective-permute-start(f32[192,256]{1,0:T(8,128)S(1)} %shard_map.99.mine), channel_id=1, source_target_pairs={{0,48},{1,49},{2,50},{3,51},{4,52},{5,53},{6,54},{7,55},{8,56},{9,... | collective-permute-start | bytes 589832 | tf_op jit(solution)/shard_map/ppermute | solution.py:60
  88.5 6.9 %collective-permute-start.26 = (f32[64,256]{1,0:T(8,128)S(1)}, f32[64,256]{1,0:T(8,128)S(1)}, u32[]{:S(2)}, u32[]{:S(2)}) collective-permute-start(f32[64,256]{1,0:T(8,128)S(1)} %get-tuple-element.63.mine), channel_id=1, source_target_pairs={{0,8},{1,9},{2,10},{3,11},{4,12},{5,13},{6,14},{7,15},{8,0},{9,1},... | collective-permute-start | bytes 196616 | tf_op jit(solution)/shard_map/ppermute | solution.py:60
  88.6 11.0 %collective-permute-start.25 = (bf16[128,256]{1,0:T(8,128)(2,1)S(1)}, bf16[128,256]{1,0:T(8,128)(2,1)S(1)}, u32[]{:S(2)}, u32[]{:S(2)}) collective-permute-start(bf16[128,256]{1,0:T(8,128)(2,1)S(1)} %get-tuple-element.62), channel_id=1, source_target_pairs={{0,1},{1,53},{2,65},{3,113},{4,129},{5,181},{6,195},{7,247},{8,9},... | collective-permute-start | bytes 196616 | tf_op jit(solution)/shard_map/ppermute | solution.py:60
  95.3 6.4 %collective-permute-start.29 = (bf16[128,256]{1,0:T(8,128)(2,1)S(1)}, bf16[128,256]{1,0:T(8,128)(2,1)S(1)}, u32[]{:S(2)}, u32[]{:S(2)}) collective-permute-start(bf16[128,256]{1,0:T(8,128)(2,1)S(1)} %shard_map.101.w0), channel_id=1, source_target_pairs={{0,6},{1,7},{2,4},{3,5},{4,2},{5,3},{6,0},{7,1},{8,14},{9,15},{10,... | collective-permute-start | bytes 196616 | tf_op jit(solution)/shard_map/ppermute | solution.py:60
  96.4 6.1 %collective-permute-start.28 = (bf16[128,256]{1,0:T(8,128)(2,1)S(1)}, bf16[128,256]{1,0:T(8,128)(2,1)S(1)}, u32[]{:S(2)}, u32[]{:S(2)}) collective-permute-start(bf16[128,256]{1,0:T(8,128)(2,1)S(1)} %shard_map.101.w0), channel_id=1, source_target_pairs={{0,4},{1,5},{2,6},{3,7},{4,0},{5,1},{6,2},{7,3},{8,12},{9,13},{10,... | collective-permute-start | bytes 196616 | tf_op jit(solution)/shard_map/ppermute | solution.py:60
  96.4 6.4 %collective-permute-start.27 = (bf16[128,256]{1,0:T(8,128)(2,1)S(1)}, bf16[128,256]{1,0:T(8,128)(2,1)S(1)}, u32[]{:S(2)}, u32[]{:S(2)}) collective-permute-start(bf16[128,256]{1,0:T(8,128)(2,1)S(1)} %shard_map.101.w0), channel_id=1, source_target_pairs={{0,2},{1,3},{2,0},{3,1},{4,6},{5,7},{6,4},{7,5},{8,10},{9,11},{10,... | collective-permute-start | bytes 196616 | tf_op jit(solution)/shard_map/ppermute | solution.py:60
  102.8 5.6 %collective-permute-start.32 = (bf16[128,256]{1,0:T(8,128)(2,1)S(1)}, bf16[128,256]{1,0:T(8,128)(2,1)S(1)}, u32[]{:S(2)}, u32[]{:S(2)}) collective-permute-start(bf16[128,256]{1,0:T(8,128)(2,1)S(1)} %collective-permute-done.25.p0), channel_id=1, source_target_pairs={{0,6},{1,7},{2,4},{3,5},{4,2},{5,3},{6,0},{7,1},{8,14},{9,15},{10,... | collective-permute-start | bytes 196616 | tf_op jit(solution)/shard_map/ppermute | solution.py:60
  104.8 5.8 %collective-permute-start.31 = (bf16[128,256]{1,0:T(8,128)(2,1)S(1)}, bf16[128,256]{1,0:T(8,128)(2,1)S(1)}, u32[]{:S(2)}, u32[]{:S(2)}) collective-permute-start(bf16[128,256]{1,0:T(8,128)(2,1)S(1)} %collective-permute-done.25.p0), channel_id=1, source_target_pairs={{0,4},{1,5},{2,6},{3,7},{4,0},{5,1},{6,2},{7,3},{8,12},{9,13},{10,... | collective-permute-start | bytes 196616 | tf_op jit(solution)/shard_map/ppermute | solution.py:60
  (14 other events, 105.5 us)

commit v5 on v4

--- a/solution.py
+++ b/solution.py
@@ -1,3 +1,4 @@
+import functools
 import itertools
 
 import jax
@@ -60,6 +61,10 @@
     return lax.ppermute(value, AXES, route)
 
 
+def spread(value, routes):
+    return [value] + [send(value, route) for route in routes[::-1]]
+
+
 def place():
     r = lax.axis_index("rows")
     p = lax.axis_index("rep")
@@ -140,12 +145,22 @@
     out[PART:, :] = high[...]
 
 
-def forward_body(dense, a0, b0, a1, b1, a2, b2, a3, b3, to3, to2, to1, own, blocks, total):
-    me = place()
-    for i, (first, second) in enumerate(((a0, b0), (a1, b1), (a2, b2), (a3, b3))):
-        for k, part in ((3, first[0:PART, :]), (0, first[PART:, :]), (2, second[0:PART, :]), (1, second[PART:, :])):
-            blocks[i, at(me["z"] ^ k, PART), :] = part
-    total[...] = dot(dense[0], blocks[0]) + dot(dense[1], blocks[1]) + (dot(dense[2], blocks[2]) + dot(dense[3], blocks[3]))
+def put_block(me, blocks, i, first, second):
+    for k, part in ((3, first[0:PART, :]), (0, first[PART:, :]), (2, second[0:PART, :]), (1, second[PART:, :])):
+        blocks[i, at(me["z"] ^ k, PART), :] = part
+
+
+def forward_body(dense, b0, a0, b1, a1, b2, a2, total, blocks):
+    me = place()
+    for i, (first, second) in enumerate(((a0, b0), (a1, b1), (a2, b2))):
+        put_block(me, blocks, i, first, second)
+    total[...] = dot(dense[0], blocks[0]) + dot(dense[1], blocks[1]) + dot(dense[2], blocks[2])
+
+
+def forward_last_body(dense, b3, a3, most, to3, to2, to1, own, blocks, total):
+    me = place()
+    put_block(me, blocks, 0, a3, b3)
+    total[...] = most[...] + dot(dense[3], blocks[0])
     for k, to in enumerate((own, to1, to2, to3)):
         to[...] = total[at(me["x"] ^ k, PART), :]
 
@@ -158,22 +173,29 @@
     to_h[2 * PART :, :] = cot[...]
 
 
-def layer_body(mine, got, weight, output, message):
-    me = place()
+def aggregate_of(mine, got):
     parts = [ref[0:PART, :].astype(F32) + ref[PART : 2 * PART, :].astype(F32) for ref in (mine, got)]
-    aggregate = (parts[0] + parts[1]).astype(BF)
+    return (parts[0] + parts[1]).astype(BF)
+
+
+def layer_body(mine, got, weight, message):
+    aggregate = aggregate_of(mine, got)
     preact = dot(aggregate, weight[...])
     gates = jax.nn.sigmoid(preact)
-    activation = (preact * gates).astype(BF)
-    first = me["h"] == 0
-    output[...] = jnp.where(first, activation[:SLICE], activation[SLICE:])
+    first = place()["h"] == 0
     a, b = mine[2 * PART :, :], got[2 * PART :, :]
     cotangent = jnp.concatenate([jnp.where(first, a, b), jnp.where(first, b, a)], axis=0).astype(F32)
     message[0:PART, :] = aggregate
     message[PART:, :] = (cotangent * gates * (1.0 + preact * (1.0 - gates))).astype(BF)
 
 
-def backward_body(dense_t, weight, m0, m1, m2, m3, to_c, aggregate, grad_pre, grad_agg):
+def output_body(message, weight, output):
+    own = message[at(place()["h"], SLICE), :]
+    preact = dot(own, weight[...])
+    output[...] = (preact * jax.nn.sigmoid(preact)).astype(BF)
+
+
+def backward_body(dense_t, weight, m0, m3, m2, m1, to_c, grad_agg, aggregate, grad_pre, grad_w):
     me = place()
     for k, m in enumerate((m0, m1, m2, m3)):
         rows = at(me["x"] ^ k, PART)
@@ -181,22 +203,23 @@
         grad_pre[rows, :] = m[PART:, :]
     grad = dot(grad_pre[...], weight[...], ((1,), (1,))).astype(BF)
     grad_agg[...] = grad
-    to_c[...] = dot(dense_t[3], grad)
-
-
-def share_body(dense_t, aggregate, grad_pre, grad_agg, keep, share, grad_w):
-    me = place()
+    to_c[0:BLOCK, :] = dot(dense_t[3], grad)
+    grad_w[...] = dot(aggregate[...], grad_pre[...], ((0,), (0,)))
+    to_c[BLOCK:, :] = grad_w[at(me["x"], SLICE), :]
+
+
+def keep_body(dense_t, grad_agg, keep):
     keep[...] = dot(dense_t[2], grad_agg[...])
-    grad_w[...] = dot(aggregate[...], grad_pre[...], ((0,), (0,)))
-    share[...] = grad_w[at(me["x"], SLICE), :].astype(BF)
-
-
-def to_u_body(keep, got, share, first, second):
-    me = place()
-    for k, out, start in ((3, first, 0), (2, first, PART), (1, second, 0), (0, second, PART)):
+
+
+def to_u_body(keep, mine, got, u3, u2, u1, u0, share):
+    me = place()
+    for k, out in ((3, u3), (2, u2), (1, u1), (0, u0)):
         rows = at(me["z"] ^ k, PART)
-        out[start : start + PART, :] = (keep[rows, :] + got[rows, :]).astype(BF)
-    first[2 * PART :, :] = share[...]
+        out[0:PART, :] = (keep[rows, :] + got[rows, :]).astype(BF)
+    both = (mine[BLOCK:, :] + got[BLOCK:, :]).astype(BF)
+    u3[PART:, :] = both
+    share[...] = both
 
 
 def kept_body(dense_t, grad_agg, to_c, keep):
@@ -211,22 +234,23 @@
         own[k * PART : (k + 1) * PART, :] = total[at(me["z"] ^ k, PART), :]
 
 
-def to_z_body(own, got, share, to3, to2):
-    pair = (share[...].astype(F32) + got[2 * PART :, :].astype(F32)).astype(BF)
-    for to, start, k in ((to3, 0, 3), (to2, PART, 2)):
-        to[0:PART, :] = (own[k * PART : (k + 1) * PART, :] + got[start : start + PART, :].astype(F32)).astype(BF)
-        to[PART:, :] = pair
-
-
-def to_z1_body(own, got, share, got_first, to, kept_share):
-    to[0:PART, :] = (own[PART : 2 * PART, :] + got[0:PART, :].astype(F32)).astype(BF)
-    pair = (share[...].astype(F32) + got_first[2 * PART :, :].astype(F32)).astype(BF)
-    to[PART:, :] = pair
-    kept_share[...] = pair
-
-
-def after_z_body(own, got, share, r3, r2, r1, to_v):
-    total = own[0:PART, :] + got[PART:, :].astype(F32) + r1[0:PART, :].astype(F32)
+def pair_share(share, got_first):
+    return (share[...].astype(F32) + got_first[PART:, :].astype(F32)).astype(BF)
+
+
+def to_z_body(k, own, got, share, got_first, to):
+    to[0:PART, :] = (own[k * PART : (k + 1) * PART, :] + got[0:PART, :].astype(F32)).astype(BF)
+    to[PART:, :] = pair_share(share, got_first)
+
+
+def to_z1_body(own, got, share, got_first, got_own, to, kept, kept_share):
+    to_z_body(1, own, got, share, got_first, to)
+    kept[...] = own[0:PART, :] + got_own[...].astype(F32)
+    kept_share[...] = pair_share(share, got_first)
+
+
+def after_z_body(kept, share, r1, r2, r3, to_v):
+    total = kept[...] + r1[0:PART, :].astype(F32)
     to_v[0:PART, :] = total + (r2[0:PART, :].astype(F32) + r3[0:PART, :].astype(F32))
     pair = share[...].astype(F32) + r1[PART:, :].astype(F32)
     to_v[PART:, :] = pair + (r2[PART:, :].astype(F32) + r3[PART:, :].astype(F32))
@@ -234,17 +258,18 @@
 
 def after_v_body(mine, got, piece, share):
     piece[...] = (mine[0:PART, :] + got[0:PART, :]).astype(BF)
-    share[...] = mine[PART:, :] + got[PART:, :]
-
-
-def last_share_body(mine, got, message):
-    put_split(message, 0, mine[...] + got[...])
-
-
-def finish_body(p0, p1, p2, p3, w0, w1, w2, w3, grad_features, grad_weight):
-    me = place()
-    for k, (piece, share) in enumerate(((p0, w0), (p1, w1), (p2, w2), (p3, w3))):
+    put_split(share, 0, mine[PART:, :] + got[PART:, :])
+
+
+def finish_body(p0, p3, p2, p1, grad_features):
+    me = place()
+    for k, piece in enumerate((p0, p1, p2, p3)):
         grad_features[at(chunk_of(me, me["x"] ^ k), PART), :] = piece[...]
+
+
+def finish_weight_body(w0, w3, w2, w1, grad_weight):
+    me = place()
+    for k, share in enumerate((w0, w1, w2, w3)):
         grad_weight[at(me["x"] ^ k, SLICE), :] = get_split(share, 0)
 
 
@@ -256,6 +281,7 @@
     share32 = ((SLICE, WIDTH), F32)
     share16 = ((SLICE, WIDTH), BF)
     two = ((2 * PART, WIDTH), BF)
+    to_z = ((PART + SLICE, WIDTH), BF)
     dense_shape = ((4, BLOCK, BLOCK), BF)
 
     (chunk,) = call(chunk_body, [part], features, specs=[HBM], scratch=[pltpu.SemaphoreType.DMA])
@@ -264,48 +290,48 @@
         dense_body, [dense_shape, dense_shape], tile_slots, tile_count, tile_values, specs=[SMEM, SMEM, VMEM]
     )
     chunk, dense, dense_t = lax.optimization_barrier((chunk, dense, dense_t))
-    chunks = [chunk] + [send(chunk, route) for route in FLIP_Z]
-    c0, c1, c2, c3 = chunks
+    chunks = spread(chunk, FLIP_Z)
+    c0, c3, c2, c1 = chunks
     mine = [call(pair_body, [two], c3, c0)[0], call(pair_body, [two], c2, c1)[0]]
     by_u = [send(value, FLIP_U) for value in mine]
     by_c = [send(value, FLIP_C) for value in mine]
     by_uc = [send(value, FLIP_C) for value in by_u]
+    total = pltpu.VMEM((BLOCK, WIDTH), F32)
+    (most,) = call(
+        forward_body, [block32], dense, *mine[::-1], *by_c[::-1], *by_u[::-1], scratch=[pltpu.VMEM((3, BLOCK, WIDTH), BF)]
+    )
     to3, to2, to1, own = call(
-        forward_body, [part32] * 4, dense, *mine, *by_c, *by_u, *by_uc,
-        scratch=[pltpu.VMEM((4, BLOCK, WIDTH), BF), pltpu.VMEM((BLOCK, WIDTH), F32)],
+        forward_last_body, [part32] * 4, dense, *by_uc[::-1], most, scratch=[pltpu.VMEM((1, BLOCK, WIDTH), BF), total]
     )
     got = [send(value, route) for value, route in zip((to3, to2, to1), FLIP_X[::-1])]
     (mine,) = call(sum_body, [((2 * PART + SLICE, WIDTH), BF)], own, *got, cotangent)
     got = send(mine, FLIP_H)
-    output, message = call(
-        layer_body, [((SLICE, WIDTH), BF), ((2 * PART, WIDTH), BF)], mine, got, weight
-    )
-    got = [send(message, route) for route in FLIP_X]
-
-    to_c, aggregate, grad_pre, grad_agg = call(
-        backward_body, [block32, block, block, block], dense_t, weight, message, *got
+    (message,) = call(layer_body, [two], mine, got, weight)
+    (output,) = call(output_body, [((SLICE, WIDTH), BF)], message, weight)
+    got = spread(message, FLIP_X)
+
+    whole = pltpu.VMEM((BLOCK, WIDTH), BF)
+    to_c, grad_agg = call(
+        backward_body, [((BLOCK + SLICE, WIDTH), F32), block], dense_t, weight, *got,
+        scratch=[whole, whole, pltpu.VMEM((WIDTH, WIDTH), F32)],
     )
     got = send(to_c, FLIP_C)
-    keep, share = call(
-        share_body, [block32, share16], dense_t, aggregate, grad_pre, grad_agg,
-        scratch=[pltpu.VMEM((WIDTH, WIDTH), F32)],
-    )
-    first, second = call(to_u_body, [((2 * PART + SLICE, WIDTH), BF), two], keep, got, share)
-    got_first, got_second = send(first, FLIP_U), send(second, FLIP_U)
+    (keep_u,) = call(keep_body, [block32], dense_t, grad_agg)
+    *to_u, share = call(to_u_body, [to_z, part, part, part, share16], keep_u, to_c, got)
+    u3, u2, u1, u0 = [send(value, FLIP_U) for value in to_u]
     to_c, keep = call(kept_body, [block32, block32], dense_t, grad_agg)
-    (own,) = call(after_c_body, [block32], keep, send(to_c, FLIP_C), scratch=[pltpu.VMEM((BLOCK, WIDTH), F32)])
-    to_z = ((PART + SLICE, WIDTH), BF)
-    to3, to2 = call(to_z_body, [to_z, to_z], own, got_first, share)
-    to1, share = call(to_z1_body, [to_z, share16], own, got_second, share, got_first)
-    from_z = [send(value, route) for value, route in zip((to3, to2, to1), FLIP_Z[::-1])]
-    (to_v,) = call(after_z_body, [((PART + SLICE, WIDTH), F32)], own, got_second, share, *from_z)
-    piece, share = call(after_v_body, [part, share32], to_v, send(to_v, FLIP_V))
+    (own,) = call(after_c_body, [block32], keep, send(to_c, FLIP_C), scratch=[total])
+    (to3,) = call(functools.partial(to_z_body, 3), [to_z], own, u3, share, u3)
+    (to2,) = call(functools.partial(to_z_body, 2), [to_z], own, u2, share, u3)
+    to1, kept, share = call(to_z1_body, [to_z, part32, share16], own, u1, share, u3, u0)
+    from_z = [send(value, route) for value, route in zip((to1, to2, to3), FLIP_Z)]
+    (to_v,) = call(after_z_body, [((PART + SLICE, WIDTH), F32)], kept, share, *from_z)
+    piece, share = call(after_v_body, [part, part], to_v, send(to_v, FLIP_V))
     piece = send(piece, TO_ROW)
-    (share,) = call(last_share_body, [((2 * SLICE, WIDTH), BF)], share, send(share, FLIP_C))
-    shares = [share] + [send(share, route) for route in FLIP_X]
-    piece, *shares = lax.optimization_barrier((piece, *shares))
-    pieces = [piece] + [send(piece, route) for route in FLIP_X]
-    grad_features, grad_weight = call(finish_body, [block, ((WIDTH, WIDTH), F32)], *pieces, *shares)
+    shares = spread(share, FLIP_X)
+    pieces = spread(piece, FLIP_X)
+    (grad_weight,) = call(finish_weight_body, [((WIDTH, WIDTH), F32)], *shares)
+    (grad_features,) = call(finish_body, [block], *pieces)
     return output, grad_weight, grad_features
 
 

time: 112 us -> 108 us (0.964)
  starting transfers between devices: 50.7 us -> 46.4 us
  waiting for transfers between devices: 51 us -> 49.6 us
    ppermute x33 -> x34, starting transfers between devices: 50.7 us -> 46.4 us  [send(): return lax.ppermute(value, AXES, route)]
    ppermute x33 -> x34, waiting for transfers between devices: 51 us -> 49.6 us  [send(): return lax.ppermute(value, AXES, route)]
    pallas_call x18 -> x21, Pallas kernels: 5.57 us -> 6.42 us  [call(): pl.pallas_call(body, out_shape=[jax.ShapeDtypeStruct(shape, dtype) for sh...]
  transfers between devices with their start and end apart: 33 -> 34, of which waited for: 23 -> 18; matrix products, arithmetic and copies ran while one was open for 1% -> 1% of each run, Pallas kernels for 2% -> 4%
where the time goes in v5:
time: 108 us; the launch traced here: 106 us
  waiting for transfers between devices  49.6 us (46%)
  starting transfers between devices  46.4 us (43%)
  Pallas kernels  6.42 us (6%)
  local copies, waits for them, and re-layouts  3.32 us (3%)
    ppermute x34, waiting for transfers between devices, send(): return lax.ppermute(value, AXES, route)  49.6 us
    ppermute x34, starting transfers between devices, send(): return lax.ppermute(value, AXES, route)  46.4 us
    pallas_call x21, Pallas kernels, call(): pl.pallas_call(body, out_shape=[jax.ShapeDtypeStruct(shape, dtype) for sh...  6.42 us
    unnamed x11, local copies, waits for them, and re-layouts  3.32 us
  transfers between devices with their start and end apart: 34, of which 18 were waited for; matrix products, arithmetic and copies ran while one was open for 1% of the time, Pallas kernels for 4%

profile of v5, /device:TPU:32, one launch (start us, length us, event | category | flops | bytes accessed | tf_op | source)
XLA Modules:
  0.0 106.5 jit_solution(15315256869677166140)
XLA Ops:
  1.6 3.6 %collective-permute-start = (bf16[128,256]{1,0:T(8,128)(2,1)S(1)}, bf16[128,256]{1,0:T(8,128)(2,1)S(1)}, u32[]{:S(2)}, u32[]{:S(2)}) collective-permute-start(bf16[128,256]{1,0:T(8,128)(2,1)S(1)} %shard_map.85), channel_id=1, source_target_pairs={{1,0},{53,1},{65,2},{113,3},{129,4},{181,5},{195,6},{247,7},{9,8},... | collective-permute-start | bytes 196616 | tf_op jit(solution)/shard_map/ppermute | solution.py:61
  8.8 3.3 %collective-permute-done.high = bf16[128,256]{1,0:T(8,128)(2,1)S(1)} collective-permute-done((bf16[128,256]{1,0:T(8,128)(2,1)S(1)}, bf16[128,256]{1,0:T(8,128)(2,1)S(1)}, u32[]{:S(2)}, u32[]{:S(2)}) %collective-permute-start) | collective-permute-done | bytes 65568 | tf_op jit(solution)/shard_map/ppermute | solution.py:61
  13.2 1.7 %collective-permute-start.1 = (bf16[128,256]{1,0:T(8,128)(2,1)S(1)}, bf16[128,256]{1,0:T(8,128)(2,1)S(1)}, u32[]{:S(2)}, u32[]{:S(2)}) collective-permute-start(bf16[128,256]{1,0:T(8,128)(2,1)S(1)} %collective-permute-done.high), channel_id=1, source_target_pairs={{0,128},{1,129},{2,130},{3,131},{4,132},{5,133},{6,134},{7,135},{8... | collective-permute-start | bytes 196616 | tf_op jit(solution)/shard_map/ppermute | solution.py:61
  15.6 3.6 %collective-permute-done.5.low = bf16[128,256]{1,0:T(8,128)(2,1)S(1)} collective-permute-done((bf16[128,256]{1,0:T(8,128)(2,1)S(1)}, bf16[128,256]{1,0:T(8,128)(2,1)S(1)}, u32[]{:S(2)}, u32[]{:S(2)}) %collective-permute-start.5) | collective-permute-done | bytes 65568 | tf_op jit(solution)/shard_map/ppermute | solution.py:61
  19.2 1.4 %collective-permute-start.6 = (bf16[256,256]{1,0:T(8,128)(2,1)S(1)}, bf16[256,256]{1,0:T(8,128)(2,1)S(1)}, u32[]{:S(2)}, u32[]{:S(2)}) collective-permute-start(bf16[256,256]{1,0:T(8,128)(2,1)S(1)} %shard_map.88.a0), channel_id=1, source_target_pairs={{0,16},{1,17},{2,18},{3,19},{4,20},{5,21},{6,22},{7,23},{8,24},{9,... | collective-permute-start | bytes 393224 | tf_op jit(solution)/shard_map/ppermute | solution.py:61
  22.1 2.1 %collective-permute-done.6.a2 = bf16[256,256]{1,0:T(8,128)(2,1)S(1)} collective-permute-done((bf16[256,256]{1,0:T(8,128)(2,1)S(1)}, bf16[256,256]{1,0:T(8,128)(2,1)S(1)}, u32[]{:S(2)}, u32[]{:S(2)}) %collective-permute-start.6) | collective-permute-done | bytes 131104 | tf_op jit(solution)/shard_map/ppermute | solution.py:61
  24.2 1.4 %collective-permute-done.3.b2 = bf16[256,256]{1,0:T(8,128)(2,1)S(1)} collective-permute-done((bf16[256,256]{1,0:T(8,128)(2,1)S(1)}, bf16[256,256]{1,0:T(8,128)(2,1)S(1)}, u32[]{:S(2)}, u32[]{:S(2)}) %collective-permute-start.3) | collective-permute-done | bytes 131104 | tf_op jit(solution)/shard_map/ppermute | solution.py:61
  27.4 4.1 %collective-permute-start.10 = (f32[128,256]{1,0:T(8,128)S(1)}, f32[128,256]{1,0:T(8,128)S(1)}, u32[]{:S(2)}, u32[]{:S(2)}) collective-permute-start(f32[128,256]{1,0:T(8,128)S(1)} %get-tuple-element.31), channel_id=1, source_target_pairs={{0,6},{1,7},{2,4},{3,5},{4,2},{5,3},{6,0},{7,1},{8,14},{9,15},{10,... | collective-permute-start | bytes 393224 | tf_op jit(solution)/shard_map/ppermute | solution.py:61
  32.5 4.8 %collective-permute-done.10.r3 = f32[128,256]{1,0:T(8,128)S(1)} collective-permute-done((f32[128,256]{1,0:T(8,128)S(1)}, f32[128,256]{1,0:T(8,128)S(1)}, u32[]{:S(2)}, u32[]{:S(2)}) %collective-permute-start.10) | collective-permute-done | bytes 131104 | tf_op jit(solution)/shard_map/ppermute | solution.py:61
  37.4 2.0 %collective-permute-done.11.r2 = f32[128,256]{1,0:T(8,128)S(1)} collective-permute-done((f32[128,256]{1,0:T(8,128)S(1)}, f32[128,256]{1,0:T(8,128)S(1)}, u32[]{:S(2)}, u32[]{:S(2)}) %collective-permute-start.11) | collective-permute-done | bytes 131104 | tf_op jit(solution)/shard_map/ppermute | solution.py:61
  39.4 3.3 %collective-permute-start.13 = (bf16[320,256]{1,0:T(8,128)(2,1)S(1)}, bf16[320,256]{1,0:T(8,128)(2,1)S(1)}, u32[]{:S(2)}, u32[]{:S(2)}) collective-permute-start(bf16[320,256]{1,0:T(8,128)(2,1)S(1)} %shard_map.91.mine), channel_id=1, source_target_pairs={{0,1},{1,0},{2,3},{3,2},{4,5},{5,4},{6,7},{7,6},{8,9},{9,8},{10,11... | collective-permute-start | bytes 491528 | tf_op jit(solution)/shard_map/ppermute | solution.py:61
  42.7 8.2 %collective-permute-done.13.got = bf16[320,256]{1,0:T(8,128)(2,1)S(1)} collective-permute-done((bf16[320,256]{1,0:T(8,128)(2,1)S(1)}, bf16[320,256]{1,0:T(8,128)(2,1)S(1)}, u32[]{:S(2)}, u32[]{:S(2)}) %collective-permute-start.13) | collective-permute-done | bytes 163872 | tf_op jit(solution)/shard_map/ppermute | solution.py:61
  51.1 3.5 %collective-permute-start.14 = (bf16[256,256]{1,0:T(8,128)(2,1)S(1)}, bf16[256,256]{1,0:T(8,128)(2,1)S(1)}, u32[]{:S(2)}, u32[]{:S(2)}) collective-permute-start(bf16[256,256]{1,0:T(8,128)(2,1)S(1)} %shard_map.92.message.m0), channel_id=1, source_target_pairs={{0,6},{1,7},{2,4},{3,5},{4,2},{5,3},{6,0},{7,1},{8,14},{9,15},{10,... | collective-permute-start | bytes 393224 | tf_op jit(solution)/shard_map/ppermute | solution.py:61
  55.6 4.7 %collective-permute-done.14.m3 = bf16[256,256]{1,0:T(8,128)(2,1)S(1)} collective-permute-done((bf16[256,256]{1,0:T(8,128)(2,1)S(1)}, bf16[256,256]{1,0:T(8,128)(2,1)S(1)}, u32[]{:S(2)}, u32[]{:S(2)}) %collective-permute-start.14) | collective-permute-done | bytes 131104 | tf_op jit(solution)/shard_map/ppermute | solution.py:61
  60.3 2.3 %collective-permute-done.15.m2 = bf16[256,256]{1,0:T(8,128)(2,1)S(1)} collective-permute-done((bf16[256,256]{1,0:T(8,128)(2,1)S(1)}, bf16[256,256]{1,0:T(8,128)(2,1)S(1)}, u32[]{:S(2)}, u32[]{:S(2)}) %collective-permute-start.15) | collective-permute-done | bytes 131104 | tf_op jit(solution)/shard_map/ppermute | solution.py:61
  69.8 1.5 %collective-permute-done.20.got_first.got = bf16[192,256]{1,0:T(8,128)(2,1)S(1)} collective-permute-done((bf16[192,256]{1,0:T(8,128)(2,1)S(1)}, bf16[192,256]{1,0:T(8,128)(2,1)S(1)}, u32[]{:S(2)}, u32[]{:S(2)}) %collective-permute-start.20) | collective-permute-done | bytes 98336 | tf_op jit(solution)/shard_map/ppermute | solution.py:61
  75.3 4.6 %collective-permute-done.25.r3 = bf16[192,256]{1,0:T(8,128)(2,1)S(1)} collective-permute-done((bf16[192,256]{1,0:T(8,128)(2,1)S(1)}, bf16[192,256]{1,0:T(8,128)(2,1)S(1)}, u32[]{:S(2)}, u32[]{:S(2)}) %collective-permute-start.25) | collective-permute-done | bytes 98336 | tf_op jit(solution)/shard_map/ppermute | solution.py:61
  80.0 3.2 %collective-permute-start.26 = (f32[192,256]{1,0:T(8,128)S(1)}, f32[192,256]{1,0:T(8,128)S(1)}, u32[]{:S(2)}, u32[]{:S(2)}) collective-permute-start(f32[192,256]{1,0:T(8,128)S(1)} %shard_map.102.mine), channel_id=1, source_target_pairs={{0,48},{1,49},{2,50},{3,51},{4,52},{5,53},{6,54},{7,55},{8,56},{9,... | collective-permute-start | bytes 589832 | tf_op jit(solution)/shard_map/ppermute | solution.py:61
  83.2 4.3 %collective-permute-done.26.got = f32[192,256]{1,0:T(8,128)S(1)} collective-permute-done((f32[192,256]{1,0:T(8,128)S(1)}, f32[192,256]{1,0:T(8,128)S(1)}, u32[]{:S(2)}, u32[]{:S(2)}) %collective-permute-start.26) | collective-permute-done | bytes 196640 | tf_op jit(solution)/shard_map/ppermute | solution.py:61
  87.5 5.2 %collective-permute-start.30 = (bf16[128,256]{1,0:T(8,128)(2,1)S(1)}, bf16[128,256]{1,0:T(8,128)(2,1)S(1)}, u32[]{:S(2)}, u32[]{:S(2)}) collective-permute-start(bf16[128,256]{1,0:T(8,128)(2,1)S(1)} %get-tuple-element.48), channel_id=1, source_target_pairs={{0,1},{1,53},{2,65},{3,113},{4,129},{5,181},{6,195},{7,247},{8,9},... | collective-permute-start | bytes 196616 | tf_op jit(solution)/shard_map/ppermute | solution.py:61
  92.7 1.8 %collective-permute-start.27 = (bf16[128,256]{1,0:T(8,128)(2,1)S(1)}, bf16[128,256]{1,0:T(8,128)(2,1)S(1)}, u32[]{:S(2)}, u32[]{:S(2)}) collective-permute-start(bf16[128,256]{1,0:T(8,128)(2,1)S(1)} %get-tuple-element.47.w0), channel_id=1, source_target_pairs={{0,6},{1,7},{2,4},{3,5},{4,2},{5,3},{6,0},{7,1},{8,14},{9,15},{10,... | collective-permute-start | bytes 196616 | tf_op jit(solution)/shard_map/ppermute | solution.py:61
  95.3 1.5 %collective-permute-start.29 = (bf16[128,256]{1,0:T(8,128)(2,1)S(1)}, bf16[128,256]{1,0:T(8,128)(2,1)S(1)}, u32[]{:S(2)}, u32[]{:S(2)}) collective-permute-start(bf16[128,256]{1,0:T(8,128)(2,1)S(1)} %get-tuple-element.47.w0), channel_id=1, source_target_pairs={{0,2},{1,3},{2,0},{3,1},{4,6},{5,7},{6,4},{7,5},{8,10},{9,11},{10,... | collective-permute-start | bytes 196616 | tf_op jit(solution)/shard_map/ppermute | solution.py:61
  96.8 3.2 %collective-permute-start.31 = (bf16[128,256]{1,0:T(8,128)(2,1)S(1)}, bf16[128,256]{1,0:T(8,128)(2,1)S(1)}, u32[]{:S(2)}, u32[]{:S(2)}) collective-permute-start(bf16[128,256]{1,0:T(8,128)(2,1)S(1)} %collective-permute-done.30.p0), channel_id=1, source_target_pairs={{0,6},{1,7},{2,4},{3,5},{4,2},{5,3},{6,0},{7,1},{8,14},{9,15},{10,... | collective-permute-start | bytes 196616 | tf_op jit(solution)/shard_map/ppermute | solution.py:61
  102.5 3.3 %collective-permute-done.32.p2 = bf16[128,256]{1,0:T(8,128)(2,1)S(1)} collective-permute-done((bf16[128,256]{1,0:T(8,128)(2,1)S(1)}, bf16[128,256]{1,0:T(8,128)(2,1)S(1)}, u32[]{:S(2)}, u32[]{:S(2)}) %collective-permute-start.32) | collective-permute-done | bytes 65568 | tf_op jit(solution)/shard_map/ppermute | solution.py:61
  (76 shorter events, 27.1 us)
Async XLA Ops:
  1.6 10.4 %collective-permute-start = (bf16[128,256]{1,0:T(8,128)(2,1)S(1)}, bf16[128,256]{1,0:T(8,128)(2,1)S(1)}, u32[]{:S(2)}, u32[]{:S(2)}) collective-permute-start(bf16[128,256]{1,0:T(8,128)(2,1)S(1)} %shard_map.85), channel_id=1, source_target_pairs={{1,0},{53,1},{65,2},{113,3},{129,4},{181,5},{195,6},{247,7},{9,8},... | collective-permute-start | bytes 196616 | tf_op jit(solution)/shard_map/ppermute | solution.py:61
  12.1 7.1 %collective-permute-start.5 = (bf16[128,256]{1,0:T(8,128)(2,1)S(1)}, bf16[128,256]{1,0:T(8,128)(2,1)S(1)}, u32[]{:S(2)}, u32[]{:S(2)}) collective-permute-start(bf16[128,256]{1,0:T(8,128)(2,1)S(1)} %collective-permute-done.high), channel_id=1, source_target_pairs={{0,192},{1,193},{2,194},{3,195},{4,196},{5,197},{6,198},{7,199},{8... | collective-permute-start | bytes 196616 | tf_op jit(solution)/shard_map/ppermute | solution.py:61
  13.2 7.3 %collective-permute-start.1 = (bf16[128,256]{1,0:T(8,128)(2,1)S(1)}, bf16[128,256]{1,0:T(8,128)(2,1)S(1)}, u32[]{:S(2)}, u32[]{:S(2)}) collective-permute-start(bf16[128,256]{1,0:T(8,128)(2,1)S(1)} %collective-permute-done.high), channel_id=1, source_target_pairs={{0,128},{1,129},{2,130},{3,131},{4,132},{5,133},{6,134},{7,135},{8... | collective-permute-start | bytes 196616 | tf_op jit(solution)/shard_map/ppermute | solution.py:61
  27.4 10.0 %collective-permute-start.10 = (f32[128,256]{1,0:T(8,128)S(1)}, f32[128,256]{1,0:T(8,128)S(1)}, u32[]{:S(2)}, u32[]{:S(2)}) collective-permute-start(f32[128,256]{1,0:T(8,128)S(1)} %get-tuple-element.31), channel_id=1, source_target_pairs={{0,6},{1,7},{2,4},{3,5},{4,2},{5,3},{6,0},{7,1},{8,14},{9,15},{10,... | collective-permute-start | bytes 393224 | tf_op jit(solution)/shard_map/ppermute | solution.py:61
  31.5 7.9 %collective-permute-start.11 = (f32[128,256]{1,0:T(8,128)S(1)}, f32[128,256]{1,0:T(8,128)S(1)}, u32[]{:S(2)}, u32[]{:S(2)}) collective-permute-start(f32[128,256]{1,0:T(8,128)S(1)} %get-tuple-element.32), channel_id=1, source_target_pairs={{0,4},{1,5},{2,6},{3,7},{4,0},{5,1},{6,2},{7,3},{8,12},{9,13},{10,... | collective-permute-start | bytes 393224 | tf_op jit(solution)/shard_map/ppermute | solution.py:61
  32.5 6.8 %collective-permute-start.12 = (f32[128,256]{1,0:T(8,128)S(1)}, f32[128,256]{1,0:T(8,128)S(1)}, u32[]{:S(2)}, u32[]{:S(2)}) collective-permute-start(f32[128,256]{1,0:T(8,128)S(1)} %get-tuple-element.33), channel_id=1, source_target_pairs={{0,2},{1,3},{2,0},{3,1},{4,6},{5,7},{6,4},{7,5},{8,10},{9,11},{10,... | collective-permute-start | bytes 393224 | tf_op jit(solution)/shard_map/ppermute | solution.py:61
  39.4 11.5 %collective-permute-start.13 = (bf16[320,256]{1,0:T(8,128)(2,1)S(1)}, bf16[320,256]{1,0:T(8,128)(2,1)S(1)}, u32[]{:S(2)}, u32[]{:S(2)}) collective-permute-start(bf16[320,256]{1,0:T(8,128)(2,1)S(1)} %shard_map.91.mine), channel_id=1, source_target_pairs={{0,1},{1,0},{2,3},{3,2},{4,5},{5,4},{6,7},{7,6},{8,9},{9,8},{10,11... | collective-permute-start | bytes 491528 | tf_op jit(solution)/shard_map/ppermute | solution.py:61
  51.1 9.2 %collective-permute-start.14 = (bf16[256,256]{1,0:T(8,128)(2,1)S(1)}, bf16[256,256]{1,0:T(8,128)(2,1)S(1)}, u32[]{:S(2)}, u32[]{:S(2)}) collective-permute-start(bf16[256,256]{1,0:T(8,128)(2,1)S(1)} %shard_map.92.message.m0), channel_id=1, source_target_pairs={{0,6},{1,7},{2,4},{3,5},{4,2},{5,3},{6,0},{7,1},{8,14},{9,15},{10,... | collective-permute-start | bytes 393224 | tf_op jit(solution)/shard_map/ppermute | solution.py:61
  54.7 7.9 %collective-permute-start.15 = (bf16[256,256]{1,0:T(8,128)(2,1)S(1)}, bf16[256,256]{1,0:T(8,128)(2,1)S(1)}, u32[]{:S(2)}, u32[]{:S(2)}) collective-permute-start(bf16[256,256]{1,0:T(8,128)(2,1)S(1)} %shard_map.92.message.m0), channel_id=1, source_target_pairs={{0,4},{1,5},{2,6},{3,7},{4,0},{5,1},{6,2},{7,3},{8,12},{9,13},{10,... | collective-permute-start | bytes 393224 | tf_op jit(solution)/shard_map/ppermute | solution.py:61
  54.7 7.9 %collective-permute-start.16 = (bf16[256,256]{1,0:T(8,128)(2,1)S(1)}, bf16[256,256]{1,0:T(8,128)(2,1)S(1)}, u32[]{:S(2)}, u32[]{:S(2)}) collective-permute-start(bf16[256,256]{1,0:T(8,128)(2,1)S(1)} %shard_map.92.message.m0), channel_id=1, source_target_pairs={{0,2},{1,3},{2,0},{3,1},{4,6},{5,7},{6,4},{7,5},{8,10},{9,11},{10,... | collective-permute-start | bytes 393224 | tf_op jit(solution)/shard_map/ppermute | solution.py:61
  64.0 5.8 %collective-permute-start.17 = (f32[512,256]{1,0:T(8,128)S(1)}, f32[512,256]{1,0:T(8,128)S(1)}, u32[]{:S(2)}, u32[]{:S(2)}) collective-permute-start(f32[512,256]{1,0:T(8,128)S(1)} %get-tuple-element.37), channel_id=1, source_target_pairs={{0,8},{1,9},{2,10},{3,11},{4,12},{5,13},{6,14},{7,15},{8,0},{9,1},... | collective-permute-start | bytes 1572872 | tf_op jit(solution)/shard_map/ppermute | solution.py:61
  66.7 6.0 %collective-permute-start.23 = (bf16[128,256]{1,0:T(8,128)(2,1)S(1)}, bf16[128,256]{1,0:T(8,128)(2,1)S(1)}, u32[]{:S(2)}, u32[]{:S(2)}) collective-permute-start(bf16[128,256]{1,0:T(8,128)(2,1)S(1)} %get-tuple-element.46), channel_id=1, source_target_pairs={{0,16},{1,17},{2,18},{3,19},{4,20},{5,21},{6,22},{7,23},{8,24},{9,... | collective-permute-start | bytes 196616 | tf_op jit(solution)/shard_map/ppermute | solution.py:61
  67.7 6.3 %collective-permute-start.19 = (bf16[128,256]{1,0:T(8,128)(2,1)S(1)}, bf16[128,256]{1,0:T(8,128)(2,1)S(1)}, u32[]{:S(2)}, u32[]{:S(2)}) collective-permute-start(bf16[128,256]{1,0:T(8,128)(2,1)S(1)} %get-tuple-element.39), channel_id=1, source_target_pairs={{0,16},{1,17},{2,18},{3,19},{4,20},{5,21},{6,22},{7,23},{8,24},{9,... | collective-permute-start | bytes 196616 | tf_op jit(solution)/shard_map/ppermute | solution.py:61
  68.8 6.0 %collective-permute-start.21 = (bf16[128,256]{1,0:T(8,128)(2,1)S(1)}, bf16[128,256]{1,0:T(8,128)(2,1)S(1)}, u32[]{:S(2)}, u32[]{:S(2)}) collective-permute-start(bf16[128,256]{1,0:T(8,128)(2,1)S(1)} %get-tuple-element.42), channel_id=1, source_target_pairs={{0,16},{1,17},{2,18},{3,19},{4,20},{5,21},{6,22},{7,23},{8,24},{9,... | collective-permute-start | bytes 196616 | tf_op jit(solution)/shard_map/ppermute | solution.py:61
  71.4 8.6 %collective-permute-start.25 = (bf16[192,256]{1,0:T(8,128)(2,1)S(1)}, bf16[192,256]{1,0:T(8,128)(2,1)S(1)}, u32[]{:S(2)}, u32[]{:S(2)}) collective-permute-start(bf16[192,256]{1,0:T(8,128)(2,1)S(1)} %shard_map.101), channel_id=1, source_target_pairs={{0,192},{1,193},{2,194},{3,195},{4,196},{5,197},{6,198},{7,199},{8... | collective-permute-start | bytes 294920 | tf_op jit(solution)/shard_map/ppermute | solution.py:61
  72.8 7.2 %collective-permute-start.24 = (bf16[192,256]{1,0:T(8,128)(2,1)S(1)}, bf16[192,256]{1,0:T(8,128)(2,1)S(1)}, u32[]{:S(2)}, u32[]{:S(2)}) collective-permute-start(bf16[192,256]{1,0:T(8,128)(2,1)S(1)} %shard_map.100), channel_id=1, source_target_pairs={{0,128},{1,129},{2,130},{3,131},{4,132},{5,133},{6,134},{7,135},{8... | collective-permute-start | bytes 294920 | tf_op jit(solution)/shard_map/ppermute | solution.py:61
  80.0 7.5 %collective-permute-start.26 = (f32[192,256]{1,0:T(8,128)S(1)}, f32[192,256]{1,0:T(8,128)S(1)}, u32[]{:S(2)}, u32[]{:S(2)}) collective-permute-start(f32[192,256]{1,0:T(8,128)S(1)} %shard_map.102.mine), channel_id=1, source_target_pairs={{0,48},{1,49},{2,50},{3,51},{4,52},{5,53},{6,54},{7,55},{8,56},{9,... | collective-permute-start | bytes 589832 | tf_op jit(solution)/shard_map/ppermute | solution.py:61
  87.5 9.3 %collective-permute-start.30 = (bf16[128,256]{1,0:T(8,128)(2,1)S(1)}, bf16[128,256]{1,0:T(8,128)(2,1)S(1)}, u32[]{:S(2)}, u32[]{:S(2)}) collective-permute-start(bf16[128,256]{1,0:T(8,128)(2,1)S(1)} %get-tuple-element.48), channel_id=1, source_target_pairs={{0,1},{1,53},{2,65},{3,113},{4,129},{5,181},{6,195},{7,247},{8,9},... | collective-permute-start | bytes 196616 | tf_op jit(solution)/shard_map/ppermute | solution.py:61
  92.7 7.3 %collective-permute-start.27 = (bf16[128,256]{1,0:T(8,128)(2,1)S(1)}, bf16[128,256]{1,0:T(8,128)(2,1)S(1)}, u32[]{:S(2)}, u32[]{:S(2)}) collective-permute-start(bf16[128,256]{1,0:T(8,128)(2,1)S(1)} %get-tuple-element.47.w0), channel_id=1, source_target_pairs={{0,6},{1,7},{2,4},{3,5},{4,2},{5,3},{6,0},{7,1},{8,14},{9,15},{10,... | collective-permute-start | bytes 196616 | tf_op jit(solution)/shard_map/ppermute | solution.py:61
  94.5 7.2 %collective-permute-start.28 = (bf16[128,256]{1,0:T(8,128)(2,1)S(1)}, bf16[128,256]{1,0:T(8,128)(2,1)S(1)}, u32[]{:S(2)}, u32[]{:S(2)}) collective-permute-start(bf16[128,256]{1,0:T(8,128)(2,1)S(1)} %get-tuple-element.47.w0), channel_id=1, source_target_pairs={{0,4},{1,5},{2,6},{3,7},{4,0},{5,1},{6,2},{7,3},{8,12},{9,13},{10,... | collective-permute-start | bytes 196616 | tf_op jit(solution)/shard_map/ppermute | solution.py:61
  95.3 6.3 %collective-permute-start.29 = (bf16[128,256]{1,0:T(8,128)(2,1)S(1)}, bf16[128,256]{1,0:T(8,128)(2,1)S(1)}, u32[]{:S(2)}, u32[]{:S(2)}) collective-permute-start(bf16[128,256]{1,0:T(8,128)(2,1)S(1)} %get-tuple-element.47.w0), channel_id=1, source_target_pairs={{0,2},{1,3},{2,0},{3,1},{4,6},{5,7},{6,4},{7,5},{8,10},{9,11},{10,... | collective-permute-start | bytes 196616 | tf_op jit(solution)/shard_map/ppermute | solution.py:61
  96.8 5.7 %collective-permute-start.31 = (bf16[128,256]{1,0:T(8,128)(2,1)S(1)}, bf16[128,256]{1,0:T(8,128)(2,1)S(1)}, u32[]{:S(2)}, u32[]{:S(2)}) collective-permute-start(bf16[128,256]{1,0:T(8,128)(2,1)S(1)} %collective-permute-done.30.p0), channel_id=1, source_target_pairs={{0,6},{1,7},{2,4},{3,5},{4,2},{5,3},{6,0},{7,1},{8,14},{9,15},{10,... | collective-permute-start | bytes 196616 | tf_op jit(solution)/shard_map/ppermute | solution.py:61
  100.0 5.8 %collective-permute-start.32 = (bf16[128,256]{1,0:T(8,128)(2,1)S(1)}, bf16[128,256]{1,0:T(8,128)(2,1)S(1)}, u32[]{:S(2)}, u32[]{:S(2)}) collective-permute-start(bf16[128,256]{1,0:T(8,128)(2,1)S(1)} %collective-permute-done.30.p0), channel_id=1, source_target_pairs={{0,4},{1,5},{2,6},{3,7},{4,0},{5,1},{6,2},{7,3},{8,12},{9,13},{10,... | collective-permute-start | bytes 196616 | tf_op jit(solution)/shard_map/ppermute | solution.py:61
  100.0 5.8 %collective-permute-start.33 = (bf16[128,256]{1,0:T(8,128)(2,1)S(1)}, bf16[128,256]{1,0:T(8,128)(2,1)S(1)}, u32[]{:S(2)}, u32[]{:S(2)}) collective-permute-start(bf16[128,256]{1,0:T(8,128)(2,1)S(1)} %collective-permute-done.30.p0), channel_id=1, source_target_pairs={{0,2},{1,3},{2,0},{3,1},{4,6},{5,7},{6,4},{7,5},{8,10},{9,11},{10,... | collective-permute-start | bytes 196616 | tf_op jit(solution)/shard_map/ppermute | solution.py:61
  (15 other events, 80.6 us)

commit v6 on v5

--- a/solution.py
+++ b/solution.py
@@ -47,6 +47,7 @@
 ROUTE = (((2, 1, 3, 0), (0, 3, 2, 1), (2, 1, 0, 3), (3, 0, 2, 1)), ((0, 1, 3, 2), (0, 1, 2, 3), (0, 1, 2, 3), (1, 0, 2, 3)))
 TO_ROW = pairs(lambda z, y, c, x, h: (x, Y_OF[u_of(y), h], c, ROUTE[v_of(y) == h][x][z], 1 - v_of(y)))
 TO_COLUMN = [(there, here) for here, there in TO_ROW]
+TO_ROW_TOO = pairs(lambda z, y, c, x, h: (x, Y_OF[u_of(y), h], c, ROUTE[1 - v_of(y) == h][x][z], v_of(y)))
 
 
 def chunk_table(same):
@@ -249,28 +250,23 @@
     kept_share[...] = pair_share(share, got_first)
 
 
-def after_z_body(kept, share, r1, r2, r3, to_v):
+def after_z_body(kept, share, r1, r2, r3, piece, total_share):
     total = kept[...] + r1[0:PART, :].astype(F32)
-    to_v[0:PART, :] = total + (r2[0:PART, :].astype(F32) + r3[0:PART, :].astype(F32))
+    piece[...] = (total + (r2[0:PART, :].astype(F32) + r3[0:PART, :].astype(F32))).astype(BF)
     pair = share[...].astype(F32) + r1[PART:, :].astype(F32)
-    to_v[PART:, :] = pair + (r2[PART:, :].astype(F32) + r3[PART:, :].astype(F32))
-
-
-def after_v_body(mine, got, piece, share):
-    piece[...] = (mine[0:PART, :] + got[0:PART, :]).astype(BF)
-    put_split(share, 0, mine[PART:, :] + got[PART:, :])
-
-
-def finish_body(p0, p3, p2, p1, grad_features):
-    me = place()
-    for k, piece in enumerate((p0, p1, p2, p3)):
-        grad_features[at(chunk_of(me, me["x"] ^ k), PART), :] = piece[...]
-
-
-def finish_weight_body(w0, w3, w2, w1, grad_weight):
-    me = place()
-    for k, share in enumerate((w0, w1, w2, w3)):
-        grad_weight[at(me["x"] ^ k, SLICE), :] = get_split(share, 0)
+    total_share[...] = pair + (r2[PART:, :].astype(F32) + r3[PART:, :].astype(F32))
+
+
+def last_body(one, two, mine, got, message):
+    message[0:PART, :] = (one[...].astype(F32) + two[...].astype(F32)).astype(BF)
+    put_split(message, PART, mine[...] + got[...])
+
+
+def finish_body(m0, m3, m2, m1, grad_features, grad_weight):
+    me = place()
+    for k, message in enumerate((m0, m1, m2, m3)):
+        grad_features[at(chunk_of(me, me["x"] ^ k), PART), :] = message[0:PART, :]
+        grad_weight[at(me["x"] ^ k, SLICE), :] = get_split(message, PART)
 
 
 def on_device(features, weight, cotangent, tile_values, tile_slots, tile_count):
@@ -325,13 +321,10 @@
     (to2,) = call(functools.partial(to_z_body, 2), [to_z], own, u2, share, u3)
     to1, kept, share = call(to_z1_body, [to_z, part32, share16], own, u1, share, u3, u0)
     from_z = [send(value, route) for value, route in zip((to1, to2, to3), FLIP_Z)]
-    (to_v,) = call(after_z_body, [((PART + SLICE, WIDTH), F32)], kept, share, *from_z)
-    piece, share = call(after_v_body, [part, part], to_v, send(to_v, FLIP_V))
-    piece = send(piece, TO_ROW)
-    shares = spread(share, FLIP_X)
-    pieces = spread(piece, FLIP_X)
-    (grad_weight,) = call(finish_weight_body, [((WIDTH, WIDTH), F32)], *shares)
-    (grad_features,) = call(finish_body, [block], *pieces)
+    piece, share = call(after_z_body, [part, share32], kept, share, *from_z)
+    routes = (TO_ROW, TO_ROW_TOO)
+    (message,) = call(last_body, [two], *[send(piece, route) for route in routes], share, send(share, FLIP_V))
+    grad_features, grad_weight = call(finish_body, [block, ((WIDTH, WIDTH), F32)], *spread(message, FLIP_X))
     return output, grad_weight, grad_features
 
 

time: 108 us -> 108 us (level)
  the two profiles are of different devices: /device:TPU:32 before, /device:TPU:28 now
where the time goes in v6:
time: 108 us; the launch traced here: 107 us
  starting transfers between devices  54.9 us (51%)
  waiting for transfers between devices  42.1 us (39%)
  Pallas kernels  5.94 us (6%)
  local copies, waits for them, and re-layouts  3.32 us (3%)
    ppermute x32, starting transfers between devices, send(): return lax.ppermute(value, AXES, route)  54.9 us
    ppermute x32, waiting for transfers between devices, send(): return lax.ppermute(value, AXES, route)  42.1 us
    pallas_call x20, Pallas kernels, call(): pl.pallas_call(body, out_shape=[jax.ShapeDtypeStruct(shape, dtype) for sh...  5.94 us
    unnamed x11, local copies, waits for them, and re-layouts  3.32 us
  transfers between devices with their start and end apart: 32, of which 22 were waited for; matrix products, arithmetic and copies ran while one was open for 1% of the time, Pallas kernels for 3%

profile of v6, /device:TPU:28, one launch (start us, length us, event | category | flops | bytes accessed | tf_op | source)
XLA Modules:
  0.0 107.1 jit_solution(9963334259386363264)
XLA Ops:
  1.6 5.9 %collective-permute-start = (bf16[128,256]{1,0:T(8,128)(2,1)S(1)}, bf16[128,256]{1,0:T(8,128)(2,1)S(1)}, u32[]{:S(2)}, u32[]{:S(2)}) collective-permute-start(bf16[128,256]{1,0:T(8,128)(2,1)S(1)} %shard_map.85), channel_id=1, source_target_pairs={{1,0},{53,1},{65,2},{113,3},{129,4},{181,5},{195,6},{247,7},{9,8},... | collective-permute-start | bytes 196616 | tf_op jit(solution)/shard_map/ppermute | solution.py:62
  11.2 3.5 %collective-permute-start.5 = (bf16[128,256]{1,0:T(8,128)(2,1)S(1)}, bf16[128,256]{1,0:T(8,128)(2,1)S(1)}, u32[]{:S(2)}, u32[]{:S(2)}) collective-permute-start(bf16[128,256]{1,0:T(8,128)(2,1)S(1)} %collective-permute-done.high), channel_id=1, source_target_pairs={{0,192},{1,193},{2,194},{3,195},{4,196},{5,197},{6,198},{7,199},{8... | collective-permute-start | bytes 196616 | tf_op jit(solution)/shard_map/ppermute | solution.py:62
  15.7 2.3 %collective-permute-done.5.low = bf16[128,256]{1,0:T(8,128)(2,1)S(1)} collective-permute-done((bf16[128,256]{1,0:T(8,128)(2,1)S(1)}, bf16[128,256]{1,0:T(8,128)(2,1)S(1)}, u32[]{:S(2)}, u32[]{:S(2)}) %collective-permute-start.5) | collective-permute-done | bytes 65568 | tf_op jit(solution)/shard_map/ppermute | solution.py:62
  18.5 2.0 %collective-permute-done.1.low = bf16[128,256]{1,0:T(8,128)(2,1)S(1)} collective-permute-done((bf16[128,256]{1,0:T(8,128)(2,1)S(1)}, bf16[128,256]{1,0:T(8,128)(2,1)S(1)}, u32[]{:S(2)}, u32[]{:S(2)}) %collective-permute-start.1) | collective-permute-done | bytes 65568 | tf_op jit(solution)/shard_map/ppermute | solution.py:62
  21.8 1.5 %collective-permute-done.6.a2 = bf16[256,256]{1,0:T(8,128)(2,1)S(1)} collective-permute-done((bf16[256,256]{1,0:T(8,128)(2,1)S(1)}, bf16[256,256]{1,0:T(8,128)(2,1)S(1)}, u32[]{:S(2)}, u32[]{:S(2)}) %collective-permute-start.6) | collective-permute-done | bytes 131104 | tf_op jit(solution)/shard_map/ppermute | solution.py:62
  23.3 2.6 %collective-permute-done.3.b2 = bf16[256,256]{1,0:T(8,128)(2,1)S(1)} collective-permute-done((bf16[256,256]{1,0:T(8,128)(2,1)S(1)}, bf16[256,256]{1,0:T(8,128)(2,1)S(1)}, u32[]{:S(2)}, u32[]{:S(2)}) %collective-permute-start.3) | collective-permute-done | bytes 131104 | tf_op jit(solution)/shard_map/ppermute | solution.py:62
  29.0 2.7 %collective-permute-start.11 = (f32[128,256]{1,0:T(8,128)S(1)}, f32[128,256]{1,0:T(8,128)S(1)}, u32[]{:S(2)}, u32[]{:S(2)}) collective-permute-start(f32[128,256]{1,0:T(8,128)S(1)} %get-tuple-element.34), channel_id=1, source_target_pairs={{0,4},{1,5},{2,6},{3,7},{4,0},{5,1},{6,2},{7,3},{8,12},{9,13},{10,... | collective-permute-start | bytes 393224 | tf_op jit(solution)/shard_map/ppermute | solution.py:62
  32.0 3.6 %collective-permute-done.10.r3 = f32[128,256]{1,0:T(8,128)S(1)} collective-permute-done((f32[128,256]{1,0:T(8,128)S(1)}, f32[128,256]{1,0:T(8,128)S(1)}, u32[]{:S(2)}, u32[]{:S(2)}) %collective-permute-start.10) | collective-permute-done | bytes 131104 | tf_op jit(solution)/shard_map/ppermute | solution.py:62
  36.6 1.7 %collective-permute-done.12.r1 = f32[128,256]{1,0:T(8,128)S(1)} collective-permute-done((f32[128,256]{1,0:T(8,128)S(1)}, f32[128,256]{1,0:T(8,128)S(1)}, u32[]{:S(2)}, u32[]{:S(2)}) %collective-permute-start.12) | collective-permute-done | bytes 131104 | tf_op jit(solution)/shard_map/ppermute | solution.py:62
  38.4 7.2 %collective-permute-start.13 = (bf16[320,256]{1,0:T(8,128)(2,1)S(1)}, bf16[320,256]{1,0:T(8,128)(2,1)S(1)}, u32[]{:S(2)}, u32[]{:S(2)}) collective-permute-start(bf16[320,256]{1,0:T(8,128)(2,1)S(1)} %shard_map.91.mine), channel_id=1, source_target_pairs={{0,1},{1,0},{2,3},{3,2},{4,5},{5,4},{6,7},{7,6},{8,9},{9,8},{10,11... | collective-permute-start | bytes 491528 | tf_op jit(solution)/shard_map/ppermute | solution.py:62
  45.6 5.4 %collective-permute-done.13.got = bf16[320,256]{1,0:T(8,128)(2,1)S(1)} collective-permute-done((bf16[320,256]{1,0:T(8,128)(2,1)S(1)}, bf16[320,256]{1,0:T(8,128)(2,1)S(1)}, u32[]{:S(2)}, u32[]{:S(2)}) %collective-permute-start.13) | collective-permute-done | bytes 163872 | tf_op jit(solution)/shard_map/ppermute | solution.py:62
  51.3 3.4 %collective-permute-start.15 = (bf16[256,256]{1,0:T(8,128)(2,1)S(1)}, bf16[256,256]{1,0:T(8,128)(2,1)S(1)}, u32[]{:S(2)}, u32[]{:S(2)}) collective-permute-start(bf16[256,256]{1,0:T(8,128)(2,1)S(1)} %shard_map.92.message.m0), channel_id=1, source_target_pairs={{0,4},{1,5},{2,6},{3,7},{4,0},{5,1},{6,2},{7,3},{8,12},{9,13},{10,... | collective-permute-start | bytes 393224 | tf_op jit(solution)/shard_map/ppermute | solution.py:62
  56.3 1.6 %collective-permute-done.15.m2 = bf16[256,256]{1,0:T(8,128)(2,1)S(1)} collective-permute-done((bf16[256,256]{1,0:T(8,128)(2,1)S(1)}, bf16[256,256]{1,0:T(8,128)(2,1)S(1)}, u32[]{:S(2)}, u32[]{:S(2)}) %collective-permute-start.15) | collective-permute-done | bytes 131104 | tf_op jit(solution)/shard_map/ppermute | solution.py:62
  57.9 1.9 %collective-permute-done.16.m1 = bf16[256,256]{1,0:T(8,128)(2,1)S(1)} collective-permute-done((bf16[256,256]{1,0:T(8,128)(2,1)S(1)}, bf16[256,256]{1,0:T(8,128)(2,1)S(1)}, u32[]{:S(2)}, u32[]{:S(2)}) %collective-permute-start.16) | collective-permute-done | bytes 131104 | tf_op jit(solution)/shard_map/ppermute | solution.py:62
  69.9 3.2 %collective-permute-start.24 = (bf16[192,256]{1,0:T(8,128)(2,1)S(1)}, bf16[192,256]{1,0:T(8,128)(2,1)S(1)}, u32[]{:S(2)}, u32[]{:S(2)}) collective-permute-start(bf16[192,256]{1,0:T(8,128)(2,1)S(1)} %shard_map.100), channel_id=1, source_target_pairs={{0,128},{1,129},{2,130},{3,131},{4,132},{5,133},{6,134},{7,135},{8... | collective-permute-start | bytes 294920 | tf_op jit(solution)/shard_map/ppermute | solution.py:62
  73.2 1.8 %collective-permute-start.22 = (bf16[192,256]{1,0:T(8,128)(2,1)S(1)}, bf16[192,256]{1,0:T(8,128)(2,1)S(1)}, u32[]{:S(2)}, u32[]{:S(2)}) collective-permute-start(bf16[192,256]{1,0:T(8,128)(2,1)S(1)} %get-tuple-element.47), channel_id=1, source_target_pairs={{0,64},{1,65},{2,66},{3,67},{4,68},{5,69},{6,70},{7,71},{8,72},{9,... | collective-permute-start | bytes 294920 | tf_op jit(solution)/shard_map/ppermute | solution.py:62
  75.8 4.1 %collective-permute-done.24.r2 = bf16[192,256]{1,0:T(8,128)(2,1)S(1)} collective-permute-done((bf16[192,256]{1,0:T(8,128)(2,1)S(1)}, bf16[192,256]{1,0:T(8,128)(2,1)S(1)}, u32[]{:S(2)}, u32[]{:S(2)}) %collective-permute-start.24) | collective-permute-done | bytes 98336 | tf_op jit(solution)/shard_map/ppermute | solution.py:62
  80.0 1.9 %collective-permute-start.26 = (bf16[128,256]{1,0:T(8,128)(2,1)S(1)}, bf16[128,256]{1,0:T(8,128)(2,1)S(1)}, u32[]{:S(2)}, u32[]{:S(2)}) collective-permute-start(bf16[128,256]{1,0:T(8,128)(2,1)S(1)} %get-tuple-element.49), channel_id=1, source_target_pairs={{0,1},{1,53},{2,65},{3,113},{4,129},{5,181},{6,195},{7,247},{8,9},... | collective-permute-start | bytes 196616 | tf_op jit(solution)/shard_map/ppermute | solution.py:62
  81.9 10.4 %collective-permute-start.27 = (bf16[128,256]{1,0:T(8,128)(2,1)S(1)}, bf16[128,256]{1,0:T(8,128)(2,1)S(1)}, u32[]{:S(2)}, u32[]{:S(2)}) collective-permute-start(bf16[128,256]{1,0:T(8,128)(2,1)S(1)} %get-tuple-element.49), channel_id=1, source_target_pairs={{0,4},{1,48},{2,64},{3,112},{4,132},{5,176},{6,198},{7,242},{8,12}... | collective-permute-start | bytes 196616 | tf_op jit(solution)/shard_map/ppermute | solution.py:62
  92.3 1.9 %collective-permute-done.27.two = bf16[128,256]{1,0:T(8,128)(2,1)S(1)} collective-permute-done((bf16[128,256]{1,0:T(8,128)(2,1)S(1)}, bf16[128,256]{1,0:T(8,128)(2,1)S(1)}, u32[]{:S(2)}, u32[]{:S(2)}) %collective-permute-start.27) | collective-permute-done | bytes 65568 | tf_op jit(solution)/shard_map/ppermute | solution.py:62
  94.2 3.6 %collective-permute-done.28.got = f32[64,256]{1,0:T(8,128)S(1)} collective-permute-done((f32[64,256]{1,0:T(8,128)S(1)}, f32[64,256]{1,0:T(8,128)S(1)}, u32[]{:S(2)}, u32[]{:S(2)}) %collective-permute-start.28) | collective-permute-done | bytes 65568 | tf_op jit(solution)/shard_map/ppermute | solution.py:62
  98.3 3.7 %collective-permute-start.31 = (bf16[256,256]{1,0:T(8,128)(2,1)S(1)}, bf16[256,256]{1,0:T(8,128)(2,1)S(1)}, u32[]{:S(2)}, u32[]{:S(2)}) collective-permute-start(bf16[256,256]{1,0:T(8,128)(2,1)S(1)} %shard_map.103.m0), channel_id=1, source_target_pairs={{0,2},{1,3},{2,0},{3,1},{4,6},{5,7},{6,4},{7,5},{8,10},{9,11},{10,... | collective-permute-start | bytes 393224 | tf_op jit(solution)/shard_map/ppermute | solution.py:62
  102.8 1.6 %collective-permute-done.30.m2 = bf16[256,256]{1,0:T(8,128)(2,1)S(1)} collective-permute-done((bf16[256,256]{1,0:T(8,128)(2,1)S(1)}, bf16[256,256]{1,0:T(8,128)(2,1)S(1)}, u32[]{:S(2)}, u32[]{:S(2)}) %collective-permute-start.30) | collective-permute-done | bytes 131104 | tf_op jit(solution)/shard_map/ppermute | solution.py:62
  104.4 1.9 %collective-permute-done.31.m1 = bf16[256,256]{1,0:T(8,128)(2,1)S(1)} collective-permute-done((bf16[256,256]{1,0:T(8,128)(2,1)S(1)}, bf16[256,256]{1,0:T(8,128)(2,1)S(1)}, u32[]{:S(2)}, u32[]{:S(2)}) %collective-permute-start.31) | collective-permute-done | bytes 131104 | tf_op jit(solution)/shard_map/ppermute | solution.py:62
  (71 shorter events, 26.8 us)
Async XLA Ops:
  1.6 9.6 %collective-permute-start = (bf16[128,256]{1,0:T(8,128)(2,1)S(1)}, bf16[128,256]{1,0:T(8,128)(2,1)S(1)}, u32[]{:S(2)}, u32[]{:S(2)}) collective-permute-start(bf16[128,256]{1,0:T(8,128)(2,1)S(1)} %shard_map.85), channel_id=1, source_target_pairs={{1,0},{53,1},{65,2},{113,3},{129,4},{181,5},{195,6},{247,7},{9,8},... | collective-permute-start | bytes 196616 | tf_op jit(solution)/shard_map/ppermute | solution.py:62
  11.2 6.8 %collective-permute-start.5 = (bf16[128,256]{1,0:T(8,128)(2,1)S(1)}, bf16[128,256]{1,0:T(8,128)(2,1)S(1)}, u32[]{:S(2)}, u32[]{:S(2)}) collective-permute-start(bf16[128,256]{1,0:T(8,128)(2,1)S(1)} %collective-permute-done.high), channel_id=1, source_target_pairs={{0,192},{1,193},{2,194},{3,195},{4,196},{5,197},{6,198},{7,199},{8... | collective-permute-start | bytes 196616 | tf_op jit(solution)/shard_map/ppermute | solution.py:62
  14.7 5.8 %collective-permute-start.1 = (bf16[128,256]{1,0:T(8,128)(2,1)S(1)}, bf16[128,256]{1,0:T(8,128)(2,1)S(1)}, u32[]{:S(2)}, u32[]{:S(2)}) collective-permute-start(bf16[128,256]{1,0:T(8,128)(2,1)S(1)} %collective-permute-done.high), channel_id=1, source_target_pairs={{0,128},{1,129},{2,130},{3,131},{4,132},{5,133},{6,134},{7,135},{8... | collective-permute-start | bytes 196616 | tf_op jit(solution)/shard_map/ppermute | solution.py:62
  14.8 5.8 %collective-permute-start.2 = (bf16[128,256]{1,0:T(8,128)(2,1)S(1)}, bf16[128,256]{1,0:T(8,128)(2,1)S(1)}, u32[]{:S(2)}, u32[]{:S(2)}) collective-permute-start(bf16[128,256]{1,0:T(8,128)(2,1)S(1)} %collective-permute-done.high), channel_id=1, source_target_pairs={{0,64},{1,65},{2,66},{3,67},{4,68},{5,69},{6,70},{7,71},{8,72},{9,... | collective-permute-start | bytes 196616 | tf_op jit(solution)/shard_map/ppermute | solution.py:62
  18.1 5.3 %collective-permute-start.6 = (bf16[256,256]{1,0:T(8,128)(2,1)S(1)}, bf16[256,256]{1,0:T(8,128)(2,1)S(1)}, u32[]{:S(2)}, u32[]{:S(2)}) collective-permute-start(bf16[256,256]{1,0:T(8,128)(2,1)S(1)} %shard_map.88.a0), channel_id=1, source_target_pairs={{0,16},{1,17},{2,18},{3,19},{4,20},{5,21},{6,22},{7,23},{8,24},{9,... | collective-permute-start | bytes 393224 | tf_op jit(solution)/shard_map/ppermute | solution.py:62
  20.5 5.4 %collective-permute-start.3 = (bf16[256,256]{1,0:T(8,128)(2,1)S(1)}, bf16[256,256]{1,0:T(8,128)(2,1)S(1)}, u32[]{:S(2)}, u32[]{:S(2)}) collective-permute-start(bf16[256,256]{1,0:T(8,128)(2,1)S(1)} %shard_map.87.b0), channel_id=1, source_target_pairs={{0,16},{1,17},{2,18},{3,19},{4,20},{5,21},{6,22},{7,23},{8,24},{9,... | collective-permute-start | bytes 393224 | tf_op jit(solution)/shard_map/ppermute | solution.py:62
  27.7 7.9 %collective-permute-start.10 = (f32[128,256]{1,0:T(8,128)S(1)}, f32[128,256]{1,0:T(8,128)S(1)}, u32[]{:S(2)}, u32[]{:S(2)}) collective-permute-start(f32[128,256]{1,0:T(8,128)S(1)} %get-tuple-element.33), channel_id=1, source_target_pairs={{0,6},{1,7},{2,4},{3,5},{4,2},{5,3},{6,0},{7,1},{8,14},{9,15},{10,... | collective-permute-start | bytes 393224 | tf_op jit(solution)/shard_map/ppermute | solution.py:62
  29.0 7.6 %collective-permute-start.11 = (f32[128,256]{1,0:T(8,128)S(1)}, f32[128,256]{1,0:T(8,128)S(1)}, u32[]{:S(2)}, u32[]{:S(2)}) collective-permute-start(f32[128,256]{1,0:T(8,128)S(1)} %get-tuple-element.34), channel_id=1, source_target_pairs={{0,4},{1,5},{2,6},{3,7},{4,0},{5,1},{6,2},{7,3},{8,12},{9,13},{10,... | collective-permute-start | bytes 393224 | tf_op jit(solution)/shard_map/ppermute | solution.py:62
  31.7 6.6 %collective-permute-start.12 = (f32[128,256]{1,0:T(8,128)S(1)}, f32[128,256]{1,0:T(8,128)S(1)}, u32[]{:S(2)}, u32[]{:S(2)}) collective-permute-start(f32[128,256]{1,0:T(8,128)S(1)} %get-tuple-element.35), channel_id=1, source_target_pairs={{0,2},{1,3},{2,0},{3,1},{4,6},{5,7},{6,4},{7,5},{8,10},{9,11},{10,... | collective-permute-start | bytes 393224 | tf_op jit(solution)/shard_map/ppermute | solution.py:62
  38.4 12.6 %collective-permute-start.13 = (bf16[320,256]{1,0:T(8,128)(2,1)S(1)}, bf16[320,256]{1,0:T(8,128)(2,1)S(1)}, u32[]{:S(2)}, u32[]{:S(2)}) collective-permute-start(bf16[320,256]{1,0:T(8,128)(2,1)S(1)} %shard_map.91.mine), channel_id=1, source_target_pairs={{0,1},{1,0},{2,3},{3,2},{4,5},{5,4},{6,7},{7,6},{8,9},{9,8},{10,11... | collective-permute-start | bytes 491528 | tf_op jit(solution)/shard_map/ppermute | solution.py:62
  51.3 6.6 %collective-permute-start.15 = (bf16[256,256]{1,0:T(8,128)(2,1)S(1)}, bf16[256,256]{1,0:T(8,128)(2,1)S(1)}, u32[]{:S(2)}, u32[]{:S(2)}) collective-permute-start(bf16[256,256]{1,0:T(8,128)(2,1)S(1)} %shard_map.92.message.m0), channel_id=1, source_target_pairs={{0,4},{1,5},{2,6},{3,7},{4,0},{5,1},{6,2},{7,3},{8,12},{9,13},{10,... | collective-permute-start | bytes 393224 | tf_op jit(solution)/shard_map/ppermute | solution.py:62
  61.1 5.8 %collective-permute-start.17 = (f32[512,256]{1,0:T(8,128)S(1)}, f32[512,256]{1,0:T(8,128)S(1)}, u32[]{:S(2)}, u32[]{:S(2)}) collective-permute-start(f32[512,256]{1,0:T(8,128)S(1)} %get-tuple-element.39), channel_id=1, source_target_pairs={{0,8},{1,9},{2,10},{3,11},{4,12},{5,13},{6,14},{7,15},{8,0},{9,1},... | collective-permute-start | bytes 1572872 | tf_op jit(solution)/shard_map/ppermute | solution.py:62
  62.8 5.7 %collective-permute-start.20 = (bf16[192,256]{1,0:T(8,128)(2,1)S(1)}, bf16[192,256]{1,0:T(8,128)(2,1)S(1)}, u32[]{:S(2)}, u32[]{:S(2)}) collective-permute-start(bf16[192,256]{1,0:T(8,128)(2,1)S(1)} %get-tuple-element.43), channel_id=1, source_target_pairs={{0,16},{1,17},{2,18},{3,19},{4,20},{5,21},{6,22},{7,23},{8,24},{9,... | collective-permute-start | bytes 294920 | tf_op jit(solution)/shard_map/ppermute | solution.py:62
  63.6 6.3 %collective-permute-start.23 = (bf16[128,256]{1,0:T(8,128)(2,1)S(1)}, bf16[128,256]{1,0:T(8,128)(2,1)S(1)}, u32[]{:S(2)}, u32[]{:S(2)}) collective-permute-start(bf16[128,256]{1,0:T(8,128)(2,1)S(1)} %get-tuple-element.48), channel_id=1, source_target_pairs={{0,16},{1,17},{2,18},{3,19},{4,20},{5,21},{6,22},{7,23},{8,24},{9,... | collective-permute-start | bytes 196616 | tf_op jit(solution)/shard_map/ppermute | solution.py:62
  64.9 8.3 %collective-permute-start.19 = (bf16[128,256]{1,0:T(8,128)(2,1)S(1)}, bf16[128,256]{1,0:T(8,128)(2,1)S(1)}, u32[]{:S(2)}, u32[]{:S(2)}) collective-permute-start(bf16[128,256]{1,0:T(8,128)(2,1)S(1)} %get-tuple-element.41), channel_id=1, source_target_pairs={{0,16},{1,17},{2,18},{3,19},{4,20},{5,21},{6,22},{7,23},{8,24},{9,... | collective-permute-start | bytes 196616 | tf_op jit(solution)/shard_map/ppermute | solution.py:62
  65.6 7.5 %collective-permute-start.21 = (bf16[128,256]{1,0:T(8,128)(2,1)S(1)}, bf16[128,256]{1,0:T(8,128)(2,1)S(1)}, u32[]{:S(2)}, u32[]{:S(2)}) collective-permute-start(bf16[128,256]{1,0:T(8,128)(2,1)S(1)} %get-tuple-element.44), channel_id=1, source_target_pairs={{0,16},{1,17},{2,18},{3,19},{4,20},{5,21},{6,22},{7,23},{8,24},{9,... | collective-permute-start | bytes 196616 | tf_op jit(solution)/shard_map/ppermute | solution.py:62
  68.5 7.3 %collective-permute-start.25 = (bf16[192,256]{1,0:T(8,128)(2,1)S(1)}, bf16[192,256]{1,0:T(8,128)(2,1)S(1)}, u32[]{:S(2)}, u32[]{:S(2)}) collective-permute-start(bf16[192,256]{1,0:T(8,128)(2,1)S(1)} %shard_map.101), channel_id=1, source_target_pairs={{0,192},{1,193},{2,194},{3,195},{4,196},{5,197},{6,198},{7,199},{8... | collective-permute-start | bytes 294920 | tf_op jit(solution)/shard_map/ppermute | solution.py:62
  69.9 10.0 %collective-permute-start.24 = (bf16[192,256]{1,0:T(8,128)(2,1)S(1)}, bf16[192,256]{1,0:T(8,128)(2,1)S(1)}, u32[]{:S(2)}, u32[]{:S(2)}) collective-permute-start(bf16[192,256]{1,0:T(8,128)(2,1)S(1)} %shard_map.100), channel_id=1, source_target_pairs={{0,128},{1,129},{2,130},{3,131},{4,132},{5,133},{6,134},{7,135},{8... | collective-permute-start | bytes 294920 | tf_op jit(solution)/shard_map/ppermute | solution.py:62
  73.2 6.7 %collective-permute-start.22 = (bf16[192,256]{1,0:T(8,128)(2,1)S(1)}, bf16[192,256]{1,0:T(8,128)(2,1)S(1)}, u32[]{:S(2)}, u32[]{:S(2)}) collective-permute-start(bf16[192,256]{1,0:T(8,128)(2,1)S(1)} %get-tuple-element.47), channel_id=1, source_target_pairs={{0,64},{1,65},{2,66},{3,67},{4,68},{5,69},{6,70},{7,71},{8,72},{9,... | collective-permute-start | bytes 294920 | tf_op jit(solution)/shard_map/ppermute | solution.py:62
  80.0 12.3 %collective-permute-start.26 = (bf16[128,256]{1,0:T(8,128)(2,1)S(1)}, bf16[128,256]{1,0:T(8,128)(2,1)S(1)}, u32[]{:S(2)}, u32[]{:S(2)}) collective-permute-start(bf16[128,256]{1,0:T(8,128)(2,1)S(1)} %get-tuple-element.49), channel_id=1, source_target_pairs={{0,1},{1,53},{2,65},{3,113},{4,129},{5,181},{6,195},{7,247},{8,9},... | collective-permute-start | bytes 196616 | tf_op jit(solution)/shard_map/ppermute | solution.py:62
  81.9 12.3 %collective-permute-start.27 = (bf16[128,256]{1,0:T(8,128)(2,1)S(1)}, bf16[128,256]{1,0:T(8,128)(2,1)S(1)}, u32[]{:S(2)}, u32[]{:S(2)}) collective-permute-start(bf16[128,256]{1,0:T(8,128)(2,1)S(1)} %get-tuple-element.49), channel_id=1, source_target_pairs={{0,4},{1,48},{2,64},{3,112},{4,132},{5,176},{6,198},{7,242},{8,12}... | collective-permute-start | bytes 196616 | tf_op jit(solution)/shard_map/ppermute | solution.py:62
  92.3 5.5 %collective-permute-start.28 = (f32[64,256]{1,0:T(8,128)S(1)}, f32[64,256]{1,0:T(8,128)S(1)}, u32[]{:S(2)}, u32[]{:S(2)}) collective-permute-start(f32[64,256]{1,0:T(8,128)S(1)} %get-tuple-element.50.mine), channel_id=1, source_target_pairs={{0,48},{1,49},{2,50},{3,51},{4,52},{5,53},{6,54},{7,55},{8,56},{9,... | collective-permute-start | bytes 196616 | tf_op jit(solution)/shard_map/ppermute | solution.py:62
  97.9 6.6 %collective-permute-start.30 = (bf16[256,256]{1,0:T(8,128)(2,1)S(1)}, bf16[256,256]{1,0:T(8,128)(2,1)S(1)}, u32[]{:S(2)}, u32[]{:S(2)}) collective-permute-start(bf16[256,256]{1,0:T(8,128)(2,1)S(1)} %shard_map.103.m0), channel_id=1, source_target_pairs={{0,4},{1,5},{2,6},{3,7},{4,0},{5,1},{6,2},{7,3},{8,12},{9,13},{10,... | collective-permute-start | bytes 393224 | tf_op jit(solution)/shard_map/ppermute | solution.py:62
  98.3 8.0 %collective-permute-start.31 = (bf16[256,256]{1,0:T(8,128)(2,1)S(1)}, bf16[256,256]{1,0:T(8,128)(2,1)S(1)}, u32[]{:S(2)}, u32[]{:S(2)}) collective-permute-start(bf16[256,256]{1,0:T(8,128)(2,1)S(1)} %shard_map.103.m0), channel_id=1, source_target_pairs={{0,2},{1,3},{2,0},{3,1},{4,6},{5,7},{6,4},{7,5},{8,10},{9,11},{10,... | collective-permute-start | bytes 393224 | tf_op jit(solution)/shard_map/ppermute | solution.py:62
  (13 other events, 70.0 us)

commit v7 on v6

--- a/solution.py
+++ b/solution.py
@@ -1,4 +1,3 @@
-import functools
 import itertools
 
 import jax
@@ -47,7 +46,6 @@
 ROUTE = (((2, 1, 3, 0), (0, 3, 2, 1), (2, 1, 0, 3), (3, 0, 2, 1)), ((0, 1, 3, 2), (0, 1, 2, 3), (0, 1, 2, 3), (1, 0, 2, 3)))
 TO_ROW = pairs(lambda z, y, c, x, h: (x, Y_OF[u_of(y), h], c, ROUTE[v_of(y) == h][x][z], 1 - v_of(y)))
 TO_COLUMN = [(there, here) for here, there in TO_ROW]
-TO_ROW_TOO = pairs(lambda z, y, c, x, h: (x, Y_OF[u_of(y), h], c, ROUTE[1 - v_of(y) == h][x][z], v_of(y)))
 
 
 def chunk_table(same):
@@ -163,11 +161,11 @@
     put_block(me, blocks, 0, a3, b3)
     total[...] = most[...] + dot(dense[3], blocks[0])
     for k, to in enumerate((own, to1, to2, to3)):
-        to[...] = total[at(me["x"] ^ k, PART), :]
+        to[...] = total[at(me["x"] ^ k, PART), :].astype(to.dtype)
 
 
 def sum_body(own, r3, r2, r1, cot, to_h):
-    total = own[...] + r1[...] + (r2[...] + r3[...])
+    total = own[...] + r1[...] + (r2[...].astype(F32) + r3[...])
     high, low = split(total)
     to_h[0:PART, :] = high
     to_h[PART : 2 * PART, :] = low
@@ -179,34 +177,38 @@
     return (parts[0] + parts[1]).astype(BF)
 
 
-def layer_body(mine, got, weight, message):
-    aggregate = aggregate_of(mine, got)
-    preact = dot(aggregate, weight[...])
+def layer_body(mine, got, weight, to3, to2, to1, own, aggregate, share, grad_w):
+    me = place()
+    agg = aggregate_of(mine, got)
+    preact = dot(agg, weight[...])
     gates = jax.nn.sigmoid(preact)
-    first = place()["h"] == 0
+    first = me["h"] == 0
     a, b = mine[2 * PART :, :], got[2 * PART :, :]
     cotangent = jnp.concatenate([jnp.where(first, a, b), jnp.where(first, b, a)], axis=0).astype(F32)
-    message[0:PART, :] = aggregate
-    message[PART:, :] = (cotangent * gates * (1.0 + preact * (1.0 - gates))).astype(BF)
-
-
-def output_body(message, weight, output):
-    own = message[at(place()["h"], SLICE), :]
-    preact = dot(own, weight[...])
+    grad_pre = (cotangent * gates * (1.0 + preact * (1.0 - gates))).astype(BF)
+    grad_w[...] = dot(agg, grad_pre, ((0,), (0,)))
+    aggregate[...] = agg
+    own[...] = grad_pre
+    share[...] = grad_w[at(me["x"], SLICE), :]
+    for k, to in ((3, to3), (2, to2), (1, to1)):
+        to[0:PART, :] = grad_pre
+        to[PART:, :] = grad_w[at(me["x"] ^ k, SLICE), :].astype(BF)
+
+
+def output_body(aggregate, weight, output):
+    preact = dot(aggregate[at(place()["h"], SLICE), :], weight[...])
     output[...] = (preact * jax.nn.sigmoid(preact)).astype(BF)
 
 
-def backward_body(dense_t, weight, m0, m3, m2, m1, to_c, grad_agg, aggregate, grad_pre, grad_w):
+def backward_body(dense_t, weight, m0, m3, m2, m1, share, to_c, grad_agg, grad_pre):
     me = place()
     for k, m in enumerate((m0, m1, m2, m3)):
-        rows = at(me["x"] ^ k, PART)
-        aggregate[rows, :] = m[0:PART, :]
-        grad_pre[rows, :] = m[PART:, :]
+        grad_pre[at(me["x"] ^ k, PART), :] = m[0:PART, :]
     grad = dot(grad_pre[...], weight[...], ((1,), (1,))).astype(BF)
     grad_agg[...] = grad
     to_c[0:BLOCK, :] = dot(dense_t[3], grad)
-    grad_w[...] = dot(aggregate[...], grad_pre[...], ((0,), (0,)))
-    to_c[BLOCK:, :] = grad_w[at(me["x"], SLICE), :]
+    total = share[...] + m1[PART:, :].astype(F32)
+    to_c[BLOCK:, :] = total + (m2[PART:, :].astype(F32) + m3[PART:, :].astype(F32))
 
 
 def keep_body(dense_t, grad_agg, keep):
@@ -235,30 +237,37 @@
         own[k * PART : (k + 1) * PART, :] = total[at(me["z"] ^ k, PART), :]
 
 
-def pair_share(share, got_first):
-    return (share[...].astype(F32) + got_first[PART:, :].astype(F32)).astype(BF)
-
-
-def to_z_body(k, own, got, share, got_first, to):
-    to[0:PART, :] = (own[k * PART : (k + 1) * PART, :] + got[0:PART, :].astype(F32)).astype(BF)
-    to[PART:, :] = pair_share(share, got_first)
-
-
-def to_z1_body(own, got, share, got_first, got_own, to, kept, kept_share):
-    to_z_body(1, own, got, share, got_first, to)
+def to_z_body(k, own, got, to):
+    to[...] = (own[k * PART : (k + 1) * PART, :] + got[0:PART, :].astype(F32)).astype(BF)
+
+
+def to_z3_body(own, got, to):
+    to_z_body(3, own, got, to)
+
+
+def to_z2_body(own, got, earlier, to):
+    to_z_body(2, own, got, to)
+
+
+def to_z1_body(own, got, got_own, share, earlier, to, kept, total):
+    to_z_body(1, own, got, to)
     kept[...] = own[0:PART, :] + got_own[...].astype(F32)
-    kept_share[...] = pair_share(share, got_first)
-
-
-def after_z_body(kept, share, r1, r2, r3, piece, total_share):
-    total = kept[...] + r1[0:PART, :].astype(F32)
-    piece[...] = (total + (r2[0:PART, :].astype(F32) + r3[0:PART, :].astype(F32))).astype(BF)
-    pair = share[...].astype(F32) + r1[PART:, :].astype(F32)
-    total_share[...] = pair + (r2[PART:, :].astype(F32) + r3[PART:, :].astype(F32))
-
-
-def last_body(one, two, mine, got, message):
-    message[0:PART, :] = (one[...].astype(F32) + two[...].astype(F32)).astype(BF)
+    total[...] = share[...].astype(F32) + earlier[PART:, :].astype(F32)
+
+
+def after_z_body(kept, r1, r2, r3, mine, got, to_v, share):
+    total = kept[...] + r1[...].astype(F32)
+    to_v[...] = total + (r2[...].astype(F32) + r3[...].astype(F32))
+    share[...] = mine[...] + got[...]
+
+
+def after_v_body(one, two, mine, got, piece, share):
+    piece[...] = (one[...] + two[...]).astype(BF)
+    share[...] = mine[...] + got[...]
+
+
+def last_body(piece, mine, got, message):
+    message[0:PART, :] = piece[...]
     put_split(message, PART, mine[...] + got[...])
 
 
@@ -297,19 +306,19 @@
         forward_body, [block32], dense, *mine[::-1], *by_c[::-1], *by_u[::-1], scratch=[pltpu.VMEM((3, BLOCK, WIDTH), BF)]
     )
     to3, to2, to1, own = call(
-        forward_last_body, [part32] * 4, dense, *by_uc[::-1], most, scratch=[pltpu.VMEM((1, BLOCK, WIDTH), BF), total]
+        forward_last_body, [part32, part, part32, part32], dense, *by_uc[::-1], most, scratch=[pltpu.VMEM((1, BLOCK, WIDTH), BF), total]
     )
     got = [send(value, route) for value, route in zip((to3, to2, to1), FLIP_X[::-1])]
     (mine,) = call(sum_body, [((2 * PART + SLICE, WIDTH), BF)], own, *got, cotangent)
     got = send(mine, FLIP_H)
-    (message,) = call(layer_body, [two], mine, got, weight)
-    (output,) = call(output_body, [((SLICE, WIDTH), BF)], message, weight)
-    got = spread(message, FLIP_X)
-
-    whole = pltpu.VMEM((BLOCK, WIDTH), BF)
+    *to, own, aggregate, share = call(
+        layer_body, [to_z, to_z, to_z, part, part, share32], mine, got, weight, scratch=[pltpu.VMEM((WIDTH, WIDTH), F32)]
+    )
+    (output,) = call(output_body, [((SLICE, WIDTH), BF)], aggregate, weight)
+    got = [send(value, route) for value, route in zip(to, FLIP_X[::-1])]
     to_c, grad_agg = call(
-        backward_body, [((BLOCK + SLICE, WIDTH), F32), block], dense_t, weight, *got,
-        scratch=[whole, whole, pltpu.VMEM((WIDTH, WIDTH), F32)],
+        backward_body, [((BLOCK + SLICE, WIDTH), F32), block], dense_t, weight, own, *got, share,
+        scratch=[pltpu.VMEM((BLOCK, WIDTH), BF)],
     )
     got = send(to_c, FLIP_C)
     (keep_u,) = call(keep_body, [block32], dense_t, grad_agg)
@@ -317,13 +326,15 @@
     u3, u2, u1, u0 = [send(value, FLIP_U) for value in to_u]
     to_c, keep = call(kept_body, [block32, block32], dense_t, grad_agg)
     (own,) = call(after_c_body, [block32], keep, send(to_c, FLIP_C), scratch=[total])
-    (to3,) = call(functools.partial(to_z_body, 3), [to_z], own, u3, share, u3)
-    (to2,) = call(functools.partial(to_z_body, 2), [to_z], own, u2, share, u3)
-    to1, kept, share = call(to_z1_body, [to_z, part32, share16], own, u1, share, u3, u0)
+    (to3,) = call(to_z3_body, [part], own, u3)
+    (to2,) = call(to_z2_body, [part], own, u2, u3)
+    to1, kept, share = call(to_z1_body, [part, part32, share32], own, u1, u0, share, u3)
     from_z = [send(value, route) for value, route in zip((to1, to2, to3), FLIP_Z)]
-    piece, share = call(after_z_body, [part, share32], kept, share, *from_z)
-    routes = (TO_ROW, TO_ROW_TOO)
-    (message,) = call(last_body, [two], *[send(piece, route) for route in routes], share, send(share, FLIP_V))
+    to_v, share = call(after_z_body, [part32, share32], kept, *from_z, share, send(share, FLIP_Z[0]))
+    piece, share = call(
+        after_v_body, [part, share32], to_v, send(to_v, FLIP_V), share, send(share, FLIP_Z[1])
+    )
+    (message,) = call(last_body, [two], send(piece, TO_ROW), share, send(share, FLIP_V))
     grad_features, grad_weight = call(finish_body, [block, ((WIDTH, WIDTH), F32)], *spread(message, FLIP_X))
     return output, grad_weight, grad_features
 

time: 108 us -> 108 us (level)
  the two profiles are of different devices: /device:TPU:28 before, /device:TPU:32 now
where the time goes in v7:
time: 108 us; the launch traced here: 106 us
  waiting for transfers between devices  50.8 us (47%)
  starting transfers between devices  45.5 us (42%)
  Pallas kernels  5.99 us (6%)
  local copies, waits for them, and re-layouts  3.32 us (3%)
    ppermute x34, waiting for transfers between devices, send(): return lax.ppermute(value, AXES, route)  50.8 us
    ppermute x34, starting transfers between devices, send(): return lax.ppermute(value, AXES, route)  45.5 us
    pallas_call x21, Pallas kernels, call(): pl.pallas_call(body, out_shape=[jax.ShapeDtypeStruct(shape, dtype) for sh...  5.99 us
    unnamed x11, local copies, waits for them, and re-layouts  3.32 us
  transfers between devices with their start and end apart: 34, of which 22 were waited for; matrix products, arithmetic and copies ran while one was open for 1% of the time, Pallas kernels for 3%

profile of v7, /device:TPU:32, one launch (start us, length us, event | category | flops | bytes accessed | tf_op | source)
XLA Modules:
  0.0 106.4 jit_solution(14933816264216197374)
XLA Ops:
  1.6 3.6 %collective-permute-start = (bf16[128,256]{1,0:T(8,128)(2,1)S(1)}, bf16[128,256]{1,0:T(8,128)(2,1)S(1)}, u32[]{:S(2)}, u32[]{:S(2)}) collective-permute-start(bf16[128,256]{1,0:T(8,128)(2,1)S(1)} %shard_map.85), channel_id=1, source_target_pairs={{1,0},{53,1},{65,2},{113,3},{129,4},{181,5},{195,6},{247,7},{9,8},... | collective-permute-start | bytes 196616 | tf_op jit(solution)/shard_map/ppermute | solution.py:60
  8.8 3.2 %collective-permute-done.high = bf16[128,256]{1,0:T(8,128)(2,1)S(1)} collective-permute-done((bf16[128,256]{1,0:T(8,128)(2,1)S(1)}, bf16[128,256]{1,0:T(8,128)(2,1)S(1)}, u32[]{:S(2)}, u32[]{:S(2)}) %collective-permute-start) | collective-permute-done | bytes 65568 | tf_op jit(solution)/shard_map/ppermute | solution.py:60
  13.2 1.8 %collective-permute-start.1 = (bf16[128,256]{1,0:T(8,128)(2,1)S(1)}, bf16[128,256]{1,0:T(8,128)(2,1)S(1)}, u32[]{:S(2)}, u32[]{:S(2)}) collective-permute-start(bf16[128,256]{1,0:T(8,128)(2,1)S(1)} %collective-permute-done.high), channel_id=1, source_target_pairs={{0,128},{1,129},{2,130},{3,131},{4,132},{5,133},{6,134},{7,135},{8... | collective-permute-start | bytes 196616 | tf_op jit(solution)/shard_map/ppermute | solution.py:60
  15.6 3.7 %collective-permute-done.5.low = bf16[128,256]{1,0:T(8,128)(2,1)S(1)} collective-permute-done((bf16[128,256]{1,0:T(8,128)(2,1)S(1)}, bf16[128,256]{1,0:T(8,128)(2,1)S(1)}, u32[]{:S(2)}, u32[]{:S(2)}) %collective-permute-start.5) | collective-permute-done | bytes 65568 | tf_op jit(solution)/shard_map/ppermute | solution.py:60
  22.1 2.2 %collective-permute-done.6.a2 = bf16[256,256]{1,0:T(8,128)(2,1)S(1)} collective-permute-done((bf16[256,256]{1,0:T(8,128)(2,1)S(1)}, bf16[256,256]{1,0:T(8,128)(2,1)S(1)}, u32[]{:S(2)}, u32[]{:S(2)}) %collective-permute-start.6) | collective-permute-done | bytes 131104 | tf_op jit(solution)/shard_map/ppermute | solution.py:60
  27.5 4.0 %collective-permute-start.10 = (f32[128,256]{1,0:T(8,128)S(1)}, f32[128,256]{1,0:T(8,128)S(1)}, u32[]{:S(2)}, u32[]{:S(2)}) collective-permute-start(f32[128,256]{1,0:T(8,128)S(1)} %get-tuple-element.41), channel_id=1, source_target_pairs={{0,6},{1,7},{2,4},{3,5},{4,2},{5,3},{6,0},{7,1},{8,14},{9,15},{10,... | collective-permute-start | bytes 393224 | tf_op jit(solution)/shard_map/ppermute | solution.py:60
  31.5 1.6 %collective-permute-start.11 = (bf16[128,256]{1,0:T(8,128)(2,1)S(1)}, bf16[128,256]{1,0:T(8,128)(2,1)S(1)}, u32[]{:S(2)}, u32[]{:S(2)}) collective-permute-start(bf16[128,256]{1,0:T(8,128)(2,1)S(1)} %get-tuple-element.42), channel_id=1, source_target_pairs={{0,4},{1,5},{2,6},{3,7},{4,0},{5,1},{6,2},{7,3},{8,12},{9,13},{10,... | collective-permute-start | bytes 196616 | tf_op jit(solution)/shard_map/ppermute | solution.py:60
  33.0 4.9 %collective-permute-done.11.r2 = bf16[128,256]{1,0:T(8,128)(2,1)S(1)} collective-permute-done((bf16[128,256]{1,0:T(8,128)(2,1)S(1)}, bf16[128,256]{1,0:T(8,128)(2,1)S(1)}, u32[]{:S(2)}, u32[]{:S(2)}) %collective-permute-start.11) | collective-permute-done | bytes 65568 | tf_op jit(solution)/shard_map/ppermute | solution.py:60
  38.0 3.3 %collective-permute-start.13 = (bf16[320,256]{1,0:T(8,128)(2,1)S(1)}, bf16[320,256]{1,0:T(8,128)(2,1)S(1)}, u32[]{:S(2)}, u32[]{:S(2)}) collective-permute-start(bf16[320,256]{1,0:T(8,128)(2,1)S(1)} %shard_map.91.mine), channel_id=1, source_target_pairs={{0,1},{1,0},{2,3},{3,2},{4,5},{5,4},{6,7},{7,6},{8,9},{9,8},{10,11... | collective-permute-start | bytes 491528 | tf_op jit(solution)/shard_map/ppermute | solution.py:60
  41.3 8.6 %collective-permute-done.13.got = bf16[320,256]{1,0:T(8,128)(2,1)S(1)} collective-permute-done((bf16[320,256]{1,0:T(8,128)(2,1)S(1)}, bf16[320,256]{1,0:T(8,128)(2,1)S(1)}, u32[]{:S(2)}, u32[]{:S(2)}) %collective-permute-start.13) | collective-permute-done | bytes 163872 | tf_op jit(solution)/shard_map/ppermute | solution.py:60
  50.3 3.4 %collective-permute-start.14 = (bf16[192,256]{1,0:T(8,128)(2,1)S(1)}, bf16[192,256]{1,0:T(8,128)(2,1)S(1)}, u32[]{:S(2)}, u32[]{:S(2)}) collective-permute-start(bf16[192,256]{1,0:T(8,128)(2,1)S(1)} %get-tuple-element.47), channel_id=1, source_target_pairs={{0,6},{1,7},{2,4},{3,5},{4,2},{5,3},{6,0},{7,1},{8,14},{9,15},{10,... | collective-permute-start | bytes 294920 | tf_op jit(solution)/shard_map/ppermute | solution.py:60
  54.7 2.8 %collective-permute-done.14.m3 = bf16[192,256]{1,0:T(8,128)(2,1)S(1)} collective-permute-done((bf16[192,256]{1,0:T(8,128)(2,1)S(1)}, bf16[192,256]{1,0:T(8,128)(2,1)S(1)}, u32[]{:S(2)}, u32[]{:S(2)}) %collective-permute-start.14) | collective-permute-done | bytes 98336 | tf_op jit(solution)/shard_map/ppermute | solution.py:60
  57.5 2.6 %collective-permute-done.15.m2 = bf16[192,256]{1,0:T(8,128)(2,1)S(1)} collective-permute-done((bf16[192,256]{1,0:T(8,128)(2,1)S(1)}, bf16[192,256]{1,0:T(8,128)(2,1)S(1)}, u32[]{:S(2)}, u32[]{:S(2)}) %collective-permute-start.15) | collective-permute-done | bytes 98336 | tf_op jit(solution)/shard_map/ppermute | solution.py:60
  63.1 1.4 %collective-permute-start.21 = (bf16[192,256]{1,0:T(8,128)(2,1)S(1)}, bf16[192,256]{1,0:T(8,128)(2,1)S(1)}, u32[]{:S(2)}, u32[]{:S(2)}) collective-permute-start(bf16[192,256]{1,0:T(8,128)(2,1)S(1)} %get-tuple-element.58), channel_id=1, source_target_pairs={{0,16},{1,17},{2,18},{3,19},{4,20},{5,21},{6,22},{7,23},{8,24},{9,... | collective-permute-start | bytes 294920 | tf_op jit(solution)/shard_map/ppermute | solution.py:60
  67.3 1.5 %collective-permute-done.21.earlier.got = bf16[192,256]{1,0:T(8,128)(2,1)S(1)} collective-permute-done((bf16[192,256]{1,0:T(8,128)(2,1)S(1)}, bf16[192,256]{1,0:T(8,128)(2,1)S(1)}, u32[]{:S(2)}, u32[]{:S(2)}) %collective-permute-start.21) | collective-permute-done | bytes 98336 | tf_op jit(solution)/shard_map/ppermute | solution.py:60
  70.2 1.6 %collective-permute-start.24 = (bf16[128,256]{1,0:T(8,128)(2,1)S(1)}, bf16[128,256]{1,0:T(8,128)(2,1)S(1)}, u32[]{:S(2)}, u32[]{:S(2)}) collective-permute-start(bf16[128,256]{1,0:T(8,128)(2,1)S(1)} %shard_map.100), channel_id=1, source_target_pairs={{0,128},{1,129},{2,130},{3,131},{4,132},{5,133},{6,134},{7,135},{8... | collective-permute-start | bytes 196616 | tf_op jit(solution)/shard_map/ppermute | solution.py:60
  72.9 1.5 %collective-permute-start.26 = (f32[64,256]{1,0:T(8,128)S(1)}, f32[64,256]{1,0:T(8,128)S(1)}, u32[]{:S(2)}, u32[]{:S(2)}) collective-permute-start(f32[64,256]{1,0:T(8,128)S(1)} %get-tuple-element.62.mine), channel_id=1, source_target_pairs={{0,64},{1,65},{2,66},{3,67},{4,68},{5,69},{6,70},{7,71},{8,72},{9,... | collective-permute-start | bytes 196616 | tf_op jit(solution)/shard_map/ppermute | solution.py:60
  74.4 1.7 %collective-permute-done.24.r2 = bf16[128,256]{1,0:T(8,128)(2,1)S(1)} collective-permute-done((bf16[128,256]{1,0:T(8,128)(2,1)S(1)}, bf16[128,256]{1,0:T(8,128)(2,1)S(1)}, u32[]{:S(2)}, u32[]{:S(2)}) %collective-permute-start.24) | collective-permute-done | bytes 65568 | tf_op jit(solution)/shard_map/ppermute | solution.py:60
  77.6 3.8 %collective-permute-start.27 = (f32[128,256]{1,0:T(8,128)S(1)}, f32[128,256]{1,0:T(8,128)S(1)}, u32[]{:S(2)}, u32[]{:S(2)}) collective-permute-start(f32[128,256]{1,0:T(8,128)S(1)} %get-tuple-element.63.one), channel_id=1, source_target_pairs={{0,48},{1,49},{2,50},{3,51},{4,52},{5,53},{6,54},{7,55},{8,56},{9,... | collective-permute-start | bytes 393224 | tf_op jit(solution)/shard_map/ppermute | solution.py:60
  82.2 4.5 %collective-permute-done.28.got = f32[64,256]{1,0:T(8,128)S(1)} collective-permute-done((f32[64,256]{1,0:T(8,128)S(1)}, f32[64,256]{1,0:T(8,128)S(1)}, u32[]{:S(2)}, u32[]{:S(2)}) %collective-permute-start.28) | collective-permute-done | bytes 65568 | tf_op jit(solution)/shard_map/ppermute | solution.py:60
  86.7 4.9 %collective-permute-start.29 = (bf16[128,256]{1,0:T(8,128)(2,1)S(1)}, bf16[128,256]{1,0:T(8,128)(2,1)S(1)}, u32[]{:S(2)}, u32[]{:S(2)}) collective-permute-start(bf16[128,256]{1,0:T(8,128)(2,1)S(1)} %get-tuple-element.65), channel_id=1, source_target_pairs={{0,1},{1,53},{2,65},{3,113},{4,129},{5,181},{6,195},{7,247},{8,9},... | collective-permute-start | bytes 196616 | tf_op jit(solution)/shard_map/ppermute | solution.py:60
  91.6 4.5 %collective-permute-done.29.piece = bf16[128,256]{1,0:T(8,128)(2,1)S(1)} collective-permute-done((bf16[128,256]{1,0:T(8,128)(2,1)S(1)}, bf16[128,256]{1,0:T(8,128)(2,1)S(1)}, u32[]{:S(2)}, u32[]{:S(2)}) %collective-permute-start.29) | collective-permute-done | bytes 65568 | tf_op jit(solution)/shard_map/ppermute | solution.py:60
  99.5 1.7 %collective-permute-start.33 = (bf16[256,256]{1,0:T(8,128)(2,1)S(1)}, bf16[256,256]{1,0:T(8,128)(2,1)S(1)}, u32[]{:S(2)}, u32[]{:S(2)}) collective-permute-start(bf16[256,256]{1,0:T(8,128)(2,1)S(1)} %shard_map.104.m0), channel_id=1, source_target_pairs={{0,2},{1,3},{2,0},{3,1},{4,6},{5,7},{6,4},{7,5},{8,10},{9,11},{10,... | collective-permute-start | bytes 393224 | tf_op jit(solution)/shard_map/ppermute | solution.py:60
  103.3 1.5 %collective-permute-done.32.m2 = bf16[256,256]{1,0:T(8,128)(2,1)S(1)} collective-permute-done((bf16[256,256]{1,0:T(8,128)(2,1)S(1)}, bf16[256,256]{1,0:T(8,128)(2,1)S(1)}, u32[]{:S(2)}, u32[]{:S(2)}) %collective-permute-start.32) | collective-permute-done | bytes 131104 | tf_op jit(solution)/shard_map/ppermute | solution.py:60
  (76 shorter events, 31.2 us)
Async XLA Ops:
  1.6 10.4 %collective-permute-start = (bf16[128,256]{1,0:T(8,128)(2,1)S(1)}, bf16[128,256]{1,0:T(8,128)(2,1)S(1)}, u32[]{:S(2)}, u32[]{:S(2)}) collective-permute-start(bf16[128,256]{1,0:T(8,128)(2,1)S(1)} %shard_map.85), channel_id=1, source_target_pairs={{1,0},{53,1},{65,2},{113,3},{129,4},{181,5},{195,6},{247,7},{9,8},... | collective-permute-start | bytes 196616 | tf_op jit(solution)/shard_map/ppermute | solution.py:60
  12.1 7.2 %collective-permute-start.5 = (bf16[128,256]{1,0:T(8,128)(2,1)S(1)}, bf16[128,256]{1,0:T(8,128)(2,1)S(1)}, u32[]{:S(2)}, u32[]{:S(2)}) collective-permute-start(bf16[128,256]{1,0:T(8,128)(2,1)S(1)} %collective-permute-done.high), channel_id=1, source_target_pairs={{0,192},{1,193},{2,194},{3,195},{4,196},{5,197},{6,198},{7,199},{8... | collective-permute-start | bytes 196616 | tf_op jit(solution)/shard_map/ppermute | solution.py:60
  13.2 7.3 %collective-permute-start.1 = (bf16[128,256]{1,0:T(8,128)(2,1)S(1)}, bf16[128,256]{1,0:T(8,128)(2,1)S(1)}, u32[]{:S(2)}, u32[]{:S(2)}) collective-permute-start(bf16[128,256]{1,0:T(8,128)(2,1)S(1)} %collective-permute-done.high), channel_id=1, source_target_pairs={{0,128},{1,129},{2,130},{3,131},{4,132},{5,133},{6,134},{7,135},{8... | collective-permute-start | bytes 196616 | tf_op jit(solution)/shard_map/ppermute | solution.py:60
  15.0 5.6 %collective-permute-start.2 = (bf16[128,256]{1,0:T(8,128)(2,1)S(1)}, bf16[128,256]{1,0:T(8,128)(2,1)S(1)}, u32[]{:S(2)}, u32[]{:S(2)}) collective-permute-start(bf16[128,256]{1,0:T(8,128)(2,1)S(1)} %collective-permute-done.high), channel_id=1, source_target_pairs={{0,64},{1,65},{2,66},{3,67},{4,68},{5,69},{6,70},{7,71},{8,72},{9,... | collective-permute-start | bytes 196616 | tf_op jit(solution)/shard_map/ppermute | solution.py:60
  27.5 10.5 %collective-permute-start.10 = (f32[128,256]{1,0:T(8,128)S(1)}, f32[128,256]{1,0:T(8,128)S(1)}, u32[]{:S(2)}, u32[]{:S(2)}) collective-permute-start(f32[128,256]{1,0:T(8,128)S(1)} %get-tuple-element.41), channel_id=1, source_target_pairs={{0,6},{1,7},{2,4},{3,5},{4,2},{5,3},{6,0},{7,1},{8,14},{9,15},{10,... | collective-permute-start | bytes 393224 | tf_op jit(solution)/shard_map/ppermute | solution.py:60
  31.5 6.5 %collective-permute-start.12 = (f32[128,256]{1,0:T(8,128)S(1)}, f32[128,256]{1,0:T(8,128)S(1)}, u32[]{:S(2)}, u32[]{:S(2)}) collective-permute-start(f32[128,256]{1,0:T(8,128)S(1)} %get-tuple-element.43), channel_id=1, source_target_pairs={{0,2},{1,3},{2,0},{3,1},{4,6},{5,7},{6,4},{7,5},{8,10},{9,11},{10,... | collective-permute-start | bytes 393224 | tf_op jit(solution)/shard_map/ppermute | solution.py:60
  31.5 6.5 %collective-permute-start.11 = (bf16[128,256]{1,0:T(8,128)(2,1)S(1)}, bf16[128,256]{1,0:T(8,128)(2,1)S(1)}, u32[]{:S(2)}, u32[]{:S(2)}) collective-permute-start(bf16[128,256]{1,0:T(8,128)(2,1)S(1)} %get-tuple-element.42), channel_id=1, source_target_pairs={{0,4},{1,5},{2,6},{3,7},{4,0},{5,1},{6,2},{7,3},{8,12},{9,13},{10,... | collective-permute-start | bytes 196616 | tf_op jit(solution)/shard_map/ppermute | solution.py:60
  38.0 11.9 %collective-permute-start.13 = (bf16[320,256]{1,0:T(8,128)(2,1)S(1)}, bf16[320,256]{1,0:T(8,128)(2,1)S(1)}, u32[]{:S(2)}, u32[]{:S(2)}) collective-permute-start(bf16[320,256]{1,0:T(8,128)(2,1)S(1)} %shard_map.91.mine), channel_id=1, source_target_pairs={{0,1},{1,0},{2,3},{3,2},{4,5},{5,4},{6,7},{7,6},{8,9},{9,8},{10,11... | collective-permute-start | bytes 491528 | tf_op jit(solution)/shard_map/ppermute | solution.py:60
  50.3 7.2 %collective-permute-start.14 = (bf16[192,256]{1,0:T(8,128)(2,1)S(1)}, bf16[192,256]{1,0:T(8,128)(2,1)S(1)}, u32[]{:S(2)}, u32[]{:S(2)}) collective-permute-start(bf16[192,256]{1,0:T(8,128)(2,1)S(1)} %get-tuple-element.47), channel_id=1, source_target_pairs={{0,6},{1,7},{2,4},{3,5},{4,2},{5,3},{6,0},{7,1},{8,14},{9,15},{10,... | collective-permute-start | bytes 294920 | tf_op jit(solution)/shard_map/ppermute | solution.py:60
  53.7 6.4 %collective-permute-start.15 = (bf16[192,256]{1,0:T(8,128)(2,1)S(1)}, bf16[192,256]{1,0:T(8,128)(2,1)S(1)}, u32[]{:S(2)}, u32[]{:S(2)}) collective-permute-start(bf16[192,256]{1,0:T(8,128)(2,1)S(1)} %get-tuple-element.48), channel_id=1, source_target_pairs={{0,4},{1,5},{2,6},{3,7},{4,0},{5,1},{6,2},{7,3},{8,12},{9,13},{10,... | collective-permute-start | bytes 294920 | tf_op jit(solution)/shard_map/ppermute | solution.py:60
  53.7 6.4 %collective-permute-start.16 = (bf16[192,256]{1,0:T(8,128)(2,1)S(1)}, bf16[192,256]{1,0:T(8,128)(2,1)S(1)}, u32[]{:S(2)}, u32[]{:S(2)}) collective-permute-start(bf16[192,256]{1,0:T(8,128)(2,1)S(1)} %get-tuple-element.49), channel_id=1, source_target_pairs={{0,2},{1,3},{2,0},{3,1},{4,6},{5,7},{6,4},{7,5},{8,10},{9,11},{10,... | collective-permute-start | bytes 294920 | tf_op jit(solution)/shard_map/ppermute | solution.py:60
  61.5 5.8 %collective-permute-start.17 = (f32[512,256]{1,0:T(8,128)S(1)}, f32[512,256]{1,0:T(8,128)S(1)}, u32[]{:S(2)}, u32[]{:S(2)}) collective-permute-start(f32[512,256]{1,0:T(8,128)S(1)} %get-tuple-element.53), channel_id=1, source_target_pairs={{0,8},{1,9},{2,10},{3,11},{4,12},{5,13},{6,14},{7,15},{8,0},{9,1},... | collective-permute-start | bytes 1572872 | tf_op jit(solution)/shard_map/ppermute | solution.py:60
  63.1 5.7 %collective-permute-start.21 = (bf16[192,256]{1,0:T(8,128)(2,1)S(1)}, bf16[192,256]{1,0:T(8,128)(2,1)S(1)}, u32[]{:S(2)}, u32[]{:S(2)}) collective-permute-start(bf16[192,256]{1,0:T(8,128)(2,1)S(1)} %get-tuple-element.58), channel_id=1, source_target_pairs={{0,16},{1,17},{2,18},{3,19},{4,20},{5,21},{6,22},{7,23},{8,24},{9,... | collective-permute-start | bytes 294920 | tf_op jit(solution)/shard_map/ppermute | solution.py:60
  64.5 5.7 %collective-permute-start.23 = (bf16[128,256]{1,0:T(8,128)(2,1)S(1)}, bf16[128,256]{1,0:T(8,128)(2,1)S(1)}, u32[]{:S(2)}, u32[]{:S(2)}) collective-permute-start(bf16[128,256]{1,0:T(8,128)(2,1)S(1)} %get-tuple-element.61), channel_id=1, source_target_pairs={{0,16},{1,17},{2,18},{3,19},{4,20},{5,21},{6,22},{7,23},{8,24},{9,... | collective-permute-start | bytes 196616 | tf_op jit(solution)/shard_map/ppermute | solution.py:60
  65.2 6.6 %collective-permute-start.19 = (bf16[128,256]{1,0:T(8,128)(2,1)S(1)}, bf16[128,256]{1,0:T(8,128)(2,1)S(1)}, u32[]{:S(2)}, u32[]{:S(2)}) collective-permute-start(bf16[128,256]{1,0:T(8,128)(2,1)S(1)} %get-tuple-element.55), channel_id=1, source_target_pairs={{0,16},{1,17},{2,18},{3,19},{4,20},{5,21},{6,22},{7,23},{8,24},{9,... | collective-permute-start | bytes 196616 | tf_op jit(solution)/shard_map/ppermute | solution.py:60
  66.5 5.7 %collective-permute-start.20 = (bf16[128,256]{1,0:T(8,128)(2,1)S(1)}, bf16[128,256]{1,0:T(8,128)(2,1)S(1)}, u32[]{:S(2)}, u32[]{:S(2)}) collective-permute-start(bf16[128,256]{1,0:T(8,128)(2,1)S(1)} %get-tuple-element.56), channel_id=1, source_target_pairs={{0,16},{1,17},{2,18},{3,19},{4,20},{5,21},{6,22},{7,23},{8,24},{9,... | collective-permute-start | bytes 196616 | tf_op jit(solution)/shard_map/ppermute | solution.py:60
  68.8 5.5 %collective-permute-start.25 = (bf16[128,256]{1,0:T(8,128)(2,1)S(1)}, bf16[128,256]{1,0:T(8,128)(2,1)S(1)}, u32[]{:S(2)}, u32[]{:S(2)}) collective-permute-start(bf16[128,256]{1,0:T(8,128)(2,1)S(1)} %shard_map.101), channel_id=1, source_target_pairs={{0,192},{1,193},{2,194},{3,195},{4,196},{5,197},{6,198},{7,199},{8... | collective-permute-start | bytes 196616 | tf_op jit(solution)/shard_map/ppermute | solution.py:60
  70.2 5.8 %collective-permute-start.24 = (bf16[128,256]{1,0:T(8,128)(2,1)S(1)}, bf16[128,256]{1,0:T(8,128)(2,1)S(1)}, u32[]{:S(2)}, u32[]{:S(2)}) collective-permute-start(bf16[128,256]{1,0:T(8,128)(2,1)S(1)} %shard_map.100), channel_id=1, source_target_pairs={{0,128},{1,129},{2,130},{3,131},{4,132},{5,133},{6,134},{7,135},{8... | collective-permute-start | bytes 196616 | tf_op jit(solution)/shard_map/ppermute | solution.py:60
  77.6 9.1 %collective-permute-start.27 = (f32[128,256]{1,0:T(8,128)S(1)}, f32[128,256]{1,0:T(8,128)S(1)}, u32[]{:S(2)}, u32[]{:S(2)}) collective-permute-start(f32[128,256]{1,0:T(8,128)S(1)} %get-tuple-element.63.one), channel_id=1, source_target_pairs={{0,48},{1,49},{2,50},{3,51},{4,52},{5,53},{6,54},{7,55},{8,56},{9,... | collective-permute-start | bytes 393224 | tf_op jit(solution)/shard_map/ppermute | solution.py:60
  86.7 9.4 %collective-permute-start.29 = (bf16[128,256]{1,0:T(8,128)(2,1)S(1)}, bf16[128,256]{1,0:T(8,128)(2,1)S(1)}, u32[]{:S(2)}, u32[]{:S(2)}) collective-permute-start(bf16[128,256]{1,0:T(8,128)(2,1)S(1)} %get-tuple-element.65), channel_id=1, source_target_pairs={{0,1},{1,53},{2,65},{3,113},{4,129},{5,181},{6,195},{7,247},{8,9},... | collective-permute-start | bytes 196616 | tf_op jit(solution)/shard_map/ppermute | solution.py:60
  91.6 5.5 %collective-permute-start.30 = (f32[64,256]{1,0:T(8,128)S(1)}, f32[64,256]{1,0:T(8,128)S(1)}, u32[]{:S(2)}, u32[]{:S(2)}) collective-permute-start(f32[64,256]{1,0:T(8,128)S(1)} %get-tuple-element.66.mine), channel_id=1, source_target_pairs={{0,48},{1,49},{2,50},{3,51},{4,52},{5,53},{6,54},{7,55},{8,56},{9,... | collective-permute-start | bytes 196616 | tf_op jit(solution)/shard_map/ppermute | solution.py:60
  97.1 6.3 %collective-permute-start.31 = (bf16[256,256]{1,0:T(8,128)(2,1)S(1)}, bf16[256,256]{1,0:T(8,128)(2,1)S(1)}, u32[]{:S(2)}, u32[]{:S(2)}) collective-permute-start(bf16[256,256]{1,0:T(8,128)(2,1)S(1)} %shard_map.104.m0), channel_id=1, source_target_pairs={{0,6},{1,7},{2,4},{3,5},{4,2},{5,3},{6,0},{7,1},{8,14},{9,15},{10,... | collective-permute-start | bytes 393224 | tf_op jit(solution)/shard_map/ppermute | solution.py:60
  98.4 6.5 %collective-permute-start.32 = (bf16[256,256]{1,0:T(8,128)(2,1)S(1)}, bf16[256,256]{1,0:T(8,128)(2,1)S(1)}, u32[]{:S(2)}, u32[]{:S(2)}) collective-permute-start(bf16[256,256]{1,0:T(8,128)(2,1)S(1)} %shard_map.104.m0), channel_id=1, source_target_pairs={{0,4},{1,5},{2,6},{3,7},{4,0},{5,1},{6,2},{7,3},{8,12},{9,13},{10,... | collective-permute-start | bytes 393224 | tf_op jit(solution)/shard_map/ppermute | solution.py:60
  99.5 6.1 %collective-permute-start.33 = (bf16[256,256]{1,0:T(8,128)(2,1)S(1)}, bf16[256,256]{1,0:T(8,128)(2,1)S(1)}, u32[]{:S(2)}, u32[]{:S(2)}) collective-permute-start(bf16[256,256]{1,0:T(8,128)(2,1)S(1)} %shard_map.104.m0), channel_id=1, source_target_pairs={{0,2},{1,3},{2,0},{3,1},{4,6},{5,7},{6,4},{7,5},{8,10},{9,11},{10,... | collective-permute-start | bytes 393224 | tf_op jit(solution)/shard_map/ppermute | solution.py:60
  (15 other events, 76.4 us)

commit v8 on v7

--- a/solution.py
+++ b/solution.py
@@ -43,6 +43,7 @@
 FLIP_H = pairs(lambda z, y, c, x, h: (z, y, c, x, 1 - h))
 FLIP_X = [pairs(lambda z, y, c, x, h, k=k: (z, y, c, x ^ k, h)) for k in (1, 2, 3)]
 FLIP_Z = [pairs(lambda z, y, c, x, h, k=k: (z ^ k, y, c, x, h)) for k in (1, 2, 3)]
+FAR_X = (FLIP_X[1], FLIP_X[2], FLIP_X[0])
 ROUTE = (((2, 1, 3, 0), (0, 3, 2, 1), (2, 1, 0, 3), (3, 0, 2, 1)), ((0, 1, 3, 2), (0, 1, 2, 3), (0, 1, 2, 3), (1, 0, 2, 3)))
 TO_ROW = pairs(lambda z, y, c, x, h: (x, Y_OF[u_of(y), h], c, ROUTE[v_of(y) == h][x][z], 1 - v_of(y)))
 TO_COLUMN = [(there, here) for here, there in TO_ROW]
@@ -58,10 +59,6 @@
 
 def send(value, route):
     return lax.ppermute(value, AXES, route)
-
-
-def spread(value, routes):
-    return [value] + [send(value, route) for route in routes[::-1]]
 
 
 def place():
@@ -116,9 +113,10 @@
     return ref[start : start + SLICE, :].astype(F32) + ref[start + SLICE : start + 2 * SLICE, :].astype(F32)
 
 
-def chunk_body(features, out, sem):
-    me = place()
-    copy = pltpu.make_async_copy(features.at[at(chunk_of(me, me["x"]), PART), :], out, sem)
+def half_body(features, out, sem):
+    me = place()
+    half = chunk_of(me, me["x"]) & 1
+    copy = pltpu.make_async_copy(features.at[at(half, 2 * PART), :], out, sem)
     copy.start()
     copy.wait()
 
@@ -139,14 +137,10 @@
                 dense_t[k, at(slot & 3, TILE), at(slot >> 2, TILE)] = tile.T
 
 
-def pair_body(low, high, out):
-    out[0:PART, :] = low[...]
-    out[PART:, :] = high[...]
-
-
-def put_block(me, blocks, i, first, second):
-    for k, part in ((3, first[0:PART, :]), (0, first[PART:, :]), (2, second[0:PART, :]), (1, second[PART:, :])):
-        blocks[i, at(me["z"] ^ k, PART), :] = part
+def put_block(me, blocks, i, mine, other):
+    half = me["z"] & 1
+    blocks[i, at(half, 2 * PART), :] = mine[...]
+    blocks[i, at(1 - half, 2 * PART), :] = other[...]
 
 
 def forward_body(dense, b0, a0, b1, a1, b2, a2, total, blocks):
@@ -156,7 +150,7 @@
     total[...] = dot(dense[0], blocks[0]) + dot(dense[1], blocks[1]) + dot(dense[2], blocks[2])
 
 
-def forward_last_body(dense, b3, a3, most, to3, to2, to1, own, blocks, total):
+def forward_last_body(dense, b3, a3, most, to2, to3, to1, own, blocks, total):
     me = place()
     put_block(me, blocks, 0, a3, b3)
     total[...] = most[...] + dot(dense[3], blocks[0])
@@ -164,8 +158,8 @@
         to[...] = total[at(me["x"] ^ k, PART), :].astype(to.dtype)
 
 
-def sum_body(own, r3, r2, r1, cot, to_h):
-    total = own[...] + r1[...] + (r2[...].astype(F32) + r3[...])
+def sum_body(own, r3, r1, r2, cot, to_h):
+    total = own[...] + r1[...].astype(F32) + (r2[...].astype(F32) + r3[...].astype(F32))
     high, low = split(total)
     to_h[0:PART, :] = high
     to_h[PART : 2 * PART, :] = low
@@ -177,7 +171,7 @@
     return (parts[0] + parts[1]).astype(BF)
 
 
-def layer_body(mine, got, weight, to3, to2, to1, own, aggregate, share, grad_w):
+def layer_body(mine, got, weight, to2, to3, to1, own, aggregate, share, grad_w):
     me = place()
     agg = aggregate_of(mine, got)
     preact = dot(agg, weight[...])
@@ -200,7 +194,7 @@
     output[...] = (preact * jax.nn.sigmoid(preact)).astype(BF)
 
 
-def backward_body(dense_t, weight, m0, m3, m2, m1, share, to_c, grad_agg, grad_pre):
+def backward_body(dense_t, weight, m0, m2, m3, m1, share, to_c, grad_agg, grad_pre):
     me = place()
     for k, m in enumerate((m0, m1, m2, m3)):
         grad_pre[at(me["x"] ^ k, PART), :] = m[0:PART, :]
@@ -271,7 +265,7 @@
     put_split(message, PART, mine[...] + got[...])
 
 
-def finish_body(m0, m3, m2, m1, grad_features, grad_weight):
+def finish_body(m0, m2, m3, m1, grad_features, grad_weight):
     me = place()
     for k, message in enumerate((m0, m1, m2, m3)):
         grad_features[at(chunk_of(me, me["x"] ^ k), PART), :] = message[0:PART, :]
@@ -289,15 +283,13 @@
     to_z = ((PART + SLICE, WIDTH), BF)
     dense_shape = ((4, BLOCK, BLOCK), BF)
 
-    (chunk,) = call(chunk_body, [part], features, specs=[HBM], scratch=[pltpu.SemaphoreType.DMA])
-    chunk = send(chunk, TO_COLUMN)
+    (half,) = call(half_body, [two], features, specs=[HBM], scratch=[pltpu.SemaphoreType.DMA])
+    half = send(half, TO_COLUMN)
     dense, dense_t = call(
         dense_body, [dense_shape, dense_shape], tile_slots, tile_count, tile_values, specs=[SMEM, SMEM, VMEM]
     )
-    chunk, dense, dense_t = lax.optimization_barrier((chunk, dense, dense_t))
-    chunks = spread(chunk, FLIP_Z)
-    c0, c3, c2, c1 = chunks
-    mine = [call(pair_body, [two], c3, c0)[0], call(pair_body, [two], c2, c1)[0]]
+    half, dense, dense_t = lax.optimization_barrier((half, dense, dense_t))
+    mine = [half, send(half, FLIP_Z[0])]
     by_u = [send(value, FLIP_U) for value in mine]
     by_c = [send(value, FLIP_C) for value in mine]
     by_uc = [send(value, FLIP_C) for value in by_u]
@@ -305,17 +297,17 @@
     (most,) = call(
         forward_body, [block32], dense, *mine[::-1], *by_c[::-1], *by_u[::-1], scratch=[pltpu.VMEM((3, BLOCK, WIDTH), BF)]
     )
-    to3, to2, to1, own = call(
-        forward_last_body, [part32, part, part32, part32], dense, *by_uc[::-1], most, scratch=[pltpu.VMEM((1, BLOCK, WIDTH), BF), total]
-    )
-    got = [send(value, route) for value, route in zip((to3, to2, to1), FLIP_X[::-1])]
-    (mine,) = call(sum_body, [((2 * PART + SLICE, WIDTH), BF)], own, *got, cotangent)
+    *to, own = call(
+        forward_last_body, [part, part, part, part32], dense, *by_uc[::-1], most, scratch=[pltpu.VMEM((1, BLOCK, WIDTH), BF), total]
+    )
+    got = [send(value, route) for value, route in zip(to, FAR_X)]
+    (mine,) = call(sum_body, [((2 * PART + SLICE, WIDTH), BF)], own, got[1], got[2], got[0], cotangent)
     got = send(mine, FLIP_H)
     *to, own, aggregate, share = call(
         layer_body, [to_z, to_z, to_z, part, part, share32], mine, got, weight, scratch=[pltpu.VMEM((WIDTH, WIDTH), F32)]
     )
     (output,) = call(output_body, [((SLICE, WIDTH), BF)], aggregate, weight)
-    got = [send(value, route) for value, route in zip(to, FLIP_X[::-1])]
+    got = [send(value, route) for value, route in zip(to, FAR_X)]
     to_c, grad_agg = call(
         backward_body, [((BLOCK + SLICE, WIDTH), F32), block], dense_t, weight, own, *got, share,
         scratch=[pltpu.VMEM((BLOCK, WIDTH), BF)],
@@ -335,7 +327,7 @@
         after_v_body, [part, share32], to_v, send(to_v, FLIP_V), share, send(share, FLIP_Z[1])
     )
     (message,) = call(last_body, [two], send(piece, TO_ROW), share, send(share, FLIP_V))
-    grad_features, grad_weight = call(finish_body, [block, ((WIDTH, WIDTH), F32)], *spread(message, FLIP_X))
+    grad_features, grad_weight = call(finish_body, [block, ((WIDTH, WIDTH), F32)], message, *[send(message, route) for route in FAR_X])
     return output, grad_weight, grad_features
 
 

time: 108 us -> 107 us (level); the launches traced: 106 us -> 107 us
  waiting for transfers between devices: 50.8 us -> 53 us
  starting transfers between devices: 45.5 us -> 43.7 us
    ppermute x34 -> x32, waiting for transfers between devices: 50.8 us -> 53 us  [send(): return lax.ppermute(value, AXES, route)]
    ppermute x34 -> x32, starting transfers between devices: 45.5 us -> 43.7 us  [send(): return lax.ppermute(value, AXES, route)]
    pallas_call x21 -> x19, Pallas kernels: 5.99 us -> 6.04 us  [call(): pl.pallas_call(body, out_shape=[jax.ShapeDtypeStruct(shape, dtype) for sh...]
  transfers between devices with their start and end apart: 34 -> 32, of which waited for: 22 -> 22; matrix products, arithmetic and copies ran while one was open for 1% -> 1% of each run, Pallas kernels for 3% -> 3%
where the time goes in v8:
time: 107 us
  waiting for transfers between devices  53 us (50%)
  starting transfers between devices  43.7 us (41%)
  Pallas kernels  6.04 us (6%)
  local copies, waits for them, and re-layouts  3.32 us (3%)
    ppermute x32, waiting for transfers between devices, send(): return lax.ppermute(value, AXES, route)  53 us
    ppermute x32, starting transfers between devices, send(): return lax.ppermute(value, AXES, route)  43.7 us
    pallas_call x19, Pallas kernels, call(): pl.pallas_call(body, out_shape=[jax.ShapeDtypeStruct(shape, dtype) for sh...  6.04 us
    unnamed x11, local copies, waits for them, and re-layouts  3.32 us
  transfers between devices with their start and end apart: 32, of which 22 were waited for; matrix products, arithmetic and copies ran while one was open for 1% of the time, Pallas kernels for 3%

profile of v8, /device:TPU:32, one launch (start us, length us, event | category | flops | bytes accessed | tf_op | source)
XLA Modules:
  0.0 106.8 jit_solution(7296866745191706356)
XLA Ops:
  1.7 3.6 %collective-permute-start = (bf16[256,256]{1,0:T(8,128)(2,1)S(1)}, bf16[256,256]{1,0:T(8,128)(2,1)S(1)}, u32[]{:S(2)}, u32[]{:S(2)}) collective-permute-start(bf16[256,256]{1,0:T(8,128)(2,1)S(1)} %shard_map.85), channel_id=1, source_target_pairs={{1,0},{53,1},{65,2},{113,3},{129,4},{181,5},{195,6},{247,7},{9,8},... | collective-permute-start | bytes 393224 | tf_op jit(solution)/shard_map/ppermute | solution.py:61
  8.9 6.5 %collective-permute-done.a0 = bf16[256,256]{1,0:T(8,128)(2,1)S(1)} collective-permute-done((bf16[256,256]{1,0:T(8,128)(2,1)S(1)}, bf16[256,256]{1,0:T(8,128)(2,1)S(1)}, u32[]{:S(2)}, u32[]{:S(2)}) %collective-permute-start) | collective-permute-done | bytes 131104 | tf_op jit(solution)/shard_map/ppermute | solution.py:61
  16.6 5.8 %collective-permute-done.1.b0 = bf16[256,256]{1,0:T(8,128)(2,1)S(1)} collective-permute-done((bf16[256,256]{1,0:T(8,128)(2,1)S(1)}, bf16[256,256]{1,0:T(8,128)(2,1)S(1)}, u32[]{:S(2)}, u32[]{:S(2)}) %collective-permute-start.1) | collective-permute-done | bytes 131104 | tf_op jit(solution)/shard_map/ppermute | solution.py:61
  22.4 1.6 %collective-permute-start.2 = (bf16[256,256]{1,0:T(8,128)(2,1)S(1)}, bf16[256,256]{1,0:T(8,128)(2,1)S(1)}, u32[]{:S(2)}, u32[]{:S(2)}) collective-permute-start(bf16[256,256]{1,0:T(8,128)(2,1)S(1)} %collective-permute-done.1.b0), channel_id=1, source_target_pairs={{0,16},{1,17},{2,18},{3,19},{4,20},{5,21},{6,22},{7,23},{8,24},{9,... | collective-permute-start | bytes 393224 | tf_op jit(solution)/shard_map/ppermute | solution.py:61
  24.5 3.3 %collective-permute-done.2.b2 = bf16[256,256]{1,0:T(8,128)(2,1)S(1)} collective-permute-done((bf16[256,256]{1,0:T(8,128)(2,1)S(1)}, bf16[256,256]{1,0:T(8,128)(2,1)S(1)}, u32[]{:S(2)}, u32[]{:S(2)}) %collective-permute-start.2) | collective-permute-done | bytes 131104 | tf_op jit(solution)/shard_map/ppermute | solution.py:61
  30.4 4.2 %collective-permute-start.8 = (bf16[128,256]{1,0:T(8,128)(2,1)S(1)}, bf16[128,256]{1,0:T(8,128)(2,1)S(1)}, u32[]{:S(2)}, u32[]{:S(2)}) collective-permute-start(bf16[128,256]{1,0:T(8,128)(2,1)S(1)} %get-tuple-element.41), channel_id=1, source_target_pairs={{0,6},{1,7},{2,4},{3,5},{4,2},{5,3},{6,0},{7,1},{8,14},{9,15},{10,... | collective-permute-start | bytes 196616 | tf_op jit(solution)/shard_map/ppermute | solution.py:61
  35.4 2.3 %collective-permute-done.8.r3 = bf16[128,256]{1,0:T(8,128)(2,1)S(1)} collective-permute-done((bf16[128,256]{1,0:T(8,128)(2,1)S(1)}, bf16[128,256]{1,0:T(8,128)(2,1)S(1)}, u32[]{:S(2)}, u32[]{:S(2)}) %collective-permute-start.8) | collective-permute-done | bytes 65568 | tf_op jit(solution)/shard_map/ppermute | solution.py:61
  39.0 3.3 %collective-permute-start.11 = (bf16[320,256]{1,0:T(8,128)(2,1)S(1)}, bf16[320,256]{1,0:T(8,128)(2,1)S(1)}, u32[]{:S(2)}, u32[]{:S(2)}) collective-permute-start(bf16[320,256]{1,0:T(8,128)(2,1)S(1)} %shard_map.89.mine), channel_id=1, source_target_pairs={{0,1},{1,0},{2,3},{3,2},{4,5},{5,4},{6,7},{7,6},{8,9},{9,8},{10,11... | collective-permute-start | bytes 491528 | tf_op jit(solution)/shard_map/ppermute | solution.py:61
  42.4 9.6 %collective-permute-done.11.got = bf16[320,256]{1,0:T(8,128)(2,1)S(1)} collective-permute-done((bf16[320,256]{1,0:T(8,128)(2,1)S(1)}, bf16[320,256]{1,0:T(8,128)(2,1)S(1)}, u32[]{:S(2)}, u32[]{:S(2)}) %collective-permute-start.11) | collective-permute-done | bytes 163872 | tf_op jit(solution)/shard_map/ppermute | solution.py:61
  52.4 1.7 %collective-permute-start.12 = (bf16[192,256]{1,0:T(8,128)(2,1)S(1)}, bf16[192,256]{1,0:T(8,128)(2,1)S(1)}, u32[]{:S(2)}, u32[]{:S(2)}) collective-permute-start(bf16[192,256]{1,0:T(8,128)(2,1)S(1)} %get-tuple-element.47), channel_id=1, source_target_pairs={{0,4},{1,5},{2,6},{3,7},{4,0},{5,1},{6,2},{7,3},{8,12},{9,13},{10,... | collective-permute-start | bytes 294920 | tf_op jit(solution)/shard_map/ppermute | solution.py:61
  56.0 3.0 %collective-permute-done.12.m2 = bf16[192,256]{1,0:T(8,128)(2,1)S(1)} collective-permute-done((bf16[192,256]{1,0:T(8,128)(2,1)S(1)}, bf16[192,256]{1,0:T(8,128)(2,1)S(1)}, u32[]{:S(2)}, u32[]{:S(2)}) %collective-permute-start.12) | collective-permute-done | bytes 98336 | tf_op jit(solution)/shard_map/ppermute | solution.py:61
  63.1 1.6 %collective-permute-start.19 = (bf16[192,256]{1,0:T(8,128)(2,1)S(1)}, bf16[192,256]{1,0:T(8,128)(2,1)S(1)}, u32[]{:S(2)}, u32[]{:S(2)}) collective-permute-start(bf16[192,256]{1,0:T(8,128)(2,1)S(1)} %get-tuple-element.58), channel_id=1, source_target_pairs={{0,16},{1,17},{2,18},{3,19},{4,20},{5,21},{6,22},{7,23},{8,24},{9,... | collective-permute-start | bytes 294920 | tf_op jit(solution)/shard_map/ppermute | solution.py:61
  65.2 1.5 %collective-permute-start.17 = (bf16[128,256]{1,0:T(8,128)(2,1)S(1)}, bf16[128,256]{1,0:T(8,128)(2,1)S(1)}, u32[]{:S(2)}, u32[]{:S(2)}) collective-permute-start(bf16[128,256]{1,0:T(8,128)(2,1)S(1)} %get-tuple-element.55), channel_id=1, source_target_pairs={{0,16},{1,17},{2,18},{3,19},{4,20},{5,21},{6,22},{7,23},{8,24},{9,... | collective-permute-start | bytes 196616 | tf_op jit(solution)/shard_map/ppermute | solution.py:61
  67.3 1.5 %collective-permute-done.19.earlier.got = bf16[192,256]{1,0:T(8,128)(2,1)S(1)} collective-permute-done((bf16[192,256]{1,0:T(8,128)(2,1)S(1)}, bf16[192,256]{1,0:T(8,128)(2,1)S(1)}, u32[]{:S(2)}, u32[]{:S(2)}) %collective-permute-start.19) | collective-permute-done | bytes 98336 | tf_op jit(solution)/shard_map/ppermute | solution.py:61
  70.2 1.7 %collective-permute-start.22 = (bf16[128,256]{1,0:T(8,128)(2,1)S(1)}, bf16[128,256]{1,0:T(8,128)(2,1)S(1)}, u32[]{:S(2)}, u32[]{:S(2)}) collective-permute-start(bf16[128,256]{1,0:T(8,128)(2,1)S(1)} %shard_map.98), channel_id=1, source_target_pairs={{0,128},{1,129},{2,130},{3,131},{4,132},{5,133},{6,134},{7,135},{8... | collective-permute-start | bytes 196616 | tf_op jit(solution)/shard_map/ppermute | solution.py:61
  74.3 1.5 %collective-permute-done.23.r3 = bf16[128,256]{1,0:T(8,128)(2,1)S(1)} collective-permute-done((bf16[128,256]{1,0:T(8,128)(2,1)S(1)}, bf16[128,256]{1,0:T(8,128)(2,1)S(1)}, u32[]{:S(2)}, u32[]{:S(2)}) %collective-permute-start.23) | collective-permute-done | bytes 65568 | tf_op jit(solution)/shard_map/ppermute | solution.py:61
  77.8 3.5 %collective-permute-start.25 = (f32[128,256]{1,0:T(8,128)S(1)}, f32[128,256]{1,0:T(8,128)S(1)}, u32[]{:S(2)}, u32[]{:S(2)}) collective-permute-start(f32[128,256]{1,0:T(8,128)S(1)} %get-tuple-element.63.one), channel_id=1, source_target_pairs={{0,48},{1,49},{2,50},{3,51},{4,52},{5,53},{6,54},{7,55},{8,56},{9,... | collective-permute-start | bytes 393224 | tf_op jit(solution)/shard_map/ppermute | solution.py:61
  82.5 4.0 %collective-permute-done.26.got = f32[64,256]{1,0:T(8,128)S(1)} collective-permute-done((f32[64,256]{1,0:T(8,128)S(1)}, f32[64,256]{1,0:T(8,128)S(1)}, u32[]{:S(2)}, u32[]{:S(2)}) %collective-permute-start.26) | collective-permute-done | bytes 65568 | tf_op jit(solution)/shard_map/ppermute | solution.py:61
  86.6 5.7 %collective-permute-start.27 = (bf16[128,256]{1,0:T(8,128)(2,1)S(1)}, bf16[128,256]{1,0:T(8,128)(2,1)S(1)}, u32[]{:S(2)}, u32[]{:S(2)}) collective-permute-start(bf16[128,256]{1,0:T(8,128)(2,1)S(1)} %get-tuple-element.65), channel_id=1, source_target_pairs={{0,1},{1,53},{2,65},{3,113},{4,129},{5,181},{6,195},{7,247},{8,9},... | collective-permute-start | bytes 196616 | tf_op jit(solution)/shard_map/ppermute | solution.py:61
  92.3 1.9 %collective-permute-done.27.piece = bf16[128,256]{1,0:T(8,128)(2,1)S(1)} collective-permute-done((bf16[128,256]{1,0:T(8,128)(2,1)S(1)}, bf16[128,256]{1,0:T(8,128)(2,1)S(1)}, u32[]{:S(2)}, u32[]{:S(2)}) %collective-permute-start.27) | collective-permute-done | bytes 65568 | tf_op jit(solution)/shard_map/ppermute | solution.py:61
  94.2 3.6 %collective-permute-done.28.got = f32[64,256]{1,0:T(8,128)S(1)} collective-permute-done((f32[64,256]{1,0:T(8,128)S(1)}, f32[64,256]{1,0:T(8,128)S(1)}, u32[]{:S(2)}, u32[]{:S(2)}) %collective-permute-start.28) | collective-permute-done | bytes 65568 | tf_op jit(solution)/shard_map/ppermute | solution.py:61
  97.8 1.5 %collective-permute-start.29 = (bf16[256,256]{1,0:T(8,128)(2,1)S(1)}, bf16[256,256]{1,0:T(8,128)(2,1)S(1)}, u32[]{:S(2)}, u32[]{:S(2)}) collective-permute-start(bf16[256,256]{1,0:T(8,128)(2,1)S(1)} %shard_map.102.m0), channel_id=1, source_target_pairs={{0,4},{1,5},{2,6},{3,7},{4,0},{5,1},{6,2},{7,3},{8,12},{9,13},{10,... | collective-permute-start | bytes 393224 | tf_op jit(solution)/shard_map/ppermute | solution.py:61
  99.3 1.7 %collective-permute-start.30 = (bf16[256,256]{1,0:T(8,128)(2,1)S(1)}, bf16[256,256]{1,0:T(8,128)(2,1)S(1)}, u32[]{:S(2)}, u32[]{:S(2)}) collective-permute-start(bf16[256,256]{1,0:T(8,128)(2,1)S(1)} %shard_map.102.m0), channel_id=1, source_target_pairs={{0,6},{1,7},{2,4},{3,5},{4,2},{5,3},{6,0},{7,1},{8,14},{9,15},{10,... | collective-permute-start | bytes 393224 | tf_op jit(solution)/shard_map/ppermute | solution.py:61
  102.2 2.2 %collective-permute-done.29.m2 = bf16[256,256]{1,0:T(8,128)(2,1)S(1)} collective-permute-done((bf16[256,256]{1,0:T(8,128)(2,1)S(1)}, bf16[256,256]{1,0:T(8,128)(2,1)S(1)}, u32[]{:S(2)}, u32[]{:S(2)}) %collective-permute-start.29) | collective-permute-done | bytes 131104 | tf_op jit(solution)/shard_map/ppermute | solution.py:61
  (70 shorter events, 29.1 us)
Async XLA Ops:
  1.7 13.7 %collective-permute-start = (bf16[256,256]{1,0:T(8,128)(2,1)S(1)}, bf16[256,256]{1,0:T(8,128)(2,1)S(1)}, u32[]{:S(2)}, u32[]{:S(2)}) collective-permute-start(bf16[256,256]{1,0:T(8,128)(2,1)S(1)} %shard_map.85), channel_id=1, source_target_pairs={{1,0},{53,1},{65,2},{113,3},{129,4},{181,5},{195,6},{247,7},{9,8},... | collective-permute-start | bytes 393224 | tf_op jit(solution)/shard_map/ppermute | solution.py:61
  15.5 6.9 %collective-permute-start.1 = (bf16[256,256]{1,0:T(8,128)(2,1)S(1)}, bf16[256,256]{1,0:T(8,128)(2,1)S(1)}, u32[]{:S(2)}, u32[]{:S(2)}) collective-permute-start(bf16[256,256]{1,0:T(8,128)(2,1)S(1)} %collective-permute-done.a0), channel_id=1, source_target_pairs={{0,64},{1,65},{2,66},{3,67},{4,68},{5,69},{6,70},{7,71},{8,72},{9,... | collective-permute-start | bytes 393224 | tf_op jit(solution)/shard_map/ppermute | solution.py:61
  15.5 9.0 %collective-permute-start.4 = (bf16[256,256]{1,0:T(8,128)(2,1)S(1)}, bf16[256,256]{1,0:T(8,128)(2,1)S(1)}, u32[]{:S(2)}, u32[]{:S(2)}) collective-permute-start(bf16[256,256]{1,0:T(8,128)(2,1)S(1)} %collective-permute-done.a0), channel_id=1, source_target_pairs={{0,16},{1,17},{2,18},{3,19},{4,20},{5,21},{6,22},{7,23},{8,24},{9,... | collective-permute-start | bytes 393224 | tf_op jit(solution)/shard_map/ppermute | solution.py:61
  22.4 5.4 %collective-permute-start.2 = (bf16[256,256]{1,0:T(8,128)(2,1)S(1)}, bf16[256,256]{1,0:T(8,128)(2,1)S(1)}, u32[]{:S(2)}, u32[]{:S(2)}) collective-permute-start(bf16[256,256]{1,0:T(8,128)(2,1)S(1)} %collective-permute-done.1.b0), channel_id=1, source_target_pairs={{0,16},{1,17},{2,18},{3,19},{4,20},{5,21},{6,22},{7,23},{8,24},{9,... | collective-permute-start | bytes 393224 | tf_op jit(solution)/shard_map/ppermute | solution.py:61
  29.5 5.9 %collective-permute-start.10 = (bf16[128,256]{1,0:T(8,128)(2,1)S(1)}, bf16[128,256]{1,0:T(8,128)(2,1)S(1)}, u32[]{:S(2)}, u32[]{:S(2)}) collective-permute-start(bf16[128,256]{1,0:T(8,128)(2,1)S(1)} %get-tuple-element.43), channel_id=1, source_target_pairs={{0,4},{1,5},{2,6},{3,7},{4,0},{5,1},{6,2},{7,3},{8,12},{9,13},{10,... | collective-permute-start | bytes 196616 | tf_op jit(solution)/shard_map/ppermute | solution.py:61
  30.4 7.3 %collective-permute-start.8 = (bf16[128,256]{1,0:T(8,128)(2,1)S(1)}, bf16[128,256]{1,0:T(8,128)(2,1)S(1)}, u32[]{:S(2)}, u32[]{:S(2)}) collective-permute-start(bf16[128,256]{1,0:T(8,128)(2,1)S(1)} %get-tuple-element.41), channel_id=1, source_target_pairs={{0,6},{1,7},{2,4},{3,5},{4,2},{5,3},{6,0},{7,1},{8,14},{9,15},{10,... | collective-permute-start | bytes 196616 | tf_op jit(solution)/shard_map/ppermute | solution.py:61
  39.0 13.0 %collective-permute-start.11 = (bf16[320,256]{1,0:T(8,128)(2,1)S(1)}, bf16[320,256]{1,0:T(8,128)(2,1)S(1)}, u32[]{:S(2)}, u32[]{:S(2)}) collective-permute-start(bf16[320,256]{1,0:T(8,128)(2,1)S(1)} %shard_map.89.mine), channel_id=1, source_target_pairs={{0,1},{1,0},{2,3},{3,2},{4,5},{5,4},{6,7},{7,6},{8,9},{9,8},{10,11... | collective-permute-start | bytes 491528 | tf_op jit(solution)/shard_map/ppermute | solution.py:61
  52.4 6.5 %collective-permute-start.12 = (bf16[192,256]{1,0:T(8,128)(2,1)S(1)}, bf16[192,256]{1,0:T(8,128)(2,1)S(1)}, u32[]{:S(2)}, u32[]{:S(2)}) collective-permute-start(bf16[192,256]{1,0:T(8,128)(2,1)S(1)} %get-tuple-element.47), channel_id=1, source_target_pairs={{0,4},{1,5},{2,6},{3,7},{4,0},{5,1},{6,2},{7,3},{8,12},{9,13},{10,... | collective-permute-start | bytes 294920 | tf_op jit(solution)/shard_map/ppermute | solution.py:61
  54.1 6.2 %collective-permute-start.13 = (bf16[192,256]{1,0:T(8,128)(2,1)S(1)}, bf16[192,256]{1,0:T(8,128)(2,1)S(1)}, u32[]{:S(2)}, u32[]{:S(2)}) collective-permute-start(bf16[192,256]{1,0:T(8,128)(2,1)S(1)} %get-tuple-element.48), channel_id=1, source_target_pairs={{0,6},{1,7},{2,4},{3,5},{4,2},{5,3},{6,0},{7,1},{8,14},{9,15},{10,... | collective-permute-start | bytes 294920 | tf_op jit(solution)/shard_map/ppermute | solution.py:61
  54.8 5.5 %collective-permute-start.14 = (bf16[192,256]{1,0:T(8,128)(2,1)S(1)}, bf16[192,256]{1,0:T(8,128)(2,1)S(1)}, u32[]{:S(2)}, u32[]{:S(2)}) collective-permute-start(bf16[192,256]{1,0:T(8,128)(2,1)S(1)} %get-tuple-element.49), channel_id=1, source_target_pairs={{0,2},{1,3},{2,0},{3,1},{4,6},{5,7},{6,4},{7,5},{8,10},{9,11},{10,... | collective-permute-start | bytes 294920 | tf_op jit(solution)/shard_map/ppermute | solution.py:61
  61.4 5.8 %collective-permute-start.15 = (f32[512,256]{1,0:T(8,128)S(1)}, f32[512,256]{1,0:T(8,128)S(1)}, u32[]{:S(2)}, u32[]{:S(2)}) collective-permute-start(f32[512,256]{1,0:T(8,128)S(1)} %get-tuple-element.53), channel_id=1, source_target_pairs={{0,8},{1,9},{2,10},{3,11},{4,12},{5,13},{6,14},{7,15},{8,0},{9,1},... | collective-permute-start | bytes 1572872 | tf_op jit(solution)/shard_map/ppermute | solution.py:61
  63.1 5.7 %collective-permute-start.19 = (bf16[192,256]{1,0:T(8,128)(2,1)S(1)}, bf16[192,256]{1,0:T(8,128)(2,1)S(1)}, u32[]{:S(2)}, u32[]{:S(2)}) collective-permute-start(bf16[192,256]{1,0:T(8,128)(2,1)S(1)} %get-tuple-element.58), channel_id=1, source_target_pairs={{0,16},{1,17},{2,18},{3,19},{4,20},{5,21},{6,22},{7,23},{8,24},{9,... | collective-permute-start | bytes 294920 | tf_op jit(solution)/shard_map/ppermute | solution.py:61
  64.7 5.5 %collective-permute-start.21 = (bf16[128,256]{1,0:T(8,128)(2,1)S(1)}, bf16[128,256]{1,0:T(8,128)(2,1)S(1)}, u32[]{:S(2)}, u32[]{:S(2)}) collective-permute-start(bf16[128,256]{1,0:T(8,128)(2,1)S(1)} %get-tuple-element.61), channel_id=1, source_target_pairs={{0,16},{1,17},{2,18},{3,19},{4,20},{5,21},{6,22},{7,23},{8,24},{9,... | collective-permute-start | bytes 196616 | tf_op jit(solution)/shard_map/ppermute | solution.py:61
  65.2 6.7 %collective-permute-start.17 = (bf16[128,256]{1,0:T(8,128)(2,1)S(1)}, bf16[128,256]{1,0:T(8,128)(2,1)S(1)}, u32[]{:S(2)}, u32[]{:S(2)}) collective-permute-start(bf16[128,256]{1,0:T(8,128)(2,1)S(1)} %get-tuple-element.55), channel_id=1, source_target_pairs={{0,16},{1,17},{2,18},{3,19},{4,20},{5,21},{6,22},{7,23},{8,24},{9,... | collective-permute-start | bytes 196616 | tf_op jit(solution)/shard_map/ppermute | solution.py:61
  66.7 5.5 %collective-permute-start.18 = (bf16[128,256]{1,0:T(8,128)(2,1)S(1)}, bf16[128,256]{1,0:T(8,128)(2,1)S(1)}, u32[]{:S(2)}, u32[]{:S(2)}) collective-permute-start(bf16[128,256]{1,0:T(8,128)(2,1)S(1)} %get-tuple-element.56), channel_id=1, source_target_pairs={{0,16},{1,17},{2,18},{3,19},{4,20},{5,21},{6,22},{7,23},{8,24},{9,... | collective-permute-start | bytes 196616 | tf_op jit(solution)/shard_map/ppermute | solution.py:61
  68.8 7.0 %collective-permute-start.23 = (bf16[128,256]{1,0:T(8,128)(2,1)S(1)}, bf16[128,256]{1,0:T(8,128)(2,1)S(1)}, u32[]{:S(2)}, u32[]{:S(2)}) collective-permute-start(bf16[128,256]{1,0:T(8,128)(2,1)S(1)} %shard_map.99), channel_id=1, source_target_pairs={{0,192},{1,193},{2,194},{3,195},{4,196},{5,197},{6,198},{7,199},{8... | collective-permute-start | bytes 196616 | tf_op jit(solution)/shard_map/ppermute | solution.py:61
  70.2 5.6 %collective-permute-start.22 = (bf16[128,256]{1,0:T(8,128)(2,1)S(1)}, bf16[128,256]{1,0:T(8,128)(2,1)S(1)}, u32[]{:S(2)}, u32[]{:S(2)}) collective-permute-start(bf16[128,256]{1,0:T(8,128)(2,1)S(1)} %shard_map.98), channel_id=1, source_target_pairs={{0,128},{1,129},{2,130},{3,131},{4,132},{5,133},{6,134},{7,135},{8... | collective-permute-start | bytes 196616 | tf_op jit(solution)/shard_map/ppermute | solution.py:61
  77.8 8.8 %collective-permute-start.25 = (f32[128,256]{1,0:T(8,128)S(1)}, f32[128,256]{1,0:T(8,128)S(1)}, u32[]{:S(2)}, u32[]{:S(2)}) collective-permute-start(f32[128,256]{1,0:T(8,128)S(1)} %get-tuple-element.63.one), channel_id=1, source_target_pairs={{0,48},{1,49},{2,50},{3,51},{4,52},{5,53},{6,54},{7,55},{8,56},{9,... | collective-permute-start | bytes 393224 | tf_op jit(solution)/shard_map/ppermute | solution.py:61
  81.3 5.3 %collective-permute-start.26 = (f32[64,256]{1,0:T(8,128)S(1)}, f32[64,256]{1,0:T(8,128)S(1)}, u32[]{:S(2)}, u32[]{:S(2)}) collective-permute-start(f32[64,256]{1,0:T(8,128)S(1)} %get-tuple-element.64.mine), channel_id=1, source_target_pairs={{0,128},{1,129},{2,130},{3,131},{4,132},{5,133},{6,134},{7,135},{8... | collective-permute-start | bytes 196616 | tf_op jit(solution)/shard_map/ppermute | solution.py:61
  86.6 7.6 %collective-permute-start.27 = (bf16[128,256]{1,0:T(8,128)(2,1)S(1)}, bf16[128,256]{1,0:T(8,128)(2,1)S(1)}, u32[]{:S(2)}, u32[]{:S(2)}) collective-permute-start(bf16[128,256]{1,0:T(8,128)(2,1)S(1)} %get-tuple-element.65), channel_id=1, source_target_pairs={{0,1},{1,53},{2,65},{3,113},{4,129},{5,181},{6,195},{7,247},{8,9},... | collective-permute-start | bytes 196616 | tf_op jit(solution)/shard_map/ppermute | solution.py:61
  92.3 5.5 %collective-permute-start.28 = (f32[64,256]{1,0:T(8,128)S(1)}, f32[64,256]{1,0:T(8,128)S(1)}, u32[]{:S(2)}, u32[]{:S(2)}) collective-permute-start(f32[64,256]{1,0:T(8,128)S(1)} %get-tuple-element.66.mine), channel_id=1, source_target_pairs={{0,48},{1,49},{2,50},{3,51},{4,52},{5,53},{6,54},{7,55},{8,56},{9,... | collective-permute-start | bytes 196616 | tf_op jit(solution)/shard_map/ppermute | solution.py:61
  97.8 6.6 %collective-permute-start.29 = (bf16[256,256]{1,0:T(8,128)(2,1)S(1)}, bf16[256,256]{1,0:T(8,128)(2,1)S(1)}, u32[]{:S(2)}, u32[]{:S(2)}) collective-permute-start(bf16[256,256]{1,0:T(8,128)(2,1)S(1)} %shard_map.102.m0), channel_id=1, source_target_pairs={{0,4},{1,5},{2,6},{3,7},{4,0},{5,1},{6,2},{7,3},{8,12},{9,13},{10,... | collective-permute-start | bytes 393224 | tf_op jit(solution)/shard_map/ppermute | solution.py:61
  99.3 6.5 %collective-permute-start.30 = (bf16[256,256]{1,0:T(8,128)(2,1)S(1)}, bf16[256,256]{1,0:T(8,128)(2,1)S(1)}, u32[]{:S(2)}, u32[]{:S(2)}) collective-permute-start(bf16[256,256]{1,0:T(8,128)(2,1)S(1)} %shard_map.102.m0), channel_id=1, source_target_pairs={{0,6},{1,7},{2,4},{3,5},{4,2},{5,3},{6,0},{7,1},{8,14},{9,15},{10,... | collective-permute-start | bytes 393224 | tf_op jit(solution)/shard_map/ppermute | solution.py:61
  101.0 5.0 %collective-permute-start.31 = (bf16[256,256]{1,0:T(8,128)(2,1)S(1)}, bf16[256,256]{1,0:T(8,128)(2,1)S(1)}, u32[]{:S(2)}, u32[]{:S(2)}) collective-permute-start(bf16[256,256]{1,0:T(8,128)(2,1)S(1)} %shard_map.102.m0), channel_id=1, source_target_pairs={{0,2},{1,3},{2,0},{3,1},{4,6},{5,7},{6,4},{7,5},{8,10},{9,11},{10,... | collective-permute-start | bytes 393224 | tf_op jit(solution)/shard_map/ppermute | solution.py:61
  (13 other events, 65.5 us)

commit v9 on v8

--- a/solution.py
+++ b/solution.py
@@ -46,7 +46,34 @@
 FAR_X = (FLIP_X[1], FLIP_X[2], FLIP_X[0])
 ROUTE = (((2, 1, 3, 0), (0, 3, 2, 1), (2, 1, 0, 3), (3, 0, 2, 1)), ((0, 1, 3, 2), (0, 1, 2, 3), (0, 1, 2, 3), (1, 0, 2, 3)))
 TO_ROW = pairs(lambda z, y, c, x, h: (x, Y_OF[u_of(y), h], c, ROUTE[v_of(y) == h][x][z], 1 - v_of(y)))
-TO_COLUMN = [(there, here) for here, there in TO_ROW]
+SERVED = (
+    (6, 0, 4, 2, 5, 3, 1, 7), (2, 4, 0, 6, 5, 1, 3, 7), (2, 0, 4, 6, 5, 1, 3, 7), (6, 4, 0, 2, 7, 3, 1, 5),
+    (5, 3, 1, 7, 0, 4, 6, 2), (5, 7, 3, 1, 6, 2, 4, 0), (1, 7, 3, 5, 0, 4, 6, 2), (5, 3, 7, 1, 2, 6, 4, 0),
+    (5, 3, 6, 4, 0, 2, 7, 1), (5, 3, 0, 2, 4, 6, 7, 1), (2, 3, 4, 0, 1, 6, 7, 5), (5, 3, 0, 6, 2, 4, 7, 1),
+    (1, 5, 3, 7, 2, 4, 0, 6), (2, 4, 7, 3, 5, 1, 0, 6), (2, 4, 7, 5, 1, 3, 0, 6), (2, 5, 1, 3, 7, 4, 0, 6),
+    (1, 7, 4, 6, 2, 0, 3, 5), (1, 7, 2, 0, 6, 4, 3, 5), (1, 7, 0, 2, 4, 6, 3, 5), (1, 7, 4, 5, 6, 2, 3, 0),
+    (2, 0, 4, 6, 5, 1, 7, 3), (6, 0, 7, 5, 1, 3, 4, 2), (6, 0, 4, 7, 5, 1, 3, 2), (6, 0, 3, 1, 5, 7, 4, 2),
+    (7, 1, 3, 5, 6, 4, 0, 2), (5, 3, 7, 1, 0, 6, 4, 2), (5, 3, 7, 1, 6, 0, 4, 2), (7, 1, 3, 5, 2, 4, 0, 6),
+    (6, 4, 0, 2, 3, 1, 7, 5), (0, 6, 4, 2, 7, 5, 3, 1), (2, 4, 0, 6, 3, 5, 7, 1), (0, 6, 4, 2, 7, 1, 3, 5),
+)
+
+
+def served(z, y, c, x, h):
+    replica = SERVED[x * 8 + h * 4 + u_of(y) * 2 + c][z * 2 + v_of(y)]
+    return x, Y_OF[u_of(y), h], c, replica >> 1, replica & 1
+
+
+TO_COLUMN = [(there, here) for here, there in pairs(served)]
+
+
+def half_words():
+    words = [0] * 8
+    for there, here in TO_COLUMN:
+        words[there >> 5] |= (here >> 6 & 1) << (there & 31)
+    return [word - (1 << 32) if word >> 31 else word for word in words]
+
+
+HALVES = half_words()
 
 
 def chunk_table(same):
@@ -114,8 +141,11 @@
 
 
 def half_body(features, out, sem):
-    me = place()
-    half = chunk_of(me, me["x"]) & 1
+    device = lax.axis_index("rows") * 8 + lax.axis_index("rep")
+    word = jnp.int32(0)
+    for i, value in enumerate(HALVES):
+        word = jnp.where(device >> 5 == i, jnp.int32(value), word)
+    half = (word >> (device & 31)) & 1
     copy = pltpu.make_async_copy(features.at[at(half, 2 * PART), :], out, sem)
     copy.start()
     copy.wait()

time: 107 us -> 104 us (0.972)
  waiting for transfers between devices: 53 us -> 44 us
  starting transfers between devices: 43.7 us -> 49.5 us
    ppermute x32, waiting for transfers between devices: 53 us -> 44 us  [send(): return lax.ppermute(value, AXES, route)]
    ppermute x32, starting transfers between devices: 43.7 us -> 49.5 us  [send(): return lax.ppermute(value, AXES, route)]
  transfers between devices with their start and end apart: 32 -> 32, of which waited for: 22 -> 23; matrix products, arithmetic and copies ran while one was open for 1% -> 1% of each run, Pallas kernels for 3% -> 3%
where the time goes in v9:
time: 104 us
  starting transfers between devices  49.5 us (48%)
  waiting for transfers between devices  44 us (42%)
  Pallas kernels  5.97 us (6%)
  local copies, waits for them, and re-layouts  3.33 us (3%)
    ppermute x32, starting transfers between devices, send(): return lax.ppermute(value, AXES, route)  49.5 us
    ppermute x32, waiting for transfers between devices, send(): return lax.ppermute(value, AXES, route)  44 us
    pallas_call x19, Pallas kernels, call(): pl.pallas_call(body, out_shape=[jax.ShapeDtypeStruct(shape, dtype) for sh...  5.97 us
    unnamed x11, local copies, waits for them, and re-layouts  3.33 us
  transfers between devices with their start and end apart: 32, of which 23 were waited for; matrix products, arithmetic and copies ran while one was open for 1% of the time, Pallas kernels for 3%

profile of v9, /device:TPU:32, one launch (start us, length us, event | category | flops | bytes accessed | tf_op | source)
XLA Modules:
  0.0 103.5 jit_solution(3773451918695987068)
XLA Ops:
  1.7 4.8 %collective-permute-start = (bf16[256,256]{1,0:T(8,128)(2,1)S(1)}, bf16[256,256]{1,0:T(8,128)(2,1)S(1)}, u32[]{:S(2)}, u32[]{:S(2)}) collective-permute-start(bf16[256,256]{1,0:T(8,128)(2,1)S(1)} %shard_map.85), channel_id=1, source_target_pairs={{6,0},{53,1},{69,2},{113,3},{129,4},{178,5},{199,6},{246,7},{10,8}... | collective-permute-start | bytes 393224 | tf_op jit(solution)/shard_map/ppermute | solution.py:88
  11.4 1.6 %collective-permute-start.1 = (bf16[256,256]{1,0:T(8,128)(2,1)S(1)}, bf16[256,256]{1,0:T(8,128)(2,1)S(1)}, u32[]{:S(2)}, u32[]{:S(2)}) collective-permute-start(bf16[256,256]{1,0:T(8,128)(2,1)S(1)} %collective-permute-done.a0), channel_id=1, source_target_pairs={{0,64},{1,65},{2,66},{3,67},{4,68},{5,69},{6,70},{7,71},{8,72},{9,... | collective-permute-start | bytes 393224 | tf_op jit(solution)/shard_map/ppermute | solution.py:88
  13.3 3.5 %collective-permute-done.1.b0 = bf16[256,256]{1,0:T(8,128)(2,1)S(1)} collective-permute-done((bf16[256,256]{1,0:T(8,128)(2,1)S(1)}, bf16[256,256]{1,0:T(8,128)(2,1)S(1)}, u32[]{:S(2)}, u32[]{:S(2)}) %collective-permute-start.1) | collective-permute-done | bytes 131104 | tf_op jit(solution)/shard_map/ppermute | solution.py:88
  16.8 1.8 %collective-permute-start.2 = (bf16[256,256]{1,0:T(8,128)(2,1)S(1)}, bf16[256,256]{1,0:T(8,128)(2,1)S(1)}, u32[]{:S(2)}, u32[]{:S(2)}) collective-permute-start(bf16[256,256]{1,0:T(8,128)(2,1)S(1)} %collective-permute-done.1.b0), channel_id=1, source_target_pairs={{0,16},{1,17},{2,18},{3,19},{4,20},{5,21},{6,22},{7,23},{8,24},{9,... | collective-permute-start | bytes 393224 | tf_op jit(solution)/shard_map/ppermute | solution.py:88
  19.1 2.7 %collective-permute-done.2.b2 = bf16[256,256]{1,0:T(8,128)(2,1)S(1)} collective-permute-done((bf16[256,256]{1,0:T(8,128)(2,1)S(1)}, bf16[256,256]{1,0:T(8,128)(2,1)S(1)}, u32[]{:S(2)}, u32[]{:S(2)}) %collective-permute-start.2) | collective-permute-done | bytes 131104 | tf_op jit(solution)/shard_map/ppermute | solution.py:88
  23.5 3.8 %collective-permute-start.10 = (bf16[128,256]{1,0:T(8,128)(2,1)S(1)}, bf16[128,256]{1,0:T(8,128)(2,1)S(1)}, u32[]{:S(2)}, u32[]{:S(2)}) collective-permute-start(bf16[128,256]{1,0:T(8,128)(2,1)S(1)} %get-tuple-element.43), channel_id=1, source_target_pairs={{0,4},{1,5},{2,6},{3,7},{4,0},{5,1},{6,2},{7,3},{8,12},{9,13},{10,... | collective-permute-start | bytes 196616 | tf_op jit(solution)/shard_map/ppermute | solution.py:88
  27.3 4.7 %collective-permute-start.8 = (bf16[128,256]{1,0:T(8,128)(2,1)S(1)}, bf16[128,256]{1,0:T(8,128)(2,1)S(1)}, u32[]{:S(2)}, u32[]{:S(2)}) collective-permute-start(bf16[128,256]{1,0:T(8,128)(2,1)S(1)} %get-tuple-element.41), channel_id=1, source_target_pairs={{0,6},{1,7},{2,4},{3,5},{4,2},{5,3},{6,0},{7,1},{8,14},{9,15},{10,... | collective-permute-start | bytes 196616 | tf_op jit(solution)/shard_map/ppermute | solution.py:88
  32.8 2.3 %collective-permute-done.8.r3 = bf16[128,256]{1,0:T(8,128)(2,1)S(1)} collective-permute-done((bf16[128,256]{1,0:T(8,128)(2,1)S(1)}, bf16[128,256]{1,0:T(8,128)(2,1)S(1)}, u32[]{:S(2)}, u32[]{:S(2)}) %collective-permute-start.8) | collective-permute-done | bytes 65568 | tf_op jit(solution)/shard_map/ppermute | solution.py:88
  36.5 8.0 %collective-permute-start.11 = (bf16[320,256]{1,0:T(8,128)(2,1)S(1)}, bf16[320,256]{1,0:T(8,128)(2,1)S(1)}, u32[]{:S(2)}, u32[]{:S(2)}) collective-permute-start(bf16[320,256]{1,0:T(8,128)(2,1)S(1)} %shard_map.89.mine), channel_id=1, source_target_pairs={{0,1},{1,0},{2,3},{3,2},{4,5},{5,4},{6,7},{7,6},{8,9},{9,8},{10,11... | collective-permute-start | bytes 491528 | tf_op jit(solution)/shard_map/ppermute | solution.py:88
  44.4 6.9 %collective-permute-done.11.got = bf16[320,256]{1,0:T(8,128)(2,1)S(1)} collective-permute-done((bf16[320,256]{1,0:T(8,128)(2,1)S(1)}, bf16[320,256]{1,0:T(8,128)(2,1)S(1)}, u32[]{:S(2)}, u32[]{:S(2)}) %collective-permute-start.11) | collective-permute-done | bytes 163872 | tf_op jit(solution)/shard_map/ppermute | solution.py:88
  51.8 2.1 %collective-permute-start.13 = (bf16[192,256]{1,0:T(8,128)(2,1)S(1)}, bf16[192,256]{1,0:T(8,128)(2,1)S(1)}, u32[]{:S(2)}, u32[]{:S(2)}) collective-permute-start(bf16[192,256]{1,0:T(8,128)(2,1)S(1)} %get-tuple-element.48), channel_id=1, source_target_pairs={{0,6},{1,7},{2,4},{3,5},{4,2},{5,3},{6,0},{7,1},{8,14},{9,15},{10,... | collective-permute-start | bytes 294920 | tf_op jit(solution)/shard_map/ppermute | solution.py:88
  55.3 3.7 %collective-permute-done.12.m2 = bf16[192,256]{1,0:T(8,128)(2,1)S(1)} collective-permute-done((bf16[192,256]{1,0:T(8,128)(2,1)S(1)}, bf16[192,256]{1,0:T(8,128)(2,1)S(1)}, u32[]{:S(2)}, u32[]{:S(2)}) %collective-permute-start.12) | collective-permute-done | bytes 98336 | tf_op jit(solution)/shard_map/ppermute | solution.py:88
  63.3 1.4 %collective-permute-start.21 = (bf16[128,256]{1,0:T(8,128)(2,1)S(1)}, bf16[128,256]{1,0:T(8,128)(2,1)S(1)}, u32[]{:S(2)}, u32[]{:S(2)}) collective-permute-start(bf16[128,256]{1,0:T(8,128)(2,1)S(1)} %get-tuple-element.61), channel_id=1, source_target_pairs={{0,16},{1,17},{2,18},{3,19},{4,20},{5,21},{6,22},{7,23},{8,24},{9,... | collective-permute-start | bytes 196616 | tf_op jit(solution)/shard_map/ppermute | solution.py:88
  65.3 1.4 %collective-permute-start.18 = (bf16[128,256]{1,0:T(8,128)(2,1)S(1)}, bf16[128,256]{1,0:T(8,128)(2,1)S(1)}, u32[]{:S(2)}, u32[]{:S(2)}) collective-permute-start(bf16[128,256]{1,0:T(8,128)(2,1)S(1)} %get-tuple-element.56), channel_id=1, source_target_pairs={{0,16},{1,17},{2,18},{3,19},{4,20},{5,21},{6,22},{7,23},{8,24},{9,... | collective-permute-start | bytes 196616 | tf_op jit(solution)/shard_map/ppermute | solution.py:88
  66.8 1.5 %collective-permute-done.19.earlier.got = bf16[192,256]{1,0:T(8,128)(2,1)S(1)} collective-permute-done((bf16[192,256]{1,0:T(8,128)(2,1)S(1)}, bf16[192,256]{1,0:T(8,128)(2,1)S(1)}, u32[]{:S(2)}, u32[]{:S(2)}) %collective-permute-start.19) | collective-permute-done | bytes 98336 | tf_op jit(solution)/shard_map/ppermute | solution.py:88
  72.1 1.7 %collective-permute-start.24 = (f32[64,256]{1,0:T(8,128)S(1)}, f32[64,256]{1,0:T(8,128)S(1)}, u32[]{:S(2)}, u32[]{:S(2)}) collective-permute-start(f32[64,256]{1,0:T(8,128)S(1)} %get-tuple-element.62.mine), channel_id=1, source_target_pairs={{0,64},{1,65},{2,66},{3,67},{4,68},{5,69},{6,70},{7,71},{8,72},{9,... | collective-permute-start | bytes 196616 | tf_op jit(solution)/shard_map/ppermute | solution.py:88
  77.1 2.0 %collective-permute-start.25 = (f32[128,256]{1,0:T(8,128)S(1)}, f32[128,256]{1,0:T(8,128)S(1)}, u32[]{:S(2)}, u32[]{:S(2)}) collective-permute-start(f32[128,256]{1,0:T(8,128)S(1)} %get-tuple-element.63.one), channel_id=1, source_target_pairs={{0,48},{1,49},{2,50},{3,51},{4,52},{5,53},{6,54},{7,55},{8,56},{9,... | collective-permute-start | bytes 393224 | tf_op jit(solution)/shard_map/ppermute | solution.py:88
  79.1 1.5 %collective-permute-start.26 = (f32[64,256]{1,0:T(8,128)S(1)}, f32[64,256]{1,0:T(8,128)S(1)}, u32[]{:S(2)}, u32[]{:S(2)}) collective-permute-start(f32[64,256]{1,0:T(8,128)S(1)} %get-tuple-element.64.mine), channel_id=1, source_target_pairs={{0,128},{1,129},{2,130},{3,131},{4,132},{5,133},{6,134},{7,135},{8... | collective-permute-start | bytes 196616 | tf_op jit(solution)/shard_map/ppermute | solution.py:88
  80.6 3.8 %collective-permute-done.26.got = f32[64,256]{1,0:T(8,128)S(1)} collective-permute-done((f32[64,256]{1,0:T(8,128)S(1)}, f32[64,256]{1,0:T(8,128)S(1)}, u32[]{:S(2)}, u32[]{:S(2)}) %collective-permute-start.26) | collective-permute-done | bytes 65568 | tf_op jit(solution)/shard_map/ppermute | solution.py:88
  84.4 4.8 %collective-permute-start.27 = (bf16[128,256]{1,0:T(8,128)(2,1)S(1)}, bf16[128,256]{1,0:T(8,128)(2,1)S(1)}, u32[]{:S(2)}, u32[]{:S(2)}) collective-permute-start(bf16[128,256]{1,0:T(8,128)(2,1)S(1)} %get-tuple-element.65), channel_id=1, source_target_pairs={{0,1},{1,53},{2,65},{3,113},{4,129},{5,181},{6,195},{7,247},{8,9},... | collective-permute-start | bytes 196616 | tf_op jit(solution)/shard_map/ppermute | solution.py:88
  89.2 2.6 %collective-permute-done.27.piece = bf16[128,256]{1,0:T(8,128)(2,1)S(1)} collective-permute-done((bf16[128,256]{1,0:T(8,128)(2,1)S(1)}, bf16[128,256]{1,0:T(8,128)(2,1)S(1)}, u32[]{:S(2)}, u32[]{:S(2)}) %collective-permute-start.27) | collective-permute-done | bytes 65568 | tf_op jit(solution)/shard_map/ppermute | solution.py:88
  91.8 2.9 %collective-permute-done.28.got = f32[64,256]{1,0:T(8,128)S(1)} collective-permute-done((f32[64,256]{1,0:T(8,128)S(1)}, f32[64,256]{1,0:T(8,128)S(1)}, u32[]{:S(2)}, u32[]{:S(2)}) %collective-permute-start.28) | collective-permute-done | bytes 65568 | tf_op jit(solution)/shard_map/ppermute | solution.py:88
  95.8 1.5 %collective-permute-start.30 = (bf16[256,256]{1,0:T(8,128)(2,1)S(1)}, bf16[256,256]{1,0:T(8,128)(2,1)S(1)}, u32[]{:S(2)}, u32[]{:S(2)}) collective-permute-start(bf16[256,256]{1,0:T(8,128)(2,1)S(1)} %shard_map.102.m0), channel_id=1, source_target_pairs={{0,6},{1,7},{2,4},{3,5},{4,2},{5,3},{6,0},{7,1},{8,14},{9,15},{10,... | collective-permute-start | bytes 393224 | tf_op jit(solution)/shard_map/ppermute | solution.py:88
  99.1 2.3 %collective-permute-done.29.m2 = bf16[256,256]{1,0:T(8,128)(2,1)S(1)} collective-permute-done((bf16[256,256]{1,0:T(8,128)(2,1)S(1)}, bf16[256,256]{1,0:T(8,128)(2,1)S(1)}, u32[]{:S(2)}, u32[]{:S(2)}) %collective-permute-start.29) | collective-permute-done | bytes 131104 | tf_op jit(solution)/shard_map/ppermute | solution.py:88
  (70 shorter events, 29.5 us)
Async XLA Ops:
  1.7 9.6 %collective-permute-start = (bf16[256,256]{1,0:T(8,128)(2,1)S(1)}, bf16[256,256]{1,0:T(8,128)(2,1)S(1)}, u32[]{:S(2)}, u32[]{:S(2)}) collective-permute-start(bf16[256,256]{1,0:T(8,128)(2,1)S(1)} %shard_map.85), channel_id=1, source_target_pairs={{6,0},{53,1},{69,2},{113,3},{129,4},{178,5},{199,6},{246,7},{10,8}... | collective-permute-start | bytes 393224 | tf_op jit(solution)/shard_map/ppermute | solution.py:88
  11.4 5.4 %collective-permute-start.1 = (bf16[256,256]{1,0:T(8,128)(2,1)S(1)}, bf16[256,256]{1,0:T(8,128)(2,1)S(1)}, u32[]{:S(2)}, u32[]{:S(2)}) collective-permute-start(bf16[256,256]{1,0:T(8,128)(2,1)S(1)} %collective-permute-done.a0), channel_id=1, source_target_pairs={{0,64},{1,65},{2,66},{3,67},{4,68},{5,69},{6,70},{7,71},{8,72},{9,... | collective-permute-start | bytes 393224 | tf_op jit(solution)/shard_map/ppermute | solution.py:88
  12.9 6.1 %collective-permute-start.4 = (bf16[256,256]{1,0:T(8,128)(2,1)S(1)}, bf16[256,256]{1,0:T(8,128)(2,1)S(1)}, u32[]{:S(2)}, u32[]{:S(2)}) collective-permute-start(bf16[256,256]{1,0:T(8,128)(2,1)S(1)} %collective-permute-done.a0), channel_id=1, source_target_pairs={{0,16},{1,17},{2,18},{3,19},{4,20},{5,21},{6,22},{7,23},{8,24},{9,... | collective-permute-start | bytes 393224 | tf_op jit(solution)/shard_map/ppermute | solution.py:88
  16.8 5.0 %collective-permute-start.2 = (bf16[256,256]{1,0:T(8,128)(2,1)S(1)}, bf16[256,256]{1,0:T(8,128)(2,1)S(1)}, u32[]{:S(2)}, u32[]{:S(2)}) collective-permute-start(bf16[256,256]{1,0:T(8,128)(2,1)S(1)} %collective-permute-done.1.b0), channel_id=1, source_target_pairs={{0,16},{1,17},{2,18},{3,19},{4,20},{5,21},{6,22},{7,23},{8,24},{9,... | collective-permute-start | bytes 393224 | tf_op jit(solution)/shard_map/ppermute | solution.py:88
  23.5 9.3 %collective-permute-start.10 = (bf16[128,256]{1,0:T(8,128)(2,1)S(1)}, bf16[128,256]{1,0:T(8,128)(2,1)S(1)}, u32[]{:S(2)}, u32[]{:S(2)}) collective-permute-start(bf16[128,256]{1,0:T(8,128)(2,1)S(1)} %get-tuple-element.43), channel_id=1, source_target_pairs={{0,4},{1,5},{2,6},{3,7},{4,0},{5,1},{6,2},{7,3},{8,12},{9,13},{10,... | collective-permute-start | bytes 196616 | tf_op jit(solution)/shard_map/ppermute | solution.py:88
  27.3 7.8 %collective-permute-start.8 = (bf16[128,256]{1,0:T(8,128)(2,1)S(1)}, bf16[128,256]{1,0:T(8,128)(2,1)S(1)}, u32[]{:S(2)}, u32[]{:S(2)}) collective-permute-start(bf16[128,256]{1,0:T(8,128)(2,1)S(1)} %get-tuple-element.41), channel_id=1, source_target_pairs={{0,6},{1,7},{2,4},{3,5},{4,2},{5,3},{6,0},{7,1},{8,14},{9,15},{10,... | collective-permute-start | bytes 196616 | tf_op jit(solution)/shard_map/ppermute | solution.py:88
  36.5 14.8 %collective-permute-start.11 = (bf16[320,256]{1,0:T(8,128)(2,1)S(1)}, bf16[320,256]{1,0:T(8,128)(2,1)S(1)}, u32[]{:S(2)}, u32[]{:S(2)}) collective-permute-start(bf16[320,256]{1,0:T(8,128)(2,1)S(1)} %shard_map.89.mine), channel_id=1, source_target_pairs={{0,1},{1,0},{2,3},{3,2},{4,5},{5,4},{6,7},{7,6},{8,9},{9,8},{10,11... | collective-permute-start | bytes 491528 | tf_op jit(solution)/shard_map/ppermute | solution.py:88
  51.7 7.3 %collective-permute-start.12 = (bf16[192,256]{1,0:T(8,128)(2,1)S(1)}, bf16[192,256]{1,0:T(8,128)(2,1)S(1)}, u32[]{:S(2)}, u32[]{:S(2)}) collective-permute-start(bf16[192,256]{1,0:T(8,128)(2,1)S(1)} %get-tuple-element.47), channel_id=1, source_target_pairs={{0,4},{1,5},{2,6},{3,7},{4,0},{5,1},{6,2},{7,3},{8,12},{9,13},{10,... | collective-permute-start | bytes 294920 | tf_op jit(solution)/shard_map/ppermute | solution.py:88
  51.8 8.0 %collective-permute-start.13 = (bf16[192,256]{1,0:T(8,128)(2,1)S(1)}, bf16[192,256]{1,0:T(8,128)(2,1)S(1)}, u32[]{:S(2)}, u32[]{:S(2)}) collective-permute-start(bf16[192,256]{1,0:T(8,128)(2,1)S(1)} %get-tuple-element.48), channel_id=1, source_target_pairs={{0,6},{1,7},{2,4},{3,5},{4,2},{5,3},{6,0},{7,1},{8,14},{9,15},{10,... | collective-permute-start | bytes 294920 | tf_op jit(solution)/shard_map/ppermute | solution.py:88
  54.0 5.9 %collective-permute-start.14 = (bf16[192,256]{1,0:T(8,128)(2,1)S(1)}, bf16[192,256]{1,0:T(8,128)(2,1)S(1)}, u32[]{:S(2)}, u32[]{:S(2)}) collective-permute-start(bf16[192,256]{1,0:T(8,128)(2,1)S(1)} %get-tuple-element.49), channel_id=1, source_target_pairs={{0,2},{1,3},{2,0},{3,1},{4,6},{5,7},{6,4},{7,5},{8,10},{9,11},{10,... | collective-permute-start | bytes 294920 | tf_op jit(solution)/shard_map/ppermute | solution.py:88
  61.0 5.8 %collective-permute-start.15 = (f32[512,256]{1,0:T(8,128)S(1)}, f32[512,256]{1,0:T(8,128)S(1)}, u32[]{:S(2)}, u32[]{:S(2)}) collective-permute-start(f32[512,256]{1,0:T(8,128)S(1)} %get-tuple-element.53), channel_id=1, source_target_pairs={{0,8},{1,9},{2,10},{3,11},{4,12},{5,13},{6,14},{7,15},{8,0},{9,1},... | collective-permute-start | bytes 1572872 | tf_op jit(solution)/shard_map/ppermute | solution.py:88
  62.6 5.7 %collective-permute-start.19 = (bf16[192,256]{1,0:T(8,128)(2,1)S(1)}, bf16[192,256]{1,0:T(8,128)(2,1)S(1)}, u32[]{:S(2)}, u32[]{:S(2)}) collective-permute-start(bf16[192,256]{1,0:T(8,128)(2,1)S(1)} %get-tuple-element.58), channel_id=1, source_target_pairs={{0,16},{1,17},{2,18},{3,19},{4,20},{5,21},{6,22},{7,23},{8,24},{9,... | collective-permute-start | bytes 294920 | tf_op jit(solution)/shard_map/ppermute | solution.py:88
  63.3 6.4 %collective-permute-start.21 = (bf16[128,256]{1,0:T(8,128)(2,1)S(1)}, bf16[128,256]{1,0:T(8,128)(2,1)S(1)}, u32[]{:S(2)}, u32[]{:S(2)}) collective-permute-start(bf16[128,256]{1,0:T(8,128)(2,1)S(1)} %get-tuple-element.61), channel_id=1, source_target_pairs={{0,16},{1,17},{2,18},{3,19},{4,20},{5,21},{6,22},{7,23},{8,24},{9,... | collective-permute-start | bytes 196616 | tf_op jit(solution)/shard_map/ppermute | solution.py:88
  64.7 6.3 %collective-permute-start.17 = (bf16[128,256]{1,0:T(8,128)(2,1)S(1)}, bf16[128,256]{1,0:T(8,128)(2,1)S(1)}, u32[]{:S(2)}, u32[]{:S(2)}) collective-permute-start(bf16[128,256]{1,0:T(8,128)(2,1)S(1)} %get-tuple-element.55), channel_id=1, source_target_pairs={{0,16},{1,17},{2,18},{3,19},{4,20},{5,21},{6,22},{7,23},{8,24},{9,... | collective-permute-start | bytes 196616 | tf_op jit(solution)/shard_map/ppermute | solution.py:88
  65.3 6.4 %collective-permute-start.18 = (bf16[128,256]{1,0:T(8,128)(2,1)S(1)}, bf16[128,256]{1,0:T(8,128)(2,1)S(1)}, u32[]{:S(2)}, u32[]{:S(2)}) collective-permute-start(bf16[128,256]{1,0:T(8,128)(2,1)S(1)} %get-tuple-element.56), channel_id=1, source_target_pairs={{0,16},{1,17},{2,18},{3,19},{4,20},{5,21},{6,22},{7,23},{8,24},{9,... | collective-permute-start | bytes 196616 | tf_op jit(solution)/shard_map/ppermute | solution.py:88
  68.3 5.6 %collective-permute-start.23 = (bf16[128,256]{1,0:T(8,128)(2,1)S(1)}, bf16[128,256]{1,0:T(8,128)(2,1)S(1)}, u32[]{:S(2)}, u32[]{:S(2)}) collective-permute-start(bf16[128,256]{1,0:T(8,128)(2,1)S(1)} %shard_map.99), channel_id=1, source_target_pairs={{0,192},{1,193},{2,194},{3,195},{4,196},{5,197},{6,198},{7,199},{8... | collective-permute-start | bytes 196616 | tf_op jit(solution)/shard_map/ppermute | solution.py:88
  69.7 5.6 %collective-permute-start.22 = (bf16[128,256]{1,0:T(8,128)(2,1)S(1)}, bf16[128,256]{1,0:T(8,128)(2,1)S(1)}, u32[]{:S(2)}, u32[]{:S(2)}) collective-permute-start(bf16[128,256]{1,0:T(8,128)(2,1)S(1)} %shard_map.98), channel_id=1, source_target_pairs={{0,128},{1,129},{2,130},{3,131},{4,132},{5,133},{6,134},{7,135},{8... | collective-permute-start | bytes 196616 | tf_op jit(solution)/shard_map/ppermute | solution.py:88
  77.1 7.3 %collective-permute-start.25 = (f32[128,256]{1,0:T(8,128)S(1)}, f32[128,256]{1,0:T(8,128)S(1)}, u32[]{:S(2)}, u32[]{:S(2)}) collective-permute-start(f32[128,256]{1,0:T(8,128)S(1)} %get-tuple-element.63.one), channel_id=1, source_target_pairs={{0,48},{1,49},{2,50},{3,51},{4,52},{5,53},{6,54},{7,55},{8,56},{9,... | collective-permute-start | bytes 393224 | tf_op jit(solution)/shard_map/ppermute | solution.py:88
  79.1 5.3 %collective-permute-start.26 = (f32[64,256]{1,0:T(8,128)S(1)}, f32[64,256]{1,0:T(8,128)S(1)}, u32[]{:S(2)}, u32[]{:S(2)}) collective-permute-start(f32[64,256]{1,0:T(8,128)S(1)} %get-tuple-element.64.mine), channel_id=1, source_target_pairs={{0,128},{1,129},{2,130},{3,131},{4,132},{5,133},{6,134},{7,135},{8... | collective-permute-start | bytes 196616 | tf_op jit(solution)/shard_map/ppermute | solution.py:88
  84.4 7.4 %collective-permute-start.27 = (bf16[128,256]{1,0:T(8,128)(2,1)S(1)}, bf16[128,256]{1,0:T(8,128)(2,1)S(1)}, u32[]{:S(2)}, u32[]{:S(2)}) collective-permute-start(bf16[128,256]{1,0:T(8,128)(2,1)S(1)} %get-tuple-element.65), channel_id=1, source_target_pairs={{0,1},{1,53},{2,65},{3,113},{4,129},{5,181},{6,195},{7,247},{8,9},... | collective-permute-start | bytes 196616 | tf_op jit(solution)/shard_map/ppermute | solution.py:88
  89.2 5.5 %collective-permute-start.28 = (f32[64,256]{1,0:T(8,128)S(1)}, f32[64,256]{1,0:T(8,128)S(1)}, u32[]{:S(2)}, u32[]{:S(2)}) collective-permute-start(f32[64,256]{1,0:T(8,128)S(1)} %get-tuple-element.66.mine), channel_id=1, source_target_pairs={{0,48},{1,49},{2,50},{3,51},{4,52},{5,53},{6,54},{7,55},{8,56},{9,... | collective-permute-start | bytes 196616 | tf_op jit(solution)/shard_map/ppermute | solution.py:88
  94.7 6.6 %collective-permute-start.29 = (bf16[256,256]{1,0:T(8,128)(2,1)S(1)}, bf16[256,256]{1,0:T(8,128)(2,1)S(1)}, u32[]{:S(2)}, u32[]{:S(2)}) collective-permute-start(bf16[256,256]{1,0:T(8,128)(2,1)S(1)} %shard_map.102.m0), channel_id=1, source_target_pairs={{0,4},{1,5},{2,6},{3,7},{4,0},{5,1},{6,2},{7,3},{8,12},{9,13},{10,... | collective-permute-start | bytes 393224 | tf_op jit(solution)/shard_map/ppermute | solution.py:88
  95.8 6.9 %collective-permute-start.30 = (bf16[256,256]{1,0:T(8,128)(2,1)S(1)}, bf16[256,256]{1,0:T(8,128)(2,1)S(1)}, u32[]{:S(2)}, u32[]{:S(2)}) collective-permute-start(bf16[256,256]{1,0:T(8,128)(2,1)S(1)} %shard_map.102.m0), channel_id=1, source_target_pairs={{0,6},{1,7},{2,4},{3,5},{4,2},{5,3},{6,0},{7,1},{8,14},{9,15},{10,... | collective-permute-start | bytes 393224 | tf_op jit(solution)/shard_map/ppermute | solution.py:88
  97.4 5.3 %collective-permute-start.31 = (bf16[256,256]{1,0:T(8,128)(2,1)S(1)}, bf16[256,256]{1,0:T(8,128)(2,1)S(1)}, u32[]{:S(2)}, u32[]{:S(2)}) collective-permute-start(bf16[256,256]{1,0:T(8,128)(2,1)S(1)} %shard_map.102.m0), channel_id=1, source_target_pairs={{0,2},{1,3},{2,0},{3,1},{4,6},{5,7},{6,4},{7,5},{8,10},{9,11},{10,... | collective-permute-start | bytes 393224 | tf_op jit(solution)/shard_map/ppermute | solution.py:88
  (13 other events, 72.6 us)

commit v10 on v9

--- a/solution.py
+++ b/solution.py
@@ -47,14 +47,14 @@
 ROUTE = (((2, 1, 3, 0), (0, 3, 2, 1), (2, 1, 0, 3), (3, 0, 2, 1)), ((0, 1, 3, 2), (0, 1, 2, 3), (0, 1, 2, 3), (1, 0, 2, 3)))
 TO_ROW = pairs(lambda z, y, c, x, h: (x, Y_OF[u_of(y), h], c, ROUTE[v_of(y) == h][x][z], 1 - v_of(y)))
 SERVED = (
-    (6, 0, 4, 2, 5, 3, 1, 7), (2, 4, 0, 6, 5, 1, 3, 7), (2, 0, 4, 6, 5, 1, 3, 7), (6, 4, 0, 2, 7, 3, 1, 5),
-    (5, 3, 1, 7, 0, 4, 6, 2), (5, 7, 3, 1, 6, 2, 4, 0), (1, 7, 3, 5, 0, 4, 6, 2), (5, 3, 7, 1, 2, 6, 4, 0),
-    (5, 3, 6, 4, 0, 2, 7, 1), (5, 3, 0, 2, 4, 6, 7, 1), (2, 3, 4, 0, 1, 6, 7, 5), (5, 3, 0, 6, 2, 4, 7, 1),
-    (1, 5, 3, 7, 2, 4, 0, 6), (2, 4, 7, 3, 5, 1, 0, 6), (2, 4, 7, 5, 1, 3, 0, 6), (2, 5, 1, 3, 7, 4, 0, 6),
-    (1, 7, 4, 6, 2, 0, 3, 5), (1, 7, 2, 0, 6, 4, 3, 5), (1, 7, 0, 2, 4, 6, 3, 5), (1, 7, 4, 5, 6, 2, 3, 0),
-    (2, 0, 4, 6, 5, 1, 7, 3), (6, 0, 7, 5, 1, 3, 4, 2), (6, 0, 4, 7, 5, 1, 3, 2), (6, 0, 3, 1, 5, 7, 4, 2),
-    (7, 1, 3, 5, 6, 4, 0, 2), (5, 3, 7, 1, 0, 6, 4, 2), (5, 3, 7, 1, 6, 0, 4, 2), (7, 1, 3, 5, 2, 4, 0, 6),
-    (6, 4, 0, 2, 3, 1, 7, 5), (0, 6, 4, 2, 7, 5, 3, 1), (2, 4, 0, 6, 3, 5, 7, 1), (0, 6, 4, 2, 7, 1, 3, 5),
+    (2, 4, 0, 6, 5, 3, 1, 7), (2, 4, 0, 6, 5, 3, 1, 7), (6, 0, 4, 2, 5, 3, 1, 7), (6, 0, 4, 2, 5, 3, 1, 7),
+    (5, 3, 7, 1, 2, 4, 6, 0), (5, 3, 7, 1, 2, 4, 6, 0), (1, 7, 5, 3, 2, 4, 6, 0), (1, 7, 5, 3, 2, 4, 6, 0),
+    (5, 3, 4, 2, 0, 6, 7, 1), (5, 3, 4, 2, 0, 6, 7, 1), (5, 3, 0, 6, 2, 4, 7, 1), (5, 3, 0, 6, 2, 4, 7, 1),
+    (2, 4, 3, 5, 7, 1, 0, 6), (2, 4, 3, 5, 7, 1, 0, 6), (2, 4, 3, 5, 7, 1, 0, 6), (2, 4, 3, 5, 7, 1, 0, 6),
+    (1, 7, 6, 0, 2, 4, 3, 5), (1, 7, 6, 0, 2, 4, 3, 5), (1, 7, 6, 4, 2, 0, 3, 5), (1, 7, 6, 4, 2, 0, 3, 5),
+    (6, 0, 1, 7, 5, 3, 4, 2), (6, 0, 1, 7, 5, 3, 4, 2), (6, 0, 7, 1, 5, 3, 4, 2), (6, 0, 7, 1, 5, 3, 4, 2),
+    (7, 1, 3, 5, 6, 0, 4, 2), (7, 1, 3, 5, 6, 0, 4, 2), (5, 3, 7, 1, 0, 6, 4, 2), (5, 3, 7, 1, 0, 6, 4, 2),
+    (0, 6, 4, 2, 1, 7, 3, 5), (0, 6, 4, 2, 1, 7, 3, 5), (2, 4, 0, 6, 1, 7, 3, 5), (2, 4, 0, 6, 1, 7, 3, 5),
 )
 
 
@@ -190,15 +190,12 @@
 
 def sum_body(own, r3, r1, r2, cot, to_h):
     total = own[...] + r1[...].astype(F32) + (r2[...].astype(F32) + r3[...].astype(F32))
-    high, low = split(total)
-    to_h[0:PART, :] = high
-    to_h[PART : 2 * PART, :] = low
-    to_h[2 * PART :, :] = cot[...]
+    to_h[0:PART, :] = total.astype(BF)
+    to_h[PART:, :] = cot[...]
 
 
 def aggregate_of(mine, got):
-    parts = [ref[0:PART, :].astype(F32) + ref[PART : 2 * PART, :].astype(F32) for ref in (mine, got)]
-    return (parts[0] + parts[1]).astype(BF)
+    return (mine[0:PART, :].astype(F32) + got[0:PART, :].astype(F32)).astype(BF)
 
 
 def layer_body(mine, got, weight, to2, to3, to1, own, aggregate, share, grad_w):
@@ -207,7 +204,7 @@
     preact = dot(agg, weight[...])
     gates = jax.nn.sigmoid(preact)
     first = me["h"] == 0
-    a, b = mine[2 * PART :, :], got[2 * PART :, :]
+    a, b = mine[PART:, :], got[PART:, :]
     cotangent = jnp.concatenate([jnp.where(first, a, b), jnp.where(first, b, a)], axis=0).astype(F32)
     grad_pre = (cotangent * gates * (1.0 + preact * (1.0 - gates))).astype(BF)
     grad_w[...] = dot(agg, grad_pre, ((0,), (0,)))
@@ -331,7 +328,7 @@
         forward_last_body, [part, part, part, part32], dense, *by_uc[::-1], most, scratch=[pltpu.VMEM((1, BLOCK, WIDTH), BF), total]
     )
     got = [send(value, route) for value, route in zip(to, FAR_X)]
-    (mine,) = call(sum_body, [((2 * PART + SLICE, WIDTH), BF)], own, got[1], got[2], got[0], cotangent)
+    (mine,) = call(sum_body, [to_z], own, got[1], got[2], got[0], cotangent)
     got = send(mine, FLIP_H)
     *to, own, aggregate, share = call(
         layer_body, [to_z, to_z, to_z, part, part, share32], mine, got, weight, scratch=[pltpu.VMEM((WIDTH, WIDTH), F32)]

time: 104 us -> 99.3 us (0.955)
  waiting for transfers between devices: 44 us -> 35.2 us
  starting transfers between devices: 49.5 us -> 53 us
    ppermute x32, waiting for transfers between devices: 44 us -> 35.2 us  [send(): return lax.ppermute(value, AXES, route)]
    ppermute x32, starting transfers between devices: 49.5 us -> 53 us  [send(): return lax.ppermute(value, AXES, route)]
  transfers between devices with their start and end apart: 32 -> 32, of which waited for: 23 -> 21; matrix products, arithmetic and copies ran while one was open for 1% -> 1% of each run, Pallas kernels for 3% -> 4%
where the time goes in v10:
time: 99.3 us; the launch traced here: 98.4 us
  starting transfers between devices  53 us (53%)
  waiting for transfers between devices  35.2 us (35%)
  Pallas kernels  6.1 us (6%)
  local copies, waits for them, and re-layouts  3.32 us (3%)
    ppermute x32, starting transfers between devices, send(): return lax.ppermute(value, AXES, route)  53 us
    ppermute x32, waiting for transfers between devices, send(): return lax.ppermute(value, AXES, route)  35.2 us
    pallas_call x19, Pallas kernels, call(): pl.pallas_call(body, out_shape=[jax.ShapeDtypeStruct(shape, dtype) for sh...  6.1 us
    unnamed x11, local copies, waits for them, and re-layouts  3.32 us
  transfers between devices with their start and end apart: 32, of which 21 were waited for; matrix products, arithmetic and copies ran while one was open for 1% of the time, Pallas kernels for 4%

profile of v10, /device:TPU:32, one launch (start us, length us, event | category | flops | bytes accessed | tf_op | source)
XLA Modules:
  0.0 98.4 jit_solution(1694230815915362074)
XLA Ops:
  1.7 2.9 %collective-permute-start = (bf16[256,256]{1,0:T(8,128)(2,1)S(1)}, bf16[256,256]{1,0:T(8,128)(2,1)S(1)}, u32[]{:S(2)}, u32[]{:S(2)}) collective-permute-start(bf16[256,256]{1,0:T(8,128)(2,1)S(1)} %shard_map.85), channel_id=1, source_target_pairs={{2,0},{53,1},{69,2},{114,3},{129,4},{182,5},{199,6},{240,7},{10,8}... | collective-permute-start | bytes 393224 | tf_op jit(solution)/shard_map/ppermute | solution.py:88
  8.6 2.4 %collective-permute-start.4 = (bf16[256,256]{1,0:T(8,128)(2,1)S(1)}, bf16[256,256]{1,0:T(8,128)(2,1)S(1)}, u32[]{:S(2)}, u32[]{:S(2)}) collective-permute-start(bf16[256,256]{1,0:T(8,128)(2,1)S(1)} %collective-permute-done.a0), channel_id=1, source_target_pairs={{0,16},{1,17},{2,18},{3,19},{4,20},{5,21},{6,22},{7,23},{8,24},{9,... | collective-permute-start | bytes 393224 | tf_op jit(solution)/shard_map/ppermute | solution.py:88
  11.0 2.4 %collective-permute-done.1.b0 = bf16[256,256]{1,0:T(8,128)(2,1)S(1)} collective-permute-done((bf16[256,256]{1,0:T(8,128)(2,1)S(1)}, bf16[256,256]{1,0:T(8,128)(2,1)S(1)}, u32[]{:S(2)}, u32[]{:S(2)}) %collective-permute-start.1) | collective-permute-done | bytes 131104 | tf_op jit(solution)/shard_map/ppermute | solution.py:88
  13.4 4.7 %collective-permute-start.2 = (bf16[256,256]{1,0:T(8,128)(2,1)S(1)}, bf16[256,256]{1,0:T(8,128)(2,1)S(1)}, u32[]{:S(2)}, u32[]{:S(2)}) collective-permute-start(bf16[256,256]{1,0:T(8,128)(2,1)S(1)} %collective-permute-done.1.b0), channel_id=1, source_target_pairs={{0,16},{1,17},{2,18},{3,19},{4,20},{5,21},{6,22},{7,23},{8,24},{9,... | collective-permute-start | bytes 393224 | tf_op jit(solution)/shard_map/ppermute | solution.py:88
  18.6 2.8 %collective-permute-done.2.b2 = bf16[256,256]{1,0:T(8,128)(2,1)S(1)} collective-permute-done((bf16[256,256]{1,0:T(8,128)(2,1)S(1)}, bf16[256,256]{1,0:T(8,128)(2,1)S(1)}, u32[]{:S(2)}, u32[]{:S(2)}) %collective-permute-start.2) | collective-permute-done | bytes 131104 | tf_op jit(solution)/shard_map/ppermute | solution.py:88
  23.2 3.9 %collective-permute-start.10 = (bf16[128,256]{1,0:T(8,128)(2,1)S(1)}, bf16[128,256]{1,0:T(8,128)(2,1)S(1)}, u32[]{:S(2)}, u32[]{:S(2)}) collective-permute-start(bf16[128,256]{1,0:T(8,128)(2,1)S(1)} %get-tuple-element.43), channel_id=1, source_target_pairs={{0,4},{1,5},{2,6},{3,7},{4,0},{5,1},{6,2},{7,3},{8,12},{9,13},{10,... | collective-permute-start | bytes 196616 | tf_op jit(solution)/shard_map/ppermute | solution.py:88
  27.0 2.0 %collective-permute-start.8 = (bf16[128,256]{1,0:T(8,128)(2,1)S(1)}, bf16[128,256]{1,0:T(8,128)(2,1)S(1)}, u32[]{:S(2)}, u32[]{:S(2)}) collective-permute-start(bf16[128,256]{1,0:T(8,128)(2,1)S(1)} %get-tuple-element.41), channel_id=1, source_target_pairs={{0,6},{1,7},{2,4},{3,5},{4,2},{5,3},{6,0},{7,1},{8,14},{9,15},{10,... | collective-permute-start | bytes 196616 | tf_op jit(solution)/shard_map/ppermute | solution.py:88
  29.8 2.7 %collective-permute-done.8.r3 = bf16[128,256]{1,0:T(8,128)(2,1)S(1)} collective-permute-done((bf16[128,256]{1,0:T(8,128)(2,1)S(1)}, bf16[128,256]{1,0:T(8,128)(2,1)S(1)}, u32[]{:S(2)}, u32[]{:S(2)}) %collective-permute-start.8) | collective-permute-done | bytes 65568 | tf_op jit(solution)/shard_map/ppermute | solution.py:88
  33.5 7.0 %collective-permute-start.11 = (bf16[192,256]{1,0:T(8,128)(2,1)S(1)}, bf16[192,256]{1,0:T(8,128)(2,1)S(1)}, u32[]{:S(2)}, u32[]{:S(2)}) collective-permute-start(bf16[192,256]{1,0:T(8,128)(2,1)S(1)} %shard_map.89.mine), channel_id=1, source_target_pairs={{0,1},{1,0},{2,3},{3,2},{4,5},{5,4},{6,7},{7,6},{8,9},{9,8},{10,11... | collective-permute-start | bytes 294920 | tf_op jit(solution)/shard_map/ppermute | solution.py:88
  40.4 4.7 %collective-permute-done.11.got = bf16[192,256]{1,0:T(8,128)(2,1)S(1)} collective-permute-done((bf16[192,256]{1,0:T(8,128)(2,1)S(1)}, bf16[192,256]{1,0:T(8,128)(2,1)S(1)}, u32[]{:S(2)}, u32[]{:S(2)}) %collective-permute-start.11) | collective-permute-done | bytes 98336 | tf_op jit(solution)/shard_map/ppermute | solution.py:88
  45.6 1.4 %collective-permute-start.12 = (bf16[192,256]{1,0:T(8,128)(2,1)S(1)}, bf16[192,256]{1,0:T(8,128)(2,1)S(1)}, u32[]{:S(2)}, u32[]{:S(2)}) collective-permute-start(bf16[192,256]{1,0:T(8,128)(2,1)S(1)} %get-tuple-element.47), channel_id=1, source_target_pairs={{0,4},{1,5},{2,6},{3,7},{4,0},{5,1},{6,2},{7,3},{8,12},{9,13},{10,... | collective-permute-start | bytes 294920 | tf_op jit(solution)/shard_map/ppermute | solution.py:88
  49.1 3.3 %collective-permute-done.12.m2 = bf16[192,256]{1,0:T(8,128)(2,1)S(1)} collective-permute-done((bf16[192,256]{1,0:T(8,128)(2,1)S(1)}, bf16[192,256]{1,0:T(8,128)(2,1)S(1)}, u32[]{:S(2)}, u32[]{:S(2)}) %collective-permute-start.12) | collective-permute-done | bytes 98336 | tf_op jit(solution)/shard_map/ppermute | solution.py:88
  55.9 2.1 %collective-permute-start.19 = (bf16[192,256]{1,0:T(8,128)(2,1)S(1)}, bf16[192,256]{1,0:T(8,128)(2,1)S(1)}, u32[]{:S(2)}, u32[]{:S(2)}) collective-permute-start(bf16[192,256]{1,0:T(8,128)(2,1)S(1)} %get-tuple-element.58), channel_id=1, source_target_pairs={{0,16},{1,17},{2,18},{3,19},{4,20},{5,21},{6,22},{7,23},{8,24},{9,... | collective-permute-start | bytes 294920 | tf_op jit(solution)/shard_map/ppermute | solution.py:88
  58.1 1.9 %collective-permute-start.17 = (bf16[128,256]{1,0:T(8,128)(2,1)S(1)}, bf16[128,256]{1,0:T(8,128)(2,1)S(1)}, u32[]{:S(2)}, u32[]{:S(2)}) collective-permute-start(bf16[128,256]{1,0:T(8,128)(2,1)S(1)} %get-tuple-element.55), channel_id=1, source_target_pairs={{0,16},{1,17},{2,18},{3,19},{4,20},{5,21},{6,22},{7,23},{8,24},{9,... | collective-permute-start | bytes 196616 | tf_op jit(solution)/shard_map/ppermute | solution.py:88
  60.2 1.4 %collective-permute-done.19.earlier.got = bf16[192,256]{1,0:T(8,128)(2,1)S(1)} collective-permute-done((bf16[192,256]{1,0:T(8,128)(2,1)S(1)}, bf16[192,256]{1,0:T(8,128)(2,1)S(1)}, u32[]{:S(2)}, u32[]{:S(2)}) %collective-permute-start.19) | collective-permute-done | bytes 98336 | tf_op jit(solution)/shard_map/ppermute | solution.py:88
  63.0 2.2 %collective-permute-start.22 = (bf16[128,256]{1,0:T(8,128)(2,1)S(1)}, bf16[128,256]{1,0:T(8,128)(2,1)S(1)}, u32[]{:S(2)}, u32[]{:S(2)}) collective-permute-start(bf16[128,256]{1,0:T(8,128)(2,1)S(1)} %shard_map.98), channel_id=1, source_target_pairs={{0,128},{1,129},{2,130},{3,131},{4,132},{5,133},{6,134},{7,135},{8... | collective-permute-start | bytes 196616 | tf_op jit(solution)/shard_map/ppermute | solution.py:88
  70.7 3.2 %collective-permute-start.25 = (f32[128,256]{1,0:T(8,128)S(1)}, f32[128,256]{1,0:T(8,128)S(1)}, u32[]{:S(2)}, u32[]{:S(2)}) collective-permute-start(f32[128,256]{1,0:T(8,128)S(1)} %get-tuple-element.63.one), channel_id=1, source_target_pairs={{0,48},{1,49},{2,50},{3,51},{4,52},{5,53},{6,54},{7,55},{8,56},{9,... | collective-permute-start | bytes 393224 | tf_op jit(solution)/shard_map/ppermute | solution.py:88
  73.8 2.8 %collective-permute-start.26 = (f32[64,256]{1,0:T(8,128)S(1)}, f32[64,256]{1,0:T(8,128)S(1)}, u32[]{:S(2)}, u32[]{:S(2)}) collective-permute-start(f32[64,256]{1,0:T(8,128)S(1)} %get-tuple-element.64.mine), channel_id=1, source_target_pairs={{0,128},{1,129},{2,130},{3,131},{4,132},{5,133},{6,134},{7,135},{8... | collective-permute-start | bytes 196616 | tf_op jit(solution)/shard_map/ppermute | solution.py:88
  76.7 2.4 %collective-permute-done.26.got = f32[64,256]{1,0:T(8,128)S(1)} collective-permute-done((f32[64,256]{1,0:T(8,128)S(1)}, f32[64,256]{1,0:T(8,128)S(1)}, u32[]{:S(2)}, u32[]{:S(2)}) %collective-permute-start.26) | collective-permute-done | bytes 65568 | tf_op jit(solution)/shard_map/ppermute | solution.py:88
  79.1 5.0 %collective-permute-start.27 = (bf16[128,256]{1,0:T(8,128)(2,1)S(1)}, bf16[128,256]{1,0:T(8,128)(2,1)S(1)}, u32[]{:S(2)}, u32[]{:S(2)}) collective-permute-start(bf16[128,256]{1,0:T(8,128)(2,1)S(1)} %get-tuple-element.65), channel_id=1, source_target_pairs={{0,1},{1,53},{2,65},{3,113},{4,129},{5,181},{6,195},{7,247},{8,9},... | collective-permute-start | bytes 196616 | tf_op jit(solution)/shard_map/ppermute | solution.py:88
  84.1 2.6 %collective-permute-done.27.piece = bf16[128,256]{1,0:T(8,128)(2,1)S(1)} collective-permute-done((bf16[128,256]{1,0:T(8,128)(2,1)S(1)}, bf16[128,256]{1,0:T(8,128)(2,1)S(1)}, u32[]{:S(2)}, u32[]{:S(2)}) %collective-permute-start.27) | collective-permute-done | bytes 65568 | tf_op jit(solution)/shard_map/ppermute | solution.py:88
  86.7 2.9 %collective-permute-done.28.got = f32[64,256]{1,0:T(8,128)S(1)} collective-permute-done((f32[64,256]{1,0:T(8,128)S(1)}, f32[64,256]{1,0:T(8,128)S(1)}, u32[]{:S(2)}, u32[]{:S(2)}) %collective-permute-start.28) | collective-permute-done | bytes 65568 | tf_op jit(solution)/shard_map/ppermute | solution.py:88
  90.9 1.8 %collective-permute-start.30 = (bf16[256,256]{1,0:T(8,128)(2,1)S(1)}, bf16[256,256]{1,0:T(8,128)(2,1)S(1)}, u32[]{:S(2)}, u32[]{:S(2)}) collective-permute-start(bf16[256,256]{1,0:T(8,128)(2,1)S(1)} %shard_map.102.m0), channel_id=1, source_target_pairs={{0,6},{1,7},{2,4},{3,5},{4,2},{5,3},{6,0},{7,1},{8,14},{9,15},{10,... | collective-permute-start | bytes 393224 | tf_op jit(solution)/shard_map/ppermute | solution.py:88
  94.0 2.3 %collective-permute-done.29.m2 = bf16[256,256]{1,0:T(8,128)(2,1)S(1)} collective-permute-done((bf16[256,256]{1,0:T(8,128)(2,1)S(1)}, bf16[256,256]{1,0:T(8,128)(2,1)S(1)}, u32[]{:S(2)}, u32[]{:S(2)}) %collective-permute-start.29) | collective-permute-done | bytes 131104 | tf_op jit(solution)/shard_map/ppermute | solution.py:88
  (70 shorter events, 26.8 us)
Async XLA Ops:
  1.7 6.6 %collective-permute-start = (bf16[256,256]{1,0:T(8,128)(2,1)S(1)}, bf16[256,256]{1,0:T(8,128)(2,1)S(1)}, u32[]{:S(2)}, u32[]{:S(2)}) collective-permute-start(bf16[256,256]{1,0:T(8,128)(2,1)S(1)} %shard_map.85), channel_id=1, source_target_pairs={{2,0},{53,1},{69,2},{114,3},{129,4},{182,5},{199,6},{240,7},{10,8}... | collective-permute-start | bytes 393224 | tf_op jit(solution)/shard_map/ppermute | solution.py:88
  8.4 5.1 %collective-permute-start.1 = (bf16[256,256]{1,0:T(8,128)(2,1)S(1)}, bf16[256,256]{1,0:T(8,128)(2,1)S(1)}, u32[]{:S(2)}, u32[]{:S(2)}) collective-permute-start(bf16[256,256]{1,0:T(8,128)(2,1)S(1)} %collective-permute-done.a0), channel_id=1, source_target_pairs={{0,64},{1,65},{2,66},{3,67},{4,68},{5,69},{6,70},{7,71},{8,72},{9,... | collective-permute-start | bytes 393224 | tf_op jit(solution)/shard_map/ppermute | solution.py:88
  8.6 10.0 %collective-permute-start.4 = (bf16[256,256]{1,0:T(8,128)(2,1)S(1)}, bf16[256,256]{1,0:T(8,128)(2,1)S(1)}, u32[]{:S(2)}, u32[]{:S(2)}) collective-permute-start(bf16[256,256]{1,0:T(8,128)(2,1)S(1)} %collective-permute-done.a0), channel_id=1, source_target_pairs={{0,16},{1,17},{2,18},{3,19},{4,20},{5,21},{6,22},{7,23},{8,24},{9,... | collective-permute-start | bytes 393224 | tf_op jit(solution)/shard_map/ppermute | solution.py:88
  13.4 8.0 %collective-permute-start.2 = (bf16[256,256]{1,0:T(8,128)(2,1)S(1)}, bf16[256,256]{1,0:T(8,128)(2,1)S(1)}, u32[]{:S(2)}, u32[]{:S(2)}) collective-permute-start(bf16[256,256]{1,0:T(8,128)(2,1)S(1)} %collective-permute-done.1.b0), channel_id=1, source_target_pairs={{0,16},{1,17},{2,18},{3,19},{4,20},{5,21},{6,22},{7,23},{8,24},{9,... | collective-permute-start | bytes 393224 | tf_op jit(solution)/shard_map/ppermute | solution.py:88
  23.2 6.6 %collective-permute-start.10 = (bf16[128,256]{1,0:T(8,128)(2,1)S(1)}, bf16[128,256]{1,0:T(8,128)(2,1)S(1)}, u32[]{:S(2)}, u32[]{:S(2)}) collective-permute-start(bf16[128,256]{1,0:T(8,128)(2,1)S(1)} %get-tuple-element.43), channel_id=1, source_target_pairs={{0,4},{1,5},{2,6},{3,7},{4,0},{5,1},{6,2},{7,3},{8,12},{9,13},{10,... | collective-permute-start | bytes 196616 | tf_op jit(solution)/shard_map/ppermute | solution.py:88
  27.0 5.5 %collective-permute-start.8 = (bf16[128,256]{1,0:T(8,128)(2,1)S(1)}, bf16[128,256]{1,0:T(8,128)(2,1)S(1)}, u32[]{:S(2)}, u32[]{:S(2)}) collective-permute-start(bf16[128,256]{1,0:T(8,128)(2,1)S(1)} %get-tuple-element.41), channel_id=1, source_target_pairs={{0,6},{1,7},{2,4},{3,5},{4,2},{5,3},{6,0},{7,1},{8,14},{9,15},{10,... | collective-permute-start | bytes 196616 | tf_op jit(solution)/shard_map/ppermute | solution.py:88
  33.5 11.7 %collective-permute-start.11 = (bf16[192,256]{1,0:T(8,128)(2,1)S(1)}, bf16[192,256]{1,0:T(8,128)(2,1)S(1)}, u32[]{:S(2)}, u32[]{:S(2)}) collective-permute-start(bf16[192,256]{1,0:T(8,128)(2,1)S(1)} %shard_map.89.mine), channel_id=1, source_target_pairs={{0,1},{1,0},{2,3},{3,2},{4,5},{5,4},{6,7},{7,6},{8,9},{9,8},{10,11... | collective-permute-start | bytes 294920 | tf_op jit(solution)/shard_map/ppermute | solution.py:88
  45.6 6.9 %collective-permute-start.12 = (bf16[192,256]{1,0:T(8,128)(2,1)S(1)}, bf16[192,256]{1,0:T(8,128)(2,1)S(1)}, u32[]{:S(2)}, u32[]{:S(2)}) collective-permute-start(bf16[192,256]{1,0:T(8,128)(2,1)S(1)} %get-tuple-element.47), channel_id=1, source_target_pairs={{0,4},{1,5},{2,6},{3,7},{4,0},{5,1},{6,2},{7,3},{8,12},{9,13},{10,... | collective-permute-start | bytes 294920 | tf_op jit(solution)/shard_map/ppermute | solution.py:88
  47.0 6.2 %collective-permute-start.13 = (bf16[192,256]{1,0:T(8,128)(2,1)S(1)}, bf16[192,256]{1,0:T(8,128)(2,1)S(1)}, u32[]{:S(2)}, u32[]{:S(2)}) collective-permute-start(bf16[192,256]{1,0:T(8,128)(2,1)S(1)} %get-tuple-element.48), channel_id=1, source_target_pairs={{0,6},{1,7},{2,4},{3,5},{4,2},{5,3},{6,0},{7,1},{8,14},{9,15},{10,... | collective-permute-start | bytes 294920 | tf_op jit(solution)/shard_map/ppermute | solution.py:88
  48.1 5.1 %collective-permute-start.14 = (bf16[192,256]{1,0:T(8,128)(2,1)S(1)}, bf16[192,256]{1,0:T(8,128)(2,1)S(1)}, u32[]{:S(2)}, u32[]{:S(2)}) collective-permute-start(bf16[192,256]{1,0:T(8,128)(2,1)S(1)} %get-tuple-element.49), channel_id=1, source_target_pairs={{0,2},{1,3},{2,0},{3,1},{4,6},{5,7},{6,4},{7,5},{8,10},{9,11},{10,... | collective-permute-start | bytes 294920 | tf_op jit(solution)/shard_map/ppermute | solution.py:88
  54.3 5.8 %collective-permute-start.15 = (f32[512,256]{1,0:T(8,128)S(1)}, f32[512,256]{1,0:T(8,128)S(1)}, u32[]{:S(2)}, u32[]{:S(2)}) collective-permute-start(f32[512,256]{1,0:T(8,128)S(1)} %get-tuple-element.53), channel_id=1, source_target_pairs={{0,8},{1,9},{2,10},{3,11},{4,12},{5,13},{6,14},{7,15},{8,0},{9,1},... | collective-permute-start | bytes 1572872 | tf_op jit(solution)/shard_map/ppermute | solution.py:88
  55.9 5.7 %collective-permute-start.19 = (bf16[192,256]{1,0:T(8,128)(2,1)S(1)}, bf16[192,256]{1,0:T(8,128)(2,1)S(1)}, u32[]{:S(2)}, u32[]{:S(2)}) collective-permute-start(bf16[192,256]{1,0:T(8,128)(2,1)S(1)} %get-tuple-element.58), channel_id=1, source_target_pairs={{0,16},{1,17},{2,18},{3,19},{4,20},{5,21},{6,22},{7,23},{8,24},{9,... | collective-permute-start | bytes 294920 | tf_op jit(solution)/shard_map/ppermute | solution.py:88
  58.0 5.0 %collective-permute-start.21 = (bf16[128,256]{1,0:T(8,128)(2,1)S(1)}, bf16[128,256]{1,0:T(8,128)(2,1)S(1)}, u32[]{:S(2)}, u32[]{:S(2)}) collective-permute-start(bf16[128,256]{1,0:T(8,128)(2,1)S(1)} %get-tuple-element.61), channel_id=1, source_target_pairs={{0,16},{1,17},{2,18},{3,19},{4,20},{5,21},{6,22},{7,23},{8,24},{9,... | collective-permute-start | bytes 196616 | tf_op jit(solution)/shard_map/ppermute | solution.py:88
  58.1 7.1 %collective-permute-start.17 = (bf16[128,256]{1,0:T(8,128)(2,1)S(1)}, bf16[128,256]{1,0:T(8,128)(2,1)S(1)}, u32[]{:S(2)}, u32[]{:S(2)}) collective-permute-start(bf16[128,256]{1,0:T(8,128)(2,1)S(1)} %get-tuple-element.55), channel_id=1, source_target_pairs={{0,16},{1,17},{2,18},{3,19},{4,20},{5,21},{6,22},{7,23},{8,24},{9,... | collective-permute-start | bytes 196616 | tf_op jit(solution)/shard_map/ppermute | solution.py:88
  60.0 5.3 %collective-permute-start.18 = (bf16[128,256]{1,0:T(8,128)(2,1)S(1)}, bf16[128,256]{1,0:T(8,128)(2,1)S(1)}, u32[]{:S(2)}, u32[]{:S(2)}) collective-permute-start(bf16[128,256]{1,0:T(8,128)(2,1)S(1)} %get-tuple-element.56), channel_id=1, source_target_pairs={{0,16},{1,17},{2,18},{3,19},{4,20},{5,21},{6,22},{7,23},{8,24},{9,... | collective-permute-start | bytes 196616 | tf_op jit(solution)/shard_map/ppermute | solution.py:88
  61.6 6.6 %collective-permute-start.23 = (bf16[128,256]{1,0:T(8,128)(2,1)S(1)}, bf16[128,256]{1,0:T(8,128)(2,1)S(1)}, u32[]{:S(2)}, u32[]{:S(2)}) collective-permute-start(bf16[128,256]{1,0:T(8,128)(2,1)S(1)} %shard_map.99), channel_id=1, source_target_pairs={{0,192},{1,193},{2,194},{3,195},{4,196},{5,197},{6,198},{7,199},{8... | collective-permute-start | bytes 196616 | tf_op jit(solution)/shard_map/ppermute | solution.py:88
  63.0 5.5 %collective-permute-start.22 = (bf16[128,256]{1,0:T(8,128)(2,1)S(1)}, bf16[128,256]{1,0:T(8,128)(2,1)S(1)}, u32[]{:S(2)}, u32[]{:S(2)}) collective-permute-start(bf16[128,256]{1,0:T(8,128)(2,1)S(1)} %shard_map.98), channel_id=1, source_target_pairs={{0,128},{1,129},{2,130},{3,131},{4,132},{5,133},{6,134},{7,135},{8... | collective-permute-start | bytes 196616 | tf_op jit(solution)/shard_map/ppermute | solution.py:88
  70.7 8.4 %collective-permute-start.25 = (f32[128,256]{1,0:T(8,128)S(1)}, f32[128,256]{1,0:T(8,128)S(1)}, u32[]{:S(2)}, u32[]{:S(2)}) collective-permute-start(f32[128,256]{1,0:T(8,128)S(1)} %get-tuple-element.63.one), channel_id=1, source_target_pairs={{0,48},{1,49},{2,50},{3,51},{4,52},{5,53},{6,54},{7,55},{8,56},{9,... | collective-permute-start | bytes 393224 | tf_op jit(solution)/shard_map/ppermute | solution.py:88
  73.8 5.3 %collective-permute-start.26 = (f32[64,256]{1,0:T(8,128)S(1)}, f32[64,256]{1,0:T(8,128)S(1)}, u32[]{:S(2)}, u32[]{:S(2)}) collective-permute-start(f32[64,256]{1,0:T(8,128)S(1)} %get-tuple-element.64.mine), channel_id=1, source_target_pairs={{0,128},{1,129},{2,130},{3,131},{4,132},{5,133},{6,134},{7,135},{8... | collective-permute-start | bytes 196616 | tf_op jit(solution)/shard_map/ppermute | solution.py:88
  79.1 7.6 %collective-permute-start.27 = (bf16[128,256]{1,0:T(8,128)(2,1)S(1)}, bf16[128,256]{1,0:T(8,128)(2,1)S(1)}, u32[]{:S(2)}, u32[]{:S(2)}) collective-permute-start(bf16[128,256]{1,0:T(8,128)(2,1)S(1)} %get-tuple-element.65), channel_id=1, source_target_pairs={{0,1},{1,53},{2,65},{3,113},{4,129},{5,181},{6,195},{7,247},{8,9},... | collective-permute-start | bytes 196616 | tf_op jit(solution)/shard_map/ppermute | solution.py:88
  84.1 5.5 %collective-permute-start.28 = (f32[64,256]{1,0:T(8,128)S(1)}, f32[64,256]{1,0:T(8,128)S(1)}, u32[]{:S(2)}, u32[]{:S(2)}) collective-permute-start(f32[64,256]{1,0:T(8,128)S(1)} %get-tuple-element.66.mine), channel_id=1, source_target_pairs={{0,48},{1,49},{2,50},{3,51},{4,52},{5,53},{6,54},{7,55},{8,56},{9,... | collective-permute-start | bytes 196616 | tf_op jit(solution)/shard_map/ppermute | solution.py:88
  89.6 6.6 %collective-permute-start.29 = (bf16[256,256]{1,0:T(8,128)(2,1)S(1)}, bf16[256,256]{1,0:T(8,128)(2,1)S(1)}, u32[]{:S(2)}, u32[]{:S(2)}) collective-permute-start(bf16[256,256]{1,0:T(8,128)(2,1)S(1)} %shard_map.102.m0), channel_id=1, source_target_pairs={{0,4},{1,5},{2,6},{3,7},{4,0},{5,1},{6,2},{7,3},{8,12},{9,13},{10,... | collective-permute-start | bytes 393224 | tf_op jit(solution)/shard_map/ppermute | solution.py:88
  90.9 6.7 %collective-permute-start.30 = (bf16[256,256]{1,0:T(8,128)(2,1)S(1)}, bf16[256,256]{1,0:T(8,128)(2,1)S(1)}, u32[]{:S(2)}, u32[]{:S(2)}) collective-permute-start(bf16[256,256]{1,0:T(8,128)(2,1)S(1)} %shard_map.102.m0), channel_id=1, source_target_pairs={{0,6},{1,7},{2,4},{3,5},{4,2},{5,3},{6,0},{7,1},{8,14},{9,15},{10,... | collective-permute-start | bytes 393224 | tf_op jit(solution)/shard_map/ppermute | solution.py:88
  92.6 5.0 %collective-permute-start.31 = (bf16[256,256]{1,0:T(8,128)(2,1)S(1)}, bf16[256,256]{1,0:T(8,128)(2,1)S(1)}, u32[]{:S(2)}, u32[]{:S(2)}) collective-permute-start(bf16[256,256]{1,0:T(8,128)(2,1)S(1)} %shard_map.102.m0), channel_id=1, source_target_pairs={{0,2},{1,3},{2,0},{3,1},{4,6},{5,7},{6,4},{7,5},{8,10},{9,11},{10,... | collective-permute-start | bytes 393224 | tf_op jit(solution)/shard_map/ppermute | solution.py:88
  (13 other events, 63.9 us)

commit v11 on v10

--- a/solution.py
+++ b/solution.py
@@ -14,6 +14,7 @@
 BLOCK = 512
 PART = 128
 SLICE = 64
+PIECE = 16
 AXES = ("rows", "rep")
 
 
@@ -258,38 +259,50 @@
         own[k * PART : (k + 1) * PART, :] = total[at(me["z"] ^ k, PART), :]
 
 
-def to_z_body(k, own, got, to):
-    to[...] = (own[k * PART : (k + 1) * PART, :] + got[0:PART, :].astype(F32)).astype(BF)
-
-
-def to_z3_body(own, got, to):
-    to_z_body(3, own, got, to)
-
-
-def to_z2_body(own, got, earlier, to):
-    to_z_body(2, own, got, to)
-
-
-def to_z1_body(own, got, got_own, share, earlier, to, kept, total):
-    to_z_body(1, own, got, to)
-    kept[...] = own[0:PART, :] + got_own[...].astype(F32)
-    total[...] = share[...].astype(F32) + earlier[PART:, :].astype(F32)
-
-
-def after_z_body(kept, r1, r2, r3, mine, got, to_v, share):
-    total = kept[...] + r1[...].astype(F32)
-    to_v[...] = total + (r2[...].astype(F32) + r3[...].astype(F32))
-    share[...] = mine[...] + got[...]
-
-
-def after_v_body(one, two, mine, got, piece, share):
-    piece[...] = (one[...] + two[...]).astype(BF)
-    share[...] = mine[...] + got[...]
-
-
-def last_body(piece, mine, got, message):
+def to_z_body(k, own, got, share, earlier, to, pair):
+    me = place()
+    to[0:PART, :] = (own[k * PART : (k + 1) * PART, :] + got[0:PART, :].astype(F32)).astype(BF)
+    pair[...] = share[...].astype(F32) + earlier[PART:, :].astype(F32)
+    to[PART:, :] = pair[at(me["z"] ^ k, PIECE), :].astype(BF)
+
+
+def to_z3_body(own, share, earlier, to, pair):
+    to_z_body(3, own, earlier, share, earlier, to, pair)
+
+
+def to_z2_body(own, got, share, earlier, to, pair):
+    to_z_body(2, own, got, share, earlier, to, pair)
+
+
+def to_z1_body(own, got, got_own, share, earlier, to, kept, pair):
+    to_z_body(1, own, got, share, earlier, to, pair)
+    kept[0:PART, :] = own[0:PART, :] + got_own[...].astype(F32)
+    kept[PART:, :] = pair[at(place()["z"], PIECE), :]
+
+
+def after_z_body(kept, r1, r2, r3, to_v):
+    total = kept[...] + r1[...].astype(F32) + (r2[...].astype(F32) + r3[...].astype(F32))
+    to_v[0:PART, :] = total[:PART].astype(BF)
+    high, low = split(total[PART:])
+    to_v[PART : PART + PIECE, :] = high
+    to_v[PART + PIECE :, :] = low
+
+
+def after_v_body(one, two, piece, share):
+    piece[...] = (one[0:PART, :].astype(F32) + two[0:PART, :].astype(F32)).astype(BF)
+    parts = [ref[PART : PART + PIECE, :].astype(F32) + ref[PART + PIECE :, :].astype(F32) for ref in (one, two)]
+    high, low = split(parts[0] + parts[1])
+    share[0:PIECE, :] = high
+    share[PIECE:, :] = low
+
+
+def last_body(piece, s0, s3, s2, s1, message):
+    me = place()
     message[0:PART, :] = piece[...]
-    put_split(message, PART, mine[...] + got[...])
+    for k, share in enumerate((s0, s1, s2, s3)):
+        for half in range(2):
+            start = pl.multiple_of(PART + half * SLICE + (me["z"] ^ k) * PIECE, PIECE)
+            message[pl.ds(start, PIECE), :] = share[half * PIECE : (half + 1) * PIECE, :]
 
 
 def finish_body(m0, m2, m3, m1, grad_features, grad_weight):
@@ -345,15 +358,17 @@
     u3, u2, u1, u0 = [send(value, FLIP_U) for value in to_u]
     to_c, keep = call(kept_body, [block32, block32], dense_t, grad_agg)
     (own,) = call(after_c_body, [block32], keep, send(to_c, FLIP_C), scratch=[total])
-    (to3,) = call(to_z3_body, [part], own, u3)
-    (to2,) = call(to_z2_body, [part], own, u2, u3)
-    to1, kept, share = call(to_z1_body, [part, part32, share32], own, u1, u0, share, u3)
+    pair = [pltpu.VMEM((SLICE, WIDTH), F32)]
+    to_z = ((PART + PIECE, WIDTH), BF)
+    both32 = ((PART + PIECE, WIDTH), F32)
+    (to3,) = call(to_z3_body, [to_z], own, share, u3, scratch=pair)
+    (to2,) = call(to_z2_body, [to_z], own, u2, share, u3, scratch=pair)
+    to1, kept = call(to_z1_body, [to_z, both32], own, u1, u0, share, u3, scratch=pair)
     from_z = [send(value, route) for value, route in zip((to1, to2, to3), FLIP_Z)]
-    to_v, share = call(after_z_body, [part32, share32], kept, *from_z, share, send(share, FLIP_Z[0]))
-    piece, share = call(
-        after_v_body, [part, share32], to_v, send(to_v, FLIP_V), share, send(share, FLIP_Z[1])
-    )
-    (message,) = call(last_body, [two], send(piece, TO_ROW), share, send(share, FLIP_V))
+    (to_v,) = call(after_z_body, [((PART + 2 * PIECE, WIDTH), BF)], kept, *from_z)
+    piece, share = call(after_v_body, [part, ((2 * PIECE, WIDTH), BF)], to_v, send(to_v, FLIP_V))
+    shares = [share] + [send(share, route) for route in FLIP_Z[::-1]]
+    (message,) = call(last_body, [two], send(piece, TO_ROW), *shares)
     grad_features, grad_weight = call(finish_body, [block, ((WIDTH, WIDTH), F32)], message, *[send(message, route) for route in FAR_X])
     return output, grad_weight, grad_features
 

time: 99.3 us -> 98.2 us (0.989)
  transfers between devices with their start and end apart: 32 -> 32, of which waited for: 21 -> 19; matrix products, arithmetic and copies ran while one was open for 1% -> 1% of each run, Pallas kernels for 4% -> 4%
where the time goes in v11:
time: 98.2 us; the launch traced here: 98 us
  starting transfers between devices  53.2 us (54%)
  waiting for transfers between devices  34.6 us (35%)
  Pallas kernels  6.15 us (6%)
  local copies, waits for them, and re-layouts  3.32 us (3%)
    ppermute x32, starting transfers between devices, send(): return lax.ppermute(value, AXES, route)  53.2 us
    ppermute x32, waiting for transfers between devices, send(): return lax.ppermute(value, AXES, route)  34.6 us
    pallas_call x19, Pallas kernels, call(): pl.pallas_call(body, out_shape=[jax.ShapeDtypeStruct(shape, dtype) for sh...  6.15 us
    unnamed x11, local copies, waits for them, and re-layouts  3.32 us
  transfers between devices with their start and end apart: 32, of which 19 were waited for; matrix products, arithmetic and copies ran while one was open for 1% of the time, Pallas kernels for 4%

profile of v11, /device:TPU:32, one launch (start us, length us, event | category | flops | bytes accessed | tf_op | source)
XLA Modules:
  0.0 98.0 jit_solution(10259468795067791297)
XLA Ops:
  1.7 2.9 %collective-permute-start = (bf16[256,256]{1,0:T(8,128)(2,1)S(1)}, bf16[256,256]{1,0:T(8,128)(2,1)S(1)}, u32[]{:S(2)}, u32[]{:S(2)}) collective-permute-start(bf16[256,256]{1,0:T(8,128)(2,1)S(1)} %shard_map.85), channel_id=1, source_target_pairs={{2,0},{53,1},{69,2},{114,3},{129,4},{182,5},{199,6},{240,7},{10,8}... | collective-permute-start | bytes 393224 | tf_op jit(solution)/shard_map/ppermute | solution.py:89
  8.6 2.4 %collective-permute-start.4 = (bf16[256,256]{1,0:T(8,128)(2,1)S(1)}, bf16[256,256]{1,0:T(8,128)(2,1)S(1)}, u32[]{:S(2)}, u32[]{:S(2)}) collective-permute-start(bf16[256,256]{1,0:T(8,128)(2,1)S(1)} %collective-permute-done.a0), channel_id=1, source_target_pairs={{0,16},{1,17},{2,18},{3,19},{4,20},{5,21},{6,22},{7,23},{8,24},{9,... | collective-permute-start | bytes 393224 | tf_op jit(solution)/shard_map/ppermute | solution.py:89
  11.0 2.4 %collective-permute-done.1.b0 = bf16[256,256]{1,0:T(8,128)(2,1)S(1)} collective-permute-done((bf16[256,256]{1,0:T(8,128)(2,1)S(1)}, bf16[256,256]{1,0:T(8,128)(2,1)S(1)}, u32[]{:S(2)}, u32[]{:S(2)}) %collective-permute-start.1) | collective-permute-done | bytes 131104 | tf_op jit(solution)/shard_map/ppermute | solution.py:89
  13.4 4.7 %collective-permute-start.2 = (bf16[256,256]{1,0:T(8,128)(2,1)S(1)}, bf16[256,256]{1,0:T(8,128)(2,1)S(1)}, u32[]{:S(2)}, u32[]{:S(2)}) collective-permute-start(bf16[256,256]{1,0:T(8,128)(2,1)S(1)} %collective-permute-done.1.b0), channel_id=1, source_target_pairs={{0,16},{1,17},{2,18},{3,19},{4,20},{5,21},{6,22},{7,23},{8,24},{9,... | collective-permute-start | bytes 393224 | tf_op jit(solution)/shard_map/ppermute | solution.py:89
  18.6 2.8 %collective-permute-done.2.b2 = bf16[256,256]{1,0:T(8,128)(2,1)S(1)} collective-permute-done((bf16[256,256]{1,0:T(8,128)(2,1)S(1)}, bf16[256,256]{1,0:T(8,128)(2,1)S(1)}, u32[]{:S(2)}, u32[]{:S(2)}) %collective-permute-start.2) | collective-permute-done | bytes 131104 | tf_op jit(solution)/shard_map/ppermute | solution.py:89
  23.2 3.9 %collective-permute-start.10 = (bf16[128,256]{1,0:T(8,128)(2,1)S(1)}, bf16[128,256]{1,0:T(8,128)(2,1)S(1)}, u32[]{:S(2)}, u32[]{:S(2)}) collective-permute-start(bf16[128,256]{1,0:T(8,128)(2,1)S(1)} %get-tuple-element.40), channel_id=1, source_target_pairs={{0,4},{1,5},{2,6},{3,7},{4,0},{5,1},{6,2},{7,3},{8,12},{9,13},{10,... | collective-permute-start | bytes 196616 | tf_op jit(solution)/shard_map/ppermute | solution.py:89
  27.0 2.0 %collective-permute-start.8 = (bf16[128,256]{1,0:T(8,128)(2,1)S(1)}, bf16[128,256]{1,0:T(8,128)(2,1)S(1)}, u32[]{:S(2)}, u32[]{:S(2)}) collective-permute-start(bf16[128,256]{1,0:T(8,128)(2,1)S(1)} %get-tuple-element.38), channel_id=1, source_target_pairs={{0,6},{1,7},{2,4},{3,5},{4,2},{5,3},{6,0},{7,1},{8,14},{9,15},{10,... | collective-permute-start | bytes 196616 | tf_op jit(solution)/shard_map/ppermute | solution.py:89
  29.8 2.7 %collective-permute-done.8.r3 = bf16[128,256]{1,0:T(8,128)(2,1)S(1)} collective-permute-done((bf16[128,256]{1,0:T(8,128)(2,1)S(1)}, bf16[128,256]{1,0:T(8,128)(2,1)S(1)}, u32[]{:S(2)}, u32[]{:S(2)}) %collective-permute-start.8) | collective-permute-done | bytes 65568 | tf_op jit(solution)/shard_map/ppermute | solution.py:89
  33.5 7.0 %collective-permute-start.11 = (bf16[192,256]{1,0:T(8,128)(2,1)S(1)}, bf16[192,256]{1,0:T(8,128)(2,1)S(1)}, u32[]{:S(2)}, u32[]{:S(2)}) collective-permute-start(bf16[192,256]{1,0:T(8,128)(2,1)S(1)} %shard_map.89.mine), channel_id=1, source_target_pairs={{0,1},{1,0},{2,3},{3,2},{4,5},{5,4},{6,7},{7,6},{8,9},{9,8},{10,11... | collective-permute-start | bytes 294920 | tf_op jit(solution)/shard_map/ppermute | solution.py:89
  40.4 4.7 %collective-permute-done.11.got = bf16[192,256]{1,0:T(8,128)(2,1)S(1)} collective-permute-done((bf16[192,256]{1,0:T(8,128)(2,1)S(1)}, bf16[192,256]{1,0:T(8,128)(2,1)S(1)}, u32[]{:S(2)}, u32[]{:S(2)}) %collective-permute-start.11) | collective-permute-done | bytes 98336 | tf_op jit(solution)/shard_map/ppermute | solution.py:89
  45.6 1.4 %collective-permute-start.12 = (bf16[192,256]{1,0:T(8,128)(2,1)S(1)}, bf16[192,256]{1,0:T(8,128)(2,1)S(1)}, u32[]{:S(2)}, u32[]{:S(2)}) collective-permute-start(bf16[192,256]{1,0:T(8,128)(2,1)S(1)} %get-tuple-element.44), channel_id=1, source_target_pairs={{0,4},{1,5},{2,6},{3,7},{4,0},{5,1},{6,2},{7,3},{8,12},{9,13},{10,... | collective-permute-start | bytes 294920 | tf_op jit(solution)/shard_map/ppermute | solution.py:89
  49.1 3.3 %collective-permute-done.12.m2 = bf16[192,256]{1,0:T(8,128)(2,1)S(1)} collective-permute-done((bf16[192,256]{1,0:T(8,128)(2,1)S(1)}, bf16[192,256]{1,0:T(8,128)(2,1)S(1)}, u32[]{:S(2)}, u32[]{:S(2)}) %collective-permute-start.12) | collective-permute-done | bytes 98336 | tf_op jit(solution)/shard_map/ppermute | solution.py:89
  55.9 2.1 %collective-permute-start.19 = (bf16[192,256]{1,0:T(8,128)(2,1)S(1)}, bf16[192,256]{1,0:T(8,128)(2,1)S(1)}, u32[]{:S(2)}, u32[]{:S(2)}) collective-permute-start(bf16[192,256]{1,0:T(8,128)(2,1)S(1)} %get-tuple-element.55), channel_id=1, source_target_pairs={{0,16},{1,17},{2,18},{3,19},{4,20},{5,21},{6,22},{7,23},{8,24},{9,... | collective-permute-start | bytes 294920 | tf_op jit(solution)/shard_map/ppermute | solution.py:89
  58.1 1.9 %collective-permute-start.17 = (bf16[128,256]{1,0:T(8,128)(2,1)S(1)}, bf16[128,256]{1,0:T(8,128)(2,1)S(1)}, u32[]{:S(2)}, u32[]{:S(2)}) collective-permute-start(bf16[128,256]{1,0:T(8,128)(2,1)S(1)} %get-tuple-element.52), channel_id=1, source_target_pairs={{0,16},{1,17},{2,18},{3,19},{4,20},{5,21},{6,22},{7,23},{8,24},{9,... | collective-permute-start | bytes 196616 | tf_op jit(solution)/shard_map/ppermute | solution.py:89
  63.1 2.2 %collective-permute-start.22 = (bf16[144,256]{1,0:T(8,128)(2,1)S(1)}, bf16[144,256]{1,0:T(8,128)(2,1)S(1)}, u32[]{:S(2)}, u32[]{:S(2)}) collective-permute-start(bf16[144,256]{1,0:T(8,128)(2,1)S(1)} %shard_map.98), channel_id=1, source_target_pairs={{0,128},{1,129},{2,130},{3,131},{4,132},{5,133},{6,134},{7,135},{8... | collective-permute-start | bytes 221192 | tf_op jit(solution)/shard_map/ppermute | solution.py:89
  66.2 2.7 %collective-permute-done.23.r3 = bf16[144,256]{1,0:T(8,128)(2,1)S(1)} collective-permute-done((bf16[144,256]{1,0:T(8,128)(2,1)S(1)}, bf16[144,256]{1,0:T(8,128)(2,1)S(1)}, u32[]{:S(2)}, u32[]{:S(2)}) %collective-permute-start.23) | collective-permute-done | bytes 73760 | tf_op jit(solution)/shard_map/ppermute | solution.py:89
  69.9 3.0 %collective-permute-start.24 = (bf16[160,256]{1,0:T(8,128)(2,1)S(1)}, bf16[160,256]{1,0:T(8,128)(2,1)S(1)}, u32[]{:S(2)}, u32[]{:S(2)}) collective-permute-start(bf16[160,256]{1,0:T(8,128)(2,1)S(1)} %shard_map.100.one), channel_id=1, source_target_pairs={{0,48},{1,49},{2,50},{3,51},{4,52},{5,53},{6,54},{7,55},{8,56},{9,... | collective-permute-start | bytes 245768 | tf_op jit(solution)/shard_map/ppermute | solution.py:89
  72.8 2.8 %collective-permute-done.24.two = bf16[160,256]{1,0:T(8,128)(2,1)S(1)} collective-permute-done((bf16[160,256]{1,0:T(8,128)(2,1)S(1)}, bf16[160,256]{1,0:T(8,128)(2,1)S(1)}, u32[]{:S(2)}, u32[]{:S(2)}) %collective-permute-start.24) | collective-permute-done | bytes 81952 | tf_op jit(solution)/shard_map/ppermute | solution.py:89
  75.6 5.3 %collective-permute-start.25 = (bf16[128,256]{1,0:T(8,128)(2,1)S(1)}, bf16[128,256]{1,0:T(8,128)(2,1)S(1)}, u32[]{:S(2)}, u32[]{:S(2)}) collective-permute-start(bf16[128,256]{1,0:T(8,128)(2,1)S(1)} %get-tuple-element.59), channel_id=1, source_target_pairs={{0,1},{1,53},{2,65},{3,113},{4,129},{5,181},{6,195},{7,247},{8,9},... | collective-permute-start | bytes 196616 | tf_op jit(solution)/shard_map/ppermute | solution.py:89
  80.9 2.2 %collective-permute-start.26 = (bf16[32,256]{1,0:T(8,128)(2,1)S(1)}, bf16[32,256]{1,0:T(8,128)(2,1)S(1)}, u32[]{:S(2)}, u32[]{:S(2)}) collective-permute-start(bf16[32,256]{1,0:T(8,128)(2,1)S(1)} %get-tuple-element.60.s0), channel_id=1, source_target_pairs={{0,192},{1,193},{2,194},{3,195},{4,196},{5,197},{6,198},{7,199},{8... | collective-permute-start | bytes 49160 | tf_op jit(solution)/shard_map/ppermute | solution.py:89
  83.1 2.0 %collective-permute-start.27 = (bf16[32,256]{1,0:T(8,128)(2,1)S(1)}, bf16[32,256]{1,0:T(8,128)(2,1)S(1)}, u32[]{:S(2)}, u32[]{:S(2)}) collective-permute-start(bf16[32,256]{1,0:T(8,128)(2,1)S(1)} %get-tuple-element.60.s0), channel_id=1, source_target_pairs={{0,128},{1,129},{2,130},{3,131},{4,132},{5,133},{6,134},{7,135},{8... | collective-permute-start | bytes 49160 | tf_op jit(solution)/shard_map/ppermute | solution.py:89
  85.1 2.6 %collective-permute-done.27.s2 = bf16[32,256]{1,0:T(8,128)(2,1)S(1)} collective-permute-done((bf16[32,256]{1,0:T(8,128)(2,1)S(1)}, bf16[32,256]{1,0:T(8,128)(2,1)S(1)}, u32[]{:S(2)}, u32[]{:S(2)}) %collective-permute-start.27) | collective-permute-done | bytes 16416 | tf_op jit(solution)/shard_map/ppermute | solution.py:89
  90.1 2.1 %collective-permute-start.30 = (bf16[256,256]{1,0:T(8,128)(2,1)S(1)}, bf16[256,256]{1,0:T(8,128)(2,1)S(1)}, u32[]{:S(2)}, u32[]{:S(2)}) collective-permute-start(bf16[256,256]{1,0:T(8,128)(2,1)S(1)} %shard_map.102.m0), channel_id=1, source_target_pairs={{0,6},{1,7},{2,4},{3,5},{4,2},{5,3},{6,0},{7,1},{8,14},{9,15},{10,... | collective-permute-start | bytes 393224 | tf_op jit(solution)/shard_map/ppermute | solution.py:89
  93.2 2.3 %collective-permute-done.29.m2 = bf16[256,256]{1,0:T(8,128)(2,1)S(1)} collective-permute-done((bf16[256,256]{1,0:T(8,128)(2,1)S(1)}, bf16[256,256]{1,0:T(8,128)(2,1)S(1)}, u32[]{:S(2)}, u32[]{:S(2)}) %collective-permute-start.29) | collective-permute-done | bytes 131104 | tf_op jit(solution)/shard_map/ppermute | solution.py:89
  (70 shorter events, 25.8 us)
Async XLA Ops:
  1.7 6.6 %collective-permute-start = (bf16[256,256]{1,0:T(8,128)(2,1)S(1)}, bf16[256,256]{1,0:T(8,128)(2,1)S(1)}, u32[]{:S(2)}, u32[]{:S(2)}) collective-permute-start(bf16[256,256]{1,0:T(8,128)(2,1)S(1)} %shard_map.85), channel_id=1, source_target_pairs={{2,0},{53,1},{69,2},{114,3},{129,4},{182,5},{199,6},{240,7},{10,8}... | collective-permute-start | bytes 393224 | tf_op jit(solution)/shard_map/ppermute | solution.py:89
  8.4 5.1 %collective-permute-start.1 = (bf16[256,256]{1,0:T(8,128)(2,1)S(1)}, bf16[256,256]{1,0:T(8,128)(2,1)S(1)}, u32[]{:S(2)}, u32[]{:S(2)}) collective-permute-start(bf16[256,256]{1,0:T(8,128)(2,1)S(1)} %collective-permute-done.a0), channel_id=1, source_target_pairs={{0,64},{1,65},{2,66},{3,67},{4,68},{5,69},{6,70},{7,71},{8,72},{9,... | collective-permute-start | bytes 393224 | tf_op jit(solution)/shard_map/ppermute | solution.py:89
  8.6 10.0 %collective-permute-start.4 = (bf16[256,256]{1,0:T(8,128)(2,1)S(1)}, bf16[256,256]{1,0:T(8,128)(2,1)S(1)}, u32[]{:S(2)}, u32[]{:S(2)}) collective-permute-start(bf16[256,256]{1,0:T(8,128)(2,1)S(1)} %collective-permute-done.a0), channel_id=1, source_target_pairs={{0,16},{1,17},{2,18},{3,19},{4,20},{5,21},{6,22},{7,23},{8,24},{9,... | collective-permute-start | bytes 393224 | tf_op jit(solution)/shard_map/ppermute | solution.py:89
  13.4 8.0 %collective-permute-start.2 = (bf16[256,256]{1,0:T(8,128)(2,1)S(1)}, bf16[256,256]{1,0:T(8,128)(2,1)S(1)}, u32[]{:S(2)}, u32[]{:S(2)}) collective-permute-start(bf16[256,256]{1,0:T(8,128)(2,1)S(1)} %collective-permute-done.1.b0), channel_id=1, source_target_pairs={{0,16},{1,17},{2,18},{3,19},{4,20},{5,21},{6,22},{7,23},{8,24},{9,... | collective-permute-start | bytes 393224 | tf_op jit(solution)/shard_map/ppermute | solution.py:89
  23.2 6.6 %collective-permute-start.10 = (bf16[128,256]{1,0:T(8,128)(2,1)S(1)}, bf16[128,256]{1,0:T(8,128)(2,1)S(1)}, u32[]{:S(2)}, u32[]{:S(2)}) collective-permute-start(bf16[128,256]{1,0:T(8,128)(2,1)S(1)} %get-tuple-element.40), channel_id=1, source_target_pairs={{0,4},{1,5},{2,6},{3,7},{4,0},{5,1},{6,2},{7,3},{8,12},{9,13},{10,... | collective-permute-start | bytes 196616 | tf_op jit(solution)/shard_map/ppermute | solution.py:89
  27.0 5.5 %collective-permute-start.8 = (bf16[128,256]{1,0:T(8,128)(2,1)S(1)}, bf16[128,256]{1,0:T(8,128)(2,1)S(1)}, u32[]{:S(2)}, u32[]{:S(2)}) collective-permute-start(bf16[128,256]{1,0:T(8,128)(2,1)S(1)} %get-tuple-element.38), channel_id=1, source_target_pairs={{0,6},{1,7},{2,4},{3,5},{4,2},{5,3},{6,0},{7,1},{8,14},{9,15},{10,... | collective-permute-start | bytes 196616 | tf_op jit(solution)/shard_map/ppermute | solution.py:89
  33.5 11.7 %collective-permute-start.11 = (bf16[192,256]{1,0:T(8,128)(2,1)S(1)}, bf16[192,256]{1,0:T(8,128)(2,1)S(1)}, u32[]{:S(2)}, u32[]{:S(2)}) collective-permute-start(bf16[192,256]{1,0:T(8,128)(2,1)S(1)} %shard_map.89.mine), channel_id=1, source_target_pairs={{0,1},{1,0},{2,3},{3,2},{4,5},{5,4},{6,7},{7,6},{8,9},{9,8},{10,11... | collective-permute-start | bytes 294920 | tf_op jit(solution)/shard_map/ppermute | solution.py:89
  45.6 6.9 %collective-permute-start.12 = (bf16[192,256]{1,0:T(8,128)(2,1)S(1)}, bf16[192,256]{1,0:T(8,128)(2,1)S(1)}, u32[]{:S(2)}, u32[]{:S(2)}) collective-permute-start(bf16[192,256]{1,0:T(8,128)(2,1)S(1)} %get-tuple-element.44), channel_id=1, source_target_pairs={{0,4},{1,5},{2,6},{3,7},{4,0},{5,1},{6,2},{7,3},{8,12},{9,13},{10,... | collective-permute-start | bytes 294920 | tf_op jit(solution)/shard_map/ppermute | solution.py:89
  47.0 6.2 %collective-permute-start.13 = (bf16[192,256]{1,0:T(8,128)(2,1)S(1)}, bf16[192,256]{1,0:T(8,128)(2,1)S(1)}, u32[]{:S(2)}, u32[]{:S(2)}) collective-permute-start(bf16[192,256]{1,0:T(8,128)(2,1)S(1)} %get-tuple-element.45), channel_id=1, source_target_pairs={{0,6},{1,7},{2,4},{3,5},{4,2},{5,3},{6,0},{7,1},{8,14},{9,15},{10,... | collective-permute-start | bytes 294920 | tf_op jit(solution)/shard_map/ppermute | solution.py:89
  48.1 5.1 %collective-permute-start.14 = (bf16[192,256]{1,0:T(8,128)(2,1)S(1)}, bf16[192,256]{1,0:T(8,128)(2,1)S(1)}, u32[]{:S(2)}, u32[]{:S(2)}) collective-permute-start(bf16[192,256]{1,0:T(8,128)(2,1)S(1)} %get-tuple-element.46), channel_id=1, source_target_pairs={{0,2},{1,3},{2,0},{3,1},{4,6},{5,7},{6,4},{7,5},{8,10},{9,11},{10,... | collective-permute-start | bytes 294920 | tf_op jit(solution)/shard_map/ppermute | solution.py:89
  54.3 5.8 %collective-permute-start.15 = (f32[512,256]{1,0:T(8,128)S(1)}, f32[512,256]{1,0:T(8,128)S(1)}, u32[]{:S(2)}, u32[]{:S(2)}) collective-permute-start(f32[512,256]{1,0:T(8,128)S(1)} %get-tuple-element.50), channel_id=1, source_target_pairs={{0,8},{1,9},{2,10},{3,11},{4,12},{5,13},{6,14},{7,15},{8,0},{9,1},... | collective-permute-start | bytes 1572872 | tf_op jit(solution)/shard_map/ppermute | solution.py:89
  55.9 5.7 %collective-permute-start.19 = (bf16[192,256]{1,0:T(8,128)(2,1)S(1)}, bf16[192,256]{1,0:T(8,128)(2,1)S(1)}, u32[]{:S(2)}, u32[]{:S(2)}) collective-permute-start(bf16[192,256]{1,0:T(8,128)(2,1)S(1)} %get-tuple-element.55), channel_id=1, source_target_pairs={{0,16},{1,17},{2,18},{3,19},{4,20},{5,21},{6,22},{7,23},{8,24},{9,... | collective-permute-start | bytes 294920 | tf_op jit(solution)/shard_map/ppermute | solution.py:89
  58.0 5.0 %collective-permute-start.21 = (bf16[128,256]{1,0:T(8,128)(2,1)S(1)}, bf16[128,256]{1,0:T(8,128)(2,1)S(1)}, u32[]{:S(2)}, u32[]{:S(2)}) collective-permute-start(bf16[128,256]{1,0:T(8,128)(2,1)S(1)} %get-tuple-element.58), channel_id=1, source_target_pairs={{0,16},{1,17},{2,18},{3,19},{4,20},{5,21},{6,22},{7,23},{8,24},{9,... | collective-permute-start | bytes 196616 | tf_op jit(solution)/shard_map/ppermute | solution.py:89
  58.1 7.2 %collective-permute-start.17 = (bf16[128,256]{1,0:T(8,128)(2,1)S(1)}, bf16[128,256]{1,0:T(8,128)(2,1)S(1)}, u32[]{:S(2)}, u32[]{:S(2)}) collective-permute-start(bf16[128,256]{1,0:T(8,128)(2,1)S(1)} %get-tuple-element.52), channel_id=1, source_target_pairs={{0,16},{1,17},{2,18},{3,19},{4,20},{5,21},{6,22},{7,23},{8,24},{9,... | collective-permute-start | bytes 196616 | tf_op jit(solution)/shard_map/ppermute | solution.py:89
  60.0 5.3 %collective-permute-start.18 = (bf16[128,256]{1,0:T(8,128)(2,1)S(1)}, bf16[128,256]{1,0:T(8,128)(2,1)S(1)}, u32[]{:S(2)}, u32[]{:S(2)}) collective-permute-start(bf16[128,256]{1,0:T(8,128)(2,1)S(1)} %get-tuple-element.53), channel_id=1, source_target_pairs={{0,16},{1,17},{2,18},{3,19},{4,20},{5,21},{6,22},{7,23},{8,24},{9,... | collective-permute-start | bytes 196616 | tf_op jit(solution)/shard_map/ppermute | solution.py:89
  61.6 7.3 %collective-permute-start.23 = (bf16[144,256]{1,0:T(8,128)(2,1)S(1)}, bf16[144,256]{1,0:T(8,128)(2,1)S(1)}, u32[]{:S(2)}, u32[]{:S(2)}) collective-permute-start(bf16[144,256]{1,0:T(8,128)(2,1)S(1)} %shard_map.99), channel_id=1, source_target_pairs={{0,192},{1,193},{2,194},{3,195},{4,196},{5,197},{6,198},{7,199},{8... | collective-permute-start | bytes 221192 | tf_op jit(solution)/shard_map/ppermute | solution.py:89
  63.1 5.9 %collective-permute-start.22 = (bf16[144,256]{1,0:T(8,128)(2,1)S(1)}, bf16[144,256]{1,0:T(8,128)(2,1)S(1)}, u32[]{:S(2)}, u32[]{:S(2)}) collective-permute-start(bf16[144,256]{1,0:T(8,128)(2,1)S(1)} %shard_map.98), channel_id=1, source_target_pairs={{0,128},{1,129},{2,130},{3,131},{4,132},{5,133},{6,134},{7,135},{8... | collective-permute-start | bytes 221192 | tf_op jit(solution)/shard_map/ppermute | solution.py:89
  65.4 4.4 %collective-permute-start.20 = (bf16[144,256]{1,0:T(8,128)(2,1)S(1)}, bf16[144,256]{1,0:T(8,128)(2,1)S(1)}, u32[]{:S(2)}, u32[]{:S(2)}) collective-permute-start(bf16[144,256]{1,0:T(8,128)(2,1)S(1)} %get-tuple-element.57), channel_id=1, source_target_pairs={{0,64},{1,65},{2,66},{3,67},{4,68},{5,69},{6,70},{7,71},{8,72},{9,... | collective-permute-start | bytes 221192 | tf_op jit(solution)/shard_map/ppermute | solution.py:89
  69.9 5.7 %collective-permute-start.24 = (bf16[160,256]{1,0:T(8,128)(2,1)S(1)}, bf16[160,256]{1,0:T(8,128)(2,1)S(1)}, u32[]{:S(2)}, u32[]{:S(2)}) collective-permute-start(bf16[160,256]{1,0:T(8,128)(2,1)S(1)} %shard_map.100.one), channel_id=1, source_target_pairs={{0,48},{1,49},{2,50},{3,51},{4,52},{5,53},{6,54},{7,55},{8,56},{9,... | collective-permute-start | bytes 245768 | tf_op jit(solution)/shard_map/ppermute | solution.py:89
  75.6 13.2 %collective-permute-start.25 = (bf16[128,256]{1,0:T(8,128)(2,1)S(1)}, bf16[128,256]{1,0:T(8,128)(2,1)S(1)}, u32[]{:S(2)}, u32[]{:S(2)}) collective-permute-start(bf16[128,256]{1,0:T(8,128)(2,1)S(1)} %get-tuple-element.59), channel_id=1, source_target_pairs={{0,1},{1,53},{2,65},{3,113},{4,129},{5,181},{6,195},{7,247},{8,9},... | collective-permute-start | bytes 196616 | tf_op jit(solution)/shard_map/ppermute | solution.py:89
  83.1 4.6 %collective-permute-start.27 = (bf16[32,256]{1,0:T(8,128)(2,1)S(1)}, bf16[32,256]{1,0:T(8,128)(2,1)S(1)}, u32[]{:S(2)}, u32[]{:S(2)}) collective-permute-start(bf16[32,256]{1,0:T(8,128)(2,1)S(1)} %get-tuple-element.60.s0), channel_id=1, source_target_pairs={{0,128},{1,129},{2,130},{3,131},{4,132},{5,133},{6,134},{7,135},{8... | collective-permute-start | bytes 49160 | tf_op jit(solution)/shard_map/ppermute | solution.py:89
  88.9 6.6 %collective-permute-start.29 = (bf16[256,256]{1,0:T(8,128)(2,1)S(1)}, bf16[256,256]{1,0:T(8,128)(2,1)S(1)}, u32[]{:S(2)}, u32[]{:S(2)}) collective-permute-start(bf16[256,256]{1,0:T(8,128)(2,1)S(1)} %shard_map.102.m0), channel_id=1, source_target_pairs={{0,4},{1,5},{2,6},{3,7},{4,0},{5,1},{6,2},{7,3},{8,12},{9,13},{10,... | collective-permute-start | bytes 393224 | tf_op jit(solution)/shard_map/ppermute | solution.py:89
  90.1 6.7 %collective-permute-start.30 = (bf16[256,256]{1,0:T(8,128)(2,1)S(1)}, bf16[256,256]{1,0:T(8,128)(2,1)S(1)}, u32[]{:S(2)}, u32[]{:S(2)}) collective-permute-start(bf16[256,256]{1,0:T(8,128)(2,1)S(1)} %shard_map.102.m0), channel_id=1, source_target_pairs={{0,6},{1,7},{2,4},{3,5},{4,2},{5,3},{6,0},{7,1},{8,14},{9,15},{10,... | collective-permute-start | bytes 393224 | tf_op jit(solution)/shard_map/ppermute | solution.py:89
  92.2 5.0 %collective-permute-start.31 = (bf16[256,256]{1,0:T(8,128)(2,1)S(1)}, bf16[256,256]{1,0:T(8,128)(2,1)S(1)}, u32[]{:S(2)}, u32[]{:S(2)}) collective-permute-start(bf16[256,256]{1,0:T(8,128)(2,1)S(1)} %shard_map.102.m0), channel_id=1, source_target_pairs={{0,2},{1,3},{2,0},{3,1},{4,6},{5,7},{6,4},{7,5},{8,10},{9,11},{10,... | collective-permute-start | bytes 393224 | tf_op jit(solution)/shard_map/ppermute | solution.py:89
  (13 other events, 62.9 us)

commit v12 on v11

--- a/solution.py
+++ b/solution.py
@@ -228,9 +228,9 @@
         grad_pre[at(me["x"] ^ k, PART), :] = m[0:PART, :]
     grad = dot(grad_pre[...], weight[...], ((1,), (1,))).astype(BF)
     grad_agg[...] = grad
-    to_c[0:BLOCK, :] = dot(dense_t[3], grad)
+    to_c[0:BLOCK, :] = dot(dense_t[3], grad).astype(BF)
     total = share[...] + m1[PART:, :].astype(F32)
-    to_c[BLOCK:, :] = total + (m2[PART:, :].astype(F32) + m3[PART:, :].astype(F32))
+    put_split(to_c, BLOCK, total + (m2[PART:, :].astype(F32) + m3[PART:, :].astype(F32)))
 
 
 def keep_body(dense_t, grad_agg, keep):
@@ -241,20 +241,20 @@
     me = place()
     for k, out in ((3, u3), (2, u2), (1, u1), (0, u0)):
         rows = at(me["z"] ^ k, PART)
-        out[0:PART, :] = (keep[rows, :] + got[rows, :]).astype(BF)
-    both = (mine[BLOCK:, :] + got[BLOCK:, :]).astype(BF)
+        out[0:PART, :] = (keep[rows, :] + got[rows, :].astype(F32)).astype(BF)
+    both = (get_split(mine, BLOCK) + get_split(got, BLOCK)).astype(BF)
     u3[PART:, :] = both
     share[...] = both
 
 
 def kept_body(dense_t, grad_agg, to_c, keep):
-    to_c[...] = dot(dense_t[1], grad_agg[...])
+    to_c[...] = dot(dense_t[1], grad_agg[...]).astype(BF)
     keep[...] = dot(dense_t[0], grad_agg[...])
 
 
 def after_c_body(keep, got, own, total):
     me = place()
-    total[...] = keep[...] + got[...]
+    total[...] = keep[...] + got[...].astype(F32)
     for k in range(4):
         own[k * PART : (k + 1) * PART, :] = total[at(me["z"] ^ k, PART), :]
 
@@ -349,14 +349,14 @@
     (output,) = call(output_body, [((SLICE, WIDTH), BF)], aggregate, weight)
     got = [send(value, route) for value, route in zip(to, FAR_X)]
     to_c, grad_agg = call(
-        backward_body, [((BLOCK + SLICE, WIDTH), F32), block], dense_t, weight, own, *got, share,
+        backward_body, [((BLOCK + 2 * SLICE, WIDTH), BF), block], dense_t, weight, own, *got, share,
         scratch=[pltpu.VMEM((BLOCK, WIDTH), BF)],
     )
     got = send(to_c, FLIP_C)
     (keep_u,) = call(keep_body, [block32], dense_t, grad_agg)
     *to_u, share = call(to_u_body, [to_z, part, part, part, share16], keep_u, to_c, got)
     u3, u2, u1, u0 = [send(value, FLIP_U) for value in to_u]
-    to_c, keep = call(kept_body, [block32, block32], dense_t, grad_agg)
+    to_c, keep = call(kept_body, [block, block32], dense_t, grad_agg)
     (own,) = call(after_c_body, [block32], keep, send(to_c, FLIP_C), scratch=[total])
     pair = [pltpu.VMEM((SLICE, WIDTH), F32)]
     to_z = ((PART + PIECE, WIDTH), BF)

time: 98.2 us -> 97.8 us (level)
  no operation moved by 1% of the time
where the time goes in v12:
time: 97.8 us; the launch traced here: 97.7 us
  starting transfers between devices  53.3 us (54%)
  waiting for transfers between devices  34.1 us (35%)
  Pallas kernels  6.09 us (6%)
  local copies, waits for them, and re-layouts  3.32 us (3%)
    ppermute x32, starting transfers between devices, send(): return lax.ppermute(value, AXES, route)  53.3 us
    ppermute x32, waiting for transfers between devices, send(): return lax.ppermute(value, AXES, route)  34.1 us
    pallas_call x19, Pallas kernels, call(): pl.pallas_call(body, out_shape=[jax.ShapeDtypeStruct(shape, dtype) for sh...  6.09 us
    unnamed x11, local copies, waits for them, and re-layouts  3.32 us
  transfers between devices with their start and end apart: 32, of which 19 were waited for; matrix products, arithmetic and copies ran while one was open for 1% of the time, Pallas kernels for 4%

profile of v12, /device:TPU:32, one launch (start us, length us, event | category | flops | bytes accessed | tf_op | source)
XLA Modules:
  0.0 97.7 jit_solution(11039170327487122646)
XLA Ops:
  1.7 2.9 %collective-permute-start = (bf16[256,256]{1,0:T(8,128)(2,1)S(1)}, bf16[256,256]{1,0:T(8,128)(2,1)S(1)}, u32[]{:S(2)}, u32[]{:S(2)}) collective-permute-start(bf16[256,256]{1,0:T(8,128)(2,1)S(1)} %shard_map.85), channel_id=1, source_target_pairs={{2,0},{53,1},{69,2},{114,3},{129,4},{182,5},{199,6},{240,7},{10,8}... | collective-permute-start | bytes 393224 | tf_op jit(solution)/shard_map/ppermute | solution.py:89
  8.6 2.4 %collective-permute-start.4 = (bf16[256,256]{1,0:T(8,128)(2,1)S(1)}, bf16[256,256]{1,0:T(8,128)(2,1)S(1)}, u32[]{:S(2)}, u32[]{:S(2)}) collective-permute-start(bf16[256,256]{1,0:T(8,128)(2,1)S(1)} %collective-permute-done.a0), channel_id=1, source_target_pairs={{0,16},{1,17},{2,18},{3,19},{4,20},{5,21},{6,22},{7,23},{8,24},{9,... | collective-permute-start | bytes 393224 | tf_op jit(solution)/shard_map/ppermute | solution.py:89
  11.0 2.3 %collective-permute-done.1.b0 = bf16[256,256]{1,0:T(8,128)(2,1)S(1)} collective-permute-done((bf16[256,256]{1,0:T(8,128)(2,1)S(1)}, bf16[256,256]{1,0:T(8,128)(2,1)S(1)}, u32[]{:S(2)}, u32[]{:S(2)}) %collective-permute-start.1) | collective-permute-done | bytes 131104 | tf_op jit(solution)/shard_map/ppermute | solution.py:89
  13.3 4.8 %collective-permute-start.2 = (bf16[256,256]{1,0:T(8,128)(2,1)S(1)}, bf16[256,256]{1,0:T(8,128)(2,1)S(1)}, u32[]{:S(2)}, u32[]{:S(2)}) collective-permute-start(bf16[256,256]{1,0:T(8,128)(2,1)S(1)} %collective-permute-done.1.b0), channel_id=1, source_target_pairs={{0,16},{1,17},{2,18},{3,19},{4,20},{5,21},{6,22},{7,23},{8,24},{9,... | collective-permute-start | bytes 393224 | tf_op jit(solution)/shard_map/ppermute | solution.py:89
  18.6 2.8 %collective-permute-done.2.b2 = bf16[256,256]{1,0:T(8,128)(2,1)S(1)} collective-permute-done((bf16[256,256]{1,0:T(8,128)(2,1)S(1)}, bf16[256,256]{1,0:T(8,128)(2,1)S(1)}, u32[]{:S(2)}, u32[]{:S(2)}) %collective-permute-start.2) | collective-permute-done | bytes 131104 | tf_op jit(solution)/shard_map/ppermute | solution.py:89
  23.2 3.9 %collective-permute-start.10 = (bf16[128,256]{1,0:T(8,128)(2,1)S(1)}, bf16[128,256]{1,0:T(8,128)(2,1)S(1)}, u32[]{:S(2)}, u32[]{:S(2)}) collective-permute-start(bf16[128,256]{1,0:T(8,128)(2,1)S(1)} %get-tuple-element.40), channel_id=1, source_target_pairs={{0,4},{1,5},{2,6},{3,7},{4,0},{5,1},{6,2},{7,3},{8,12},{9,13},{10,... | collective-permute-start | bytes 196616 | tf_op jit(solution)/shard_map/ppermute | solution.py:89
  27.0 2.0 %collective-permute-start.8 = (bf16[128,256]{1,0:T(8,128)(2,1)S(1)}, bf16[128,256]{1,0:T(8,128)(2,1)S(1)}, u32[]{:S(2)}, u32[]{:S(2)}) collective-permute-start(bf16[128,256]{1,0:T(8,128)(2,1)S(1)} %get-tuple-element.38), channel_id=1, source_target_pairs={{0,6},{1,7},{2,4},{3,5},{4,2},{5,3},{6,0},{7,1},{8,14},{9,15},{10,... | collective-permute-start | bytes 196616 | tf_op jit(solution)/shard_map/ppermute | solution.py:89
  29.8 2.7 %collective-permute-done.8.r3 = bf16[128,256]{1,0:T(8,128)(2,1)S(1)} collective-permute-done((bf16[128,256]{1,0:T(8,128)(2,1)S(1)}, bf16[128,256]{1,0:T(8,128)(2,1)S(1)}, u32[]{:S(2)}, u32[]{:S(2)}) %collective-permute-start.8) | collective-permute-done | bytes 65568 | tf_op jit(solution)/shard_map/ppermute | solution.py:89
  33.5 7.0 %collective-permute-start.11 = (bf16[192,256]{1,0:T(8,128)(2,1)S(1)}, bf16[192,256]{1,0:T(8,128)(2,1)S(1)}, u32[]{:S(2)}, u32[]{:S(2)}) collective-permute-start(bf16[192,256]{1,0:T(8,128)(2,1)S(1)} %shard_map.89.mine), channel_id=1, source_target_pairs={{0,1},{1,0},{2,3},{3,2},{4,5},{5,4},{6,7},{7,6},{8,9},{9,8},{10,11... | collective-permute-start | bytes 294920 | tf_op jit(solution)/shard_map/ppermute | solution.py:89
  40.4 4.7 %collective-permute-done.11.got = bf16[192,256]{1,0:T(8,128)(2,1)S(1)} collective-permute-done((bf16[192,256]{1,0:T(8,128)(2,1)S(1)}, bf16[192,256]{1,0:T(8,128)(2,1)S(1)}, u32[]{:S(2)}, u32[]{:S(2)}) %collective-permute-start.11) | collective-permute-done | bytes 98336 | tf_op jit(solution)/shard_map/ppermute | solution.py:89
  45.6 1.4 %collective-permute-start.12 = (bf16[192,256]{1,0:T(8,128)(2,1)S(1)}, bf16[192,256]{1,0:T(8,128)(2,1)S(1)}, u32[]{:S(2)}, u32[]{:S(2)}) collective-permute-start(bf16[192,256]{1,0:T(8,128)(2,1)S(1)} %get-tuple-element.44), channel_id=1, source_target_pairs={{0,4},{1,5},{2,6},{3,7},{4,0},{5,1},{6,2},{7,3},{8,12},{9,13},{10,... | collective-permute-start | bytes 294920 | tf_op jit(solution)/shard_map/ppermute | solution.py:89
  49.1 3.3 %collective-permute-done.12.m2 = bf16[192,256]{1,0:T(8,128)(2,1)S(1)} collective-permute-done((bf16[192,256]{1,0:T(8,128)(2,1)S(1)}, bf16[192,256]{1,0:T(8,128)(2,1)S(1)}, u32[]{:S(2)}, u32[]{:S(2)}) %collective-permute-start.12) | collective-permute-done | bytes 98336 | tf_op jit(solution)/shard_map/ppermute | solution.py:89
  55.6 2.1 %collective-permute-start.19 = (bf16[192,256]{1,0:T(8,128)(2,1)S(1)}, bf16[192,256]{1,0:T(8,128)(2,1)S(1)}, u32[]{:S(2)}, u32[]{:S(2)}) collective-permute-start(bf16[192,256]{1,0:T(8,128)(2,1)S(1)} %get-tuple-element.55), channel_id=1, source_target_pairs={{0,16},{1,17},{2,18},{3,19},{4,20},{5,21},{6,22},{7,23},{8,24},{9,... | collective-permute-start | bytes 294920 | tf_op jit(solution)/shard_map/ppermute | solution.py:89
  57.8 1.9 %collective-permute-start.17 = (bf16[128,256]{1,0:T(8,128)(2,1)S(1)}, bf16[128,256]{1,0:T(8,128)(2,1)S(1)}, u32[]{:S(2)}, u32[]{:S(2)}) collective-permute-start(bf16[128,256]{1,0:T(8,128)(2,1)S(1)} %get-tuple-element.52), channel_id=1, source_target_pairs={{0,16},{1,17},{2,18},{3,19},{4,20},{5,21},{6,22},{7,23},{8,24},{9,... | collective-permute-start | bytes 196616 | tf_op jit(solution)/shard_map/ppermute | solution.py:89
  62.7 2.2 %collective-permute-start.22 = (bf16[144,256]{1,0:T(8,128)(2,1)S(1)}, bf16[144,256]{1,0:T(8,128)(2,1)S(1)}, u32[]{:S(2)}, u32[]{:S(2)}) collective-permute-start(bf16[144,256]{1,0:T(8,128)(2,1)S(1)} %shard_map.98), channel_id=1, source_target_pairs={{0,128},{1,129},{2,130},{3,131},{4,132},{5,133},{6,134},{7,135},{8... | collective-permute-start | bytes 221192 | tf_op jit(solution)/shard_map/ppermute | solution.py:89
  65.8 2.8 %collective-permute-done.23.r3 = bf16[144,256]{1,0:T(8,128)(2,1)S(1)} collective-permute-done((bf16[144,256]{1,0:T(8,128)(2,1)S(1)}, bf16[144,256]{1,0:T(8,128)(2,1)S(1)}, u32[]{:S(2)}, u32[]{:S(2)}) %collective-permute-start.23) | collective-permute-done | bytes 73760 | tf_op jit(solution)/shard_map/ppermute | solution.py:89
  69.5 3.0 %collective-permute-start.24 = (bf16[160,256]{1,0:T(8,128)(2,1)S(1)}, bf16[160,256]{1,0:T(8,128)(2,1)S(1)}, u32[]{:S(2)}, u32[]{:S(2)}) collective-permute-start(bf16[160,256]{1,0:T(8,128)(2,1)S(1)} %shard_map.100.one), channel_id=1, source_target_pairs={{0,48},{1,49},{2,50},{3,51},{4,52},{5,53},{6,54},{7,55},{8,56},{9,... | collective-permute-start | bytes 245768 | tf_op jit(solution)/shard_map/ppermute | solution.py:89
  72.5 2.8 %collective-permute-done.24.two = bf16[160,256]{1,0:T(8,128)(2,1)S(1)} collective-permute-done((bf16[160,256]{1,0:T(8,128)(2,1)S(1)}, bf16[160,256]{1,0:T(8,128)(2,1)S(1)}, u32[]{:S(2)}, u32[]{:S(2)}) %collective-permute-start.24) | collective-permute-done | bytes 81952 | tf_op jit(solution)/shard_map/ppermute | solution.py:89
  75.2 5.3 %collective-permute-start.25 = (bf16[128,256]{1,0:T(8,128)(2,1)S(1)}, bf16[128,256]{1,0:T(8,128)(2,1)S(1)}, u32[]{:S(2)}, u32[]{:S(2)}) collective-permute-start(bf16[128,256]{1,0:T(8,128)(2,1)S(1)} %get-tuple-element.59), channel_id=1, source_target_pairs={{0,1},{1,53},{2,65},{3,113},{4,129},{5,181},{6,195},{7,247},{8,9},... | collective-permute-start | bytes 196616 | tf_op jit(solution)/shard_map/ppermute | solution.py:89
  80.5 2.2 %collective-permute-start.26 = (bf16[32,256]{1,0:T(8,128)(2,1)S(1)}, bf16[32,256]{1,0:T(8,128)(2,1)S(1)}, u32[]{:S(2)}, u32[]{:S(2)}) collective-permute-start(bf16[32,256]{1,0:T(8,128)(2,1)S(1)} %get-tuple-element.60.s0), channel_id=1, source_target_pairs={{0,192},{1,193},{2,194},{3,195},{4,196},{5,197},{6,198},{7,199},{8... | collective-permute-start | bytes 49160 | tf_op jit(solution)/shard_map/ppermute | solution.py:89
  82.7 2.0 %collective-permute-start.27 = (bf16[32,256]{1,0:T(8,128)(2,1)S(1)}, bf16[32,256]{1,0:T(8,128)(2,1)S(1)}, u32[]{:S(2)}, u32[]{:S(2)}) collective-permute-start(bf16[32,256]{1,0:T(8,128)(2,1)S(1)} %get-tuple-element.60.s0), channel_id=1, source_target_pairs={{0,128},{1,129},{2,130},{3,131},{4,132},{5,133},{6,134},{7,135},{8... | collective-permute-start | bytes 49160 | tf_op jit(solution)/shard_map/ppermute | solution.py:89
  84.7 2.6 %collective-permute-done.27.s2 = bf16[32,256]{1,0:T(8,128)(2,1)S(1)} collective-permute-done((bf16[32,256]{1,0:T(8,128)(2,1)S(1)}, bf16[32,256]{1,0:T(8,128)(2,1)S(1)}, u32[]{:S(2)}, u32[]{:S(2)}) %collective-permute-start.27) | collective-permute-done | bytes 16416 | tf_op jit(solution)/shard_map/ppermute | solution.py:89
  89.7 2.1 %collective-permute-start.30 = (bf16[256,256]{1,0:T(8,128)(2,1)S(1)}, bf16[256,256]{1,0:T(8,128)(2,1)S(1)}, u32[]{:S(2)}, u32[]{:S(2)}) collective-permute-start(bf16[256,256]{1,0:T(8,128)(2,1)S(1)} %shard_map.102.m0), channel_id=1, source_target_pairs={{0,6},{1,7},{2,4},{3,5},{4,2},{5,3},{6,0},{7,1},{8,14},{9,15},{10,... | collective-permute-start | bytes 393224 | tf_op jit(solution)/shard_map/ppermute | solution.py:89
  92.9 2.3 %collective-permute-done.29.m2 = bf16[256,256]{1,0:T(8,128)(2,1)S(1)} collective-permute-done((bf16[256,256]{1,0:T(8,128)(2,1)S(1)}, bf16[256,256]{1,0:T(8,128)(2,1)S(1)}, u32[]{:S(2)}, u32[]{:S(2)}) %collective-permute-start.29) | collective-permute-done | bytes 131104 | tf_op jit(solution)/shard_map/ppermute | solution.py:89
  (70 shorter events, 25.4 us)
Async XLA Ops:
  1.7 6.5 %collective-permute-start = (bf16[256,256]{1,0:T(8,128)(2,1)S(1)}, bf16[256,256]{1,0:T(8,128)(2,1)S(1)}, u32[]{:S(2)}, u32[]{:S(2)}) collective-permute-start(bf16[256,256]{1,0:T(8,128)(2,1)S(1)} %shard_map.85), channel_id=1, source_target_pairs={{2,0},{53,1},{69,2},{114,3},{129,4},{182,5},{199,6},{240,7},{10,8}... | collective-permute-start | bytes 393224 | tf_op jit(solution)/shard_map/ppermute | solution.py:89
  8.3 5.1 %collective-permute-start.1 = (bf16[256,256]{1,0:T(8,128)(2,1)S(1)}, bf16[256,256]{1,0:T(8,128)(2,1)S(1)}, u32[]{:S(2)}, u32[]{:S(2)}) collective-permute-start(bf16[256,256]{1,0:T(8,128)(2,1)S(1)} %collective-permute-done.a0), channel_id=1, source_target_pairs={{0,64},{1,65},{2,66},{3,67},{4,68},{5,69},{6,70},{7,71},{8,72},{9,... | collective-permute-start | bytes 393224 | tf_op jit(solution)/shard_map/ppermute | solution.py:89
  8.6 10.0 %collective-permute-start.4 = (bf16[256,256]{1,0:T(8,128)(2,1)S(1)}, bf16[256,256]{1,0:T(8,128)(2,1)S(1)}, u32[]{:S(2)}, u32[]{:S(2)}) collective-permute-start(bf16[256,256]{1,0:T(8,128)(2,1)S(1)} %collective-permute-done.a0), channel_id=1, source_target_pairs={{0,16},{1,17},{2,18},{3,19},{4,20},{5,21},{6,22},{7,23},{8,24},{9,... | collective-permute-start | bytes 393224 | tf_op jit(solution)/shard_map/ppermute | solution.py:89
  13.3 8.1 %collective-permute-start.2 = (bf16[256,256]{1,0:T(8,128)(2,1)S(1)}, bf16[256,256]{1,0:T(8,128)(2,1)S(1)}, u32[]{:S(2)}, u32[]{:S(2)}) collective-permute-start(bf16[256,256]{1,0:T(8,128)(2,1)S(1)} %collective-permute-done.1.b0), channel_id=1, source_target_pairs={{0,16},{1,17},{2,18},{3,19},{4,20},{5,21},{6,22},{7,23},{8,24},{9,... | collective-permute-start | bytes 393224 | tf_op jit(solution)/shard_map/ppermute | solution.py:89
  23.2 6.6 %collective-permute-start.10 = (bf16[128,256]{1,0:T(8,128)(2,1)S(1)}, bf16[128,256]{1,0:T(8,128)(2,1)S(1)}, u32[]{:S(2)}, u32[]{:S(2)}) collective-permute-start(bf16[128,256]{1,0:T(8,128)(2,1)S(1)} %get-tuple-element.40), channel_id=1, source_target_pairs={{0,4},{1,5},{2,6},{3,7},{4,0},{5,1},{6,2},{7,3},{8,12},{9,13},{10,... | collective-permute-start | bytes 196616 | tf_op jit(solution)/shard_map/ppermute | solution.py:89
  27.0 5.5 %collective-permute-start.8 = (bf16[128,256]{1,0:T(8,128)(2,1)S(1)}, bf16[128,256]{1,0:T(8,128)(2,1)S(1)}, u32[]{:S(2)}, u32[]{:S(2)}) collective-permute-start(bf16[128,256]{1,0:T(8,128)(2,1)S(1)} %get-tuple-element.38), channel_id=1, source_target_pairs={{0,6},{1,7},{2,4},{3,5},{4,2},{5,3},{6,0},{7,1},{8,14},{9,15},{10,... | collective-permute-start | bytes 196616 | tf_op jit(solution)/shard_map/ppermute | solution.py:89
  33.5 11.7 %collective-permute-start.11 = (bf16[192,256]{1,0:T(8,128)(2,1)S(1)}, bf16[192,256]{1,0:T(8,128)(2,1)S(1)}, u32[]{:S(2)}, u32[]{:S(2)}) collective-permute-start(bf16[192,256]{1,0:T(8,128)(2,1)S(1)} %shard_map.89.mine), channel_id=1, source_target_pairs={{0,1},{1,0},{2,3},{3,2},{4,5},{5,4},{6,7},{7,6},{8,9},{9,8},{10,11... | collective-permute-start | bytes 294920 | tf_op jit(solution)/shard_map/ppermute | solution.py:89
  45.6 6.9 %collective-permute-start.12 = (bf16[192,256]{1,0:T(8,128)(2,1)S(1)}, bf16[192,256]{1,0:T(8,128)(2,1)S(1)}, u32[]{:S(2)}, u32[]{:S(2)}) collective-permute-start(bf16[192,256]{1,0:T(8,128)(2,1)S(1)} %get-tuple-element.44), channel_id=1, source_target_pairs={{0,4},{1,5},{2,6},{3,7},{4,0},{5,1},{6,2},{7,3},{8,12},{9,13},{10,... | collective-permute-start | bytes 294920 | tf_op jit(solution)/shard_map/ppermute | solution.py:89
  47.0 6.2 %collective-permute-start.13 = (bf16[192,256]{1,0:T(8,128)(2,1)S(1)}, bf16[192,256]{1,0:T(8,128)(2,1)S(1)}, u32[]{:S(2)}, u32[]{:S(2)}) collective-permute-start(bf16[192,256]{1,0:T(8,128)(2,1)S(1)} %get-tuple-element.45), channel_id=1, source_target_pairs={{0,6},{1,7},{2,4},{3,5},{4,2},{5,3},{6,0},{7,1},{8,14},{9,15},{10,... | collective-permute-start | bytes 294920 | tf_op jit(solution)/shard_map/ppermute | solution.py:89
  48.1 5.1 %collective-permute-start.14 = (bf16[192,256]{1,0:T(8,128)(2,1)S(1)}, bf16[192,256]{1,0:T(8,128)(2,1)S(1)}, u32[]{:S(2)}, u32[]{:S(2)}) collective-permute-start(bf16[192,256]{1,0:T(8,128)(2,1)S(1)} %get-tuple-element.46), channel_id=1, source_target_pairs={{0,2},{1,3},{2,0},{3,1},{4,6},{5,7},{6,4},{7,5},{8,10},{9,11},{10,... | collective-permute-start | bytes 294920 | tf_op jit(solution)/shard_map/ppermute | solution.py:89
  54.3 5.5 %collective-permute-start.15 = (bf16[512,256]{1,0:T(8,128)(2,1)S(1)}, bf16[512,256]{1,0:T(8,128)(2,1)S(1)}, u32[]{:S(2)}, u32[]{:S(2)}) collective-permute-start(bf16[512,256]{1,0:T(8,128)(2,1)S(1)} %get-tuple-element.50), channel_id=1, source_target_pairs={{0,8},{1,9},{2,10},{3,11},{4,12},{5,13},{6,14},{7,15},{8,0},{9,1},... | collective-permute-start | bytes 786440 | tf_op jit(solution)/shard_map/ppermute | solution.py:89
  55.6 5.7 %collective-permute-start.19 = (bf16[192,256]{1,0:T(8,128)(2,1)S(1)}, bf16[192,256]{1,0:T(8,128)(2,1)S(1)}, u32[]{:S(2)}, u32[]{:S(2)}) collective-permute-start(bf16[192,256]{1,0:T(8,128)(2,1)S(1)} %get-tuple-element.55), channel_id=1, source_target_pairs={{0,16},{1,17},{2,18},{3,19},{4,20},{5,21},{6,22},{7,23},{8,24},{9,... | collective-permute-start | bytes 294920 | tf_op jit(solution)/shard_map/ppermute | solution.py:89
  57.7 5.0 %collective-permute-start.21 = (bf16[128,256]{1,0:T(8,128)(2,1)S(1)}, bf16[128,256]{1,0:T(8,128)(2,1)S(1)}, u32[]{:S(2)}, u32[]{:S(2)}) collective-permute-start(bf16[128,256]{1,0:T(8,128)(2,1)S(1)} %get-tuple-element.58), channel_id=1, source_target_pairs={{0,16},{1,17},{2,18},{3,19},{4,20},{5,21},{6,22},{7,23},{8,24},{9,... | collective-permute-start | bytes 196616 | tf_op jit(solution)/shard_map/ppermute | solution.py:89
  57.8 7.2 %collective-permute-start.17 = (bf16[128,256]{1,0:T(8,128)(2,1)S(1)}, bf16[128,256]{1,0:T(8,128)(2,1)S(1)}, u32[]{:S(2)}, u32[]{:S(2)}) collective-permute-start(bf16[128,256]{1,0:T(8,128)(2,1)S(1)} %get-tuple-element.52), channel_id=1, source_target_pairs={{0,16},{1,17},{2,18},{3,19},{4,20},{5,21},{6,22},{7,23},{8,24},{9,... | collective-permute-start | bytes 196616 | tf_op jit(solution)/shard_map/ppermute | solution.py:89
  59.7 5.3 %collective-permute-start.18 = (bf16[128,256]{1,0:T(8,128)(2,1)S(1)}, bf16[128,256]{1,0:T(8,128)(2,1)S(1)}, u32[]{:S(2)}, u32[]{:S(2)}) collective-permute-start(bf16[128,256]{1,0:T(8,128)(2,1)S(1)} %get-tuple-element.53), channel_id=1, source_target_pairs={{0,16},{1,17},{2,18},{3,19},{4,20},{5,21},{6,22},{7,23},{8,24},{9,... | collective-permute-start | bytes 196616 | tf_op jit(solution)/shard_map/ppermute | solution.py:89
  61.3 7.3 %collective-permute-start.23 = (bf16[144,256]{1,0:T(8,128)(2,1)S(1)}, bf16[144,256]{1,0:T(8,128)(2,1)S(1)}, u32[]{:S(2)}, u32[]{:S(2)}) collective-permute-start(bf16[144,256]{1,0:T(8,128)(2,1)S(1)} %shard_map.99), channel_id=1, source_target_pairs={{0,192},{1,193},{2,194},{3,195},{4,196},{5,197},{6,198},{7,199},{8... | collective-permute-start | bytes 221192 | tf_op jit(solution)/shard_map/ppermute | solution.py:89
  62.7 5.9 %collective-permute-start.22 = (bf16[144,256]{1,0:T(8,128)(2,1)S(1)}, bf16[144,256]{1,0:T(8,128)(2,1)S(1)}, u32[]{:S(2)}, u32[]{:S(2)}) collective-permute-start(bf16[144,256]{1,0:T(8,128)(2,1)S(1)} %shard_map.98), channel_id=1, source_target_pairs={{0,128},{1,129},{2,130},{3,131},{4,132},{5,133},{6,134},{7,135},{8... | collective-permute-start | bytes 221192 | tf_op jit(solution)/shard_map/ppermute | solution.py:89
  65.0 4.4 %collective-permute-start.20 = (bf16[144,256]{1,0:T(8,128)(2,1)S(1)}, bf16[144,256]{1,0:T(8,128)(2,1)S(1)}, u32[]{:S(2)}, u32[]{:S(2)}) collective-permute-start(bf16[144,256]{1,0:T(8,128)(2,1)S(1)} %get-tuple-element.57), channel_id=1, source_target_pairs={{0,64},{1,65},{2,66},{3,67},{4,68},{5,69},{6,70},{7,71},{8,72},{9,... | collective-permute-start | bytes 221192 | tf_op jit(solution)/shard_map/ppermute | solution.py:89
  69.5 5.7 %collective-permute-start.24 = (bf16[160,256]{1,0:T(8,128)(2,1)S(1)}, bf16[160,256]{1,0:T(8,128)(2,1)S(1)}, u32[]{:S(2)}, u32[]{:S(2)}) collective-permute-start(bf16[160,256]{1,0:T(8,128)(2,1)S(1)} %shard_map.100.one), channel_id=1, source_target_pairs={{0,48},{1,49},{2,50},{3,51},{4,52},{5,53},{6,54},{7,55},{8,56},{9,... | collective-permute-start | bytes 245768 | tf_op jit(solution)/shard_map/ppermute | solution.py:89
  75.2 13.2 %collective-permute-start.25 = (bf16[128,256]{1,0:T(8,128)(2,1)S(1)}, bf16[128,256]{1,0:T(8,128)(2,1)S(1)}, u32[]{:S(2)}, u32[]{:S(2)}) collective-permute-start(bf16[128,256]{1,0:T(8,128)(2,1)S(1)} %get-tuple-element.59), channel_id=1, source_target_pairs={{0,1},{1,53},{2,65},{3,113},{4,129},{5,181},{6,195},{7,247},{8,9},... | collective-permute-start | bytes 196616 | tf_op jit(solution)/shard_map/ppermute | solution.py:89
  82.7 4.6 %collective-permute-start.27 = (bf16[32,256]{1,0:T(8,128)(2,1)S(1)}, bf16[32,256]{1,0:T(8,128)(2,1)S(1)}, u32[]{:S(2)}, u32[]{:S(2)}) collective-permute-start(bf16[32,256]{1,0:T(8,128)(2,1)S(1)} %get-tuple-element.60.s0), channel_id=1, source_target_pairs={{0,128},{1,129},{2,130},{3,131},{4,132},{5,133},{6,134},{7,135},{8... | collective-permute-start | bytes 49160 | tf_op jit(solution)/shard_map/ppermute | solution.py:89
  88.5 6.6 %collective-permute-start.29 = (bf16[256,256]{1,0:T(8,128)(2,1)S(1)}, bf16[256,256]{1,0:T(8,128)(2,1)S(1)}, u32[]{:S(2)}, u32[]{:S(2)}) collective-permute-start(bf16[256,256]{1,0:T(8,128)(2,1)S(1)} %shard_map.102.m0), channel_id=1, source_target_pairs={{0,4},{1,5},{2,6},{3,7},{4,0},{5,1},{6,2},{7,3},{8,12},{9,13},{10,... | collective-permute-start | bytes 393224 | tf_op jit(solution)/shard_map/ppermute | solution.py:89
  89.7 6.7 %collective-permute-start.30 = (bf16[256,256]{1,0:T(8,128)(2,1)S(1)}, bf16[256,256]{1,0:T(8,128)(2,1)S(1)}, u32[]{:S(2)}, u32[]{:S(2)}) collective-permute-start(bf16[256,256]{1,0:T(8,128)(2,1)S(1)} %shard_map.102.m0), channel_id=1, source_target_pairs={{0,6},{1,7},{2,4},{3,5},{4,2},{5,3},{6,0},{7,1},{8,14},{9,15},{10,... | collective-permute-start | bytes 393224 | tf_op jit(solution)/shard_map/ppermute | solution.py:89
  91.9 5.0 %collective-permute-start.31 = (bf16[256,256]{1,0:T(8,128)(2,1)S(1)}, bf16[256,256]{1,0:T(8,128)(2,1)S(1)}, u32[]{:S(2)}, u32[]{:S(2)}) collective-permute-start(bf16[256,256]{1,0:T(8,128)(2,1)S(1)} %shard_map.102.m0), channel_id=1, source_target_pairs={{0,2},{1,3},{2,0},{3,1},{4,6},{5,7},{6,4},{7,5},{8,10},{9,11},{10,... | collective-permute-start | bytes 393224 | tf_op jit(solution)/shard_map/ppermute | solution.py:89
  (13 other events, 62.6 us)
